TPU v7x, 32 devices: a whole 2x2x4 slice. The times are simulated.
32 devices in a mesh: section: 2 (over core), dp: 16 (over z, y, x).
Axes of the slice: x: 2, y: 2, z: 4, core: 2. Of those that a mesh axis runs over, the one named last changes fastest.
Arguments:
- boundary: bfloat16 [2, 16384, 768], P('section', 'dp'), may hold values from -6 to 6
- lengths: int32 [32, 4], P('dp'), may hold values from 32 to 384, as said below
- norm_one_gain: float32 [2, 768], P('section'), may hold values from 0.1 to 1.9
- norm_one_bias: float32 [2, 768], P('section'), may hold values from -3 to 3
- query_weight: bfloat16 [2, 768, 768], P('section'), may hold values from -0.21875 to 0.21875
- query_bias: float32 [2, 768], P('section'), may hold values from -3 to 3
- key_weight: bfloat16 [2, 768, 768], P('section'), may hold values from -0.21875 to 0.21875
- value_weight: bfloat16 [2, 768, 384], P('section'), may hold values from -0.21875 to 0.21875
- value_bias: float32 [2, 384], P('section'), may hold values from -3 to 3
- first_value_weight: bfloat16 [768, 384], replicated, may hold values from -0.21875 to 0.21875
- first_value_bias: float32 [384], replicated, may hold values from -3 to 3
- out_weight: bfloat16 [2, 768, 768], P('section'), may hold values from -0.875 to 0.875
- out_bias: float32 [2, 768], P('section'), may hold values from -3 to 3
- norm_two_gain: float32 [2, 768], P('section'), may hold values from 0.1 to 1.9
- norm_two_bias: float32 [2, 768], P('section'), may hold values from -3 to 3
- up_weight: bfloat16 [2, 768, 3072], P('section'), may hold values from -0.21875 to 0.21875
- up_bias: float32 [2, 3072], P('section'), may hold values from -3 to 3
- down_weight: bfloat16 [2, 3072, 768], P('section'), may hold values from -0.109375 to 0.109375
- down_bias: float32 [2, 768], P('section'), may hold values from -3 to 3
Outputs:
- block_ends: bfloat16 [2, 16384, 768], P('section', 'dp')
- norm_one_gain_grad: float32 [2, 768], P('section')
- norm_one_bias_grad: float32 [2, 768], P('section')
- query_weight_grad: float32 [2, 768, 768], P('section')
- query_bias_grad: float32 [2, 768], P('section')
- key_weight_grad: float32 [2, 768, 768], P('section')
- value_weight_grad: float32 [2, 768, 384], P('section')
- value_bias_grad: float32 [2, 384], P('section')
- first_value_weight_grad: float32 [768, 384], P('section')
- first_value_bias_grad: float32 [384], P('section')
- out_weight_grad: float32 [2, 768, 768], P('section')
- out_bias_grad: float32 [2, 768], P('section')
- norm_two_gain_grad: float32 [2, 768], P('section')
- norm_two_bias_grad: float32 [2, 768], P('section')
- up_weight_grad: float32 [2, 768, 3072], P('section')
- up_bias_grad: float32 [2, 3072], P('section')
- down_weight_grad: float32 [2, 3072, 768], P('section')
- down_bias_grad: float32 [2, 768], P('section')
Inputs may be any that keep to these rules, and one draw needn't show every extreme that they name: Row s holds, in order, the lengths of the 4 sequences that fill slot s of 512 tokens; in every row the longest is exactly 384.
All inputs are finite; a program needn't handle non-finite values.
Results may differ from a plain program's by a relative error of at most 0.017.
Values may be sent and summed in bfloat16 or wider, within the bound.
No kernel may reach another device: no remote copies, remote signals or barrier semaphores. Data moves between devices by JAX's collectives and lax.ppermute only.
A program may use at most 256 MiB of HBM per device.

v0:
```python
import jax
import jax.numpy as jnp
from jax import lax
from jax.sharding import PartitionSpec as P

HEADS = 12


eps_norm = 1e-05
neg_fill = -1e30


def passed_along(shard, axis, by):
    devices = lax.axis_size(axis)
    pairs = [(i, i + by) for i in range(devices) if 0 <= i + by < devices]
    return lax.ppermute(shard, axis, pairs)


def normed(rows_in, gain, bias):
    centre = jnp.mean(rows_in, axis=-1, keepdims=True)
    centred = rows_in - centre
    spread = jnp.mean(centred * centred, axis=-1, keepdims=True)
    return centred * lax.rsqrt(spread + eps_norm) * gain + bias


def smooth_gate(pre_active):
    return jax.nn.gelu(pre_active, approximate=True)


def dense_product(left, right):
    return jnp.dot(left, right, preferred_element_type=jnp.float32)


def dense_back(grad_rows, weight):
    return lax.dot_general(
        grad_rows, weight, (((1,), (1,)), ((), ())), preferred_element_type=jnp.float32
    )


def dense_outer(input_rows, grad_rows):
    return lax.dot_general(
        input_rows, grad_rows, (((0,), (0,)), ((), ())), preferred_element_type=jnp.float32
    )


def column_sum(grad_rows):
    return jnp.sum(grad_rows.astype(jnp.float32), axis=0)


def segment_ids(lengths_row, slot_rows):
    cut_points = jnp.cumsum(lengths_row)
    positions = jnp.arange(slot_rows, dtype=jnp.int32)
    segments = jnp.sum((positions[:, None] >= cut_points[None, :]).astype(jnp.int32), axis=1)
    return (segments, positions)


def block_scores(query_block, key_heads, segments, positions, score_scale):
    scores = (
        jnp.einsum("qhd,khd->hqk", query_block, key_heads, preferred_element_type=jnp.float32)
        * score_scale
    )
    allowed = (segments[:, None] == segments[None, :]) & (positions[None, :] <= positions[:, None])
    return jnp.where(allowed[None], scores, neg_fill)


def attend_forward(queries, key_rows, values, segments, positions):
    row_count = queries.shape[0]
    head_count = HEADS
    head_width = queries.shape[1] // head_count
    block_rows = min(512, row_count)
    score_scale = head_width ** (-0.5)
    query_heads = queries.reshape(row_count, head_count, head_width)
    key_heads = key_rows.reshape(row_count, head_count, head_width)
    value_heads = values.reshape(row_count, head_count, head_width)

    def one_block(block_index):
        scores = block_scores(query_heads, key_heads, segments, positions, score_scale)
        row_peak = jnp.max(scores, axis=-1, keepdims=True)
        exponent = jnp.exp(scores - row_peak)
        row_total = jnp.sum(exponent, axis=-1, keepdims=True)
        low_probs = (exponent / row_total).astype(jnp.bfloat16)
        mixed = jnp.einsum(
            "hqk,khd->qhd", low_probs, value_heads, preferred_element_type=jnp.float32
        )
        return (
            mixed.reshape(block_rows, head_count * head_width).astype(jnp.bfloat16),
            row_peak,
            row_total,
        )

    block_outputs, peaks, totals = lax.map(one_block, jnp.arange(row_count // block_rows))
    return (block_outputs.reshape(row_count, head_count * head_width), peaks, totals)


def attend_backward(queries, key_rows, values, segments, positions, peaks, totals, grad_out):
    row_count = queries.shape[0]
    head_count = HEADS
    head_width = queries.shape[1] // head_count
    block_rows = min(512, row_count)
    score_scale = head_width ** (-0.5)
    query_heads = queries.reshape(row_count, head_count, head_width)
    key_heads = key_rows.reshape(row_count, head_count, head_width)
    value_heads = values.reshape(row_count, head_count, head_width)
    grad_heads = grad_out.reshape(row_count, head_count, head_width)

    def one_block(carried, scan_item):
        grad_keys, grad_values = carried
        block_index, row_peak, row_total = scan_item
        scores = block_scores(query_heads, key_heads, segments, positions, score_scale)
        probability = jnp.exp(scores - row_peak) / row_total
        low_probs = probability.astype(jnp.bfloat16)
        grad_probs = jnp.einsum(
            "qhd,khd->hqk", grad_heads, value_heads, preferred_element_type=jnp.float32
        )
        grad_values = grad_values + jnp.einsum(
            "hqk,qhd->khd", low_probs, grad_heads, preferred_element_type=jnp.float32
        )
        grad_scores = probability * (
            grad_probs - jnp.sum(grad_probs * probability, axis=-1, keepdims=True)
        )
        low_scores = grad_scores.astype(jnp.bfloat16)
        grad_query = (
            jnp.einsum("hqk,khd->qhd", low_scores, key_heads, preferred_element_type=jnp.float32)
            * score_scale
        )
        grad_keys = (
            grad_keys
            + jnp.einsum(
                "hqk,qhd->khd", low_scores, query_heads, preferred_element_type=jnp.float32
            )
            * score_scale
        )
        return ((grad_keys, grad_values), grad_query.reshape(block_rows, head_count * head_width))

    zero_grad = jnp.zeros((row_count, head_count, head_width), jnp.float32)
    carried, grad_query = lax.scan(
        one_block, (zero_grad, zero_grad), (jnp.arange(row_count // block_rows), peaks, totals)
    )
    grad_keys, grad_values = carried
    return (
        grad_query.reshape(row_count, -1),
        grad_keys.reshape(row_count, -1),
        grad_values.reshape(row_count, -1),
    )


def empty_stored(slot_rows, model_width, inner_width):
    block_rows = min(512, slot_rows)
    plain = jnp.zeros((slot_rows, model_width), jnp.bfloat16)
    stats = jnp.zeros((slot_rows // block_rows, HEADS, block_rows, 1), jnp.float32)
    return (
        plain,
        plain,
        plain,
        plain,
        plain,
        plain,
        stats,
        stats,
        jnp.zeros((slot_rows, model_width), jnp.float32),
        plain,
        jnp.zeros((slot_rows, inner_width), jnp.float32),
        jnp.zeros((slot_rows, inner_width), jnp.bfloat16),
    )


def layer_forward(is_first, slot_input, reused, weights, first_pair, segments, positions):
    wide_input = slot_input.astype(jnp.float32)
    hidden = normed(wide_input, weights[0], weights[1]).astype(jnp.bfloat16)
    queries = (dense_product(hidden, weights[2]) + weights[3]).astype(jnp.bfloat16)
    key_rows = dense_product(hidden, weights[4]).astype(jnp.bfloat16)
    fresh_values = (dense_product(hidden, weights[5]) + weights[6]).astype(jnp.bfloat16)
    if is_first:
        shared = (dense_product(hidden, first_pair[0]) + first_pair[1]).astype(jnp.bfloat16)
    else:
        shared = reused
    values = jnp.concatenate([shared, fresh_values], axis=1)
    attended, peaks, totals = attend_forward(queries, key_rows, values, segments, positions)
    middle = wide_input + (dense_product(attended, weights[7]) + weights[8])
    second = normed(middle, weights[9], weights[10]).astype(jnp.bfloat16)
    pre_active = dense_product(second, weights[11]) + weights[12]
    active = smooth_gate(pre_active).astype(jnp.bfloat16)
    result = (middle + (dense_product(active, weights[13]) + weights[14])).astype(jnp.bfloat16)
    stored = (
        slot_input,
        hidden,
        queries,
        key_rows,
        values,
        attended,
        peaks,
        totals,
        middle,
        second,
        pre_active,
        active,
    )
    return (result, shared, stored)


def feed_backward(grad_result, stored, weights, feed_grads):
    middle, second, pre_active, active = (stored[8], stored[9], stored[10], stored[11])
    grad_active = dense_back(grad_result, weights[13])
    low_gate = jax.vjp(smooth_gate, pre_active)[1](grad_active)[0].astype(jnp.bfloat16)
    grad_second = dense_back(low_gate, weights[11])
    grad_middle, grad_gain, grad_bias = jax.vjp(normed, middle, weights[9], weights[10])[1](
        grad_second
    )
    grad_middle = grad_middle + grad_result.astype(jnp.float32)
    updated = (
        feed_grads[0] + grad_gain,
        feed_grads[1] + grad_bias,
        feed_grads[2] + dense_outer(second, low_gate),
        feed_grads[3] + column_sum(low_gate),
        feed_grads[4] + dense_outer(active, grad_result),
        feed_grads[5] + column_sum(grad_result),
    )
    return (grad_middle, updated)


def attention_backward(
    is_first,
    grad_middle,
    grad_shared_in,
    stored,
    weights,
    first_pair,
    segments,
    positions,
    attention_grads,
    first_grads,
):
    slot_input, hidden, queries, key_rows, values, attended, peaks, totals = stored[:8]
    half_width = first_pair[0].shape[1]
    low_middle = grad_middle.astype(jnp.bfloat16)
    grad_attended = dense_back(low_middle, weights[7]).astype(jnp.bfloat16)
    grad_query, grad_keys, grad_values = attend_backward(
        queries, key_rows, values, segments, positions, peaks, totals, grad_attended
    )
    grad_shared = grad_values[:, :half_width]
    low_query = grad_query.astype(jnp.bfloat16)
    low_keys = grad_keys.astype(jnp.bfloat16)
    low_fresh = grad_values[:, half_width:].astype(jnp.bfloat16)
    grad_hidden = (
        dense_back(low_query, weights[2])
        + dense_back(low_keys, weights[4])
        + dense_back(low_fresh, weights[5])
    )
    new_first = first_grads
    if is_first:
        low_shared = (grad_shared + grad_shared_in).astype(jnp.bfloat16)
        grad_hidden = grad_hidden + dense_back(low_shared, first_pair[0])
        new_first = (
            first_grads[0] + dense_outer(hidden, low_shared),
            first_grads[1] + column_sum(low_shared),
        )
    grad_wide, grad_gain, grad_bias = jax.vjp(
        normed, slot_input.astype(jnp.float32), weights[0], weights[1]
    )[1](grad_hidden)
    grad_inputs = (grad_middle + grad_wide).astype(jnp.bfloat16)
    updated = (
        attention_grads[0] + grad_gain,
        attention_grads[1] + grad_bias,
        attention_grads[2] + dense_outer(hidden, low_query),
        attention_grads[3] + column_sum(low_query),
        attention_grads[4] + dense_outer(hidden, low_keys),
        attention_grads[5] + dense_outer(hidden, low_fresh),
        attention_grads[6] + column_sum(low_fresh),
        attention_grads[7] + dense_outer(attended, low_middle),
        attention_grads[8] + column_sum(low_middle),
    )
    return (grad_inputs, updated, new_first, grad_shared)


def local(
    boundary,
    lengths,
    norm_one_gain,
    norm_one_bias,
    query_weight,
    query_bias,
    key_weight,
    value_weight,
    value_bias,
    first_value_weight,
    first_value_bias,
    out_weight,
    out_bias,
    norm_two_gain,
    norm_two_bias,
    up_weight,
    up_bias,
    down_weight,
    down_bias,
):
    on_first = lax.axis_index("section") == 0
    micro_count = lengths.shape[0]
    slot_rows = boundary.shape[1] // micro_count
    model_width = boundary.shape[2]
    half_width = first_value_weight.shape[1]
    inner_width = up_weight.shape[2]
    weights = (
        norm_one_gain[0],
        norm_one_bias[0],
        query_weight[0],
        query_bias[0],
        key_weight[0],
        value_weight[0],
        value_bias[0],
        out_weight[0],
        out_bias[0],
        norm_two_gain[0],
        norm_two_bias[0],
        up_weight[0],
        up_bias[0],
        down_weight[0],
        down_bias[0],
    )
    first_pair = (first_value_weight, first_value_bias)
    boundary_rows = boundary[0]
    blank_rows = jnp.zeros((slot_rows, model_width), jnp.bfloat16)
    blank_shared = jnp.zeros((slot_rows, half_width), jnp.bfloat16)
    blank_wide = jnp.zeros((slot_rows, model_width), jnp.float32)
    blank_back = jnp.zeros((slot_rows, half_width), jnp.float32)
    stored_list = []
    output_rows = []
    for micro_index in range(micro_count):
        segments, positions = segment_ids(lengths[micro_index], slot_rows)
        slot_input = boundary_rows[micro_index * slot_rows : (micro_index + 1) * slot_rows]
        head_result, shared, stored = lax.cond(
            on_first,
            lambda: layer_forward(True, slot_input, None, weights, first_pair, segments, positions),
            lambda: (blank_rows, blank_shared, empty_stored(slot_rows, model_width, inner_width)),
        )
        arrived, arrived_shared = passed_along((head_result, shared), "section", 1)
        tail_result, stored = lax.cond(
            on_first,
            lambda: (head_result, stored),
            lambda: layer_forward(
                False, arrived, arrived_shared, weights, first_pair, segments, positions
            )[0::2],
        )
        stored_list.append(stored)
        output_rows.append(tail_result)
    attention_grads = tuple((jnp.zeros(item.shape, jnp.float32) for item in weights[:9]))
    feed_grads = tuple((jnp.zeros(item.shape, jnp.float32) for item in weights[9:]))
    first_grads = (
        jnp.zeros(first_value_weight.shape, jnp.float32),
        jnp.zeros(first_value_bias.shape, jnp.float32),
    )
    input_grads = []
    for micro_index in range(micro_count):
        segments, positions = segment_ids(lengths[micro_index], slot_rows)
        slot_input = boundary_rows[micro_index * slot_rows : (micro_index + 1) * slot_rows]
        stored = stored_list[micro_index]

        def tail_backward():
            grad_middle, new_feed = feed_backward(slot_input, stored, weights, feed_grads)
            outcome = attention_backward(
                False,
                grad_middle,
                None,
                stored,
                weights,
                first_pair,
                segments,
                positions,
                attention_grads,
                first_grads,
            )
            return (outcome[0], outcome[3], new_feed, outcome[1])

        sent_grad, sent_shared, feed_grads, attention_grads = lax.cond(
            on_first, lambda: (blank_rows, blank_back, feed_grads, attention_grads), tail_backward
        )
        back_grad = passed_along(sent_grad, "section", -1)
        back_shared = passed_along(sent_shared.astype(jnp.bfloat16), "section", -1).astype(
            sent_shared.dtype
        )
        grad_middle, feed_grads = lax.cond(
            on_first,
            lambda: feed_backward(back_grad, stored, weights, feed_grads),
            lambda: (blank_wide, feed_grads),
        )
        grad_inputs, attention_grads, first_grads = lax.cond(
            on_first,
            lambda: attention_backward(
                True,
                grad_middle,
                back_shared,
                stored,
                weights,
                first_pair,
                segments,
                positions,
                attention_grads,
                first_grads,
            )[:3],
            lambda: (blank_rows, attention_grads, first_grads),
        )
        input_grads.append(grad_inputs)
    summed = lax.psum(
        (
            attention_grads[0],
            attention_grads[1],
            attention_grads[2],
            attention_grads[3],
            attention_grads[4],
            attention_grads[5],
            attention_grads[6],
            attention_grads[7],
            attention_grads[8],
            feed_grads[0],
            feed_grads[1],
            feed_grads[2],
            feed_grads[3],
            feed_grads[4],
            feed_grads[5],
            first_grads[0],
            first_grads[1],
        ),
        "dp",
    )
    attention_total = summed[:9]
    feed_total = summed[9:15]
    first_total = summed[15:]
    weight_rows = first_total[0].shape[0] // 2
    bias_cols = first_total[1].shape[0] // 2
    moved_weight, moved_bias = (
        passed_along(first_total[0][weight_rows:].astype(jnp.bfloat16), "section", 1).astype(
            jnp.float32
        ),
        passed_along(first_total[1][bias_cols:].astype(jnp.bfloat16), "section", 1).astype(
            jnp.float32
        ),
    )
    first_weight_out = jnp.where(on_first, first_total[0][:weight_rows], moved_weight)
    first_bias_out = jnp.where(on_first, first_total[1][:bias_cols], moved_bias)
    block_ends = jnp.where(
        on_first, jnp.concatenate(input_grads, axis=0), jnp.concatenate(output_rows, axis=0)
    )[None]
    return (
        block_ends,
        attention_total[0][None],
        attention_total[1][None],
        attention_total[2][None],
        attention_total[3][None],
        attention_total[4][None],
        attention_total[5][None],
        attention_total[6][None],
        first_weight_out,
        first_bias_out,
        attention_total[7][None],
        attention_total[8][None],
        feed_total[0][None],
        feed_total[1][None],
        feed_total[2][None],
        feed_total[3][None],
        feed_total[4][None],
        feed_total[5][None],
    )


def solution(mesh):
    return jax.shard_map(
        local,
        mesh=mesh,
        in_specs=(
            P("section", "dp", None),
            P("dp", None),
            P("section", None),
            P("section", None),
            P("section", None, None),
            P("section", None),
            P("section", None, None),
            P("section", None, None),
            P("section", None),
            P(),
            P(),
            P("section", None, None),
            P("section", None),
            P("section", None),
            P("section", None),
            P("section", None, None),
            P("section", None),
            P("section", None, None),
            P("section", None),
        ),
        out_specs=(
            P("section", "dp", None),
            P("section", None),
            P("section", None),
            P("section", None, None),
            P("section", None),
            P("section", None, None),
            P("section", None, None),
            P("section", None),
            P("section", None),
            P("section"),
            P("section", None, None),
            P("section", None),
            P("section", None),
            P("section", None),
            P("section", None, None),
            P("section", None),
            P("section", None, None),
            P("section", None),
        ),
        check_vma=False,
    )
```

profile of v0, /device:TPU:0, one launch (start us, length us, event | category | flops | bytes accessed | tf_op | source)
XLA Modules:
  0.0 1361.2 jit_solution(7692480271396161907)
XLA Ops:
  10.8 58.6 %conditional.10 = (bf16[512,768]{1,0:T(8,128)(2,1)}, bf16[512,384]{0,1:T(8,128)(2,1)}, bf16[512,768]{1,0:T(8,128)(2,1)}, bf16[512,768]{1,0:T(8,128)(2,1)}, bf16[...) conditional(s32[]{:T(128)} %convert_element_type.462, ...), branch_computations={%region_2.3_spmd, %region_3.10_spmd} | conditional | flops 8121865216 | bytes 157992272 | solution.py:330
  20.8 3.4 fusion
  33.7 9.3 fusion.17
  43.1 3.3 fusion.198
  50.8 10.1 fusion.9
  60.9 7.2 add_convert_fusion
  73.1 59.5 %conditional.15 = (bf16[512,768]{1,0:T(8,128)(2,1)}, bf16[512,384]{0,1:T(8,128)(2,1)}, bf16[512,768]{1,0:T(8,128)(2,1)}, bf16[512,768]{1,0:T(8,128)(2,1)}, bf16[...) conditional(s32[]{:T(128)} %convert_element_type.462, ...), branch_computations={%region_63.64_spmd, %region_64.0_spmd} | conditional | flops 8121865216 | bytes 158102992 | solution.py:330
  84.1 3.4 fusion.91
  97.1 9.4 fusion.108
  114.1 10.2 fusion.100
  124.3 7.2 add_convert_fusion.8
  134.0 14.2 %conditional.11 = (bf16[512,768]{1,0:T(8,128)(2,1)S(1)}, bf16[512,768]{1,0:T(8,128)(2,1)}, bf16[512,768]{1,0:T(8,128)(2,1)}, bf16[512,768]{1,0:T(8,128)(2,1)}, b...) conditional(s32[]{:T(128)} %convert_element_type.462, ...), branch_computations={%region_10.17_spmd, %region_17.18_spmd} | conditional | flops 7819482112 | bytes 144473856 | solution.py:336
  149.1 31.6 %conditional.12 = (bf16[512,768]{1,0:T(8,128)(2,1)}, bf16[512,384]{0,1:T(8,128)(2,1)}, f32[768]{0:T(1024)S(1)}, f32[768]{0:T(1024)S(1)}, f32[768,3072]{0,1:T(8,1...) conditional(s32[]{:T(128)} %convert_element_type.462, ...), branch_computations={%region_18.37_spmd, %region_37.38_spmd} | conditional | flops 15999164416 | bytes 288221408 | solution.py:373
  163.9 4.4 broadcast_in_dim.366
  168.3 4.3 broadcast_in_dim.368
  182.0 48.3 %collective-permute-start.5 = (bf16[512,384]{0,1:T(8,128)(2,1)}, bf16[512,384]{0,1:T(8,128)(2,1)}, u32[]{:S(2)}, u32[]{:S(2)}) collective-permute-start(bf16[512,384]{0,1:T(8,128)(2,1)} %get-tuple-element.1360), channel_id=1, source_target_pairs={{0,16},{1,17},{2,18},{3,19},{4,20},{5,21},{6,22},{7,23},{8,24},{9,... | collective-permute-start | bytes 1179656 | tf_op jit(solution)/shard_map/ppermute | solution.py:16
  231.7 10.6 conditional.16
  244.6 43.3 %conditional.13 = (f32[512,768]{1,0:T(8,128)S(1)}, f32[768]{0:T(1024)S(1)}, f32[768]{0:T(1024)S(1)}, f32[768,3072]{0,1:T(8,128)}, f32[3072]{0:T(1024)S(1)}, /*index=5*/f32[3072,768]{1,0:T(8,128)}, f32[768]{0:T(1024)S(1)}) conditional(s32[]{:T(128)} %convert_element_type.462, (f32[768]{0:T(1024)S(1)}, f32[768]{0:T(1024)S(1)}, ...), branch_computations={%region_38.39_spmd, %region_39.48_spmd} | conditional | flops 9712046080 | bytes 96084056 | solution.py:380
  247.9 10.1 convert_reduce_fusion.8
  258.0 6.7 multiply_reduce_fusion.6
  268.9 7.8 bitcast_add_fusion
  276.6 11.3 convolution_add_fusion.5
  288.5 83.5 %conditional.14 = (f32[768]{0:T(1024)}, f32[768]{0:T(1024)}, f32[768,768]{0,1:T(8,128)}, f32[768]{0:T(1024)}, f32[768,768]{0,1:T(8,128)}, /*index=5*/f32[768,384...) conditional(s32[]{:T(128)} %convert_element_type.462, ...), branch_computations={%region_48.49_spmd, %region_49.61_spmd} | conditional | flops 6898676736 | bytes 296852832 | solution.py:385
  294.2 9.9 exponential_divide_fusion.1
  308.2 12.0 multiply_reduce_fusion.9
  320.2 7.0 multiply_convert_fusion.3
  341.9 3.6 fusion.82
  351.7 4.0 bitcast_add_fusion.2
  372.1 22.3 %conditional.17 = (bf16[512,768]{1,0:T(8,128)(2,1)}, bf16[512,384]{0,1:T(8,128)(2,1)S(1)}, f32[768]{0:T(1024)}, f32[768]{0:T(1024)}, f32[768,3072]{0,1:T(8,128)}...) conditional(s32[]{:T(128)} %convert_element_type.462, ...), branch_computations={%region_79.98_spmd, %region_98.99_spmd} | conditional | flops 16005957632 | bytes 351894752 | solution.py:373
  397.0 17.5 %collective-permute-done.7 = bf16[512,384]{0,1:T(8,128)(2,1)S(1)} collective-permute-done((bf16[512,384]{0,1:T(8,128)(2,1)S(1)}, bf16[512,384]{0,1:T(8,128)(2,1)S(1)}, u32[]{:S(2)}, u32[]{:S(2)}) %collective-permute-start.7) | collective-permute-done | bytes 393248 | tf_op jit(solution)/shard_map/ppermute | solution.py:16
  415.6 44.3 %conditional.18 = (f32[512,768]{1,0:T(8,128)}, f32[768]{0:T(1024)}, f32[768]{0:T(1024)}, f32[768,3072]{0,1:T(8,128)}, f32[3072]{0:T(1024)}, /*index=5*/f32[3072,768]{1,0:T(8,128)}, f32[768]{0:T(1024)}) conditional(s32[]{:T(128)} %convert_element_type.462, (f32[768]{0:T(1024)}, f32[768]{0:T(1024)}, f32[768,3072]{0,1:T(8,128)}, f32[3072]{0:T(1024)}, ...), branch_computations={%region_99.100_spmd, %region_100.109_spmd} | conditional | flops 9712046080 | bytes 96256320 | solution.py:380
  419.0 10.1 convert_reduce_fusion.23
  429.1 6.7 multiply_reduce_fusion.16
  440.7 7.8 bitcast_add_fusion.7
  448.5 11.3 convolution_add_fusion.13
  459.9 98.4 %conditional.19 = (f32[768]{0:T(1024)}, f32[768]{0:T(1024)}, f32[768,768]{0,1:T(8,128)}, f32[768]{0:T(1024)}, f32[768,768]{0,1:T(8,128)S(1)}, /*index=5*/f32[768...) conditional(s32[]{:T(128)} %convert_element_type.462, ...), branch_computations={%region_109.110_spmd, %region_110.122_spmd} | conditional | flops 6898972160 | bytes 282339264 | solution.py:385
  478.3 9.9 exponential_divide_fusion.3
  493.7 12.0 multiply_reduce_fusion.19
  505.7 6.8 multiply_convert_fusion.9
  526.7 3.6 fusion.174
  531.3 3.5 fusion.177
  538.5 3.9 bitcast_add_fusion.9
  553.5 4.6 convolution_add_fusion.14
  568.6 9.7 copy.205
  581.9 84.0 %all-reduce = (f32[1,768]{1,0:T(1,128)}, f32[1,768]{1,0:T(1,128)}, f32[1,768]{1,0:T(1,128)}, f32[1,384]{1,0:T(1,128)}, f32[384]{0:T(512)S(1)}, /*index=5*/f32[1,...) all-reduce(f32[1,768]{1,0:T(1,128)S(1)} %broadcast_in_dim.412, ...), channel_id=1, replica_groups=mesh['section'=2,'dp'=16] {'dp'}, use_global_device_ids=true, to_apply=%region_122.123 | all-reduce | flops 9216 | bytes 73728 | tf_op jit(solution)/shard_map/psum | solution.py:402
  667.3 658.4 %all-reduce.4.cloned.1.call-done = (f32[1,768,768]{2,1,0:T(8,128)}, f32[1,768,768]{2,1,0:T(8,128)}, f32[1,768,384]{2,1,0:T(8,128)}, f32[768,384]{1,0:T(8,128)}, ...) async-done(((f32[1,768,768]{2,1,0:T(8,128)}, f32[1,768,768]{2,1,0:T(8,128)}, f32[1,768,384]{2,1,0:T(8,128)}, f32[768,384]{1,0:T(8,128)}, ...) | async-done | bytes 28311568 | tf_op jit(solution)/shard_map/psum | solution.py:402
  1340.9 9.3 copy.489
  1350.2 3.7 copy.490
  (471 shorter events, 219.9 us)
Async XLA Ops:
  7.2 1318.4 %all-reduce.4.cloned.1.call-start = ((), (), s32[]{:S(2)}) async-start(), calls=%async_computation | async-start | bytes 56623104 | tf_op jit(solution)/shard_map/psum | solution.py:402
  9.9 63.2 %copy-start.14 = (bf16[512,768]{1,0:T(8,128)(2,1)}, bf16[512,768]{1,0:T(8,128)(2,1)S(1)}, u32[]{:S(2)}) copy-start(bf16[512,768]{1,0:T(8,128)(2,1)S(1)} %get-tuple-element.2126) | copy-start | bytes 2359300
  11.7 19.5 %copy-start.18 = (bf16[512,768]{1,0:T(8,128)(2,1)}, bf16[512,768]{1,0:T(8,128)(2,1)S(1)}, u32[]{:S(2)}) copy-start(bf16[512,768]{1,0:T(8,128)(2,1)S(1)} %fusion.16) | copy-start | bytes 2359300 | tf_op jit(solution)/shard_map/cond
  24.2 9.5 copy-start.97
  33.7 9.4 copy-start.168
  69.4 64.6 %collective-permute-start = (bf16[512,768]{1,0:T(8,128)(2,1)}, bf16[512,768]{1,0:T(8,128)(2,1)S(1)}, u32[]{:S(2)}, u32[]{:S(2)}) collective-permute-start(bf16[512,768]{1,0:T(8,128)(2,1)} %get-tuple-element.1314), channel_id=1, source_target_pairs={{0,16},{1,17},{2,18},{3,19},{4,20},{5,21},{6,22},{7,23},{8,24},{9,... | collective-permute-start | bytes 2359304 | tf_op jit(solution)/shard_map/ppermute | solution.py:16
  70.8 63.2 %collective-permute-start.1 = (bf16[512,384]{0,1:T(8,128)(2,1)}, bf16[512,384]{0,1:T(8,128)(2,1)}, u32[]{:S(2)}, u32[]{:S(2)}) collective-permute-start(bf16[512,384]{0,1:T(8,128)(2,1)} %get-tuple-element.1315), channel_id=1, source_target_pairs={{0,16},{1,17},{2,18},{3,19},{4,20},{5,21},{6,22},{7,23},{8,24},{9,... | collective-permute-start | bytes 1179656 | tf_op jit(solution)/shard_map/ppermute | solution.py:16
  73.1 299.0 %copy-start.114 = (s32[512]{0:T(512)}, s32[512]{0:T(512)S(1)}, u32[]{:S(2)}) copy-start(s32[512]{0:T(512)S(1)} %convert_reduce_fusion.30) | copy-start | bytes 6148
  75.1 19.5 %copy-start.5 = (bf16[512,768]{1,0:T(8,128)(2,1)}, bf16[512,768]{1,0:T(8,128)(2,1)S(1)}, u32[]{:S(2)}) copy-start(bf16[512,768]{1,0:T(8,128)(2,1)S(1)} %fusion.107) | copy-start | bytes 2359300 | tf_op jit(solution)/shard_map/cond
  77.4 10.1 copy-start.34
  87.6 9.5 copy-start.101
  97.1 9.4 copy-start.169
  132.6 99.0 %collective-permute-start.4 = (bf16[512,768]{1,0:T(8,128)(2,1)}, bf16[512,768]{1,0:T(8,128)(2,1)S(1)}, u32[]{:S(2)}, u32[]{:S(2)}) collective-permute-start(bf16[512,768]{1,0:T(8,128)(2,1)} %get-tuple-element.1359), channel_id=1, source_target_pairs={{0,16},{1,17},{2,18},{3,19},{4,20},{5,21},{6,22},{7,23},{8,24},{9,... | collective-permute-start | bytes 2359304 | tf_op jit(solution)/shard_map/ppermute | solution.py:16
  134.0 14.2 %copy-start.24 = (bf16[512,768]{1,0:T(8,128)(2,1)S(1)}, bf16[512,768]{1,0:T(8,128)(2,1)}, u32[]{:S(2)}) copy-start(bf16[512,768]{1,0:T(8,128)(2,1)} %copy-done.23) | copy-start | bytes 2359300
  180.7 51.0 %copy-start.25 = (f32[768,384]{0,1:T(8,128)}, f32[768,384]{0,1:T(8,128)S(1)}, u32[]{:S(2)}) copy-start(f32[768,384]{0,1:T(8,128)S(1)} %get-tuple-element.1345) | copy-start | bytes 3538948
  180.7 51.0 %copy-start.31 = (f32[768,768]{0,1:T(8,128)}, f32[768,768]{0,1:T(8,128)S(1)}, u32[]{:S(2)}) copy-start(f32[768,768]{0,1:T(8,128)S(1)} %get-tuple-element.1347) | copy-start | bytes 7077892
  180.7 63.9 %collective-permute-start.2 = (bf16[512,768]{1,0:T(8,128)(2,1)}, bf16[512,768]{1,0:T(8,128)(2,1)}, u32[]{:S(2)}, u32[]{:S(2)}) collective-permute-start(bf16[512,768]{1,0:T(8,128)(2,1)} %get-tuple-element.1355), channel_id=1, source_target_pairs={{16,0},{17,1},{18,2},{19,3},{20,4},{21,5},{22,6},{23,7},{24,8},{25... | collective-permute-start | bytes 2359304 | tf_op jit(solution)/shard_map/ppermute | solution.py:16
  182.0 49.6 %collective-permute-start.5 = (bf16[512,384]{0,1:T(8,128)(2,1)}, bf16[512,384]{0,1:T(8,128)(2,1)}, u32[]{:S(2)}, u32[]{:S(2)}) collective-permute-start(bf16[512,384]{0,1:T(8,128)(2,1)} %get-tuple-element.1360), channel_id=1, source_target_pairs={{0,16},{1,17},{2,18},{3,19},{4,20},{5,21},{6,22},{7,23},{8,24},{9,... | collective-permute-start | bytes 1179656 | tf_op jit(solution)/shard_map/ppermute | solution.py:16
  230.4 12.0 collective-permute-start.3
  244.6 43.3 %copy-start.99 = (f32[1,12,512,1]{2,1,3,0:T(8,128)S(1)}, f32[1,12,512,1]{2,1,3,0:T(8,128)}, u32[]{:S(2)}) copy-start(f32[1,12,512,1]{2,1,3,0:T(8,128)} %get-tuple-element.1332) | copy-start | bytes 73732
  244.6 43.3 %copy-start.141 = (f32[1,12,512,1]{2,1,3,0:T(8,128)S(1)}, f32[1,12,512,1]{2,1,3,0:T(8,128)}, u32[]{:S(2)}) copy-start(f32[1,12,512,1]{2,1,3,0:T(8,128)} %get-tuple-element.1333) | copy-start | bytes 73732
  288.7 57.7 %copy-start.37 = (f32[512,768]{1,0:T(8,128)}, f32[512,768]{1,0:T(8,128)S(1)}, u32[]{:S(2)}) copy-start(f32[512,768]{1,0:T(8,128)S(1)} %get-tuple-element.986) | copy-start | bytes 4718596 | tf_op jit(solution)/shard_map/cond
  294.2 9.9 copy-start.172
  308.2 12.0 slice-start
  308.2 12.0 slice-start.1
  308.2 12.0 slice-start.2
  356.6 11.8 copy-start.1
  394.4 21.1 %collective-permute-start.6 = (bf16[512,768]{1,0:T(8,128)(2,1)}, bf16[512,768]{1,0:T(8,128)(2,1)}, u32[]{:S(2)}, u32[]{:S(2)}) collective-permute-start(bf16[512,768]{1,0:T(8,128)(2,1)} %get-tuple-element.1417), channel_id=1, source_target_pairs={{16,0},{17,1},{18,2},{19,3},{20,4},{21,5},{22,6},{23,7},{24,8},{25... | collective-permute-start | bytes 2359304 | tf_op jit(solution)/shard_map/ppermute | solution.py:16
  395.7 18.8 %collective-permute-start.7 = (bf16[512,384]{0,1:T(8,128)(2,1)S(1)}, bf16[512,384]{0,1:T(8,128)(2,1)S(1)}, u32[]{:S(2)}, u32[]{:S(2)}) collective-permute-start(bf16[512,384]{0,1:T(8,128)(2,1)S(1)} %get-tuple-element.1419), channel_id=1, source_target_pairs={{16,0},{17,1},{18,2},{19,3},{20,4},{21,5},{22,6},{23,7},{24,8},{25... | collective-permute-start | bytes 1179656 | tf_op jit(solution)/shard_map/ppermute | solution.py:16
  415.5 44.3 %copy-start.4 = (f32[768,768]{0,1:T(8,128)S(1)}, f32[768,768]{0,1:T(8,128)}, u32[]{:S(2)}) copy-start(f32[768,768]{0,1:T(8,128)} %get-tuple-element.1404) | copy-start | bytes 7077892
  415.5 44.3 %copy-start.103 = (f32[1,12,512,1]{2,1,3,0:T(8,128)S(1)}, f32[1,12,512,1]{2,1,3,0:T(8,128)}, u32[]{:S(2)}) copy-start(f32[1,12,512,1]{2,1,3,0:T(8,128)} %get-tuple-element.1377) | copy-start | bytes 73732
  415.5 44.3 %copy-start.115 = (s32[512]{0:T(512)S(1)}, s32[512]{0:T(512)}, u32[]{:S(2)}) copy-start(s32[512]{0:T(512)} %copy-done.114) | copy-start | bytes 6148
  415.5 44.3 %copy-start.145 = (f32[1,12,512,1]{2,1,3,0:T(8,128)S(1)}, f32[1,12,512,1]{2,1,3,0:T(8,128)}, u32[]{:S(2)}) copy-start(f32[1,12,512,1]{2,1,3,0:T(8,128)} %get-tuple-element.1378) | copy-start | bytes 73732
  440.6 7.9 copy-start.120
  440.7 7.8 copy-start.126
  440.7 7.8 copy-start.132
  448.5 11.3 copy-start.109
  478.3 9.9 copy-start.174
  493.7 12.0 slice-start.3
  493.7 12.0 slice-start.4
  493.7 12.0 slice-start.5
  578.3 750.2 %copy-start.88 = (bf16[1,512,768]{2,1,0:T(8,128)(2,1)S(1)}, bf16[1,512,768]{2,1,0:T(8,128)(2,1)}, u32[]{:S(2)}) copy-start(bf16[1,512,768]{2,1,0:T(8,128)(2,1)} %copy-done.87) | copy-start | bytes 2359300
  578.3 750.2 %copy-start.90 = (bf16[1,512,768]{2,1,0:T(8,128)(2,1)S(1)}, bf16[1,512,768]{2,1,0:T(8,128)(2,1)}, u32[]{:S(2)}) copy-start(bf16[1,512,768]{2,1,0:T(8,128)(2,1)} %copy-done.89) | copy-start | bytes 2359300
  666.0 665.3 %collective-permute-start.9 = (bf16[192]{0:T(256)(128)(2,1)S(1)}, bf16[192]{0:T(256)(128)(2,1)S(1)}, u32[]{:S(2)}, u32[]{:S(2)}) collective-permute-start(bf16[192]{0:T(256)(128)(2,1)S(1)} %slice.73), channel_id=1, source_target_pairs={{0,16},{1,17},{2,18},{3,19},{4,20},{5,21},{6,22},{7,23},{8,24},{9,... | collective-permute-start | bytes 1160 | tf_op jit(solution)/shard_map/ppermute | solution.py:16
  1326.7 5.2 collective-permute-start.8
  1339.5 10.7 slice-start.6
  1340.9 9.3 slice-start.7
  1340.9 9.3 slice-start.8
  (87 other events, 245.6 us)
Sparse Core Ops, SparseCore 0:
  578.5 747.1 all-reduce.3
where the time goes:
time: 1370 us; the launch traced here: 1360 us
  waiting for transfers between devices  676 us (49%)
  matrix products  258 us (19%)
  local copies, waits for them, and re-layouts  116 us (8%)
  blocking collectives  84 us (6%)
  other arithmetic  80.5 us (6%)
  loops' own time  70.6 us (5%)
  starting transfers between devices  61.3 us (4%)
  between operations  15 us (1%)
    psum x1, waiting for transfers between devices, local(): lax.psum((attention_grads[0], attention_grads[1], attention_grads[2], att...  658 us
    psum x1, blocking collectives, local(): lax.psum((attention_grads[0], attention_grads[1], attention_grads[2], att...  84 us
    dot_general x14, matrix products, dense_outer(): lax.dot_general(input_rows, grad_rows, (((0,), (0,)), ((), ())), preferre...  63.2 us
    ppermute x10, starting transfers between devices, passed_along(): return lax.ppermute(shard, axis, pairs)  61.3 us
    dot_general x14, matrix products, dense_product(): return jnp.dot(left, right, preferred_element_type=jnp.float32)  57.5 us
    dot_general x14, matrix products, dense_back(): lax.dot_general(grad_rows, weight, (((1,), (1,)), ((), ())), preferred_el...  57 us
    another operation x2, loops' own time, local(): lax.cond(on_first, lambda: (blank_rows, blank_back, feed_grads, attention...  34.2 us
  transfers between devices with their start and end apart: 11, of which 2 were waited for; matrix products, arithmetic and copies ran while one was open for 7% of the time, Pallas kernels for 0%

commit v1 on v0

v1 whole, which is shorter than its diff:
```python
import functools

import jax
import jax.numpy as jnp
from jax import lax
from jax.experimental import pallas as pl
from jax.experimental.pallas import tpu as pltpu
from jax.sharding import PartitionSpec as P

HEADS = 12
HEAD = 64
PAIR = 2 * HEAD
VMEM_BYTES = 48 * 1024 * 1024

eps_norm = 1e-05
neg_fill = -1e30

f32 = jnp.float32
bf16 = jnp.bfloat16

NN = (((1,), (0,)), ((), ()))
NT = (((1,), (1,)), ((), ()))
TN = (((0,), (0,)), ((), ()))

ANY = pl.BlockSpec(memory_space=pl.ANY)
SMEM = pl.BlockSpec(memory_space=pltpu.SMEM)
VMEM = pl.BlockSpec(memory_space=pltpu.VMEM)

GAIN1, BIAS1, QBIAS, VBIAS, OBIAS, GAIN2, BIAS2, DBIAS, UBIAS = range(9)
VEC_ROWS = 16


def mm(left, right, dims=NN):
    return lax.dot_general(left, right, dims, preferred_element_type=f32)


def sds(shape, dtype):
    return jax.ShapeDtypeStruct(shape, dtype)


def params():
    return pltpu.CompilerParams(vmem_limit_bytes=VMEM_BYTES)


def cost(flops, nbytes, trans=0):
    return pl.CostEstimate(flops=int(flops), bytes_accessed=int(nbytes), transcendentals=int(trans))


def start_fetch(mine, own, recv, dst, sem):
    @pl.when(mine)
    def _():
        pltpu.make_async_copy(own, dst, sem).start()

    @pl.when(jnp.logical_not(mine))
    def _():
        pltpu.make_async_copy(recv, dst, sem).start()


def wait_fetch(own, dst, sem):
    pltpu.make_async_copy(own, dst, sem).wait()


def norm_parts(rows):
    centre = jnp.mean(rows, axis=-1, keepdims=True)
    centred = rows - centre
    spread = jnp.mean(centred * centred, axis=-1, keepdims=True)
    factor = lax.rsqrt(spread + eps_norm)
    return centred * factor, factor


def norm_back(grad_t, n, w):
    return w * (
        grad_t
        - jnp.mean(grad_t, axis=-1, keepdims=True)
        - n * jnp.mean(grad_t * n, axis=-1, keepdims=True)
    )


def row_sum(x):
    return jnp.sum(x, axis=0, keepdims=True)


def attn_forward_kernel(layer, sec_ref, x_ref, r_ref, start_ref, vec_ref,
                        qw_o, qw_r, kw_o, kw_r, vw_o, vw_r, fw, ow_o, ow_r,
                        h_out, q_out, k_out, v_out, o_out, m_out, e_out, lse_out,
                        wq, wk, wv, wo, h_s, q_s, k_s, v_s, o_s, m_s, e_s, lse_s, lset_s, bias_s,
                        in_sem, out_sem):
    mine = sec_ref[0] == layer
    rows = x_ref.shape[0]
    half = fw.shape[1]
    start_fetch(mine, qw_o, qw_r, wq, in_sem.at[0])
    start_fetch(mine, kw_o, kw_r, wk, in_sem.at[1])
    start_fetch(mine, vw_o, vw_r, wv.at[:, half:], in_sem.at[2])
    if layer == 0:
        pltpu.make_async_copy(fw, wv.at[:, :half], in_sem.at[3]).start()
    start_fetch(mine, ow_o, ow_r, wo, in_sem.at[4])

    def put(index, src, dst):
        pltpu.make_async_copy(src, dst, out_sem.at[index]).start()

    wide = x_ref[...].astype(f32)
    n, _ = norm_parts(wide)
    h_s[...] = (n * vec_ref[GAIN1:GAIN1 + 1, :] + vec_ref[BIAS1:BIAS1 + 1, :]).astype(bf16)
    put(0, h_s, h_out)
    at_row = lax.broadcasted_iota(jnp.int32, (rows, rows), 0)
    at_col = lax.broadcasted_iota(jnp.int32, (rows, rows), 1)
    bias_s[...] = jnp.where((at_col <= at_row) & (at_col >= start_ref[...]), 0.0, neg_fill)
    wait_fetch(qw_o, wq, in_sem.at[0])
    q_s[...] = (mm(h_s[...], wq[...]) + vec_ref[QBIAS:QBIAS + 1, :]).astype(bf16)
    put(1, q_s, q_out)
    wait_fetch(kw_o, wk, in_sem.at[1])
    k_s[...] = mm(h_s[...], wk[...]).astype(bf16)
    put(2, k_s, k_out)
    wait_fetch(vw_o, wv.at[:, half:], in_sem.at[2])
    if layer == 0:
        wait_fetch(fw, wv.at[:, :half], in_sem.at[3])
        v_s[...] = (mm(h_s[...], wv[...]) + vec_ref[VBIAS:VBIAS + 1, :]).astype(bf16)
    else:
        v_s[:, :half] = r_ref[:, :half]
        v_s[:, half:] = (mm(h_s[...], wv[:, half:]) + vec_ref[VBIAS:VBIAS + 1, half:]).astype(bf16)
    put(3, v_s, v_out)

    lane = lax.broadcasted_iota(jnp.int32, (1, PAIR), 1)
    step = rows // 2

    def pair(hp, carry):
        ls = pl.ds(pl.multiple_of(hp * PAIR, PAIR), PAIR)
        q2 = q_s[:, ls] * jnp.asarray(HEAD ** -0.5, bf16)
        k2 = k_s[:, ls]
        v2 = v_s[:, ls]
        zero = jnp.zeros((), bf16)
        for qb in range(2):
            qr = slice(qb * step, (qb + 1) * step)
            keys = (qb + 1) * step
            mixed = None
            for j in range(2):
                inside = (lane >= j * HEAD) & (lane < (j + 1) * HEAD)
                kh = jnp.where(inside, k2[:keys], zero)
                vh = jnp.where(inside, v2[:keys], zero)
                s = mm(q2[qr], kh, NT) + bias_s[qr, :keys]
                peak = jnp.max(s, axis=-1, keepdims=True)
                p = jnp.exp(s - peak)
                total = jnp.sum(p, axis=-1, keepdims=True)
                low = (p * (1.0 / total)).astype(bf16)
                part = mm(low, vh)
                mixed = part if mixed is None else mixed + part
                lse_s[qr, :] = jnp.where(lane == 2 * hp + j, peak + jnp.log(total), lse_s[qr, :])
            o_s[qr, ls] = mixed.astype(bf16)
        return carry

    lse_s[...] = jnp.zeros(lse_s.shape, f32)
    lax.fori_loop(0, HEADS // 2, pair, 0)
    put(4, o_s, o_out)
    lset_s[...] = jnp.transpose(lse_s[...])[:VEC_ROWS, :]
    put(7, lset_s, lse_out)
    wait_fetch(ow_o, wo, in_sem.at[4])
    m = x_ref[...].astype(f32) + (mm(o_s[...], wo[...]) + vec_ref[OBIAS:OBIAS + 1, :])
    m_s[...] = m
    put(5, m_s, m_out)
    n, _ = norm_parts(m)
    e_s[...] = (n * vec_ref[GAIN2:GAIN2 + 1, :] + vec_ref[BIAS2:BIAS2 + 1, :]).astype(bf16)
    put(6, e_s, e_out)
    for index, (src, dst) in enumerate(((h_s, h_out), (q_s, q_out), (k_s, k_out), (v_s, v_out),
                                        (o_s, o_out), (m_s, m_out), (e_s, e_out), (lset_s, lse_out))):
        pltpu.make_async_copy(src, dst, out_sem.at[index]).wait()


def attn_forward(layer, sec, x, r, start, vec, w):
    rows, d = x.shape
    act = sds((rows, d), bf16)
    wbuf = pltpu.VMEM((d, d), bf16)
    abuf = pltpu.VMEM((rows, d), bf16)
    return pl.pallas_call(
        functools.partial(attn_forward_kernel, layer),
        out_shape=[act, act, act, act, act, sds((rows, d), f32), act, sds((VEC_ROWS, rows), f32)],
        in_specs=[SMEM, VMEM, VMEM, VMEM, VMEM] + [ANY] * 9,
        out_specs=[ANY] * 8,
        scratch_shapes=[wbuf, wbuf, wbuf, wbuf, abuf, abuf, abuf, abuf, abuf,
                        pltpu.VMEM((rows, d), f32), abuf, pltpu.VMEM((rows, PAIR), f32),
                        pltpu.VMEM((VEC_ROWS, rows), f32), pltpu.VMEM((rows, rows), f32),
                        pltpu.SemaphoreType.DMA((5,)), pltpu.SemaphoreType.DMA((8,))],
        compiler_params=params(),
        cost_estimate=cost(10 * rows * d * d, 12 * rows * d * 2, HEADS * rows * rows),
        name="attn_forward",
    )(sec, x, r, start, vec, w["qo"], w["qr"], w["ko"], w["kr"], w["vo"], w["vr"], w["f"], w["oo"], w["or"])


def feed_forward_kernel(layer, blk, sec_ref, e_ref, m_ref, vec_ref, up_o, up_r, dn_o, dn_r,
                        u_ref, a_ref, z_ref, wu, wd, acc, sem):
    j = pl.program_id(0)
    steps = pl.num_programs(0)
    mine = sec_ref[0] == layer

    @pl.when(j == 0)
    def _():
        for b in range(up_o.shape[1] // blk):
            cols = pl.ds(b * blk, blk)
            start_fetch(mine, up_o.at[:, cols], up_r.at[:, cols], wu.at[b], sem.at[0, b])
            start_fetch(mine, dn_o.at[cols, :], dn_r.at[cols, :], wd.at[b], sem.at[1, b])

    wait_fetch(up_o.at[:, pl.ds(0, blk)], wu.at[j], sem.at[0, j])
    u = mm(e_ref[...], wu[j]) + vec_ref[pl.ds(UBIAS + j, 1), :]
    u_ref[...] = u.astype(bf16)
    half_u = 0.5 * u
    th = jnp.tanh(u * (0.7978845608028654 + 0.035677408136300125 * (u * u)))
    a = (half_u + half_u * th).astype(bf16)
    a_ref[...] = a
    wait_fetch(dn_o.at[pl.ds(0, blk), :], wd.at[j], sem.at[1, j])
    part = mm(a, wd[j])

    @pl.when(j == 0)
    def _():
        acc[...] = part

    @pl.when((j > 0) & (j < steps - 1))
    def _():
        acc[...] += part

    @pl.when(j == steps - 1)
    def _():
        z_ref[...] = (m_ref[...] + (acc[...] + part + vec_ref[DBIAS:DBIAS + 1, :])).astype(bf16)


def feed_forward(layer, sec, e, m, vec, w):
    rows, d = e.shape
    ff = w["uo"].shape[1]
    blk = d
    n = ff // blk
    return pl.pallas_call(
        functools.partial(feed_forward_kernel, layer, blk),
        grid=(n,),
        out_shape=[sds((rows, ff), bf16), sds((rows, ff), bf16), sds((rows, d), bf16)],
        in_specs=[SMEM, VMEM, VMEM, VMEM, ANY, ANY, ANY, ANY],
        out_specs=[pl.BlockSpec((rows, blk), lambda j: (0, j)), pl.BlockSpec((rows, blk), lambda j: (0, j)),
                   pl.BlockSpec((rows, d), lambda j: (0, 0))],
        scratch_shapes=[pltpu.VMEM((n, d, blk), bf16), pltpu.VMEM((n, blk, d), bf16), pltpu.VMEM((rows, d), f32),
                        pltpu.SemaphoreType.DMA((2, n))],
        compiler_params=params(),
        cost_estimate=cost(4 * rows * d * ff, 4 * d * ff + 4 * rows * ff, rows * ff),
        name="feed_forward",
    )(sec, e, m, vec, w["uo"], w["ur"], w["do"], w["dr"])


def feed_backward_kernel(layer, blk, sec_ref, dz_ref, u_ref, m_ref, vec_ref, up_o, up_r, dn_o, dn_r,
                         du_ref, dm_ref, low_ref, small_ref, wu, wd, acc, sem):
    j = pl.program_id(0)
    steps = pl.num_programs(0)
    mine = sec_ref[0] == layer

    @pl.when(j == 0)
    def _():
        for b in range(up_o.shape[1] // blk):
            cols = pl.ds(b * blk, blk)
            start_fetch(mine, dn_o.at[cols, :], dn_r.at[cols, :], wd.at[b], sem.at[1, b])
            start_fetch(mine, up_o.at[:, cols], up_r.at[:, cols], wu.at[b], sem.at[0, b])
        acc[...] = jnp.zeros(acc.shape, f32)
        small_ref[...] = jnp.zeros(small_ref.shape, f32)

    wait_fetch(dn_o.at[pl.ds(0, blk), :], wd.at[j], sem.at[1, j])
    da = mm(dz_ref[...], wd[j], NT)
    u = u_ref[...].astype(f32)
    sq = u * u
    th = jnp.tanh(u * (0.7978845608028654 + 0.035677408136300125 * sq))
    slope = 0.5 + 0.5 * th + (0.5 * u) * (1.0 - th * th) * (0.7978845608028654 + 0.10703222440890037 * sq)
    du = (slope * da).astype(bf16)
    du_ref[...] = du
    small_ref[pl.ds(UBIAS + j, 1), :] = row_sum(du.astype(f32))
    wait_fetch(up_o.at[:, pl.ds(0, blk)], wu.at[j], sem.at[0, j])
    acc[...] += mm(du, wu[j], NT)

    @pl.when(j == steps - 1)
    def _():
        de = acc[...]
        n, w = norm_parts(m_ref[...])
        dz = dz_ref[...].astype(f32)
        dm = dz + norm_back(de * vec_ref[GAIN2:GAIN2 + 1, :], n, w)
        dm_ref[...] = dm
        low_ref[...] = dm.astype(bf16)
        small_ref[GAIN2:GAIN2 + 1, :] = row_sum(de * n)
        small_ref[BIAS2:BIAS2 + 1, :] = row_sum(de)
        small_ref[DBIAS:DBIAS + 1, :] = row_sum(dz)


def feed_backward(layer, sec, dz, u, m, vec, w):
    rows, d = dz.shape
    ff = u.shape[1]
    blk = d
    n = ff // blk
    whole = lambda j: (0, 0)
    return pl.pallas_call(
        functools.partial(feed_backward_kernel, layer, blk),
        grid=(n,),
        out_shape=[sds((rows, ff), bf16), sds((rows, d), f32), sds((rows, d), bf16), sds((VEC_ROWS, d), f32)],
        in_specs=[SMEM, VMEM, pl.BlockSpec((rows, blk), lambda j: (0, j)), VMEM, VMEM, ANY, ANY, ANY, ANY],
        out_specs=[pl.BlockSpec((rows, blk), lambda j: (0, j)), pl.BlockSpec((rows, d), whole),
                   pl.BlockSpec((rows, d), whole), pl.BlockSpec((VEC_ROWS, d), whole)],
        scratch_shapes=[pltpu.VMEM((n, d, blk), bf16), pltpu.VMEM((n, blk, d), bf16), pltpu.VMEM((rows, d), f32),
                        pltpu.SemaphoreType.DMA((2, n))],
        compiler_params=params(),
        cost_estimate=cost(4 * rows * d * ff, 4 * d * ff + 4 * rows * ff, rows * ff),
        name="feed_backward",
    )(sec, dz, u, m, vec, w["uo"], w["ur"], w["do"], w["dr"])


def attn_backward_kernel(layer, sec_ref, x_ref, dm_ref, low_ref, q_ref, k_ref, v_ref, o_ref, lse_ref,
                         start_ref, vec_ref, dr2_ref,
                         qw_o, qw_r, kw_o, kw_r, vw_o, vw_r, fw, ow_o, ow_r,
                         dx_ref, dq_ref, dk_ref, dv_ref, shared_ref, small_ref,
                         wq, wk, wv, wo, do_s, delta_s, bias_s, sem):
    mine = sec_ref[0] == layer
    rows, d = x_ref.shape
    half = fw.shape[1]
    start_fetch(mine, ow_o, ow_r, wo, sem.at[4])
    start_fetch(mine, qw_o, qw_r, wq, sem.at[0])
    start_fetch(mine, kw_o, kw_r, wk, sem.at[1])
    start_fetch(mine, vw_o, vw_r, wv.at[:, half:], sem.at[2])
    if layer == 0:
        pltpu.make_async_copy(fw, wv.at[:, :half], sem.at[3]).start()

    at_key = lax.broadcasted_iota(jnp.int32, (rows, rows), 0)
    at_query = lax.broadcasted_iota(jnp.int32, (rows, rows), 1)
    bias_s[...] = jnp.where((at_key <= at_query) & (at_key >= start_ref[...]), 0.0, neg_fill)
    wait_fetch(ow_o, wo, sem.at[4])
    do = mm(low_ref[...], wo[...], NT).astype(bf16)
    do_s[...] = do
    head_row = lax.broadcasted_iota(jnp.int32, (VEC_ROWS, d), 0)
    head_col = lax.broadcasted_iota(jnp.int32, (VEC_ROWS, d), 1) // HEAD
    pick = (head_row == head_col).astype(f32)
    delta_s[...] = lax.dot_general(pick, do.astype(f32) * o_ref[...].astype(f32), NT,
                                   precision=lax.Precision.HIGHEST, preferred_element_type=f32)
    lane = lax.broadcasted_iota(jnp.int32, (1, PAIR), 1)
    step = rows // 2
    scale = HEAD ** -0.5
    zero = jnp.zeros((), bf16)

    def pair(hp, carry):
        ls = pl.ds(pl.multiple_of(hp * PAIR, PAIR), PAIR)
        q2 = q_ref[:, ls] * jnp.asarray(scale, bf16)
        k2 = k_ref[:, ls]
        v2 = v_ref[:, ls]
        do2 = do_s[:, ls]
        dq_parts = []
        for kb in range(2):
            kr = slice(kb * step, (kb + 1) * step)
            first = kb * step
            dk = dv = dq = None
            for j in range(2):
                inside = (lane >= j * HEAD) & (lane < (j + 1) * HEAD)
                kh = jnp.where(inside, k2[kr], zero)
                vh = jnp.where(inside, v2[kr], zero)
                qh = jnp.where(inside, q2[first:], zero)
                doh = jnp.where(inside, do2[first:], zero)
                row = pl.ds(2 * hp + j, 1)
                st = mm(kh, qh, NT) + bias_s[kr, first:]
                pt = jnp.exp(st - lse_ref[row, first:])
                dpt = mm(vh, doh, NT)
                dst = (pt * (dpt - delta_s[row, first:])).astype(bf16)
                dv_j = mm(pt.astype(bf16), doh)
                dk_j = mm(dst, qh)
                dq_j = mm(dst, kh, TN)
                dk = dk_j if dk is None else dk + dk_j
                dv = dv_j if dv is None else dv + dv_j
                dq = dq_j if dq is None else dq + dq_j
            dk_ref[kr, ls] = dk.astype(bf16)
            if layer == 1:
                dv_ref[kr, ls] = dv.astype(bf16)

                @pl.when(hp < HEADS // 4)
                def _():
                    shared_ref[kr, ls] = dv
            else:
                extra = jnp.where(hp < HEADS // 4, dr2_ref[kr, pl.ds(pl.multiple_of((hp % (HEADS // 4)) * PAIR, PAIR), PAIR)], 0.0)
                dv_ref[kr, ls] = (dv + extra).astype(bf16)
            dq_parts.append(dq)
        dq_ref[:step, ls] = (dq_parts[0][:step] * scale).astype(bf16)
        dq_ref[step:, ls] = ((dq_parts[0][step:] + dq_parts[1]) * scale).astype(bf16)
        return carry

    if layer == 0:
        shared_ref[...] = jnp.zeros(shared_ref.shape, f32)
    lax.fori_loop(0, HEADS // 2, pair, 0)

    wait_fetch(qw_o, wq, sem.at[0])
    dh = mm(dq_ref[...], wq[...], NT)
    wait_fetch(kw_o, wk, sem.at[1])
    dh = dh + mm(dk_ref[...], wk[...], NT)
    wait_fetch(vw_o, wv.at[:, half:], sem.at[2])
    if layer == 0:
        wait_fetch(fw, wv.at[:, :half], sem.at[3])
        dh = dh + mm(dv_ref[...], wv[...], NT)
    else:
        dh = dh + mm(dv_ref[:, half:], wv[:, half:], NT)
    n, w = norm_parts(x_ref[...].astype(f32))
    dx_ref[...] = (dm_ref[...] + norm_back(dh * vec_ref[GAIN1:GAIN1 + 1, :], n, w)).astype(bf16)
    small_ref[...] = jnp.zeros(small_ref.shape, f32)
    small_ref[GAIN1:GAIN1 + 1, :] = row_sum(dh * n)
    small_ref[BIAS1:BIAS1 + 1, :] = row_sum(dh)
    small_ref[QBIAS:QBIAS + 1, :] = row_sum(dq_ref[...].astype(f32))
    small_ref[VBIAS:VBIAS + 1, :] = row_sum(dv_ref[...].astype(f32))
    small_ref[OBIAS:OBIAS + 1, :] = row_sum(low_ref[...].astype(f32))


def attn_backward(layer, sec, x, dm, low, q, k, v, o, lse, start_row, vec, dr2, w):
    rows, d = x.shape
    half = w["f"].shape[1]
    act = sds((rows, d), bf16)
    wbuf = pltpu.VMEM((d, d), bf16)
    return pl.pallas_call(
        functools.partial(attn_backward_kernel, layer),
        out_shape=[act, act, act, act, sds((rows, half), f32), sds((VEC_ROWS, d), f32)],
        in_specs=[SMEM] + [VMEM] * 11 + [ANY] * 9,
        out_specs=[VMEM] * 6,
        scratch_shapes=[wbuf, wbuf, wbuf, wbuf, pltpu.VMEM((rows, d), bf16), pltpu.VMEM((VEC_ROWS, rows), f32),
                        pltpu.VMEM((rows, rows), f32), pltpu.SemaphoreType.DMA((5,))],
        compiler_params=params(),
        cost_estimate=cost(16 * rows * d * d, 16 * rows * d * 2, HEADS * rows * rows),
        name="attn_backward",
    )(sec, x, dm, low, q, k, v, o, lse, start_row, vec, dr2,
      w["qo"], w["qr"], w["ko"], w["kr"], w["vo"], w["vr"], w["f"], w["oo"], w["or"])


def store_chunks(ref, value):
    c, r, _ = ref.shape
    for i in range(c):
        ref[i] = value[i * r:(i + 1) * r].astype(bf16)


def two_way(body, grid, in_specs, steps, chunk_rows, block_rows, width, scalars, operands, flops, nbytes, name):
    per = block_rows // chunk_rows
    total = steps * per

    def kernel(s_ref, *refs):
        g = pl.program_id(0)
        *ins, send_ref, keep_ref = refs
        value = body(g % steps, *ins)

        @pl.when(g < steps)
        def _():
            store_chunks(send_ref, value)

        @pl.when(g >= steps)
        def _():
            store_chunks(keep_ref, value)

    return pl.pallas_call(
        kernel,
        grid_spec=pltpu.PrefetchScalarGridSpec(
            num_scalar_prefetch=1, grid=(2 * steps,), in_specs=in_specs,
            out_specs=[pl.BlockSpec((per, chunk_rows, width), lambda g, s: (jnp.minimum(g, steps - 1), 0, 0)),
                       pl.BlockSpec((per, chunk_rows, width), lambda g, s: (jnp.maximum(g - steps, 0), 0, 0))]),
        out_shape=[sds((total, chunk_rows, width), bf16)] * 2,
        compiler_params=params(),
        cost_estimate=cost(flops, nbytes),
        name=name,
    )(scalars, *operands)


def part_of(g, steps, s):
    return jnp.where(g < steps, 1 - s[0], s[0])


def down_gradient(sec, a, dz, chunk_rows):
    rows, ff = a.shape
    d = dz.shape[1]
    steps = ff // d // 2

    def body(i, a_ref, dz_ref):
        return mm(a_ref[...], dz_ref[...], TN)

    return two_way(body, None,
                   [pl.BlockSpec((rows, d), lambda g, s: (0, part_of(g, steps, s) * steps + g % steps)),
                    pl.BlockSpec((rows, d), lambda g, s: (0, 0))],
                   steps, chunk_rows, d, d, sec, (a, dz), 2 * rows * ff * d, 2 * rows * ff + 2 * d * ff, "down_gradient")


def up_gradient(sec, e, du, chunk_rows):
    rows, ff = du.shape
    d = e.shape[1]
    steps = ff // d // 2

    def body(i, e_ref, du_ref):
        return mm(e_ref[...], du_ref[...], TN)

    return two_way(body, None,
                   [pl.BlockSpec((rows, d), lambda g, s: (0, 0)),
                    pl.BlockSpec((rows, d), lambda g, s: (0, part_of(g, steps, s) * steps + g % steps))],
                   steps, chunk_rows, d, d, sec, (e, du), 2 * rows * ff * d, 2 * rows * ff + 2 * d * ff, "up_gradient")


def attn_gradient(sec, o, low, h, dq, dk, dv, chunk_rows):
    rows, d = o.shape
    steps = 4

    def kernel(s_ref, o_ref, low_ref, h_ref, dq_ref, dk_ref, dv_ref, send_ref, keep_ref):
        g = pl.program_id(0)
        for i, (left, right) in enumerate(((o_ref, low_ref), (h_ref, dq_ref), (h_ref, dk_ref), (h_ref, dv_ref))):
            for side, ref in enumerate((send_ref, keep_ref)):
                @pl.when(g == side * steps + i)
                def _():
                    store_chunks(ref, mm(left[...], right[...], TN))

    half = pl.BlockSpec((rows, d // 2), lambda g, s: (0, part_of(g, steps, s)))
    full = pl.BlockSpec((rows, d), lambda g, s: (0, 0))
    per = d // 2 // chunk_rows
    return pl.pallas_call(
        kernel,
        grid_spec=pltpu.PrefetchScalarGridSpec(
            num_scalar_prefetch=1, grid=(2 * steps,), in_specs=[half, full, half, full, full, full],
            out_specs=[pl.BlockSpec((per, chunk_rows, d), lambda g, s: (jnp.minimum(g, steps - 1), 0, 0)),
                       pl.BlockSpec((per, chunk_rows, d), lambda g, s: (jnp.maximum(g - steps, 0), 0, 0))]),
        out_shape=[sds((steps * per, chunk_rows, d), bf16)] * 2,
        compiler_params=params(),
        cost_estimate=cost(8 * rows * d * d, 8 * d * d + 12 * rows * d),
        name="attn_gradient",
    )(sec, o, low, h, dq, dk, dv)


AXES = ("section", "dp")
SWAP = [(0, 1), (1, 0)]


def bit_orders(dp):
    bits = list(range(dp.bit_length() - 1))
    if len(bits) < 3:
        return bits, bits[::-1]
    return [0, 2, 1] + bits[3:], [1, 2, 0] + bits[3:]


def exchange(array, dp, step):
    first, second = bit_orders(dp)
    pairs = [(i, i ^ (1 << first[step])) for i in range(dp)]
    pairs += [(dp + i, dp + (i ^ (1 << second[step]))) for i in range(dp)]
    return lax.ppermute(array, AXES, pairs)


def block_of(chunks, rows):
    best = 1
    for c in range(1, chunks + 1):
        if chunks % c == 0 and c * rows <= 768:
            best = c
    return best


def add_split(bit, parts):
    _, c, r, w = parts[0][0].shape
    counts = [p[0].shape[0] for p in parts]
    n = sum(counts)
    h = c // 2
    cb = block_of(h, r)
    nb = h // cb
    ends = [sum(counts[:i + 1]) for i in range(len(counts))]
    begins = [e - k for e, k in zip(ends, counts)]

    def kernel(s_ref, *refs):
        send_ref, keep_ref = refs[-2:]
        g, i = pl.program_id(0), pl.program_id(1)
        for t in range(len(parts)):
            @pl.when((i >= begins[t]) & (i < ends[t]))
            def _():
                total = (refs[2 * t][...].astype(f32) + refs[2 * t + 1][...].astype(f32)).astype(bf16)

                @pl.when(g == 0)
                def _():
                    send_ref[...] = total

                @pl.when(g == 1)
                def _():
                    keep_ref[...] = total

    def source(t):
        def index(g, i, j, s):
            inside = (i >= begins[t]) & (i < ends[t])
            side = jnp.where(g == 0, 1 - s[0], s[0])
            return (jnp.clip(i - begins[t], 0, counts[t] - 1), jnp.where(inside, side * nb + j, 0), 0, 0)
        return pl.BlockSpec((1, cb, r, w), index)

    def send_at(g, i, j, s):
        return (jnp.where(g == 0, i, n - 1), jnp.where(g == 0, j, nb - 1), 0, 0)

    def keep_at(g, i, j, s):
        return (jnp.where(g == 0, 0, i), jnp.where(g == 0, 0, j), 0, 0)

    flat = [x for p in parts for x in p]
    return pl.pallas_call(
        kernel,
        grid_spec=pltpu.PrefetchScalarGridSpec(
            num_scalar_prefetch=1, grid=(2, n, nb),
            in_specs=[source(t) for t in range(len(parts)) for _ in range(2)],
            out_specs=[pl.BlockSpec((1, cb, r, w), send_at), pl.BlockSpec((1, cb, r, w), keep_at)]),
        out_shape=[sds((n, h, r, w), bf16)] * 2,
        compiler_params=params(),
        cost_estimate=cost(n * c * r * w, 6 * n * c * r * w),
        name="add_split",
    )(bit, *flat)


def merge(bit, cur, arrived):
    n, c, r, w = cur.shape
    cb = block_of(c, r)
    nb = c // cb

    def kernel(s_ref, a_ref, b_ref, out_ref):
        g = pl.program_id(1)

        @pl.when(g == s_ref[0])
        def _():
            out_ref[...] = a_ref[...]

        @pl.when(g != s_ref[0])
        def _():
            out_ref[...] = b_ref[...]

    def at(own):
        def index(i, g, j, s):
            mine = (g == s[0]) if own else (g != s[0])
            return (i, jnp.where(mine, j, 0), 0, 0)
        return pl.BlockSpec((1, cb, r, w), index)

    return pl.pallas_call(
        kernel,
        grid_spec=pltpu.PrefetchScalarGridSpec(
            num_scalar_prefetch=1, grid=(n, 2, nb), in_specs=[at(True), at(False)],
            out_specs=pl.BlockSpec((1, cb, r, w), lambda i, g, j, s: (i, g * nb + j, 0, 0))),
        out_shape=sds((n, 2 * c, r, w), bf16),
        compiler_params=params(),
        cost_estimate=cost(0, 8 * n * c * r * w),
        name="merge",
    )(bit, cur, arrived)


def assemble(scalars, sources, outs, place, name):
    c, r, w = sources[0][0][0].shape[1:]
    block = w // 2
    cb = block // r
    nb = c // cb
    flat = [item for layer in sources for item in layer]

    def chosen(g, s):
        part = g // 2
        bit = jnp.where(part == 0, s[1], s[2])
        return 4 * s[0] + jnp.where(part == s[0], 0, 2) + jnp.where(g % 2 == bit, 0, 1)

    def kernel(s_ref, *refs):
        g, j = pl.program_id(0), pl.program_id(1)
        which = chosen(g, s_ref)
        out_refs = refs[len(flat):]
        for i in range(len(flat)):
            @pl.when(which == i)
            def _():
                value = refs[i][0].astype(f32).reshape(block, w)
                if len(outs) == 1:
                    out_refs[0][...] = value
                else:
                    for t, out_ref in enumerate(out_refs):
                        @pl.when((g % 2) * nb + j == t)
                        def _():
                            out_ref[...] = value

    def source(i):
        index = flat[i][1]
        return pl.BlockSpec((1, cb, r, w), lambda g, j, s: (index, jnp.where(chosen(g, s) == i, j, 0), 0, 0))

    def out_at(t):
        def index(g, j, s):
            return place(g // 2, (g % 2) * nb + j, t)
        return pl.BlockSpec((block, w), index)

    return pl.pallas_call(
        kernel,
        grid_spec=pltpu.PrefetchScalarGridSpec(
            num_scalar_prefetch=1, grid=(4, nb), in_specs=[source(i) for i in range(len(flat))],
            out_specs=[out_at(t) for t in range(len(outs))]),
        out_shape=[sds(o, f32) for o in outs],
        compiler_params=params(),
        cost_estimate=cost(0, 6 * 4 * c * r * w),
        name=name,
    )(scalars, *[a for a, _ in flat])


def local(
    boundary,
    lengths,
    norm_one_gain,
    norm_one_bias,
    query_weight,
    query_bias,
    key_weight,
    value_weight,
    value_bias,
    first_value_weight,
    first_value_bias,
    out_weight,
    out_bias,
    norm_two_gain,
    norm_two_bias,
    up_weight,
    up_bias,
    down_weight,
    down_bias,
):
    section = lax.axis_index("section")
    spot = lax.axis_index("dp")
    dp = lax.axis_size("dp")
    on_first = section == 0
    sec = jnp.reshape(section, (1,)).astype(jnp.int32)
    rows = boundary.shape[1] // 2
    d = boundary.shape[2]
    half = value_weight.shape[2]
    ff = up_weight.shape[2]

    def swap(array):
        return lax.ppermute(array, "section", SWAP)

    def row(vector):
        return jnp.reshape(vector, (-1, d))

    vec_own = jnp.concatenate([
        norm_one_gain, norm_one_bias, query_bias,
        jnp.concatenate([first_value_bias[None], value_bias], axis=1),
        out_bias, norm_two_gain, norm_two_bias, down_bias, row(up_bias)], axis=0)
    vec_own = jnp.pad(vec_own, ((0, VEC_ROWS - vec_own.shape[0]), (0, 0)))
    top, bottom = boundary[0, :rows], boundary[0, rows:]
    arrived_rows = swap(jnp.where(on_first, bottom, top))
    kept_rows = jnp.where(on_first, top, bottom)
    x0 = jnp.where(on_first, kept_rows, arrived_rows)
    dz1 = jnp.where(on_first, arrived_rows, kept_rows)
    vec_arrived = swap(vec_own)
    vec = (jnp.where(on_first, vec_own, vec_arrived), jnp.where(on_first, vec_arrived, vec_own))
    w = {"qo": query_weight[0], "ko": key_weight[0], "vo": value_weight[0], "oo": out_weight[0],
         "uo": up_weight[0], "do": down_weight[0], "f": first_value_weight}
    for name in "qkvoud":
        w[name + "r"] = swap(w[name + "o"])

    own_lengths = jnp.where(on_first, lengths[0], lengths[1])
    cuts = jnp.cumsum(own_lengths)
    at = jnp.arange(rows, dtype=jnp.int32)
    start = jnp.max(jnp.where(at[:, None] >= cuts[None, :], cuts[None, :], 0), axis=1).astype(jnp.int32)
    start_col, start_row = start[:, None], start[None, :]

    kept = []
    x, shared = x0, x0
    for layer in range(2):
        h, q, k, v, o, m, e, lse = attn_forward(layer, sec, x, shared, start_col, vec[layer], w)
        u, a, z = feed_forward(layer, sec, e, m, vec[layer], w)
        kept.append((x, h, q, k, v, o, m, e, lse, u, a))
        x, shared = z, v
    y = x

    chunk_rows = ff // (2 * dp)
    first_bits, second_bits = bit_orders(dp)
    bits = [jnp.reshape((spot >> jnp.where(on_first, first_bits[s], second_bits[s])) & 1, (1,)).astype(jnp.int32)
            for s in range(len(first_bits))]

    def begin(pieces):
        send, keep = pieces
        arrived = swap(send)
        send, keep = add_split(bits[0], [(keep[None], arrived[None])])
        return keep, exchange(send, dp, 0)

    def reduce_rest(parts):
        for s in range(1, len(bits)):
            send, keep = add_split(bits[s], parts)
            parts = [(keep, exchange(send, dp, s))]
        keep, arrived = parts[0]
        return (keep.astype(f32) + arrived.astype(f32)).astype(bf16)

    def gather(cur):
        for s in reversed(range(1, len(bits))):
            cur = merge(bits[s], cur, exchange(cur, dp, s))
        return cur, exchange(cur, dp, 0)

    dz = dz1
    dr2 = jnp.zeros((rows, half), f32)
    started, small = [], []
    for layer in (1, 0):
        x, h, q, k, v, o, m, e, lse, u, a = kept[layer]
        started.append(begin(down_gradient(sec, a, dz, chunk_rows)))
        du, dm, low, small_feed = feed_backward(layer, sec, dz, u, m, vec[layer], w)
        started.append(begin(up_gradient(sec, e, du, chunk_rows)))
        dz, dq, dk, dv, dr2, small_attn = attn_backward(
            layer, sec, x, dm, low, q, k, v, o, lse, start_row, vec[layer], dr2, w)
        started.append(begin(attn_gradient(sec, o, low, h, dq, dk, dv, chunk_rows)))
        small.append(small_feed + small_attn)
    dx0 = dz

    to_second = lambda t: lax.ppermute(t, "section", [(0, 1)])
    to_first = lambda t: lax.ppermute(t, "section", [(1, 0)])

    cur_a, got_a = gather(reduce_rest(started[0:2]))
    cur_b, got_b = gather(reduce_rest(started[2:4]))
    cur_c, got_c = gather(reduce_rest(started[4:6]))
    other_a = (to_second(cur_a), to_second(got_a))
    other_b = tuple(swap(jnp.where(on_first, t[0], t[1]))[None] for t in (cur_b, got_b))
    other_c = (to_first(cur_c), to_first(got_c))
    scalars = jnp.stack([section, (spot >> first_bits[0]) & 1, (spot >> second_bits[0]) & 1]).astype(jnp.int32)

    down_grad, = assemble(
        scalars, (((cur_b, 1), (got_b, 1), (other_b[0], 0), (other_b[1], 0)),
                  ((cur_a, 0), (got_a, 0), (other_a[0], 0), (other_a[1], 0))),
        [(ff, d)], lambda part, block, t: (part * 4 + block, 0), "assemble_down")
    up_grad, = assemble(
        scalars, (((cur_c, 0), (got_c, 0), (other_c[0], 0), (other_c[1], 0)),
                  ((cur_a, 1), (got_a, 1), (other_a[0], 1), (other_a[1], 1))),
        [(d, ff)], lambda part, block, t: (block % 2, part * 2 + block // 2), "assemble_up")
    out_grad, query_grad, key_grad, mixed_grad = assemble(
        scalars, (((cur_c, 1), (got_c, 1), (other_c[0], 1), (other_c[1], 1)),
                  ((cur_b, 0), (got_b, 0), (other_b[0], 0), (other_b[1], 0))),
        [(d, d)] * 4, lambda part, block, t: (jnp.where(block < t, jnp.maximum(part - 1, 0), part), 0),
        "assemble_attn")
    last = jnp.where(bits[0][0] == 1, cur_c[1], got_c[1])
    first_grad = last.reshape(-1, d)[-(d // 2):, :half].astype(f32)

    own_small = jnp.where(on_first, small[1], small[0])
    total = own_small + swap(jnp.where(on_first, small[0], small[1]))
    for s in range(len(bits)):
        total = total + lax.ppermute(total, "dp", [(i, i ^ (1 << s)) for i in range(dp)])
    first_bias = to_second(total[VBIAS, :half])
    first_bias = jnp.where(on_first, total[VBIAS, :half // 2], first_bias[half // 2:])

    send_end = swap(jnp.where(on_first, y, dx0))
    keep_end = jnp.where(on_first, dx0, y)
    block_ends = jnp.where(on_first, jnp.concatenate([keep_end, send_end], axis=0),
                           jnp.concatenate([send_end, keep_end], axis=0))[None]
    return (
        block_ends,
        total[GAIN1][None],
        total[BIAS1][None],
        query_grad[None],
        total[QBIAS][None],
        key_grad[None],
        mixed_grad[None, :, half:],
        total[VBIAS, half:][None],
        first_grad,
        first_bias,
        out_grad[None],
        total[OBIAS][None],
        total[GAIN2][None],
        total[BIAS2][None],
        up_grad[None],
        total[UBIAS:UBIAS + ff // d].reshape(1, ff),
        down_grad[None],
        total[DBIAS][None],
    )


def solution(mesh):
    stacked = P("section", None, None)
    vector = P("section", None)
    return jax.shard_map(
        local,
        mesh=mesh,
        in_specs=(
            P("section", "dp", None), P("dp", None),
            vector, vector, stacked, vector, stacked, stacked, vector, P(), P(),
            stacked, vector, vector, vector, stacked, vector, stacked, vector,
        ),
        out_specs=(
            P("section", "dp", None),
            vector, vector, stacked, vector, stacked, stacked, vector, P("section"), P("section"),
            stacked, vector, vector, vector, stacked, vector, stacked, vector,
        ),
        check_vma=False,
    )
```

time: 1370 us -> 602 us (0.44)
  waiting for transfers between devices: 676 us -> 247 us
  matrix products: 258 us -> 0 us
  Pallas kernels: 0 us -> 239 us
  blocking collectives: 84 us -> 0 us
  local copies, waits for them, and re-layouts: 116 us -> 38.9 us
  loops' own time: 70.6 us -> 0 us
  other arithmetic: 80.5 us -> 13.2 us
    psum x1 -> x0, waiting for transfers between devices: 658 us -> none  [local(): lax.psum((attention_grads[0], attention_grads[1], attention_grads[2], att...]
    dot_general x56 -> x0, matrix products: 258 us -> none  [the longest x14 63.2 us: dense_outer(): lax.dot_general(input_rows, grad_rows, (((0,), (0,)), ((), ())), preferre...]
    pallas_call x0 -> x41, Pallas kernels: none -> 239 us  [the longest x15 44.9 us: add_split(): pl.pallas_call(kernel, grid_spec=pltpu.PrefetchScalarGridSpec(num_scalar_...]
    ppermute x10 -> x54, waiting for transfers between devices: 17.6 us -> 247 us  [the longest x27 194 us: exchange(): return lax.ppermute(array, AXES, pairs)]
    psum x1 -> x0, blocking collectives: 84 us -> none  [local(): lax.psum((attention_grads[0], attention_grads[1], attention_grads[2], att...]
    another operation x10 -> x0, loops' own time: 70.6 us -> none  [the longest x2 34.2 us: local(): lax.cond(on_first, lambda: (blank_rows, blank_back, feed_grads, attention...]
    cond x173 -> x0, local copies, waits for them, and re-layouts: 37.2 us -> none
    reduce_sum x24 -> x0, other arithmetic: 28.5 us -> none  [the longest x6 7.51 us: normed(): spread = jnp.mean(centred * centred, axis=-1, keepdims=True)]
  transfers between devices with their start and end apart: 11 -> 54, of which waited for: 2 -> 27; matrix products, arithmetic and copies ran while one was open for 7% -> 3% of each run, Pallas kernels for 0% -> 21%
where the time goes in v1:
time: 602 us; the launch traced here: 594 us
  waiting for transfers between devices  247 us (41%)
  Pallas kernels  239 us (40%)
  starting transfers between devices  53.9 us (9%)
  local copies, waits for them, and re-layouts  38.9 us (6%)
  other arithmetic  13.2 us (2%)
    ppermute x27, waiting for transfers between devices, exchange(): return lax.ppermute(array, AXES, pairs)  194 us
    pallas_call x15, Pallas kernels, add_split(): pl.pallas_call(kernel, grid_spec=pltpu.PrefetchScalarGridSpec(num_scalar_...  44.9 us
    ppermute x4, waiting for transfers between devices, local(): lax.ppermute(total, 'dp', [(i, i ^ 1 << s) for i in range(dp)])  38.9 us
    pallas_call x2, Pallas kernels, attn_backward(): pl.pallas_call(functools.partial(attn_backward_kernel, layer), out_shape=...  37.9 us
    unnamed x197, local copies, waits for them, and re-layouts  35.4 us
    ppermute x27, starting transfers between devices, exchange(): return lax.ppermute(array, AXES, pairs)  31.9 us
    pallas_call x2, Pallas kernels, feed_backward(): pl.pallas_call(functools.partial(feed_backward_kernel, layer, blk), grid=...  30.9 us
    pallas_call x2, Pallas kernels, attn_forward(): pl.pallas_call(functools.partial(attn_forward_kernel, layer), out_shape=[...  30.4 us
  transfers between devices with their start and end apart: 54, of which 27 were waited for; matrix products, arithmetic and copies ran while one was open for 3% of the time, Pallas kernels for 21%

profile of v1, /device:TPU:0, one launch (start us, length us, event | category | flops | bytes accessed | tf_op | source)
XLA Modules:
  0.0 594.0 jit_solution(1494126404653813990)
XLA Ops:
  6.2 4.5 collective-permute-done.1
  11.2 6.8 %collective-permute-done = bf16[512,768]{1,0:T(8,128)(2,1)} collective-permute-done((bf16[512,768]{1,0:T(8,128)(2,1)}, bf16[512,768]{1,0:T(8,128)(2,1)}, u32[]{:S(2)}, u32[]{:S(2)}) %collective-permute-start) | collective-permute-done | bytes 786464 | tf_op jit(solution)/shard_map/ppermute | solution.py:712
  23.0 15.3 %attn_forward.2 = (bf16[512,768]{1,0:T(8,128)(2,1)S(1)}, bf16[512,768]{1,0:T(8,128)(2,1)S(1)}, bf16[512,768]{1,0:T(8,128)(2,1)S(1)}, bf16[512,768]{1,0:T(8,128)(...) custom-call(s32[1]{0:T(128)} %bitcast.sec_ref.s_ref, ...), custom_call_target="tpu_custom_call" | custom-call | flops 3019898880 | bytes 9437184 | tf_op jit(solution)/shard_map/attn_forward/pallas_call | solution.py:173
  43.0 11.3 %feed_forward.2 = (bf16[512,3072]{1,0:T(8,128)(2,1)}, bf16[512,3072]{1,0:T(8,128)(2,1)}, bf16[512,768]{1,0:T(8,128)(2,1)S(1)}) custom-call(s32[1]{0:T(128)} %bitcast.sec_ref.s_ref, bf16[512,768]{1,0:T(8,128)(2,1)S(1)} %copy-done.31, f32[512,768]{1,0:T(8,128)S(1)} %copy-done.2, f32[16,768]{1,0:T(8,128)S(1)} %get-tuple-element.197.vec_ref, ...), custom_call_target="tpu_custom_call" | custom-call | flops 4831838208 | bytes 15728640 | tf_op jit(solution)/shard_map/feed_forward/pallas_call | solution.py:229
  55.2 15.1 %attn_forward.3 = (bf16[512,768]{1,0:T(8,128)(2,1)S(1)}, bf16[512,768]{1,0:T(8,128)(2,1)S(1)}, bf16[512,768]{1,0:T(8,128)(2,1)S(1)}, bf16[512,768]{1,0:T(8,128)(...) custom-call(s32[1]{0:T(128)} %bitcast.sec_ref.s_ref, ...), custom_call_target="tpu_custom_call" | custom-call | flops 3019898880 | bytes 9437184 | tf_op jit(solution)/shard_map/attn_forward/pallas_call | solution.py:173
  74.1 11.4 %feed_forward.3 = (bf16[512,3072]{1,0:T(8,128)(2,1)}, bf16[512,3072]{1,0:T(8,128)(2,1)}, bf16[512,768]{1,0:T(8,128)(2,1)S(1)}) custom-call(s32[1]{0:T(128)} %bitcast.sec_ref.s_ref, bf16[512,768]{1,0:T(8,128)(2,1)S(1)} %copy-done.29, f32[512,768]{1,0:T(8,128)S(1)} %copy-done.4, f32[16,768]{1,0:T(8,128)S(1)} %get-tuple-element.196.vec_ref, ...), custom_call_target="tpu_custom_call" | custom-call | flops 4831838208 | bytes 15728640 | tf_op jit(solution)/shard_map/feed_forward/pallas_call | solution.py:229
  86.4 15.2 %feed_backward.2 = (bf16[512,3072]{1,0:T(8,128)(2,1)}, f32[512,768]{1,0:T(8,128)S(1)}, bf16[512,768]{1,0:T(8,128)(2,1)S(1)}, f32[16,768]{1,0:T(8,128)S(1)}) custom-call(s32[1]{0:T(128)} %bitcast.sec_ref.s_ref, bf16[512,768]{1,0:T(8,128)(2,1)S(1)} %get-tuple-element.192.dz_ref.refs_1_, bf16[512,3072]{1,0:T(8,128)(2,1)} %get-tuple-element.111.u_ref, ...), custom_call_target="tpu_custom_call" | custom-call | flops 4831838208 | bytes 15728640 | tf_op jit(solution)/shard_map/feed_backward/pallas_call | solution.py:290
  105.2 19.6 %attn_backward.2 = (bf16[512,768]{1,0:T(8,128)(2,1)S(1)}, bf16[512,768]{1,0:T(8,128)(2,1)S(1)}, bf16[512,768]{1,0:T(8,128)(2,1)S(1)}, bf16[512,768]{1,0:T(8,128)...) custom-call(s32[1]{0:T(128)} %bitcast.sec_ref.s_ref, bf16[512,768]{1,0:T(8,128)(2,1)} %copy-done.49, ...), custom_call_target="tpu_custom_call" | custom-call | flops 4831838208 | bytes 12582912 | tf_op jit(solution)/shard_map/attn_backward/pallas_call | solution.py:408
  126.6 15.8 %feed_backward.3 = (bf16[512,3072]{1,0:T(8,128)(2,1)}, f32[512,768]{1,0:T(8,128)S(1)}, bf16[512,768]{1,0:T(8,128)(2,1)S(1)}, f32[16,768]{1,0:T(8,128)S(1)}) custom-call(s32[1]{0:T(128)} %bitcast.sec_ref.s_ref, bf16[512,768]{1,0:T(8,128)(2,1)S(1)} %get-tuple-element.119.dz_ref.refs_1_, bf16[512,3072]{1,0:T(8,128)(2,1)} %get-tuple-element.120.u_ref, ...), custom_call_target="tpu_custom_call" | custom-call | flops 4831838208 | bytes 15728640 | tf_op jit(solution)/shard_map/feed_backward/pallas_call | solution.py:290
  142.4 5.8 up_gradient.2
  148.7 18.3 %attn_backward.3 = (bf16[512,768]{1,0:T(8,128)(2,1)S(1)}, bf16[512,768]{1,0:T(8,128)(2,1)S(1)}, bf16[512,768]{1,0:T(8,128)(2,1)S(1)}, bf16[512,768]{1,0:T(8,128)...) custom-call(s32[1]{0:T(128)} %bitcast.sec_ref.s_ref, bf16[512,768]{1,0:T(8,128)(2,1)} %get-tuple-element.193.x_ref.r_ref, ...), custom_call_target="tpu_custom_call" | custom-call | flops 4831838208 | bytes 12582912 | tf_op jit(solution)/shard_map/attn_backward/pallas_call | solution.py:408
  174.6 6.4 %attn_gradient.2 = (bf16[16,96,768]{2,1,0:T(8,128)(2,1)}, bf16[16,96,768]{2,1,0:T(8,128)(2,1)}) custom-call(s32[1]{0:T(128)} %bitcast.sec_ref.s_ref, bf16[512,768]{1,0:T(8,128)(2,1)S(1)} %copy-done.55, bf16[512,768]{1,0:T(8,128)(2,1)S(1)} %copy-done.48, bf16[512,768]{1,0:T(8,128)(2,1)S(1)} %copy-done.53, bf16[512,768]{1,0:T(8,128)(2,1)S(1)} %copy-done.74, ...), custom_call_target="tpu_custom_call" | custom-call | flops 2415919104 | bytes 9437184 | tf_op jit(solution)/shard_map/attn_gradient/pallas_call | solution.py:505
  181.1 6.6 %attn_gradient.3 = (bf16[16,96,768]{2,1,0:T(8,128)(2,1)}, bf16[16,96,768]{2,1,0:T(8,128)(2,1)}) custom-call(s32[1]{0:T(128)} %bitcast.sec_ref.s_ref, bf16[512,768]{1,0:T(8,128)(2,1)S(1)} %copy-done.59, bf16[512,768]{1,0:T(8,128)(2,1)S(1)} %copy-done.46, bf16[512,768]{1,0:T(8,128)(2,1)S(1)} %copy-done.57, bf16[512,768]{1,0:T(8,128)(2,1)S(1)} %copy-done.67, ...), custom_call_target="tpu_custom_call" | custom-call | flops 2415919104 | bytes 9437184 | tf_op jit(solution)/shard_map/attn_gradient/pallas_call | solution.py:505
  188.1 6.6 %down_gradient.2 = (bf16[16,96,768]{2,1,0:T(8,128)(2,1)}, bf16[16,96,768]{2,1,0:T(8,128)(2,1)S(1)}) custom-call(s32[1]{0:T(128)} %bitcast.sec_ref.s_ref, bf16[512,3072]{1,0:T(8,128)(2,1)} %get-tuple-element.161.refs_0_, bf16[512,768]{1,0:T(8,128)(2,1)S(1)} %get-tuple-element.119.dz_ref.refs_1_), custom_call_target="tpu_custom_call" | custom-call | flops 2415919104 | bytes 7864320 | tf_op jit(solution)/shard_map/down_gradient/pallas_call | solution.py:445
  196.2 6.7 %down_gradient.3 = (bf16[16,96,768]{2,1,0:T(8,128)(2,1)}, bf16[16,96,768]{2,1,0:T(8,128)(2,1)S(1)}) custom-call(s32[1]{0:T(128)} %bitcast.sec_ref.s_ref, bf16[512,3072]{1,0:T(8,128)(2,1)} %get-tuple-element.176.refs_0_, bf16[512,768]{1,0:T(8,128)(2,1)S(1)} %get-tuple-element.192.dz_ref.refs_1_), custom_call_target="tpu_custom_call" | custom-call | flops 2415919104 | bytes 7864320 | tf_op jit(solution)/shard_map/down_gradient/pallas_call | solution.py:445
  204.8 6.6 %up_gradient.3 = (bf16[16,96,768]{2,1,0:T(8,128)(2,1)}, bf16[16,96,768]{2,1,0:T(8,128)(2,1)S(1)}) custom-call(s32[1]{0:T(128)} %bitcast.sec_ref.s_ref, bf16[512,768]{1,0:T(8,128)(2,1)S(1)} %copy-done.30, bf16[512,3072]{1,0:T(8,128)(2,1)} %get-tuple-element.181.refs_1_), custom_call_target="tpu_custom_call" | custom-call | flops 2415919104 | bytes 7864320 | tf_op jit(solution)/shard_map/up_gradient/pallas_call | solution.py:445
  218.5 3.7 add_split.16
  222.3 4.0 add_split.20
  228.0 3.7 add_split.21
  233.0 3.7 add_split.25
  239.5 3.6 add_split.26
  246.7 4.5 add_split.17
  254.5 3.5 collective-permute-done.28.refs_1_
  258.1 12.6 %collective-permute-done.30.refs_3_ = bf16[1,8,96,768]{3,2,1,0:T(8,128)(2,1)} collective-permute-done((bf16[1,8,96,768]{3,2,1,0:T(8,128)(2,1)}, bf16[1,8,96,768]{3,2,1,0:T(8,128)(2,1)}, u32[]{:S(2)}, u32[]{:S(2)}) %collective-permute-start.30) | collective-permute-done | bytes 1179680 | tf_op jit(solution)/shard_map/ppermute | solution.py:533
  270.7 4.5 add_split.22
  277.8 5.6 collective-permute-done.42.refs_1_
  283.4 12.6 %collective-permute-done.44.refs_3_ = bf16[1,8,96,768]{3,2,1,0:T(8,128)(2,1)} collective-permute-done((bf16[1,8,96,768]{3,2,1,0:T(8,128)(2,1)}, bf16[1,8,96,768]{3,2,1,0:T(8,128)(2,1)}, u32[]{:S(2)}, u32[]{:S(2)}) %collective-permute-start.44) | collective-permute-done | bytes 1179680 | tf_op jit(solution)/shard_map/ppermute | solution.py:533
  296.0 4.5 add_split.27
  308.2 3.6 add_split.23
  312.4 18.5 %collective-permute-done.45.refs_1_ = bf16[2,4,96,768]{3,2,1,0:T(8,128)(2,1)} collective-permute-done((bf16[2,4,96,768]{3,2,1,0:T(8,128)(2,1)}, bf16[2,4,96,768]{3,2,1,0:T(8,128)(2,1)}, u32[]{:S(2)}, u32[]{:S(2)}) %collective-permute-start.45) | collective-permute-done | bytes 1179680 | tf_op jit(solution)/shard_map/ppermute | solution.py:533
  330.8 3.6 add_split.28
  339.7 4.9 collective-permute-done.46.refs_1_
  347.5 17.7 %collective-permute-done.20 = bf16[2,1,96,768]{3,2,1,0:T(8,128)(2,1)S(1)} collective-permute-done((bf16[2,1,96,768]{3,2,1,0:T(8,128)(2,1)S(1)}, bf16[2,1,96,768]{3,2,1,0:T(8,128)(2,1)S(1)}, u32[]{:S(2)}, u32[]{:S(2)}) %collective-permute-start.20) | collective-permute-done | bytes 294944 | tf_op jit(solution)/shard_map/ppermute | solution.py:533
  365.4 12.5 %collective-permute-done.33 = bf16[2,1,96,768]{3,2,1,0:T(8,128)(2,1)S(1)} collective-permute-done((bf16[2,1,96,768]{3,2,1,0:T(8,128)(2,1)S(1)}, bf16[2,1,96,768]{3,2,1,0:T(8,128)(2,1)S(1)}, u32[]{:S(2)}, u32[]{:S(2)}) %collective-permute-start.33) | collective-permute-done | bytes 294944 | tf_op jit(solution)/shard_map/ppermute | solution.py:533
  378.1 12.5 %collective-permute-done.47 = bf16[2,1,96,768]{3,2,1,0:T(8,128)(2,1)S(1)} collective-permute-done((bf16[2,1,96,768]{3,2,1,0:T(8,128)(2,1)S(1)}, bf16[2,1,96,768]{3,2,1,0:T(8,128)(2,1)S(1)}, u32[]{:S(2)}, u32[]{:S(2)}) %collective-permute-start.47) | collective-permute-done | bytes 294944 | tf_op jit(solution)/shard_map/ppermute | solution.py:533
  390.7 12.5 %collective-permute-done.21.b_ref = bf16[2,1,96,768]{3,2,1,0:T(8,128)(2,1)S(1)} collective-permute-done((bf16[2,1,96,768]{3,2,1,0:T(8,128)(2,1)S(1)}, bf16[2,1,96,768]{3,2,1,0:T(8,128)(2,1)S(1)}, u32[]{:S(2)}, u32[]{:S(2)}) %collective-permute-start.21) | collective-permute-done | bytes 294944 | tf_op jit(solution)/shard_map/ppermute | solution.py:533
  404.8 4.7 collective-permute-done.34.b_ref
  411.1 3.4 collective-permute-done.48.b_ref
  419.9 6.1 %collective-permute-done.49.b_ref = bf16[2,2,96,768]{3,2,1,0:T(8,128)(2,1)S(1)} collective-permute-done((bf16[2,2,96,768]{3,2,1,0:T(8,128)(2,1)S(1)}, bf16[2,2,96,768]{3,2,1,0:T(8,128)(2,1)S(1)}, u32[]{:S(2)}, u32[]{:S(2)}) %collective-permute-start.49) | collective-permute-done | bytes 589856 | tf_op jit(solution)/shard_map/ppermute | solution.py:533
  426.2 19.2 %collective-permute-done.23.b_ref = bf16[2,4,96,768]{3,2,1,0:T(8,128)(2,1)S(1)} collective-permute-done((bf16[2,4,96,768]{3,2,1,0:T(8,128)(2,1)S(1)}, bf16[2,4,96,768]{3,2,1,0:T(8,128)(2,1)S(1)}, u32[]{:S(2)}, u32[]{:S(2)}) %collective-permute-start.23) | collective-permute-done | bytes 1179680 | tf_op jit(solution)/shard_map/ppermute | solution.py:533
  447.8 22.8 %collective-permute-done.36.b_ref = bf16[2,4,96,768]{3,2,1,0:T(8,128)(2,1)S(1)} collective-permute-done((bf16[2,4,96,768]{3,2,1,0:T(8,128)(2,1)S(1)}, bf16[2,4,96,768]{3,2,1,0:T(8,128)(2,1)S(1)}, u32[]{:S(2)}, u32[]{:S(2)}) %collective-permute-start.36) | collective-permute-done | bytes 1179680 | tf_op jit(solution)/shard_map/ppermute | solution.py:533
  471.6 21.0 %collective-permute-done.50.b_ref = bf16[2,4,96,768]{3,2,1,0:T(8,128)(2,1)S(1)} collective-permute-done((bf16[2,4,96,768]{3,2,1,0:T(8,128)(2,1)S(1)}, bf16[2,4,96,768]{3,2,1,0:T(8,128)(2,1)S(1)}, u32[]{:S(2)}, u32[]{:S(2)}) %collective-permute-start.50) | collective-permute-done | bytes 1179680 | tf_op jit(solution)/shard_map/ppermute | solution.py:533
  498.0 29.9 %collective-permute-done.10 = f32[16,768]{1,0:T(8,128)S(1)} collective-permute-done((f32[16,768]{1,0:T(8,128)S(1)}, f32[16,768]{1,0:T(8,128)S(1)}, u32[]{:S(2)}, u32[]{:S(2)}) %collective-permute-start.10) | collective-permute-done | bytes 49184 | tf_op jit(solution)/shard_map/ppermute | solution.py:816
  528.5 3.6 collective-permute-done.11
  547.0 7.3 %collective-permute-start.52 = (bf16[2,8,96,768]{3,2,1,0:T(8,128)(2,1)}, bf16[2,8,96,768]{3,2,1,0:T(8,128)(2,1)}, u32[]{:S(2)}, u32[]{:S(2)}) collective-permute-start(bf16[2,8,96,768]{3,2,1,0:T(8,128)(2,1)} %merge.17.refs_4_), channel_id=1, source_target_pairs={{0,16},{1,17},{2,18},{3,19},{4,20},{5,21},{6,22},{7,23},{8,24},{9,... | collective-permute-start | bytes 7077896 | tf_op jit(solution)/shard_map/ppermute | solution.py:786
  564.3 10.1 %assemble_attn.1 = (f32[768,768]{1,0:T(8,128)}, f32[768,768]{1,0:T(8,128)}, f32[768,768]{1,0:T(8,128)}, f32[768,768]{1,0:T(8,128)S(1)}) custom-call(s32[3]{0:T(128)S(1)} %pad_add_fusion.s_ref, bf16[2,8,96,768]{3,2,1,0:T(8,128)(2,1)} %merge.11.refs_0_, bf16[2,8,96,768]{3,2,1,0:T(8,128)(2,1)} %collective-permute-done.24.refs_1_, ...), custom_call_target="tpu_custom_call" | custom-call | bytes 14155776 | tf_op jit(solution)/shard_map/assemble_attn/pallas_call | solution.py:668
  575.5 9.9 %assemble_up.1 = f32[768,3072]{1,0:T(8,128)} custom-call(s32[3]{0:T(128)S(1)} %pad_add_fusion.s_ref, bf16[2,8,96,768]{3,2,1,0:T(8,128)(2,1)} %merge.11.refs_0_, bf16[2,8,96,768]{3,2,1,0:T(8,128)(2,1)} %collective-permute-done.24.refs_1_, bf16[2,8,96,768]{3,2,1,0:T(8,128)(2,1)} %collective-permute-done.25.refs_2_, ...), custom_call_target="tpu_custom_call" | custom-call | bytes 14155776 | tf_op jit(solution)/shard_map/assemble_up/pallas_call | solution.py:668
  585.4 8.1 %assemble_down.1 = f32[3072,768]{1,0:T(8,128)} custom-call(s32[3]{0:T(128)S(1)} %pad_add_fusion.s_ref, bf16[2,8,96,768]{3,2,1,0:T(8,128)(2,1)S(1)} %copy-done.1, bf16[2,8,96,768]{3,2,1,0:T(8,128)(2,1)} %copy-done.79, bf16[1,8,96,768]{3,2,1,0:T(8,128)(2,1)S(1)} %bitcast.58, bf16[1,8,96,768]{3,2,1,0:T(8,128)(2,1)S(1)} %bitcast.60, ...), custom_call_target="tpu_custom_call" | custom-call | bytes 14155776 | tf_op jit(solution)/shard_map/assemble_down/pallas_call | solution.py:668
  (333 shorter events, 121.4 us)
Async XLA Ops:
  0.8 38.5 %collective-permute-start.6 = (bf16[768,3072]{1,0:T(8,128)(2,1)}, bf16[768,3072]{1,0:T(8,128)(2,1)}, u32[]{:S(2)}, u32[]{:S(2)}) collective-permute-start(bf16[768,3072]{1,0:T(8,128)(2,1)} %bitcast.75), channel_id=1, source_target_pairs={{0,16},{16,0},{1,17},{17,1},{2,18},{18,2},{3,19},{19,3},{4,20},{20... | collective-permute-start | bytes 14155784 | tf_op jit(solution)/shard_map/ppermute | solution.py:712
  1.3 38.0 %collective-permute-start.7 = (bf16[3072,768]{1,0:T(8,128)(2,1)}, bf16[3072,768]{1,0:T(8,128)(2,1)}, u32[]{:S(2)}, u32[]{:S(2)}) collective-permute-start(bf16[3072,768]{1,0:T(8,128)(2,1)} %bitcast.80), channel_id=1, source_target_pairs={{0,16},{16,0},{1,17},{17,1},{2,18},{18,2},{3,19},{19,3},{4,20},{20... | collective-permute-start | bytes 14155784 | tf_op jit(solution)/shard_map/ppermute | solution.py:712
  3.8 14.2 %collective-permute-start = (bf16[512,768]{1,0:T(8,128)(2,1)}, bf16[512,768]{1,0:T(8,128)(2,1)}, u32[]{:S(2)}, u32[]{:S(2)}) collective-permute-start(bf16[512,768]{1,0:T(8,128)(2,1)} %select_bitcast_fusion.1), channel_id=1, source_target_pairs={{0,16},{16,0},{1,17},{17,1},{2,18},{18,2},{3,19},{19,3},{4,20},{20... | collective-permute-start | bytes 2359304 | tf_op jit(solution)/shard_map/ppermute | solution.py:712
  4.2 6.9 %collective-permute-start.4 = (bf16[768,384]{1,0:T(8,128)(2,1)S(1)}, bf16[768,384]{1,0:T(8,128)(2,1)S(1)}, u32[]{:S(2)}, u32[]{:S(2)}) collective-permute-start(bf16[768,384]{1,0:T(8,128)(2,1)S(1)} %bitcast.70), channel_id=1, source_target_pairs={{0,16},{16,0},{1,17},{17,1},{2,18},{18,2},{3,19},{19,3},{4,20},{20... | collective-permute-start | bytes 1769480 | tf_op jit(solution)/shard_map/ppermute | solution.py:712
  10.7 10.4 %collective-permute-start.2 = (bf16[768,768]{1,0:T(8,128)(2,1)}, bf16[768,768]{1,0:T(8,128)(2,1)}, u32[]{:S(2)}, u32[]{:S(2)}) collective-permute-start(bf16[768,768]{1,0:T(8,128)(2,1)} %bitcast.95), channel_id=1, source_target_pairs={{0,16},{16,0},{1,17},{17,1},{2,18},{18,2},{3,19},{19,3},{4,20},{20... | collective-permute-start | bytes 3538952 | tf_op jit(solution)/shard_map/ppermute | solution.py:712
  11.0 10.3 %collective-permute-start.3 = (bf16[768,768]{1,0:T(8,128)(2,1)}, bf16[768,768]{1,0:T(8,128)(2,1)}, u32[]{:S(2)}, u32[]{:S(2)}) collective-permute-start(bf16[768,768]{1,0:T(8,128)(2,1)} %bitcast.100), channel_id=1, source_target_pairs={{0,16},{16,0},{1,17},{17,1},{2,18},{18,2},{3,19},{19,3},{4,20},{20... | collective-permute-start | bytes 3538952 | tf_op jit(solution)/shard_map/ppermute | solution.py:712
  18.0 5.1 collective-permute-start.5
  148.3 64.5 %collective-permute-start.14 = (bf16[16,96,768]{2,1,0:T(8,128)(2,1)S(1)}, bf16[16,96,768]{2,1,0:T(8,128)(2,1)}, u32[]{:S(2)}, u32[]{:S(2)}) collective-permute-start(bf16[16,96,768]{2,1,0:T(8,128)(2,1)S(1)} %get-tuple-element.136), channel_id=1, source_target_pairs={{0,16},{16,0},{1,17},{17,1},{2,18},{18,2},{3,19},{19,3},{4,20},{20... | collective-permute-start | bytes 7077896 | tf_op jit(solution)/shard_map/ppermute | solution.py:712
  180.9 34.6 %collective-permute-start.16 = (bf16[16,96,768]{2,1,0:T(8,128)(2,1)}, bf16[16,96,768]{2,1,0:T(8,128)(2,1)}, u32[]{:S(2)}, u32[]{:S(2)}) collective-permute-start(bf16[16,96,768]{2,1,0:T(8,128)(2,1)} %get-tuple-element.144), channel_id=1, source_target_pairs={{0,16},{16,0},{1,17},{17,1},{2,18},{18,2},{3,19},{19,3},{4,20},{20... | collective-permute-start | bytes 7077896 | tf_op jit(solution)/shard_map/ppermute | solution.py:712
  187.7 34.5 %collective-permute-start.27 = (bf16[16,96,768]{2,1,0:T(8,128)(2,1)}, bf16[16,96,768]{2,1,0:T(8,128)(2,1)}, u32[]{:S(2)}, u32[]{:S(2)}) collective-permute-start(bf16[16,96,768]{2,1,0:T(8,128)(2,1)} %get-tuple-element.158), channel_id=1, source_target_pairs={{0,16},{16,0},{1,17},{17,1},{2,18},{18,2},{3,19},{19,3},{4,20},{20... | collective-permute-start | bytes 7077896 | tf_op jit(solution)/shard_map/ppermute | solution.py:712
  196.1 30.2 %collective-permute-start.29 = (bf16[16,96,768]{2,1,0:T(8,128)(2,1)}, bf16[16,96,768]{2,1,0:T(8,128)(2,1)}, u32[]{:S(2)}, u32[]{:S(2)}) collective-permute-start(bf16[16,96,768]{2,1,0:T(8,128)(2,1)} %get-tuple-element.163), channel_id=1, source_target_pairs={{0,16},{16,0},{1,17},{17,1},{2,18},{18,2},{3,19},{19,3},{4,20},{20... | collective-permute-start | bytes 7077896 | tf_op jit(solution)/shard_map/ppermute | solution.py:712
  204.4 28.3 %collective-permute-start.41 = (bf16[16,96,768]{2,1,0:T(8,128)(2,1)}, bf16[16,96,768]{2,1,0:T(8,128)(2,1)}, u32[]{:S(2)}, u32[]{:S(2)}) collective-permute-start(bf16[16,96,768]{2,1,0:T(8,128)(2,1)} %get-tuple-element.178), channel_id=1, source_target_pairs={{0,16},{16,0},{1,17},{17,1},{2,18},{18,2},{3,19},{19,3},{4,20},{20... | collective-permute-start | bytes 7077896 | tf_op jit(solution)/shard_map/ppermute | solution.py:712
  212.7 25.0 %collective-permute-start.43 = (bf16[16,96,768]{2,1,0:T(8,128)(2,1)}, bf16[16,96,768]{2,1,0:T(8,128)(2,1)}, u32[]{:S(2)}, u32[]{:S(2)}) collective-permute-start(bf16[16,96,768]{2,1,0:T(8,128)(2,1)} %get-tuple-element.183), channel_id=1, source_target_pairs={{0,16},{16,0},{1,17},{17,1},{2,18},{18,2},{3,19},{19,3},{4,20},{20... | collective-permute-start | bytes 7077896 | tf_op jit(solution)/shard_map/ppermute | solution.py:712
  215.6 28.5 %collective-permute-start.15 = (bf16[1,8,96,768]{3,2,1,0:T(8,128)(2,1)S(1)}, bf16[1,8,96,768]{3,2,1,0:T(8,128)(2,1)S(1)}, u32[]{:S(2)}, u32[]{:S(2)}) collective-permute-start(bf16[1,8,96,768]{3,2,1,0:T(8,128)(2,1)S(1)} %get-tuple-element.138), channel_id=1, source_target_pairs={{0,1},{1,0},{2,3},{3,2},{4,5},{5,4},{6,7},{7,6},{8,9},{9,8},{10,11... | collective-permute-start | bytes 3538952 | tf_op jit(solution)/shard_map/ppermute | solution.py:533
  222.2 23.2 %collective-permute-start.17 = (bf16[1,8,96,768]{3,2,1,0:T(8,128)(2,1)}, bf16[1,8,96,768]{3,2,1,0:T(8,128)(2,1)}, u32[]{:S(2)}, u32[]{:S(2)}) collective-permute-start(bf16[1,8,96,768]{3,2,1,0:T(8,128)(2,1)} %get-tuple-element.146), channel_id=1, source_target_pairs={{0,1},{1,0},{2,3},{3,2},{4,5},{5,4},{6,7},{7,6},{8,9},{9,8},{10,11... | collective-permute-start | bytes 3538952 | tf_op jit(solution)/shard_map/ppermute | solution.py:533
  226.3 31.8 %collective-permute-start.28 = (bf16[1,8,96,768]{3,2,1,0:T(8,128)(2,1)}, bf16[1,8,96,768]{3,2,1,0:T(8,128)(2,1)}, u32[]{:S(2)}, u32[]{:S(2)}) collective-permute-start(bf16[1,8,96,768]{3,2,1,0:T(8,128)(2,1)} %get-tuple-element.160), channel_id=1, source_target_pairs={{0,1},{1,0},{2,3},{3,2},{4,5},{5,4},{6,7},{7,6},{8,9},{9,8},{10,11... | collective-permute-start | bytes 3538952 | tf_op jit(solution)/shard_map/ppermute | solution.py:533
  232.7 38.0 %collective-permute-start.30 = (bf16[1,8,96,768]{3,2,1,0:T(8,128)(2,1)}, bf16[1,8,96,768]{3,2,1,0:T(8,128)(2,1)}, u32[]{:S(2)}, u32[]{:S(2)}) collective-permute-start(bf16[1,8,96,768]{3,2,1,0:T(8,128)(2,1)} %get-tuple-element.165), channel_id=1, source_target_pairs={{0,1},{1,0},{2,3},{3,2},{4,5},{5,4},{6,7},{7,6},{8,9},{9,8},{10,11... | collective-permute-start | bytes 3538952 | tf_op jit(solution)/shard_map/ppermute | solution.py:533
  237.8 45.6 %collective-permute-start.42 = (bf16[1,8,96,768]{3,2,1,0:T(8,128)(2,1)}, bf16[1,8,96,768]{3,2,1,0:T(8,128)(2,1)}, u32[]{:S(2)}, u32[]{:S(2)}) collective-permute-start(bf16[1,8,96,768]{3,2,1,0:T(8,128)(2,1)} %get-tuple-element.180), channel_id=1, source_target_pairs={{0,1},{1,0},{2,3},{3,2},{4,5},{5,4},{6,7},{7,6},{8,9},{9,8},{10,11... | collective-permute-start | bytes 3538952 | tf_op jit(solution)/shard_map/ppermute | solution.py:533
  244.1 51.9 %collective-permute-start.44 = (bf16[1,8,96,768]{3,2,1,0:T(8,128)(2,1)}, bf16[1,8,96,768]{3,2,1,0:T(8,128)(2,1)}, u32[]{:S(2)}, u32[]{:S(2)}) collective-permute-start(bf16[1,8,96,768]{3,2,1,0:T(8,128)(2,1)} %get-tuple-element.185), channel_id=1, source_target_pairs={{0,1},{1,0},{2,3},{3,2},{4,5},{5,4},{6,7},{7,6},{8,9},{9,8},{10,11... | collective-permute-start | bytes 3538952 | tf_op jit(solution)/shard_map/ppermute | solution.py:533
  252.2 51.8 %collective-permute-start.18 = (bf16[2,4,96,768]{3,2,1,0:T(8,128)(2,1)}, bf16[2,4,96,768]{3,2,1,0:T(8,128)(2,1)S(1)}, u32[]{:S(2)}, u32[]{:S(2)}) collective-permute-start(bf16[2,4,96,768]{3,2,1,0:T(8,128)(2,1)} %get-tuple-element.148), channel_id=1, source_target_pairs={{0,4},{1,5},{2,6},{3,7},{4,0},{5,1},{6,2},{7,3},{8,12},{9,13},{10,... | collective-permute-start | bytes 3538952 | tf_op jit(solution)/shard_map/ppermute | solution.py:533
  275.2 33.0 %collective-permute-start.31 = (bf16[2,4,96,768]{3,2,1,0:T(8,128)(2,1)}, bf16[2,4,96,768]{3,2,1,0:T(8,128)(2,1)}, u32[]{:S(2)}, u32[]{:S(2)}) collective-permute-start(bf16[2,4,96,768]{3,2,1,0:T(8,128)(2,1)} %get-tuple-element.167), channel_id=1, source_target_pairs={{0,4},{1,5},{2,6},{3,7},{4,0},{5,1},{6,2},{7,3},{8,12},{9,13},{10,... | collective-permute-start | bytes 3538952 | tf_op jit(solution)/shard_map/ppermute | solution.py:533
  301.5 29.4 %collective-permute-start.45 = (bf16[2,4,96,768]{3,2,1,0:T(8,128)(2,1)}, bf16[2,4,96,768]{3,2,1,0:T(8,128)(2,1)}, u32[]{:S(2)}, u32[]{:S(2)}) collective-permute-start(bf16[2,4,96,768]{3,2,1,0:T(8,128)(2,1)} %get-tuple-element.187), channel_id=1, source_target_pairs={{0,4},{1,5},{2,6},{3,7},{4,0},{5,1},{6,2},{7,3},{8,12},{9,13},{10,... | collective-permute-start | bytes 3538952 | tf_op jit(solution)/shard_map/ppermute | solution.py:533
  306.7 29.3 %collective-permute-start.19 = (bf16[2,2,96,768]{3,2,1,0:T(8,128)(2,1)}, bf16[2,2,96,768]{3,2,1,0:T(8,128)(2,1)S(1)}, u32[]{:S(2)}, u32[]{:S(2)}) collective-permute-start(bf16[2,2,96,768]{3,2,1,0:T(8,128)(2,1)} %get-tuple-element.150), channel_id=1, source_target_pairs={{0,2},{1,3},{2,0},{3,1},{4,6},{5,7},{6,4},{7,5},{8,10},{9,11},{10,... | collective-permute-start | bytes 1769480 | tf_op jit(solution)/shard_map/ppermute | solution.py:533
  311.9 27.1 %collective-permute-start.32 = (bf16[2,2,96,768]{3,2,1,0:T(8,128)(2,1)}, bf16[2,2,96,768]{3,2,1,0:T(8,128)(2,1)S(1)}, u32[]{:S(2)}, u32[]{:S(2)}) collective-permute-start(bf16[2,2,96,768]{3,2,1,0:T(8,128)(2,1)} %get-tuple-element.169), channel_id=1, source_target_pairs={{0,2},{1,3},{2,0},{3,1},{4,6},{5,7},{6,4},{7,5},{8,10},{9,11},{10,... | collective-permute-start | bytes 1769480 | tf_op jit(solution)/shard_map/ppermute | solution.py:533
  334.5 10.1 %collective-permute-start.46 = (bf16[2,2,96,768]{3,2,1,0:T(8,128)(2,1)}, bf16[2,2,96,768]{3,2,1,0:T(8,128)(2,1)S(1)}, u32[]{:S(2)}, u32[]{:S(2)}) collective-permute-start(bf16[2,2,96,768]{3,2,1,0:T(8,128)(2,1)} %get-tuple-element.189), channel_id=1, source_target_pairs={{0,2},{1,3},{2,0},{3,1},{4,6},{5,7},{6,4},{7,5},{8,10},{9,11},{10,... | collective-permute-start | bytes 1769480 | tf_op jit(solution)/shard_map/ppermute | solution.py:533
  336.3 29.0 %collective-permute-start.20 = (bf16[2,1,96,768]{3,2,1,0:T(8,128)(2,1)S(1)}, bf16[2,1,96,768]{3,2,1,0:T(8,128)(2,1)S(1)}, u32[]{:S(2)}, u32[]{:S(2)}) collective-permute-start(bf16[2,1,96,768]{3,2,1,0:T(8,128)(2,1)S(1)} %get-tuple-element.152), channel_id=1, source_target_pairs={{0,8},{1,9},{2,10},{3,11},{4,12},{5,13},{6,14},{7,15},{8,0},{9,1},... | collective-permute-start | bytes 884744 | tf_op jit(solution)/shard_map/ppermute | solution.py:533
  339.3 38.6 %collective-permute-start.33 = (bf16[2,1,96,768]{3,2,1,0:T(8,128)(2,1)S(1)}, bf16[2,1,96,768]{3,2,1,0:T(8,128)(2,1)S(1)}, u32[]{:S(2)}, u32[]{:S(2)}) collective-permute-start(bf16[2,1,96,768]{3,2,1,0:T(8,128)(2,1)S(1)} %get-tuple-element.171), channel_id=1, source_target_pairs={{0,8},{1,9},{2,10},{3,11},{4,12},{5,13},{6,14},{7,15},{8,0},{9,1},... | collective-permute-start | bytes 884744 | tf_op jit(solution)/shard_map/ppermute | solution.py:533
  344.9 45.7 %collective-permute-start.47 = (bf16[2,1,96,768]{3,2,1,0:T(8,128)(2,1)S(1)}, bf16[2,1,96,768]{3,2,1,0:T(8,128)(2,1)S(1)}, u32[]{:S(2)}, u32[]{:S(2)}) collective-permute-start(bf16[2,1,96,768]{3,2,1,0:T(8,128)(2,1)S(1)} %get-tuple-element.191), channel_id=1, source_target_pairs={{0,8},{1,9},{2,10},{3,11},{4,12},{5,13},{6,14},{7,15},{8,0},{9,1},... | collective-permute-start | bytes 884744 | tf_op jit(solution)/shard_map/ppermute | solution.py:533
  365.4 37.8 %collective-permute-start.21 = (bf16[2,1,96,768]{3,2,1,0:T(8,128)(2,1)S(1)}, bf16[2,1,96,768]{3,2,1,0:T(8,128)(2,1)S(1)}, u32[]{:S(2)}, u32[]{:S(2)}) collective-permute-start(bf16[2,1,96,768]{3,2,1,0:T(8,128)(2,1)S(1)} %add_convert_fusion.2.a_ref), channel_id=1, source_target_pairs={{0,8},{1,9},{2,10},{3,11},{4,12},{5,13},{6,14},{7,15},{8,0},{9,1},... | collective-permute-start | bytes 884744 | tf_op jit(solution)/shard_map/ppermute | solution.py:533
  378.0 31.5 %collective-permute-start.34 = (bf16[2,1,96,768]{3,2,1,0:T(8,128)(2,1)S(1)}, bf16[2,1,96,768]{3,2,1,0:T(8,128)(2,1)S(1)}, u32[]{:S(2)}, u32[]{:S(2)}) collective-permute-start(bf16[2,1,96,768]{3,2,1,0:T(8,128)(2,1)S(1)} %add_convert_fusion.1.a_ref), channel_id=1, source_target_pairs={{0,8},{1,9},{2,10},{3,11},{4,12},{5,13},{6,14},{7,15},{8,0},{9,1},... | collective-permute-start | bytes 884744 | tf_op jit(solution)/shard_map/ppermute | solution.py:533
  390.6 23.9 %collective-permute-start.48 = (bf16[2,1,96,768]{3,2,1,0:T(8,128)(2,1)S(1)}, bf16[2,1,96,768]{3,2,1,0:T(8,128)(2,1)S(1)}, u32[]{:S(2)}, u32[]{:S(2)}) collective-permute-start(bf16[2,1,96,768]{3,2,1,0:T(8,128)(2,1)S(1)} %add_convert_fusion.a_ref), channel_id=1, source_target_pairs={{0,8},{1,9},{2,10},{3,11},{4,12},{5,13},{6,14},{7,15},{8,0},{9,1},... | collective-permute-start | bytes 884744 | tf_op jit(solution)/shard_map/ppermute | solution.py:533
  403.3 12.9 %collective-permute-start.22 = (bf16[2,2,96,768]{3,2,1,0:T(8,128)(2,1)S(1)}, bf16[2,2,96,768]{3,2,1,0:T(8,128)(2,1)S(1)}, u32[]{:S(2)}, u32[]{:S(2)}) collective-permute-start(bf16[2,2,96,768]{3,2,1,0:T(8,128)(2,1)S(1)} %merge.9.a_ref), channel_id=1, source_target_pairs={{0,2},{1,3},{2,0},{3,1},{4,6},{5,7},{6,4},{7,5},{8,10},{9,11},{10,... | collective-permute-start | bytes 1769480 | tf_op jit(solution)/shard_map/ppermute | solution.py:533
  409.7 9.9 %collective-permute-start.35 = (bf16[2,2,96,768]{3,2,1,0:T(8,128)(2,1)S(1)}, bf16[2,2,96,768]{3,2,1,0:T(8,128)(2,1)S(1)}, u32[]{:S(2)}, u32[]{:S(2)}) collective-permute-start(bf16[2,2,96,768]{3,2,1,0:T(8,128)(2,1)S(1)} %merge.12.a_ref), channel_id=1, source_target_pairs={{0,2},{1,3},{2,0},{3,1},{4,6},{5,7},{6,4},{7,5},{8,10},{9,11},{10,... | collective-permute-start | bytes 1769480 | tf_op jit(solution)/shard_map/ppermute | solution.py:533
  414.6 11.3 %collective-permute-start.49 = (bf16[2,2,96,768]{3,2,1,0:T(8,128)(2,1)S(1)}, bf16[2,2,96,768]{3,2,1,0:T(8,128)(2,1)S(1)}, u32[]{:S(2)}, u32[]{:S(2)}) collective-permute-start(bf16[2,2,96,768]{3,2,1,0:T(8,128)(2,1)S(1)} %merge.15.a_ref), channel_id=1, source_target_pairs={{0,2},{1,3},{2,0},{3,1},{4,6},{5,7},{6,4},{7,5},{8,10},{9,11},{10,... | collective-permute-start | bytes 1769480 | tf_op jit(solution)/shard_map/ppermute | solution.py:533
  416.4 29.0 %collective-permute-start.23 = (bf16[2,4,96,768]{3,2,1,0:T(8,128)(2,1)S(1)}, bf16[2,4,96,768]{3,2,1,0:T(8,128)(2,1)S(1)}, u32[]{:S(2)}, u32[]{:S(2)}) collective-permute-start(bf16[2,4,96,768]{3,2,1,0:T(8,128)(2,1)S(1)} %merge.10.a_ref), channel_id=1, source_target_pairs={{0,4},{1,5},{2,6},{3,7},{4,0},{5,1},{6,2},{7,3},{8,12},{9,13},{10,... | collective-permute-start | bytes 3538952 | tf_op jit(solution)/shard_map/ppermute | solution.py:533
  419.8 50.9 %collective-permute-start.36 = (bf16[2,4,96,768]{3,2,1,0:T(8,128)(2,1)S(1)}, bf16[2,4,96,768]{3,2,1,0:T(8,128)(2,1)S(1)}, u32[]{:S(2)}, u32[]{:S(2)}) collective-permute-start(bf16[2,4,96,768]{3,2,1,0:T(8,128)(2,1)S(1)} %merge.13.a_ref), channel_id=1, source_target_pairs={{0,4},{1,5},{2,6},{3,7},{4,0},{5,1},{6,2},{7,3},{8,12},{9,13},{10,... | collective-permute-start | bytes 3538952 | tf_op jit(solution)/shard_map/ppermute | solution.py:533
  426.1 66.5 %collective-permute-start.50 = (bf16[2,4,96,768]{3,2,1,0:T(8,128)(2,1)S(1)}, bf16[2,4,96,768]{3,2,1,0:T(8,128)(2,1)S(1)}, u32[]{:S(2)}, u32[]{:S(2)}) collective-permute-start(bf16[2,4,96,768]{3,2,1,0:T(8,128)(2,1)S(1)} %merge.16.a_ref), channel_id=1, source_target_pairs={{0,4},{1,5},{2,6},{3,7},{4,0},{5,1},{6,2},{7,3},{8,12},{9,13},{10,... | collective-permute-start | bytes 3538952 | tf_op jit(solution)/shard_map/ppermute | solution.py:533
  447.3 98.4 %collective-permute-start.24 = (bf16[2,8,96,768]{3,2,1,0:T(8,128)(2,1)}, bf16[2,8,96,768]{3,2,1,0:T(8,128)(2,1)}, u32[]{:S(2)}, u32[]{:S(2)}) collective-permute-start(bf16[2,8,96,768]{3,2,1,0:T(8,128)(2,1)} %merge.11.refs_0_), channel_id=1, source_target_pairs={{0,1},{1,0},{2,3},{3,2},{4,5},{5,4},{6,7},{7,6},{8,9},{9,8},{10,11... | collective-permute-start | bytes 7077896 | tf_op jit(solution)/shard_map/ppermute | solution.py:533
  471.0 76.0 %collective-permute-start.37 = (bf16[2,8,96,768]{3,2,1,0:T(8,128)(2,1)S(1)}, bf16[2,8,96,768]{3,2,1,0:T(8,128)(2,1)S(1)}, u32[]{:S(2)}, u32[]{:S(2)}) collective-permute-start(bf16[2,8,96,768]{3,2,1,0:T(8,128)(2,1)S(1)} %merge.14.refs_4_.refs_0_), channel_id=1, source_target_pairs={{0,1},{1,0},{2,3},{3,2},{4,5},{5,4},{6,7},{7,6},{8,9},{9,8},{10,11... | collective-permute-start | bytes 7077896 | tf_op jit(solution)/shard_map/ppermute | solution.py:533
  494.6 59.8 %collective-permute-start.51 = (bf16[2,8,96,768]{3,2,1,0:T(8,128)(2,1)}, bf16[2,8,96,768]{3,2,1,0:T(8,128)(2,1)}, u32[]{:S(2)}, u32[]{:S(2)}) collective-permute-start(bf16[2,8,96,768]{3,2,1,0:T(8,128)(2,1)} %merge.17.refs_4_), channel_id=1, source_target_pairs={{0,1},{1,0},{2,3},{3,2},{4,5},{5,4},{6,7},{7,6},{8,9},{9,8},{10,11... | collective-permute-start | bytes 7077896 | tf_op jit(solution)/shard_map/ppermute | solution.py:533
  497.4 30.5 %collective-permute-start.10 = (f32[16,768]{1,0:T(8,128)S(1)}, f32[16,768]{1,0:T(8,128)S(1)}, u32[]{:S(2)}, u32[]{:S(2)}) collective-permute-start(f32[16,768]{1,0:T(8,128)S(1)} %select_add_fusion), channel_id=1, source_target_pairs={{0,1},{1,0},{2,3},{3,2},{4,5},{5,4},{6,7},{7,6},{8,9},{9,8},{10,11... | collective-permute-start | bytes 147464 | tf_op jit(solution)/shard_map/ppermute | solution.py:816
  533.8 10.5 %collective-permute-start.8 = (bf16[512,768]{1,0:T(8,128)(2,1)S(1)}, bf16[512,768]{1,0:T(8,128)(2,1)S(1)}, u32[]{:S(2)}, u32[]{:S(2)}) collective-permute-start(bf16[512,768]{1,0:T(8,128)(2,1)S(1)} %get-tuple-element.195), channel_id=1, source_target_pairs={{0,16},{16,0},{1,17},{17,1},{2,18},{18,2},{3,19},{19,3},{4,20},{20... | collective-permute-start | bytes 2359304 | tf_op jit(solution)/shard_map/ppermute | solution.py:712
  544.4 12.9 %collective-permute-start.38 = (bf16[8,96,768]{2,1,0:T(8,128)(2,1)}, bf16[8,96,768]{2,1,0:T(8,128)(2,1)S(1)}, u32[]{:S(2)}, u32[]{:S(2)}) collective-permute-start(bf16[8,96,768]{2,1,0:T(8,128)(2,1)} %fusion.1), channel_id=1, source_target_pairs={{0,16},{16,0},{1,17},{17,1},{2,18},{18,2},{3,19},{19,3},{4,20},{20... | collective-permute-start | bytes 3538952 | tf_op jit(solution)/shard_map/ppermute | solution.py:712
  544.4 19.8 %collective-permute-start.25 = (bf16[2,8,96,768]{3,2,1,0:T(8,128)(2,1)}, bf16[2,8,96,768]{3,2,1,0:T(8,128)(2,1)}, u32[]{:S(2)}, u32[]{:S(2)}) collective-permute-start(bf16[2,8,96,768]{3,2,1,0:T(8,128)(2,1)} %merge.11.refs_0_), channel_id=1, source_target_pairs={{16,0},{17,1},{18,2},{19,3},{20,4},{21,5},{22,6},{23,7},{24,8},{25... | collective-permute-start | bytes 7077896 | tf_op jit(solution)/shard_map/ppermute | solution.py:787
  545.7 18.5 %collective-permute-start.26 = (bf16[2,8,96,768]{3,2,1,0:T(8,128)(2,1)}, bf16[2,8,96,768]{3,2,1,0:T(8,128)(2,1)}, u32[]{:S(2)}, u32[]{:S(2)}) collective-permute-start(bf16[2,8,96,768]{3,2,1,0:T(8,128)(2,1)} %collective-permute-done.24.refs_1_), channel_id=1, source_target_pairs={{16,0},{17,1},{18,2},{19,3},{20,4},{21,5},{22,6},{23,7},{24,8},{25... | collective-permute-start | bytes 7077896 | tf_op jit(solution)/shard_map/ppermute | solution.py:787
  547.0 28.5 %collective-permute-start.52 = (bf16[2,8,96,768]{3,2,1,0:T(8,128)(2,1)}, bf16[2,8,96,768]{3,2,1,0:T(8,128)(2,1)}, u32[]{:S(2)}, u32[]{:S(2)}) collective-permute-start(bf16[2,8,96,768]{3,2,1,0:T(8,128)(2,1)} %merge.17.refs_4_), channel_id=1, source_target_pairs={{0,16},{1,17},{2,18},{3,19},{4,20},{5,21},{6,22},{7,23},{8,24},{9,... | collective-permute-start | bytes 7077896 | tf_op jit(solution)/shard_map/ppermute | solution.py:786
  554.4 21.1 %collective-permute-start.53 = (bf16[2,8,96,768]{3,2,1,0:T(8,128)(2,1)}, bf16[2,8,96,768]{3,2,1,0:T(8,128)(2,1)}, u32[]{:S(2)}, u32[]{:S(2)}) collective-permute-start(bf16[2,8,96,768]{3,2,1,0:T(8,128)(2,1)} %collective-permute-done.51.refs_5_), channel_id=1, source_target_pairs={{0,16},{1,17},{2,18},{3,19},{4,20},{5,21},{6,22},{7,23},{8,24},{9,... | collective-permute-start | bytes 7077896 | tf_op jit(solution)/shard_map/ppermute | solution.py:786
  557.3 7.0 %collective-permute-start.39 = (bf16[8,96,768]{2,1,0:T(8,128)(2,1)S(1)}, bf16[8,96,768]{2,1,0:T(8,128)(2,1)S(1)}, u32[]{:S(2)}, u32[]{:S(2)}) collective-permute-start(bf16[8,96,768]{2,1,0:T(8,128)(2,1)S(1)} %fusion), channel_id=1, source_target_pairs={{0,16},{16,0},{1,17},{17,1},{2,18},{18,2},{3,19},{19,3},{4,20},{20... | collective-permute-start | bytes 3538952 | tf_op jit(solution)/shard_map/ppermute | solution.py:712
  (103 other events, 994.2 us)

commit v2 on v1

v2 whole, which is shorter than its diff:
```python
import functools

import jax
import jax.numpy as jnp
from jax import lax
from jax.experimental import pallas as pl
from jax.experimental.pallas import tpu as pltpu
from jax.sharding import PartitionSpec as P

HEADS = 12
HEAD = 64
PAIR = 2 * HEAD
VMEM_BYTES = 64 * 1024 * 1024

eps_norm = 1e-05
neg_fill = -1e30

f32 = jnp.float32
bf16 = jnp.bfloat16

NN = (((1,), (0,)), ((), ()))
NT = (((1,), (1,)), ((), ()))
TN = (((0,), (0,)), ((), ()))

ANY = pl.BlockSpec(memory_space=pl.ANY)
SMEM = pl.BlockSpec(memory_space=pltpu.SMEM)
VMEM = pl.BlockSpec(memory_space=pltpu.VMEM)

GAIN1, BIAS1, QBIAS, VBIAS, OBIAS, GAIN2, BIAS2, DBIAS, UBIAS = range(9)
VEC_ROWS = 16

TIME_SCALE = 0.5


def mm(left, right, dims=NN):
    return lax.dot_general(left, right, dims, preferred_element_type=f32)


def sds(shape, dtype):
    return jax.ShapeDtypeStruct(shape, dtype)


def params():
    return pltpu.CompilerParams(vmem_limit_bytes=VMEM_BYTES)


def cost(micros):
    return pl.CostEstimate(flops=int(1e11), bytes_accessed=1, transcendentals=0)


def start_fetch(mine, own, recv, dst, sem):
    @pl.when(mine)
    def _():
        pltpu.make_async_copy(own, dst, sem).start()

    @pl.when(jnp.logical_not(mine))
    def _():
        pltpu.make_async_copy(recv, dst, sem).start()


def wait_fetch(own, dst, sem):
    pltpu.make_async_copy(own, dst, sem).wait()


def norm_parts(rows):
    centre = jnp.mean(rows, axis=-1, keepdims=True)
    centred = rows - centre
    spread = jnp.mean(centred * centred, axis=-1, keepdims=True)
    factor = lax.rsqrt(spread + eps_norm)
    return centred * factor, factor


def norm_back(grad_t, n, w):
    return w * (
        grad_t
        - jnp.mean(grad_t, axis=-1, keepdims=True)
        - n * jnp.mean(grad_t * n, axis=-1, keepdims=True)
    )


def row_sum(x):
    return jnp.sum(x, axis=0, keepdims=True)


def attend(rows, q_s, k_s, v_s, o_s, lse_s, bias_s):
    lane = lax.broadcasted_iota(jnp.int32, (1, PAIR), 1)
    step = rows // 2

    def pair(hp, carry):
        ls = pl.ds(pl.multiple_of(hp * PAIR, PAIR), PAIR)
        q2 = q_s[:, ls] * jnp.asarray(HEAD ** -0.5, bf16)
        k2 = k_s[:, ls]
        v2 = v_s[:, ls]
        zero = jnp.zeros((), bf16)
        for qb in range(2):
            qr = slice(qb * step, (qb + 1) * step)
            keys = (qb + 1) * step
            mixed = None
            for j in range(2):
                inside = (lane >= j * HEAD) & (lane < (j + 1) * HEAD)
                kh = jnp.where(inside, k2[:keys], zero)
                vh = jnp.where(inside, v2[:keys], zero)
                s = mm(q2[qr], kh, NT) + bias_s[qr, :keys]
                peak = jnp.max(s, axis=-1, keepdims=True)
                p = jnp.exp(s - peak)
                total = jnp.sum(p, axis=-1, keepdims=True)
                low = (p * (1.0 / total)).astype(bf16)
                part = mm(low, vh)
                mixed = part if mixed is None else mixed + part
                lse_s[qr, :] = jnp.where(lane == 2 * hp + j, peak + jnp.log(total), lse_s[qr, :])
            o_s[qr, ls] = mixed.astype(bf16)
        return carry

    lse_s[...] = jnp.zeros(lse_s.shape, f32)
    lax.fori_loop(0, HEADS // 2, pair, 0)


def attn_forward_steps(layer, sec_ref, x_ref, r_ref, start_ref, vec_ref, weights, outs, held, in_sem, out_sem):
    (qw_o, qw_r, kw_o, kw_r, vw_o, vw_r, fw, ow_o, ow_r), (wq, wk, wv, wo) = weights
    h_out, q_out, k_out, v_out, o_out, m_out, e_out, lse_out, sent_out = outs
    h_s, q_s, k_s, v_s, o_s, m_s, e_s, lse_s, lset_s, bias_s = held
    mine = sec_ref[0] == layer
    rows = x_ref.shape[0]
    half = fw.shape[1]
    copies = []

    def fetch():
        start_fetch(mine, qw_o, qw_r, wq, in_sem.at[0])
        start_fetch(mine, kw_o, kw_r, wk, in_sem.at[1])
        start_fetch(mine, vw_o, vw_r, wv.at[:, half:], in_sem.at[2])
        if layer == 0:
            pltpu.make_async_copy(fw, wv.at[:, :half], in_sem.at[3]).start()
        start_fetch(mine, ow_o, ow_r, wo, in_sem.at[4])

    def put(src, dst):
        copy = pltpu.make_async_copy(src, dst, out_sem.at[len(copies)])
        copy.start()
        copies.append(copy)

    def run():
        wide = x_ref[...].astype(f32)
        n, _ = norm_parts(wide)
        h_s[...] = (n * vec_ref[GAIN1:GAIN1 + 1, :] + vec_ref[BIAS1:BIAS1 + 1, :]).astype(bf16)
        put(h_s, h_out)
        theirs = pl.ds(pl.multiple_of((1 - sec_ref[0]) * half, half), half)
        put(h_s.at[:, theirs], sent_out.at[0, :, half:])
        at_row = lax.broadcasted_iota(jnp.int32, (rows, rows), 0)
        at_col = lax.broadcasted_iota(jnp.int32, (rows, rows), 1)
        bias_s[...] = jnp.where((at_col <= at_row) & (at_col >= start_ref[...]), 0.0, neg_fill)
        wait_fetch(qw_o, wq, in_sem.at[0])
        q_s[...] = (mm(h_s[...], wq[...]) + vec_ref[QBIAS:QBIAS + 1, :]).astype(bf16)
        put(q_s, q_out)
        wait_fetch(kw_o, wk, in_sem.at[1])
        k_s[...] = mm(h_s[...], wk[...]).astype(bf16)
        put(k_s, k_out)
        wait_fetch(vw_o, wv.at[:, half:], in_sem.at[2])
        if layer == 0:
            wait_fetch(fw, wv.at[:, :half], in_sem.at[3])
            v_s[...] = (mm(h_s[...], wv[...]) + vec_ref[VBIAS:VBIAS + 1, :]).astype(bf16)
        else:
            v_s[:, :half] = r_ref[:, :half]
            v_s[:, half:] = (mm(h_s[...], wv[:, half:]) + vec_ref[VBIAS:VBIAS + 1, half:]).astype(bf16)
        put(v_s, v_out)
        attend(rows, q_s, k_s, v_s, o_s, lse_s, bias_s)
        put(o_s, o_out)
        put(o_s.at[:, theirs], sent_out.at[0, :, :half])
        lset_s[...] = jnp.transpose(lse_s[...])[:VEC_ROWS, :]
        put(lset_s, lse_out)
        wait_fetch(ow_o, wo, in_sem.at[4])
        m = x_ref[...].astype(f32) + (mm(o_s[...], wo[...]) + vec_ref[OBIAS:OBIAS + 1, :])
        m_s[...] = m
        put(m_s, m_out)
        n, _ = norm_parts(m)
        e_s[...] = (n * vec_ref[GAIN2:GAIN2 + 1, :] + vec_ref[BIAS2:BIAS2 + 1, :]).astype(bf16)
        put(e_s, e_out)
        put(e_s, sent_out.at[1])

    return fetch, run, copies


def attn_forward_kernel(layer, sec_ref, x_ref, r_ref, start_ref, vec_ref, *refs):
    fetch, run, copies = attn_forward_steps(
        layer, sec_ref, x_ref, r_ref, start_ref, vec_ref, (refs[:9], refs[18:22]), refs[9:18], refs[22:32],
        refs[32], refs[33])
    fetch()
    run()
    for copy in copies:
        copy.wait()


def attn_forward_shapes(rows, d):
    act = sds((rows, d), bf16)
    wbuf = pltpu.VMEM((d, d), bf16)
    abuf = pltpu.VMEM((rows, d), bf16)
    outs = [act, act, act, act, act, sds((rows, d), f32), act, sds((VEC_ROWS, rows), f32), sds((2, rows, d), bf16)]
    scratch = [wbuf, wbuf, wbuf, wbuf, abuf, abuf, abuf, abuf, abuf,
               pltpu.VMEM((rows, d), f32), abuf, pltpu.VMEM((rows, PAIR), f32),
               pltpu.VMEM((VEC_ROWS, rows), f32), pltpu.VMEM((rows, rows), f32),
               pltpu.SemaphoreType.DMA((5,)), pltpu.SemaphoreType.DMA((11,))]
    return outs, scratch


def attn_forward(layer, sec, x, r, start, vec, w):
    outs, scratch = attn_forward_shapes(*x.shape)
    return pl.pallas_call(
        functools.partial(attn_forward_kernel, layer),
        out_shape=outs,
        in_specs=[SMEM, VMEM, VMEM, VMEM, VMEM] + [ANY] * 9,
        out_specs=[ANY] * 9,
        scratch_shapes=scratch,
        compiler_params=params(),
        cost_estimate=cost(15),
        name="attn_forward",
    )(sec, x, r, start, vec, w["qo"], w["qr"], w["ko"], w["kr"], w["vo"], w["vr"], w["f"], w["oo"], w["or"])


def gelu(u):
    half_u = 0.5 * u
    return half_u + half_u * jnp.tanh(u * (0.7978845608028654 + 0.035677408136300125 * (u * u)))


def middle_kernel(blk, sec_ref, e_ref, m_ref, r_ref, start_ref, vec0_ref, vec1_ref, *refs):
    up_o, up_r, dn_o, dn_r = refs[:4]
    attn_w, outs = refs[4:13], refs[13:28]
    wu0, wd0, wu1, u_s, a_s, f_s, x_s, acc, up_sem, put_sem = refs[28:38]
    wbufs, held, in_sem, out_sem = refs[38:42], refs[42:52], refs[52], refs[53]
    u0_out, a0_out, x_out, u1_out, a1_out, sent_out = outs[:6]
    steps = wu0.shape[0]
    section = sec_ref[0]
    cols = [pl.ds(b * blk, blk) for b in range(steps)]
    for b in range(steps):
        start_fetch(section == 0, up_o.at[:, cols[b]], up_r.at[:, cols[b]], wu0.at[b], up_sem.at[0, b])
    for b in range(steps):
        start_fetch(section == 0, dn_o.at[cols[b], :], dn_r.at[cols[b], :], wd0.at[b], up_sem.at[1, b])
    fetch, run, copies = attn_forward_steps(
        1, sec_ref, x_s, r_ref, start_ref, vec1_ref, (attn_w, wbufs), outs[6:], held, in_sem, out_sem)
    fetch()
    for b in range(steps):
        start_fetch(section == 1, up_o.at[:, cols[b]], up_r.at[:, cols[b]], wu1.at[b], up_sem.at[2, b])
    own = []

    def put(src, dst):
        copy = pltpu.make_async_copy(src, dst, put_sem.at[len(own)])
        copy.start()
        own.append(copy)

    def expand(layer, b, source, weights, vec_ref):
        wait_fetch(up_o.at[:, cols[0]], weights.at[b], up_sem.at[2 * layer, b])
        f_s[b % 2] = mm(source[...], weights[b]) + vec_ref[UBIAS + b:UBIAS + b + 1, :]

    def activate(layer, b, u_out, a_out):
        u = f_s[b % 2]
        u_s[layer, b] = u.astype(bf16)
        a_s[layer, b] = gelu(u).astype(bf16)
        put(u_s.at[layer, b], u_out.at[:, cols[b]])
        put(a_s.at[layer, b], a_out.at[:, cols[b]])

    expand(0, 0, e_ref, wu0, vec0_ref)
    for b in range(steps):
        if b + 1 < steps:
            expand(0, b + 1, e_ref, wu0, vec0_ref)
        activate(0, b, u0_out, a0_out)
        wait_fetch(dn_o.at[cols[0], :], wd0.at[b], up_sem.at[1, b])
        part = mm(a_s[0, b], wd0[b])
        acc[...] = part if b == 0 else acc[...] + part
    x_s[...] = (m_ref[...] + (acc[...] + vec0_ref[DBIAS:DBIAS + 1, :])).astype(bf16)
    put(x_s, x_out)
    run()
    expand(1, 0, held[6], wu1, vec1_ref)
    for b in range(steps):
        if b + 1 < steps:
            expand(1, b + 1, held[6], wu1, vec1_ref)
        activate(1, b, u1_out, a1_out)
    theirs = (1 - section) * (steps // 2)
    for b in range(steps // 2):
        for layer in range(2):
            put(a_s.at[layer, theirs + b], sent_out.at[layer, :, cols[b]])
    for copy in own + copies:
        copy.wait()


def middle(sec, e, m, r, start, vec, w):
    rows, d = e.shape
    ff = w["uo"].shape[1]
    blk = d
    n = ff // blk
    outs, scratch = attn_forward_shapes(rows, d)
    wide = sds((rows, ff), bf16)
    return pl.pallas_call(
        functools.partial(middle_kernel, blk),
        out_shape=[wide, wide, sds((rows, d), bf16), wide, wide, sds((2, rows, ff // 2), bf16)] + outs,
        in_specs=[SMEM] + [VMEM] * 6 + [ANY] * 13,
        out_specs=[ANY] * 15,
        scratch_shapes=[pltpu.VMEM((n, d, blk), bf16), pltpu.VMEM((n, blk, d), bf16), pltpu.VMEM((n, d, blk), bf16),
                        pltpu.VMEM((2, n, rows, blk), bf16), pltpu.VMEM((2, n, rows, blk), bf16),
                        pltpu.VMEM((2, rows, blk), f32), pltpu.VMEM((rows, d), bf16), pltpu.VMEM((rows, d), f32),
                        pltpu.SemaphoreType.DMA((3, n)), pltpu.SemaphoreType.DMA((4 * n + 1 + n,))] + scratch,
        compiler_params=params(),
        cost_estimate=cost(15),
        name="middle",
    )(sec, e, m, r, start, vec[0], vec[1], w["uo"], w["ur"], w["do"], w["dr"],
      w["qo"], w["qr"], w["ko"], w["kr"], w["vo"], w["vr"], w["f"], w["oo"], w["or"])


def theirs_at(steps):
    half = steps // 2

    def index(j, s):
        return (0, jnp.where(s[0] == 0, jnp.maximum(j - half, 0), jnp.minimum(j, half - 1)))
    return index


def feed_down_kernel(layer, blk, sec_ref, a_ref, m_ref, vec_ref, dn_o, dn_r, z_ref, wd, acc, sem):
    j = pl.program_id(0)
    steps = pl.num_programs(0)
    mine = sec_ref[0] == layer

    @pl.when(j == 0)
    def _():
        for b in range(dn_o.shape[0] // blk):
            cols = pl.ds(b * blk, blk)
            start_fetch(mine, dn_o.at[cols, :], dn_r.at[cols, :], wd.at[b], sem.at[b])

    wait_fetch(dn_o.at[pl.ds(0, blk), :], wd.at[j], sem.at[j])
    part = mm(a_ref[...], wd[j])

    @pl.when(j == 0)
    def _():
        acc[...] = part

    @pl.when((j > 0) & (j < steps - 1))
    def _():
        acc[...] += part

    @pl.when(j == steps - 1)
    def _():
        z_ref[...] = (m_ref[...] + (acc[...] + part + vec_ref[DBIAS:DBIAS + 1, :])).astype(bf16)


def feed_down(layer, sec, a, m, vec, w):
    rows, ff = a.shape
    d = m.shape[1]
    blk = d
    n = ff // blk
    return pl.pallas_call(
        functools.partial(feed_down_kernel, layer, blk),
        grid=(n,),
        out_shape=sds((rows, d), bf16),
        in_specs=[SMEM, pl.BlockSpec((rows, blk), lambda j: (0, j)), VMEM, VMEM, ANY, ANY],
        out_specs=pl.BlockSpec((rows, d), lambda j: (0, 0)),
        scratch_shapes=[pltpu.VMEM((n, blk, d), bf16), pltpu.VMEM((rows, d), f32), pltpu.SemaphoreType.DMA((n,))],
        compiler_params=params(),
        cost_estimate=cost(8),
        name="feed_down",
    )(sec, a, m, vec, w["do"], w["dr"])


def layer_backward_kernel(layer, blk, sec_ref, dz_ref, m_ref, lse_ref, start_ref, vec_ref, dr2_ref,
                          u_in, x_in, q_in, k_in, v_in, o_in,
                          up_o, up_r, dn_o, dn_r, qw_o, qw_r, kw_o, kw_r, vw_o, vw_r, fw, ow_o, ow_r,
                          du_out, sent_out, bundle_out, shared_ref, small_ref,
                          wu, wd, wq, wk, wv, wo, u_s, x_s, q_ref, k_ref, v_ref, o_ref, du_s, da_s, acc, dm_s,
                          bundle_ref, do_s, delta_s, bias_s, feed_sem, sem, in_sem, out_sem):
    mine = sec_ref[0] == layer
    rows, d = dz_ref.shape
    half = fw.shape[1]
    steps = wu.shape[0]
    cols = [pl.ds(b * blk, blk) for b in range(steps)]
    for b in range(steps):
        start_fetch(mine, dn_o.at[cols[b], :], dn_r.at[cols[b], :], wd.at[b], feed_sem.at[0, b])
        pltpu.make_async_copy(u_in.at[:, cols[b]], u_s.at[b], feed_sem.at[2, b]).start()
        start_fetch(mine, up_o.at[:, cols[b]], up_r.at[:, cols[b]], wu.at[b], feed_sem.at[1, b])
    start_fetch(mine, ow_o, ow_r, wo, sem.at[4])
    loads = [pltpu.make_async_copy(src, dst, in_sem.at[i]) for i, (src, dst) in enumerate(
        ((q_in, q_ref), (k_in, k_ref), (v_in, v_ref), (o_in, o_ref), (x_in, x_s)))]
    for load in loads:
        load.start()
    start_fetch(mine, qw_o, qw_r, wq, sem.at[0])
    start_fetch(mine, kw_o, kw_r, wk, sem.at[1])
    start_fetch(mine, vw_o, vw_r, wv.at[:, half:], sem.at[2])
    if layer == 0:
        pltpu.make_async_copy(fw, wv.at[:, :half], sem.at[3]).start()
    copies = []

    def put(src, dst):
        copy = pltpu.make_async_copy(src, dst, out_sem.at[len(copies)])
        copy.start()
        copies.append(copy)

    small_ref[...] = jnp.zeros(small_ref.shape, f32)

    def expand(b):
        wait_fetch(dn_o.at[cols[0], :], wd.at[b], feed_sem.at[0, b])
        da_s[b % 2] = mm(dz_ref[...], wd[b], NT)

    def activate(b):
        pltpu.make_async_copy(u_in.at[:, cols[b]], u_s.at[b], feed_sem.at[2, b]).wait()
        u = u_s[b].astype(f32)
        sq = u * u
        th = jnp.tanh(u * (0.7978845608028654 + 0.035677408136300125 * sq))
        slope = 0.5 + 0.5 * th + (0.5 * u) * (1.0 - th * th) * (0.7978845608028654 + 0.10703222440890037 * sq)
        du = (slope * da_s[b % 2]).astype(bf16)
        du_s[b] = du
        small_ref[UBIAS + b:UBIAS + b + 1, :] = row_sum(du.astype(f32))
        put(du_s.at[b], du_out.at[:, cols[b]])

    expand(0)
    for b in range(steps):
        if b + 1 < steps:
            expand(b + 1)
        activate(b)
        wait_fetch(up_o.at[:, cols[0]], wu.at[b], feed_sem.at[1, b])
        part = mm(du_s[b], wu[b], NT)
        acc[...] = part if b == 0 else acc[...] + part
    theirs = (1 - sec_ref[0]) * (steps // 2)
    for b in range(steps // 2):
        put(du_s.at[theirs + b], sent_out.at[b])
    de = acc[...]
    n, w = norm_parts(m_ref[...])
    dz = dz_ref[...].astype(f32)
    dm_s[...] = dz + norm_back(de * vec_ref[GAIN2:GAIN2 + 1, :], n, w)
    small_ref[GAIN2:GAIN2 + 1, :] = row_sum(de * n)
    small_ref[BIAS2:BIAS2 + 1, :] = row_sum(de)
    small_ref[DBIAS:DBIAS + 1, :] = row_sum(dz)

    low_ref, dq_ref, dk_ref, dv_ref, dx_ref = (bundle_ref.at[pl.ds(i * rows, rows), :] for i in range(5))
    low_ref[...] = dm_s[...].astype(bf16)
    at_key = lax.broadcasted_iota(jnp.int32, (rows, rows), 0)
    at_query = lax.broadcasted_iota(jnp.int32, (rows, rows), 1)
    bias_s[...] = jnp.where((at_key <= at_query) & (at_key >= start_ref[...]), 0.0, neg_fill)
    wait_fetch(ow_o, wo, sem.at[4])
    do = mm(low_ref[...], wo[...], NT).astype(bf16)
    do_s[...] = do
    for load in loads:
        load.wait()
    head_row = lax.broadcasted_iota(jnp.int32, (VEC_ROWS, d), 0)
    head_col = lax.broadcasted_iota(jnp.int32, (VEC_ROWS, d), 1) // HEAD
    pick = (head_row == head_col).astype(f32)
    delta_s[...] = lax.dot_general(pick, do.astype(f32) * o_ref[...].astype(f32), NT,
                                   precision=lax.Precision.HIGHEST, preferred_element_type=f32)
    lane = lax.broadcasted_iota(jnp.int32, (1, PAIR), 1)
    step = rows // 2
    scale = HEAD ** -0.5
    zero = jnp.zeros((), bf16)

    def pair(hp, carry):
        ls = pl.ds(pl.multiple_of(hp * PAIR, PAIR), PAIR)
        q2 = q_ref[:, ls] * jnp.asarray(scale, bf16)
        k2 = k_ref[:, ls]
        v2 = v_ref[:, ls]
        do2 = do_s[:, ls]
        dq_parts = []
        for kb in range(2):
            kr = slice(kb * step, (kb + 1) * step)
            first = kb * step
            dk = dv = dq = None
            for j in range(2):
                inside = (lane >= j * HEAD) & (lane < (j + 1) * HEAD)
                kh = jnp.where(inside, k2[kr], zero)
                vh = jnp.where(inside, v2[kr], zero)
                qh = jnp.where(inside, q2[first:], zero)
                doh = jnp.where(inside, do2[first:], zero)
                row = pl.ds(2 * hp + j, 1)
                st = mm(kh, qh, NT) + bias_s[kr, first:]
                pt = jnp.exp(st - lse_ref[row, first:])
                dpt = mm(vh, doh, NT)
                dst = (pt * (dpt - delta_s[row, first:])).astype(bf16)
                dv_j = mm(pt.astype(bf16), doh)
                dk_j = mm(dst, qh)
                dq_j = mm(dst, kh, TN)
                dk = dk_j if dk is None else dk + dk_j
                dv = dv_j if dv is None else dv + dv_j
                dq = dq_j if dq is None else dq + dq_j
            dk_ref[kr, ls] = dk.astype(bf16)
            if layer == 1:
                dv_ref[kr, ls] = dv.astype(bf16)

                @pl.when(hp < HEADS // 4)
                def _():
                    shared_ref[kr, ls] = dv
            else:
                extra = jnp.where(hp < HEADS // 4, dr2_ref[kr, pl.ds(pl.multiple_of((hp % (HEADS // 4)) * PAIR, PAIR), PAIR)], 0.0)
                dv_ref[kr, ls] = (dv + extra).astype(bf16)
            dq_parts.append(dq)
        dq_ref[:step, ls] = (dq_parts[0][:step] * scale).astype(bf16)
        dq_ref[step:, ls] = ((dq_parts[0][step:] + dq_parts[1]) * scale).astype(bf16)
        return carry

    if layer == 0:
        shared_ref[...] = jnp.zeros(shared_ref.shape, f32)
    lax.fori_loop(0, HEADS // 2, pair, 0)
    put(bundle_ref.at[pl.ds(0, 4 * rows), :], bundle_out.at[pl.ds(0, 4 * rows), :])

    wait_fetch(qw_o, wq, sem.at[0])
    dh = mm(dq_ref[...], wq[...], NT)
    wait_fetch(kw_o, wk, sem.at[1])
    dh = dh + mm(dk_ref[...], wk[...], NT)
    wait_fetch(vw_o, wv.at[:, half:], sem.at[2])
    if layer == 0:
        wait_fetch(fw, wv.at[:, :half], sem.at[3])
        dh = dh + mm(dv_ref[...], wv[...], NT)
    else:
        dh = dh + mm(dv_ref[:, half:], wv[:, half:], NT)
    n, w = norm_parts(x_s[...].astype(f32))
    dx_ref[...] = (dm_s[...] + norm_back(dh * vec_ref[GAIN1:GAIN1 + 1, :], n, w)).astype(bf16)
    small_ref[GAIN1:GAIN1 + 1, :] = row_sum(dh * n)
    small_ref[BIAS1:BIAS1 + 1, :] = row_sum(dh)
    small_ref[QBIAS:QBIAS + 1, :] = row_sum(dq_ref[...].astype(f32))
    small_ref[VBIAS:VBIAS + 1, :] = row_sum(dv_ref[...].astype(f32))
    small_ref[OBIAS:OBIAS + 1, :] = row_sum(low_ref[...].astype(f32))
    bundle_ref[5 * rows:, :] = small_ref[...].astype(bf16)
    put(bundle_ref.at[pl.ds(4 * rows, rows + VEC_ROWS), :], bundle_out.at[pl.ds(4 * rows, rows + VEC_ROWS), :])
    for copy in copies:
        copy.wait()


def layer_backward(layer, sec, dz, dz_at, t, start_row, vec, dr2, w):
    rows, ff = t["u"].shape
    d = t["m"].shape[1]
    half = w["f"].shape[1]
    blk = d
    n = ff // blk
    wbuf = pltpu.VMEM((d, d), bf16)
    act = pltpu.VMEM((rows, d), bf16)
    wide = pltpu.VMEM((rows, d), f32)
    blocks = pltpu.VMEM((n, rows, blk), bf16)
    dma = pltpu.SemaphoreType.DMA
    bundle = (5 * rows + VEC_ROWS, d)
    return pl.pallas_call(
        functools.partial(layer_backward_kernel, layer, blk),
        grid=(1,),
        out_shape=[sds((rows, ff), bf16), sds((n // 2, rows, blk), bf16), sds(bundle, bf16), sds((rows, half), f32),
                   sds((VEC_ROWS, d), f32)],
        in_specs=[SMEM, pl.BlockSpec((rows, d), lambda i: (dz_at, 0))] + [VMEM] * 5 + [ANY] * 19,
        out_specs=[ANY] * 3 + [VMEM] * 2,
        scratch_shapes=[pltpu.VMEM((n, d, blk), bf16), pltpu.VMEM((n, blk, d), bf16), wbuf, wbuf, wbuf, wbuf,
                        blocks, act, act, act, act, act, blocks, pltpu.VMEM((2, rows, blk), f32), wide, wide,
                        pltpu.VMEM(bundle, bf16), act, pltpu.VMEM((VEC_ROWS, rows), f32), pltpu.VMEM((rows, rows), f32),
                        dma((3, n)), dma((5,)), dma((5,)), dma((n + n // 2 + 2,))],
        compiler_params=params(),
        cost_estimate=cost(30),
        name="layer_backward",
    )(sec, dz, t["m"], t["lse"], start_row, vec, dr2, t["u"], t["x"], t["q"], t["k"], t["v"], t["o"],
      w["uo"], w["ur"], w["do"], w["dr"],
      w["qo"], w["qr"], w["ko"], w["kr"], w["vo"], w["vr"], w["f"], w["oo"], w["or"])


def store_chunks(ref, value):
    c, r, _ = ref.shape
    for i in range(c):
        ref[i] = value[i * r:(i + 1) * r].astype(bf16)


def quarter_of(g, s):
    return 2 * jnp.where(g < 2, 1 - s[1], s[1]) + g % 2


def quarters(kernel, scalars, in_specs, operands, shape, name):
    per = shape[0] // 2
    return pl.pallas_call(
        kernel,
        grid_spec=pltpu.PrefetchScalarGridSpec(
            num_scalar_prefetch=1, grid=(4,), in_specs=in_specs,
            out_specs=[pl.BlockSpec((per,) + shape[1:], lambda g, s: (jnp.minimum(g, 1), 0, 0)),
                       pl.BlockSpec((per,) + shape[1:], lambda g, s: (jnp.maximum(g - 2, 0), 0, 0))]),
        out_shape=[sds(shape, bf16)] * 2,
        compiler_params=params(),
        cost_estimate=cost(8),
        name=name,
    )(scalars, *operands)


def store_quarter(send_ref, keep_ref, value):
    g = pl.program_id(0)

    @pl.when(g < 2)
    def _():
        store_chunks(send_ref, value)

    @pl.when(g >= 2)
    def _():
        store_chunks(keep_ref, value)


def down_gradient(scalars, a, a_got, dz, dz_got, dz_at, chunk_rows):
    a_got, a_at = a_got
    rows, ff = a.shape
    d = dz.shape[1]
    q = d // 2

    def kernel(s_ref, a_ref, b_ref, x_ref, y_ref, send_ref, keep_ref):
        store_quarter(send_ref, keep_ref, mm(a_ref[...], x_ref[...], TN) + mm(b_ref[0], y_ref[...], TN))

    whole = pl.BlockSpec((rows, d), lambda g, s: (dz_at, 0))
    return quarters(
        kernel, scalars,
        [pl.BlockSpec((rows, q), lambda g, s: (0, 4 * s[0] + quarter_of(g, s))),
         pl.BlockSpec((1, rows, q), lambda g, s: (a_at, 0, quarter_of(g, s))), whole, whole],
        (a, a_got, dz, dz_got), (2 * q // chunk_rows, chunk_rows, d), "down_gradient")


def up_gradient(scalars, e, sent_got, du, du_got, chunk_rows):
    rows, ff = du.shape
    d = e.shape[1]
    q = d // 2

    def kernel(s_ref, e_ref, f_ref, du_ref, dg_ref, send_ref, keep_ref):
        store_quarter(send_ref, keep_ref, mm(e_ref[...], du_ref[...], TN) + mm(f_ref[0], dg_ref[0], TN))

    return quarters(
        kernel, scalars,
        [pl.BlockSpec((rows, q), lambda g, s: (0, g % 2)),
         pl.BlockSpec((1, rows, q), lambda g, s: (1, 0, g % 2)),
         pl.BlockSpec((rows, d), lambda g, s: (0, 2 * s[0] + quarter_of(g, s) // 2)),
         pl.BlockSpec((1, rows, d), lambda g, s: (quarter_of(g, s) // 2, 0, 0))],
        (e, sent_got, du, du_got), (2 * q // chunk_rows, chunk_rows, d), "up_gradient")


def vector_share(width, chunks):
    return max(PAIR, VEC_ROWS * width // chunks)


def attn_gradient(scalars, o, h, sent_got, bundle, bundle_got, small, chunk_rows, extra):
    rows, d = o.shape
    q = d // 2
    per = q // chunk_rows
    share = vector_share(d, 8 * per)

    def kernel(s_ref, o_ref, h_ref, l_ref, own_ref, got_ref, small_ref, small_got_ref, send_ref, keep_ref, sum_ref):
        sum_ref[...] = small_ref[...] + small_got_ref[...].astype(f32)
        g = pl.program_id(0)
        which = quarter_of(g, s_ref)
        for i in range(4):
            @pl.when(which == i)
            def _():
                left = o_ref if i == 0 else h_ref
                value = mm(left[...], own_ref[...], TN) + mm(l_ref[0], got_ref[...], TN)
                for side, ref in enumerate((send_ref, keep_ref)):
                    @pl.when(g // 2 == side)
                    def _():
                        ref[:, chunk_rows:, :] = jnp.zeros((per, extra, d), bf16)
                        for c in range(per):
                            ref[c, :chunk_rows, :] = value[c * chunk_rows:(c + 1) * chunk_rows].astype(bf16)
                        for part_index in range(2):
                            @pl.when(s_ref[0] == part_index)
                            def _():
                                for c in range(per):
                                    at = ((4 * part_index + i) * per + c) * share
                                    if at < VEC_ROWS * d:
                                        row = sum_ref[at // d:at // d + 1, at % d:at % d + share]
                                        ref[c, chunk_rows:chunk_rows + 1, :share] = row.astype(bf16)

    part = pl.BlockSpec((rows, q), lambda g, s: (0, s[0]))
    right = pl.BlockSpec((rows, d), lambda g, s: (quarter_of(g, s), 0))
    shape = (2 * per, chunk_rows + extra, d)
    return pl.pallas_call(
        kernel,
        grid_spec=pltpu.PrefetchScalarGridSpec(
            num_scalar_prefetch=1, grid=(4,),
            in_specs=[part, part,
                      pl.BlockSpec((1, rows, q), lambda g, s: (0, 0, jnp.minimum(quarter_of(g, s), 1))),
                      right, right, pl.BlockSpec((VEC_ROWS, d), lambda g, s: (0, 0)),
                      pl.BlockSpec((VEC_ROWS, d), lambda g, s: (5 * rows // VEC_ROWS, 0))],
            out_specs=[pl.BlockSpec((per,) + shape[1:], lambda g, s: (jnp.minimum(g, 1), 0, 0)),
                       pl.BlockSpec((per,) + shape[1:], lambda g, s: (jnp.maximum(g - 2, 0), 0, 0))],
            scratch_shapes=[pltpu.VMEM((VEC_ROWS, d), f32)]),
        out_shape=[sds(shape, bf16)] * 2,
        compiler_params=params(),
        cost_estimate=cost(9),
        name="attn_gradient",
    )(scalars, o, h, sent_got, bundle, bundle_got, small, bundle_got)


AXES = ("section", "dp")
SWAP = [(0, 1), (1, 0)]


def bit_orders(dp):
    bits = list(range(dp.bit_length() - 1))
    if len(bits) < 3:
        return bits, bits[::-1]
    return [0, 2, 1] + bits[3:], [1, 2, 0] + bits[3:]


def exchange(array, dp, step):
    first, second = bit_orders(dp)
    pairs = [(i, i ^ (1 << first[step])) for i in range(dp)]
    pairs += [(dp + i, dp + (i ^ (1 << second[step]))) for i in range(dp)]
    return lax.ppermute(array, AXES, pairs)


def block_of(chunks, rows):
    best = 1
    for c in range(1, chunks + 1):
        if chunks % c == 0 and c * rows <= 768:
            best = c
    return best


def add_split(bit, parts):
    _, c, r, w = parts[0][0].shape
    counts = [p[0].shape[0] for p in parts]
    n = sum(counts)
    h = c // 2
    cb = block_of(h, r)
    nb = h // cb
    ends = [sum(counts[:i + 1]) for i in range(len(counts))]
    begins = [e - k for e, k in zip(ends, counts)]

    def kernel(s_ref, *refs):
        send_ref, keep_ref = refs[-2:]
        g, i = pl.program_id(0), pl.program_id(1)
        for t in range(len(parts)):
            @pl.when((i >= begins[t]) & (i < ends[t]))
            def _():
                total = (refs[2 * t][...].astype(f32) + refs[2 * t + 1][...].astype(f32)).astype(bf16)

                @pl.when(g == 0)
                def _():
                    send_ref[...] = total

                @pl.when(g == 1)
                def _():
                    keep_ref[...] = total

    def source(t):
        def index(g, i, j, s):
            inside = (i >= begins[t]) & (i < ends[t])
            side = jnp.where(g == 0, 1 - s[0], s[0])
            return (jnp.clip(i - begins[t], 0, counts[t] - 1), jnp.where(inside, side * nb + j, 0), 0, 0)
        return pl.BlockSpec((1, cb, r, w), index)

    def send_at(g, i, j, s):
        return (jnp.where(g == 0, i, n - 1), jnp.where(g == 0, j, nb - 1), 0, 0)

    def keep_at(g, i, j, s):
        return (jnp.where(g == 0, 0, i), jnp.where(g == 0, 0, j), 0, 0)

    flat = [x for p in parts for x in p]
    return pl.pallas_call(
        kernel,
        grid_spec=pltpu.PrefetchScalarGridSpec(
            num_scalar_prefetch=1, grid=(2, n, nb),
            in_specs=[source(t) for t in range(len(parts)) for _ in range(2)],
            out_specs=[pl.BlockSpec((1, cb, r, w), send_at), pl.BlockSpec((1, cb, r, w), keep_at)]),
        out_shape=[sds((n, h, r, w), bf16)] * 2,
        compiler_params=params(),
        cost_estimate=cost(1.5 + 3.5 * n * c / 8),
        name="add_split",
    )(bit, *flat)


def merge(bit, cur, arrived):
    n, c, r, w = cur.shape
    cb = block_of(c, r)
    nb = c // cb

    def kernel(s_ref, a_ref, b_ref, out_ref):
        g = pl.program_id(1)

        @pl.when(g == s_ref[0])
        def _():
            out_ref[...] = a_ref[...]

        @pl.when(g != s_ref[0])
        def _():
            out_ref[...] = b_ref[...]

    def at(own):
        def index(i, g, j, s):
            mine = (g == s[0]) if own else (g != s[0])
            return (i, jnp.where(mine, j, 0), 0, 0)
        return pl.BlockSpec((1, cb, r, w), index)

    return pl.pallas_call(
        kernel,
        grid_spec=pltpu.PrefetchScalarGridSpec(
            num_scalar_prefetch=1, grid=(n, 2, nb), in_specs=[at(True), at(False)],
            out_specs=pl.BlockSpec((1, cb, r, w), lambda i, g, j, s: (i, g * nb + j, 0, 0))),
        out_shape=sds((n, 2 * c, r, w), bf16),
        compiler_params=params(),
        cost_estimate=cost(1.5 + 2 * n * c / 8),
        name="merge",
    )(bit, cur, arrived)


def assemble(scalars, sources, chunk_rows, outs, place, name, extra=0):
    _, c, r, w = sources[0].shape
    cb = c // 2
    block = cb * chunk_rows

    def position(g, s):
        part, t = g // 8, g % 8
        own = part == s[0]
        top, mid, low = t // 4, (t // 2) % 2, t % 2
        return jnp.where(own, top, low), mid, jnp.where(own, low, top)

    def chosen(g, s):
        top, mid, _ = position(g, s)
        return 2 * jnp.where(top == s[1], 0, 1) + jnp.where(mid == s[2], 0, 1)

    def kernel(s_ref, *refs):
        g = pl.program_id(0)
        which = chosen(g, s_ref)
        out_refs = refs[4:]
        for i in range(4):
            @pl.when(which == i)
            def _():
                held = refs[i][0].astype(f32)
                value = held[:, :chunk_rows].reshape(block, w)
                if len(outs) == 1:
                    out_refs[0][...] = value
                else:
                    for t in range(len(outs)):
                        @pl.when((g % 8) // 2 == t)
                        def _():
                            out_refs[t][...] = value
                if extra:
                    out_refs[len(outs)][0] = held[:, chunk_rows, :]

    def source(i):
        def index(g, s):
            return (jnp.where(chosen(g, s) == i, g // 8, 0), jnp.where(chosen(g, s) == i, position(g, s)[2], 0), 0, 0)
        return pl.BlockSpec((1, cb, r, w), index)

    def out_at(t):
        return pl.BlockSpec((block, w), lambda g, s: place(g // 8, g % 8, t))

    out_specs = [out_at(t) for t in range(len(outs))]
    out_shape = [sds(o, f32) for o in outs]
    if extra:
        out_specs.append(pl.BlockSpec((1, cb, w), lambda g, s: (g, 0, 0)))
        out_shape.append(sds((16, cb, w), f32))
    return pl.pallas_call(
        kernel,
        grid_spec=pltpu.PrefetchScalarGridSpec(
            num_scalar_prefetch=1, grid=(16,), in_specs=[source(i) for i in range(4)], out_specs=out_specs),
        out_shape=out_shape,
        compiler_params=params(),
        cost_estimate=cost(12),
        name=name,
    )(scalars, *sources)


def after(array, *earlier):
    return lax.optimization_barrier((array,) + earlier)[0]


class Order:
    def __init__(self):
        self.last = ()

    def mark(self, *arrays):
        self.last = arrays

    def also(self, *arrays):
        self.last = self.last + arrays

    def tie(self, array):
        return after(array, *self.last) if self.last else array


def local(
    boundary,
    lengths,
    norm_one_gain,
    norm_one_bias,
    query_weight,
    query_bias,
    key_weight,
    value_weight,
    value_bias,
    first_value_weight,
    first_value_bias,
    out_weight,
    out_bias,
    norm_two_gain,
    norm_two_bias,
    up_weight,
    up_bias,
    down_weight,
    down_bias,
):
    section = lax.axis_index("section")
    spot = lax.axis_index("dp")
    dp = lax.axis_size("dp")
    on_first = section == 0
    sec = jnp.reshape(section, (1,)).astype(jnp.int32)
    rows = boundary.shape[1] // 2
    d = boundary.shape[2]
    half = value_weight.shape[2]
    ff = up_weight.shape[2]

    def swap(array):
        return lax.ppermute(array, "section", SWAP)

    def row(vector):
        return jnp.reshape(vector, (-1, d))

    vec_own = jnp.concatenate([
        norm_one_gain, norm_one_bias, query_bias,
        jnp.concatenate([first_value_bias[None], value_bias], axis=1),
        out_bias, norm_two_gain, norm_two_bias, down_bias, row(up_bias)], axis=0)
    vec_own = jnp.pad(vec_own, ((0, VEC_ROWS - vec_own.shape[0]), (0, 0)))
    top, bottom = boundary[0, :rows], boundary[0, rows:]
    arrived_rows = swap(jnp.where(on_first, bottom, top))
    kept_rows = jnp.where(on_first, top, bottom)
    x0 = jnp.where(on_first, kept_rows, arrived_rows)
    dz1 = jnp.where(on_first, arrived_rows, kept_rows)
    dz1_moved = lax.ppermute(bottom, "section", [(1, 0)])
    dz1_got = jnp.where(on_first, dz1_moved, top)
    vec_arrived = swap(vec_own)
    vec = (jnp.where(on_first, vec_own, vec_arrived), jnp.where(on_first, vec_arrived, vec_own))
    w = {"qo": query_weight[0], "ko": key_weight[0], "vo": value_weight[0], "oo": out_weight[0],
         "uo": up_weight[0], "do": down_weight[0], "f": first_value_weight}
    for name in "qkvo":
        w[name + "r"] = swap(w[name + "o"])
    w["ur"] = swap(after(w["uo"], w["qr"]))
    w["dr"] = swap(after(w["do"], w["kr"]))

    own_lengths = jnp.where(on_first, lengths[0], lengths[1])
    cuts = jnp.cumsum(own_lengths)
    at = jnp.arange(rows, dtype=jnp.int32)
    start = jnp.max(jnp.where(at[:, None] >= cuts[None, :], cuts[None, :], 0), axis=1).astype(jnp.int32)
    start_col, start_row = start[:, None], start[None, :]

    chunk_rows = ff // (2 * dp)
    extra = 16
    first_bits, second_bits = bit_orders(dp)
    levels = len(first_bits)
    bit = [((spot >> jnp.where(on_first, first_bits[s], second_bits[s])) & 1).astype(jnp.int32) for s in range(levels)]
    bits = [jnp.reshape(b, (1,)) for b in bit]
    scalars = jnp.stack([sec[0], bit[0], bit[1]])
    order = Order()

    h, q, k, v, o, m, e, lse, sent = attn_forward(0, sec, x0, x0, start_col, vec[0], w)
    kept = [dict(x=x0, h=h, q=q, k=k, v=v, o=o, m=m, e=e, lse=lse, sent_got=swap(sent))]
    u0, a0, x1, u1, a1, a_sent, h, q, k, v, o, m, e, lse, sent = middle(sec, e, m, v, start_col, vec, w)
    a_got = swap(a_sent)
    kept[0].update(u=u0, a=a0, a_got=(a_got, 0))
    kept.append(dict(x=x1, h=h, q=q, k=k, v=v, o=o, m=m, e=e, lse=lse, u=u1, a=a1, sent_got=swap(sent), a_got=(a_got, 1)))
    order.mark(x1)
    y = feed_down(1, sec, a1, order.tie(m), vec[1], w)
    order.mark(y, a_got, kept[0]["sent_got"], kept[1]["sent_got"])

    def cut(level, parts):
        (first_keep, first_got), *rest = parts
        send, keep = add_split(bits[level], [(order.tie(first_keep), first_got)] + rest)
        order.mark(send)
        return keep, exchange(send, dp, level)

    def deep(part):
        for s in range(4, levels):
            part = cut(s, [part])
        return part

    def add_last(part):
        keep, got = part
        total = (order.tie(keep).astype(f32) + got.astype(f32)).astype(bf16)
        order.mark(total)
        return total

    def grow(level, cur, got):
        cur = merge(bits[level], order.tie(cur), got)
        order.mark(cur)
        return cur

    def first_sent(grads):
        send, keep = grads
        order.mark(send)
        return keep[None], exchange(send[None], dp, 0)

    def down_step(layer, dz, dz_got, dz_at):
        t = kept[layer]
        return first_sent(down_gradient(scalars, order.tie(t["a"]), t["a_got"], dz, dz_got, dz_at, chunk_rows))

    def back_step(layer, dz, dz_at, dr2):
        du, sent, bundle, dr2, small = layer_backward(
            layer, sec, dz, dz_at, dict(kept[layer], u=order.tie(kept[layer]["u"])), start_row, vec[layer], dr2, w)
        order.mark(dr2)
        return bundle, swap(bundle), dr2, small, du, swap(sent)

    def up_step(layer, back):
        t = kept[layer]
        return first_sent(up_gradient(scalars, order.tie(t["e"]), t["sent_got"], back[4], back[5], chunk_rows))

    def attn_grad_step(layer, attn):
        t = kept[layer]
        return first_sent(attn_gradient(scalars, order.tie(t["o"]), t["h"], t["sent_got"], attn[0], attn[1], attn[3],
                                        chunk_rows, extra))

    to_second = lambda t: lax.ppermute(t, "section", [(0, 1)])

    def hand_over(second, first):
        sent = jnp.where(on_first, second, first)
        own = jnp.where(on_first, first, second)
        return own, swap(sent)

    def both_parts(pair):
        own, got = pair
        cur = merge(sec, order.tie(own), got)
        order.mark(cur)
        cur = jnp.swapaxes(cur, 0, 1)
        for s in range(levels - 1, 3, -1):
            cur = grow(s, cur, exchange(cur, dp, s))
        return cur, exchange(cur, dp, 3)

    y_moved = to_second(y)
    back1 = back_step(1, dz1, 0, jnp.zeros((rows, half), f32))
    order.also(y_moved)
    down1 = down_step(1, dz1, dz1_got, 0)
    up1 = up_step(1, back1)
    square1 = attn_grad_step(1, back1)
    down0 = down_step(0, back1[0], back1[1], 4)
    down1 = cut(1, [down1])
    back0 = back_step(0, back1[0], 4, back1[2])
    dx0, dx_moved = (t[4 * rows:5 * rows] for t in back0[:2])
    up1 = cut(1, [up1])
    square1 = cut(1, [square1])
    down1 = cut(2, [down1])
    up0 = up_step(0, back0)
    square0 = attn_grad_step(0, back0)
    down0 = cut(1, [down0])
    up1 = cut(2, [up1])
    down1 = deep(cut(3, [down1]))
    square1 = cut(2, [square1])
    up1 = deep(cut(3, [up1]))
    up0 = cut(1, [up0])
    down0 = cut(2, [down0])
    down1 = add_last(down1)
    square1 = deep(cut(3, [square1]))
    up1 = add_last(up1)
    down0 = deep(cut(3, [down0]))
    square1 = add_last(square1)
    up0 = cut(2, [up0])
    down0 = add_last(down0)
    pair_d = hand_over(down1, down0)
    square0 = cut(1, [square0])
    up0 = deep(cut(3, [up0]))
    cur_d, got_d = both_parts(pair_d)
    square0 = cut(2, [square0])
    up0 = add_last(up0)
    pair_u = hand_over(up1, up0)
    cur_d = grow(3, cur_d, got_d)
    got_d = exchange(cur_d, dp, 2)
    square0 = deep(cut(3, [square0]))
    cur_u, got_u = both_parts(pair_u)
    cur_d = grow(2, cur_d, got_d)
    far_d = exchange(cur_d, dp, 1)
    side_d = exchange(cur_d, dp, 0)
    square0 = add_last(square0)
    b, e = square1, square0

    chunk = sum(bit[s] << (levels - 1 - s) for s in range(levels))
    at_row = lax.broadcasted_iota(jnp.int32, e.shape, 2)
    at_col = lax.broadcasted_iota(jnp.int32, e.shape, 3)
    share = vector_share(d, 2 * dp)
    matrix_rows = (at_row < chunk_rows) & (at_col < half) & (chunk >= 3 * dp // 4)
    vector_row = (at_row >= chunk_rows) & (chunk * share >= VBIAS * d) & (chunk * share < VBIAS * d + half)
    b = jnp.where(matrix_rows | (vector_row & on_first), e, b)
    pair_a = hand_over(b, e)

    cur_u = grow(3, cur_u, got_u)
    got_u = exchange(cur_u, dp, 2)
    cur_a, got_a = both_parts(pair_a)
    cur_u = grow(2, cur_u, got_u)
    far_u = exchange(cur_u, dp, 1)
    side_u = exchange(cur_u, dp, 0)
    cur_a = grow(3, cur_a, got_a)
    got_a = exchange(cur_a, dp, 2)
    order.also(far_d)
    last_d = exchange(order.tie(far_d), dp, 0)
    cur_a = grow(2, cur_a, got_a)
    far_a = exchange(cur_a, dp, 1)
    side_a = exchange(cur_a, dp, 0)
    order.also(far_u)
    last_u = exchange(order.tie(far_u), dp, 0)
    down_grad, = assemble(scalars, (order.tie(cur_d), far_d, side_d, last_d), chunk_rows, [(ff, d)],
                          lambda part, block, t: (part * 8 + block, 0), "assemble_down")
    order.mark(down_grad, far_a)
    last_a = exchange(far_a, dp, 0)
    up_grad, = assemble(scalars, (order.tie(cur_u), far_u, side_u, last_u), chunk_rows, [(d, ff)],
                        lambda part, block, t: (block % 4, part * 2 + block // 4), "assemble_up")
    order.mark(up_grad)
    out_grad, query_grad, key_grad, mixed_grad, vectors = assemble(
        scalars, (order.tie(cur_a), far_a, side_a, last_a), chunk_rows, [(d, d)] * 4,
        lambda part, block, t: (jnp.where(block // 2 == t, part * 2 + block % 2,
                                          jnp.where(block // 2 < t, jnp.maximum(part * 2 - 1, 0), part * 2 + 1)), 0),
        "assemble_attn", extra)
    total = vectors[:, :, :share].reshape(-1)[:VEC_ROWS * d].reshape(VEC_ROWS, d)

    spot_half = lambda t: jnp.where(on_first, t[:t.shape[0] // 2], t[t.shape[0] // 2:])
    block_ends = jnp.where(on_first, jnp.concatenate([dx0, dx_moved], axis=0),
                           jnp.concatenate([y_moved, y], axis=0))[None]
    return (
        block_ends,
        total[GAIN1][None],
        total[BIAS1][None],
        query_grad[None],
        total[QBIAS][None],
        key_grad[None],
        mixed_grad[None, :, half:],
        total[VBIAS, half:][None],
        spot_half(mixed_grad[:, :half]),
        spot_half(total[VBIAS, :half]),
        out_grad[None],
        total[OBIAS][None],
        total[GAIN2][None],
        total[BIAS2][None],
        up_grad[None],
        total[UBIAS:UBIAS + ff // d].reshape(1, ff),
        down_grad[None],
        total[DBIAS][None],
    )


def solution(mesh):
    stacked = P("section", None, None)
    vector = P("section", None)
    return jax.shard_map(
        local,
        mesh=mesh,
        in_specs=(
            P("section", "dp", None), P("dp", None),
            vector, vector, stacked, vector, stacked, stacked, vector, P(), P(),
            stacked, vector, vector, vector, stacked, vector, stacked, vector,
        ),
        out_specs=(
            P("section", "dp", None),
            vector, vector, stacked, vector, stacked, stacked, vector, P("section"), P("section"),
            stacked, vector, vector, vector, stacked, vector, stacked, vector,
        ),
        check_vma=False,
    )
```

time: 602 us -> 495 us (0.82)
  waiting for transfers between devices: 247 us -> 112 us
  Pallas kernels: 239 us -> 278 us
  local copies, waits for them, and re-layouts: 38.9 us -> 12.7 us
  other arithmetic: 13.2 us -> 27.4 us
    ppermute x27 -> x39, waiting for transfers between devices: 194 us -> 112 us  [exchange(): return lax.ppermute(array, AXES, pairs)]
    ppermute x6 -> x1, waiting for transfers between devices: 38.9 us -> 0.01 us  [local(): dz1_moved = lax.ppermute(bottom, 'section', [(1, 0)])]
    unnamed x197 -> x42, local copies, waits for them, and re-layouts: 35.4 us -> 4.66 us
    pallas_call x9, Pallas kernels: 5.08 us -> 23.5 us  [merge(): pl.pallas_call(kernel, grid_spec=pltpu.PrefetchScalarGridSpec(num_scalar_...]
    ppermute x18, waiting for transfers between devices: 14.6 us -> 0.2 us  [swap(): return lax.ppermute(array, 'section', SWAP)]
    ppermute x27 -> x39, starting transfers between devices: 31.9 us -> 46.1 us  [exchange(): return lax.ppermute(array, AXES, pairs)]
    pallas_call x3, Pallas kernels: 28.1 us -> 39.3 us  [assemble(): pl.pallas_call(kernel, grid_spec=pltpu.PrefetchScalarGridSpec(num_scalar_...]
    select_n x7 -> x10, other arithmetic: 7.69 us -> 16.9 us  [the longest x3 5.57 us: hand_over(): sent = jnp.where(on_first, second, first)]
  transfers between devices with their start and end apart: 54 -> 59, of which waited for: 27 -> 18; matrix products, arithmetic and copies ran while one was open for 3% -> 6% of each run, Pallas kernels for 21% -> 53%
where the time goes in v2:
time: 495 us; the launch traced here: 488 us
  Pallas kernels  278 us (56%)
  waiting for transfers between devices  112 us (23%)
  starting transfers between devices  56.5 us (11%)
  other arithmetic  27.4 us (6%)
  local copies, waits for them, and re-layouts  12.7 us (3%)
    ppermute x39, waiting for transfers between devices, exchange(): return lax.ppermute(array, AXES, pairs)  112 us
    pallas_call x2, Pallas kernels, layer_backward(): pl.pallas_call(functools.partial(layer_backward_kernel, layer, blk), grid...  66 us
    ppermute x39, starting transfers between devices, exchange(): return lax.ppermute(array, AXES, pairs)  46.1 us
    pallas_call x18, Pallas kernels, add_split(): pl.pallas_call(kernel, grid_spec=pltpu.PrefetchScalarGridSpec(num_scalar_...  43.6 us
    pallas_call x3, Pallas kernels, assemble(): pl.pallas_call(kernel, grid_spec=pltpu.PrefetchScalarGridSpec(num_scalar_...  39.3 us
    pallas_call x1, Pallas kernels, middle(): pl.pallas_call(functools.partial(middle_kernel, blk), out_shape=[wide, wi...  35.5 us
    pallas_call x4, Pallas kernels, quarters(): pl.pallas_call(kernel, grid_spec=pltpu.PrefetchScalarGridSpec(num_scalar_...  30.4 us
    pallas_call x9, Pallas kernels, merge(): pl.pallas_call(kernel, grid_spec=pltpu.PrefetchScalarGridSpec(num_scalar_...  23.5 us
  transfers between devices with their start and end apart: 59, of which 18 were waited for; matrix products, arithmetic and copies ran while one was open for 6% of the time, Pallas kernels for 53%

profile of v2, /device:TPU:0, one launch (start us, length us, event | category | flops | bytes accessed | tf_op | source)
XLA Modules:
  0.0 488.0 jit_solution(8393006104265283497)
XLA Ops:
  11.4 3.0 broadcast_select_fusion
  15.0 15.6 %attn_forward.1 = (bf16[512,768]{1,0:T(8,128)(2,1)}, bf16[512,768]{1,0:T(8,128)(2,1)}, bf16[512,768]{1,0:T(8,128)(2,1)}, bf16[512,768]{1,0:T(8,128)(2,1)}, bf16[...) custom-call(s32[1]{0:T(128)} %bitcast.sec_ref.s_ref, ...), custom_call_target="tpu_custom_call" | custom-call | flops 99999997952 | bytes 1 | tf_op jit(solution)/shard_map/attn_forward/pallas_call | solution.py:205
  30.8 35.5 %middle.1 = (bf16[512,3072]{1,0:T(8,128)(2,1)}, bf16[512,3072]{1,0:T(8,128)(2,1)}, bf16[512,768]{1,0:T(8,128)(2,1)}, bf16[512,3072]{1,0:T(8,128)(2,1)}, bf16[512...) custom-call(s32[1]{0:T(128)} %bitcast.sec_ref.s_ref, ...), custom_call_target="tpu_custom_call" | custom-call | flops 99999997952 | bytes 1 | tf_op jit(solution)/shard_map/middle/pallas_call | solution.py:289
  66.9 7.9 %feed_down.1 = bf16[512,768]{1,0:T(8,128)(2,1)} custom-call(s32[1]{0:T(128)} %bitcast.sec_ref.s_ref, bf16[512,3072]{1,0:T(8,128)(2,1)} %get-tuple-element.175.a_ref, f32[512,768]{1,0:T(8,128)} %get-tuple-element.162.m_ref, f32[16,768]{1,0:T(8,128)} %get-tuple-element.302.vec1_ref.vec_ref, bf16[3072,768]{1,0:T(8,128)(2,1)} %bitcast.11.refs_2_.dn_o, ...), custom_call_target="tpu_custom_call" | custom-call | flops 99999997952 | bytes 1 | tf_op jit(solution)/shard_map/feed_down/pallas_call | solution.py:345
  74.8 3.3 collective-permute-start.11
  79.1 33.7 %layer_backward.2 = (bf16[512,3072]{1,0:T(8,128)(2,1)}, bf16[2,512,768]{2,1,0:T(8,128)(2,1)}, bf16[2576,768]{1,0:T(8,128)(2,1)}, f32[512,384]{1,0:T(8,128)}, f32[16,768]{1,0:T(8,128)}) custom-call(s32[1]{0:T(128)} %bitcast.sec_ref.s_ref, bf16[512,768]{1,0:T(8,128)(2,1)} %get-tuple-element.293.dz_ref.x_ref, f32[512,768]{1,0:T(8,128)} %get-tuple-element.162.m_ref, ...), custom_call_target="tpu_custom_call" | custom-call | flops 99999997952 | bytes 1 | tf_op jit(solution)/shard_map/layer_backward/pallas_call | solution.py:529
  112.9 7.4 %down_gradient.2 = (bf16[8,96,768]{2,1,0:T(8,128)(2,1)}, bf16[8,96,768]{2,1,0:T(8,128)(2,1)}) custom-call(s32[3]{0:T(128)} %pad_add_fusion.s_ref, bf16[512,3072]{1,0:T(8,128)(2,1)} %get-tuple-element.175.a_ref, bf16[2,512,1536]{2,1,0:T(8,128)(2,1)} %collective-permute-done.8.b_ref, bf16[512,768]{1,0:T(8,128)(2,1)} %get-tuple-element.293.dz_ref.x_ref, ...), custom_call_target="tpu_custom_call" | custom-call | flops 99999997952 | bytes 1 | tf_op jit(solution)/shard_map/down_gradient/pallas_call | solution.py:560
  120.3 7.8 %up_gradient.2 = (bf16[8,96,768]{2,1,0:T(8,128)(2,1)}, bf16[8,96,768]{2,1,0:T(8,128)(2,1)}) custom-call(s32[3]{0:T(128)} %pad_add_fusion.s_ref, bf16[512,768]{1,0:T(8,128)(2,1)} %get-tuple-element.180.e_ref, bf16[2,512,768]{2,1,0:T(8,128)(2,1)} %collective-permute-done.10.f_ref.l_ref, bf16[512,3072]{1,0:T(8,128)(2,1)} %get-tuple-element.181.du_ref, ...), custom_call_target="tpu_custom_call" | custom-call | flops 99999997952 | bytes 1 | tf_op jit(solution)/shard_map/up_gradient/pallas_call | solution.py:560
  128.1 2.9 collective-permute-start.17
  134.4 11.1 %collective-permute-done.17.refs_1_ = bf16[1,8,96,768]{3,2,1,0:T(8,128)(2,1)} collective-permute-done((bf16[1,8,96,768]{3,2,1,0:T(8,128)(2,1)}, bf16[1,8,96,768]{3,2,1,0:T(8,128)(2,1)}, u32[]{:S(2)}, u32[]{:S(2)}) %collective-permute-start.17) | collective-permute-done | bytes 1179680 | tf_op jit(solution)/shard_map/ppermute | solution.py:689
  145.5 2.9 add_split.19
  150.5 8.1 %attn_gradient.2 = (bf16[8,112,768]{2,1,0:T(8,128)(2,1)}, bf16[8,112,768]{2,1,0:T(8,128)(2,1)}) custom-call(s32[3]{0:T(128)} %pad_add_fusion.s_ref, bf16[512,768]{1,0:T(8,128)(2,1)} %get-tuple-element.184.o_in.o_ref, bf16[512,768]{1,0:T(8,128)(2,1)} %get-tuple-element.185.h_ref, bf16[2,512,768]{2,1,0:T(8,128)(2,1)} %collective-permute-done.10.f_ref.l_ref, ...), custom_call_target="tpu_custom_call" | custom-call | flops 99999997952 | bytes 1 | tf_op jit(solution)/shard_map/attn_gradient/pallas_call | solution.py:656
  160.0 7.4 %down_gradient.3 = (bf16[8,96,768]{2,1,0:T(8,128)(2,1)}, bf16[8,96,768]{2,1,0:T(8,128)(2,1)}) custom-call(s32[3]{0:T(128)} %pad_add_fusion.s_ref, bf16[512,3072]{1,0:T(8,128)(2,1)} %get-tuple-element.188.a_ref, bf16[2,512,1536]{2,1,0:T(8,128)(2,1)} %collective-permute-done.8.b_ref, bf16[2576,768]{1,0:T(8,128)(2,1)} %get-tuple-element.171.own_ref.x_ref.dz_ref, ...), custom_call_target="tpu_custom_call" | custom-call | flops 99999997952 | bytes 1 | tf_op jit(solution)/shard_map/down_gradient/pallas_call | solution.py:560
  167.4 3.3 add_split.18
  171.2 32.3 %layer_backward.3 = (bf16[512,3072]{1,0:T(8,128)(2,1)}, bf16[2,512,768]{2,1,0:T(8,128)(2,1)}, bf16[2576,768]{1,0:T(8,128)(2,1)}, f32[512,384]{1,0:T(8,128)}, f32[16,768]{1,0:T(8,128)}) custom-call(s32[1]{0:T(128)} %bitcast.sec_ref.s_ref, bf16[2576,768]{1,0:T(8,128)(2,1)} %get-tuple-element.171.own_ref.x_ref.dz_ref, f32[512,768]{1,0:T(8,128)} %get-tuple-element.153.m_ref, ...), custom_call_target="tpu_custom_call" | custom-call | flops 99999997952 | bytes 1 | tf_op jit(solution)/shard_map/layer_backward/pallas_call | solution.py:529
  204.4 3.2 add_split.20
  213.3 7.8 %up_gradient.3 = (bf16[8,96,768]{2,1,0:T(8,128)(2,1)}, bf16[8,96,768]{2,1,0:T(8,128)(2,1)}) custom-call(s32[3]{0:T(128)} %pad_add_fusion.s_ref, bf16[512,768]{1,0:T(8,128)(2,1)} %get-tuple-element.205.e_ref, bf16[2,512,768]{2,1,0:T(8,128)(2,1)} %collective-permute-done.9.f_ref.l_ref, bf16[512,3072]{1,0:T(8,128)(2,1)} %get-tuple-element.206.du_ref, ...), custom_call_target="tpu_custom_call" | custom-call | flops 99999997952 | bytes 1 | tf_op jit(solution)/shard_map/up_gradient/pallas_call | solution.py:560
  222.5 8.1 %attn_gradient.3 = (bf16[8,112,768]{2,1,0:T(8,128)(2,1)}, bf16[8,112,768]{2,1,0:T(8,128)(2,1)}) custom-call(s32[3]{0:T(128)} %pad_add_fusion.s_ref, bf16[512,768]{1,0:T(8,128)(2,1)} %get-tuple-element.209.o_in.o_ref, bf16[512,768]{1,0:T(8,128)(2,1)} %get-tuple-element.210.h_ref, bf16[2,512,768]{2,1,0:T(8,128)(2,1)} %collective-permute-done.9.f_ref.l_ref, ...), custom_call_target="tpu_custom_call" | custom-call | flops 99999997952 | bytes 1 | tf_op jit(solution)/shard_map/attn_gradient/pallas_call | solution.py:656
  230.6 3.0 add_split.22
  238.6 2.6 collective-permute-start.28
  241.2 2.3 add_split.25
  248.3 2.9 add_split.27
  279.1 3.2 add_split.32
  282.2 2.9 collective-permute-start.38
  288.7 2.9 collective-permute-start.40
  291.6 18.9 %collective-permute-done.38.refs_1_ = bf16[1,4,112,768]{3,2,1,0:T(8,128)(2,1)} collective-permute-done((bf16[1,4,112,768]{3,2,1,0:T(8,128)(2,1)}, bf16[1,4,112,768]{3,2,1,0:T(8,128)(2,1)}, u32[]{:S(2)}, u32[]{:S(2)}) %collective-permute-start.38) | collective-permute-done | bytes 688160 | tf_op jit(solution)/shard_map/ppermute | solution.py:689
  310.5 2.3 add_split.34
  315.4 2.9 merge.10.a_ref
  324.8 2.9 collective-permute-start.45
  328.4 3.2 merge.12.refs_0_
  331.6 8.6 %collective-permute-done.44 = bf16[1,1,112,768]{3,2,1,0:T(8,128)(2,1)} collective-permute-done((bf16[1,1,112,768]{3,2,1,0:T(8,128)(2,1)}, bf16[1,1,112,768]{3,2,1,0:T(8,128)(2,1)}, u32[]{:S(2)}, u32[]{:S(2)}) %collective-permute-start.44) | collective-permute-done | bytes 172064 | tf_op jit(solution)/shard_map/ppermute | solution.py:689
  343.9 2.5 collective-permute-done.45.b_ref
  346.5 2.8 merge.13.a_ref
  352.4 7.1 %collective-permute-done.47.b_ref = bf16[2,2,96,768]{3,2,1,0:T(8,128)(2,1)} collective-permute-done((bf16[2,2,96,768]{3,2,1,0:T(8,128)(2,1)}, bf16[2,2,96,768]{3,2,1,0:T(8,128)(2,1)}, u32[]{:S(2)}, u32[]{:S(2)}) %collective-permute-start.47) | collective-permute-done | bytes 589856 | tf_op jit(solution)/shard_map/ppermute | solution.py:689
  359.5 3.2 merge.15.refs_0_
  362.7 8.7 %collective-permute-done.48.b_ref = bf16[2,1,112,768]{3,2,1,0:T(8,128)(2,1)} collective-permute-done((bf16[2,1,112,768]{3,2,1,0:T(8,128)(2,1)}, bf16[2,1,112,768]{3,2,1,0:T(8,128)(2,1)}, u32[]{:S(2)}, u32[]{:S(2)}) %collective-permute-start.48) | collective-permute-done | bytes 344096 | tf_op jit(solution)/shard_map/ppermute | solution.py:689
  371.5 2.9 merge.16.a_ref
  377.7 2.7 maximum_select_fusion
  382.9 6.3 %collective-permute-done.50.b_ref = bf16[2,2,112,768]{3,2,1,0:T(8,128)(2,1)} collective-permute-done((bf16[2,2,112,768]{3,2,1,0:T(8,128)(2,1)}, bf16[2,2,112,768]{3,2,1,0:T(8,128)(2,1)}, u32[]{:S(2)}, u32[]{:S(2)}) %collective-permute-start.50) | collective-permute-done | bytes 688160 | tf_op jit(solution)/shard_map/ppermute | solution.py:689
  389.2 3.3 merge.17.refs_0_
  392.6 17.5 %collective-permute-done.51.refs_1_ = bf16[2,4,96,768]{3,2,1,0:T(8,128)(2,1)} collective-permute-done((bf16[2,4,96,768]{3,2,1,0:T(8,128)(2,1)}, bf16[2,4,96,768]{3,2,1,0:T(8,128)(2,1)}, u32[]{:S(2)}, u32[]{:S(2)}) %collective-permute-start.51) | collective-permute-done | bytes 1179680 | tf_op jit(solution)/shard_map/ppermute | solution.py:689
  412.1 10.1 %collective-permute-done.53.refs_3_ = bf16[2,4,96,768]{3,2,1,0:T(8,128)(2,1)} collective-permute-done((bf16[2,4,96,768]{3,2,1,0:T(8,128)(2,1)}, bf16[2,4,96,768]{3,2,1,0:T(8,128)(2,1)}, u32[]{:S(2)}, u32[]{:S(2)}) %collective-permute-start.53) | collective-permute-done | bytes 1179680 | tf_op jit(solution)/shard_map/ppermute | solution.py:689
  422.3 12.7 %assemble_down.1 = f32[3072,768]{1,0:T(8,128)} custom-call(s32[3]{0:T(128)} %pad_add_fusion.s_ref, bf16[2,4,96,768]{3,2,1,0:T(8,128)(2,1)} %merge.12.refs_0_, bf16[2,4,96,768]{3,2,1,0:T(8,128)(2,1)} %collective-permute-done.49.refs_1_, bf16[2,4,96,768]{3,2,1,0:T(8,128)(2,1)} %collective-permute-done.52.refs_2_, ...), custom_call_target="tpu_custom_call" | custom-call | flops 99999997952 | bytes 1 | tf_op jit(solution)/shard_map/assemble_down/pallas_call | solution.py:834
  434.9 2.7 collective-permute-done.54.refs_1_
  439.3 10.3 %collective-permute-done.56.refs_3_ = bf16[2,4,96,768]{3,2,1,0:T(8,128)(2,1)} collective-permute-done((bf16[2,4,96,768]{3,2,1,0:T(8,128)(2,1)}, bf16[2,4,96,768]{3,2,1,0:T(8,128)(2,1)}, u32[]{:S(2)}, u32[]{:S(2)}) %collective-permute-start.56) | collective-permute-done | bytes 1179680 | tf_op jit(solution)/shard_map/ppermute | solution.py:689
  449.6 12.7 %assemble_up.1 = f32[768,3072]{1,0:T(8,128)} custom-call(s32[3]{0:T(128)} %pad_add_fusion.s_ref, bf16[2,4,96,768]{3,2,1,0:T(8,128)(2,1)} %merge.15.refs_0_, bf16[2,4,96,768]{3,2,1,0:T(8,128)(2,1)} %collective-permute-done.51.refs_1_, bf16[2,4,96,768]{3,2,1,0:T(8,128)(2,1)} %collective-permute-done.55.refs_2_, ...), custom_call_target="tpu_custom_call" | custom-call | flops 99999997952 | bytes 1 | tf_op jit(solution)/shard_map/assemble_up/pallas_call | solution.py:834
  464.4 14.0 %assemble_attn.1 = (f32[768,768]{1,0:T(8,128)}, f32[768,768]{1,0:T(8,128)}, f32[768,768]{1,0:T(8,128)}, f32[768,768]{1,0:T(8,128)}, f32[16,2,768]{2,1,0:T(2,128)}) custom-call(s32[3]{0:T(128)} %pad_add_fusion.s_ref, bf16[2,4,112,768]{3,2,1,0:T(8,128)(2,1)} %merge.17.refs_0_, bf16[2,4,112,768]{3,2,1,0:T(8,128)(2,1)} %collective-permute-done.54.refs_1_, ...), custom_call_target="tpu_custom_call" | custom-call | flops 99999997952 | bytes 1 | tf_op jit(solution)/shard_map/assemble_attn/pallas_call | solution.py:834
  478.4 2.5 slice_bitcast_fusion
  (191 shorter events, 104.5 us)
Async XLA Ops:
  4.5 10.0 %collective-permute-start.2 = (bf16[768,768]{1,0:T(8,128)(2,1)}, bf16[768,768]{1,0:T(8,128)(2,1)}, u32[]{:S(2)}, u32[]{:S(2)}) collective-permute-start(bf16[768,768]{1,0:T(8,128)(2,1)} %bitcast.102), channel_id=1, source_target_pairs={{0,16},{16,0},{1,17},{17,1},{2,18},{18,2},{3,19},{19,3},{4,20},{20... | collective-permute-start | bytes 3538952 | tf_op jit(solution)/shard_map/ppermute | solution.py:895
  4.9 9.5 %collective-permute-start.3 = (bf16[768,768]{1,0:T(8,128)(2,1)}, bf16[768,768]{1,0:T(8,128)(2,1)}, u32[]{:S(2)}, u32[]{:S(2)}) collective-permute-start(bf16[768,768]{1,0:T(8,128)(2,1)} %bitcast.107), channel_id=1, source_target_pairs={{0,16},{16,0},{1,17},{17,1},{2,18},{18,2},{3,19},{19,3},{4,20},{20... | collective-permute-start | bytes 3538952 | tf_op jit(solution)/shard_map/ppermute | solution.py:895
  5.0 10.0 %collective-permute-start.5 = (bf16[768,768]{1,0:T(8,128)(2,1)}, bf16[768,768]{1,0:T(8,128)(2,1)}, u32[]{:S(2)}, u32[]{:S(2)}) collective-permute-start(bf16[768,768]{1,0:T(8,128)(2,1)} %bitcast.112), channel_id=1, source_target_pairs={{0,16},{16,0},{1,17},{17,1},{2,18},{18,2},{3,19},{19,3},{4,20},{20... | collective-permute-start | bytes 3538952 | tf_op jit(solution)/shard_map/ppermute | solution.py:895
  14.5 16.3 %collective-permute-start.7 = (bf16[3072,768]{1,0:T(8,128)(2,1)}, bf16[3072,768]{1,0:T(8,128)(2,1)}, u32[]{:S(2)}, u32[]{:S(2)}) collective-permute-start(bf16[3072,768]{1,0:T(8,128)(2,1)} %bitcast.11.refs_2_.dn_o), channel_id=1, source_target_pairs={{0,16},{16,0},{1,17},{17,1},{2,18},{18,2},{3,19},{19,3},{4,20},{20... | collective-permute-start | bytes 14155784 | tf_op jit(solution)/shard_map/ppermute | solution.py:895
  14.5 16.3 %collective-permute-start.6 = (bf16[768,3072]{1,0:T(8,128)(2,1)}, bf16[768,3072]{1,0:T(8,128)(2,1)}, u32[]{:S(2)}, u32[]{:S(2)}) collective-permute-start(bf16[768,3072]{1,0:T(8,128)(2,1)} %bitcast.10.refs_0_.up_o), channel_id=1, source_target_pairs={{0,16},{16,0},{1,17},{17,1},{2,18},{18,2},{3,19},{19,3},{4,20},{20... | collective-permute-start | bytes 14155784 | tf_op jit(solution)/shard_map/ppermute | solution.py:895
  30.6 47.5 %collective-permute-start.9 = (bf16[2,512,768]{2,1,0:T(8,128)(2,1)}, bf16[2,512,768]{2,1,0:T(8,128)(2,1)}, u32[]{:S(2)}, u32[]{:S(2)}) collective-permute-start(bf16[2,512,768]{2,1,0:T(8,128)(2,1)} %get-tuple-element.164), channel_id=1, source_target_pairs={{0,16},{16,0},{1,17},{17,1},{2,18},{18,2},{3,19},{19,3},{4,20},{20... | collective-permute-start | bytes 4718600 | tf_op jit(solution)/shard_map/ppermute | solution.py:895
  66.3 11.9 %collective-permute-start.8 = (bf16[2,512,1536]{2,1,0:T(8,128)(2,1)}, bf16[2,512,1536]{2,1,0:T(8,128)(2,1)}, u32[]{:S(2)}, u32[]{:S(2)}) collective-permute-start(bf16[2,512,1536]{2,1,0:T(8,128)(2,1)} %get-tuple-element.163), channel_id=1, source_target_pairs={{0,16},{16,0},{1,17},{17,1},{2,18},{18,2},{3,19},{19,3},{4,20},{20... | collective-permute-start | bytes 9437192 | tf_op jit(solution)/shard_map/ppermute | solution.py:895
  66.7 11.4 %collective-permute-start.10 = (bf16[2,512,768]{2,1,0:T(8,128)(2,1)}, bf16[2,512,768]{2,1,0:T(8,128)(2,1)}, u32[]{:S(2)}, u32[]{:S(2)}) collective-permute-start(bf16[2,512,768]{2,1,0:T(8,128)(2,1)} %get-tuple-element.165), channel_id=1, source_target_pairs={{0,16},{16,0},{1,17},{17,1},{2,18},{18,2},{3,19},{19,3},{4,20},{20... | collective-permute-start | bytes 4718600 | tf_op jit(solution)/shard_map/ppermute | solution.py:895
  74.8 38.0 %collective-permute-start.11 = (bf16[512,768]{1,0:T(8,128)(2,1)}, bf16[512,768]{1,0:T(8,128)(2,1)}, u32[]{:S(2)}, u32[]{:S(2)}) collective-permute-start(bf16[512,768]{1,0:T(8,128)(2,1)} %feed_down.1), channel_id=1, source_target_pairs={{0,16},{1,17},{2,18},{3,19},{4,20},{5,21},{6,22},{7,23},{8,24},{9,... | collective-permute-start | bytes 2359304 | tf_op jit(solution)/shard_map/ppermute | solution.py:992
  128.1 17.4 %collective-permute-start.17 = (bf16[1,8,96,768]{3,2,1,0:T(8,128)(2,1)}, bf16[1,8,96,768]{3,2,1,0:T(8,128)(2,1)}, u32[]{:S(2)}, u32[]{:S(2)}) collective-permute-start(bf16[1,8,96,768]{3,2,1,0:T(8,128)(2,1)} %bitcast.120), channel_id=1, source_target_pairs={{0,1},{1,0},{2,3},{3,2},{4,5},{5,4},{6,7},{7,6},{8,9},{9,8},{10,11... | collective-permute-start | bytes 3538952 | tf_op jit(solution)/shard_map/ppermute | solution.py:689
  132.6 17.9 %collective-permute-start.14 = (bf16[2576,768]{1,0:T(8,128)(2,1)}, bf16[2576,768]{1,0:T(8,128)(2,1)}, u32[]{:S(2)}, u32[]{:S(2)}) collective-permute-start(bf16[2576,768]{1,0:T(8,128)(2,1)} %get-tuple-element.171.own_ref.x_ref.dz_ref), channel_id=1, source_target_pairs={{0,16},{16,0},{1,17},{17,1},{2,18},{18,2},{3,19},{19,3},{4,20},{20... | collective-permute-start | bytes 11870216 | tf_op jit(solution)/shard_map/ppermute | solution.py:895
  132.9 34.5 %collective-permute-start.15 = (bf16[1,8,96,768]{3,2,1,0:T(8,128)(2,1)}, bf16[1,8,96,768]{3,2,1,0:T(8,128)(2,1)}, u32[]{:S(2)}, u32[]{:S(2)}) collective-permute-start(bf16[1,8,96,768]{3,2,1,0:T(8,128)(2,1)} %bitcast.118), channel_id=1, source_target_pairs={{0,1},{1,0},{2,3},{3,2},{4,5},{5,4},{6,7},{7,6},{8,9},{9,8},{10,11... | collective-permute-start | bytes 3538952 | tf_op jit(solution)/shard_map/ppermute | solution.py:689
  148.4 85.5 %collective-permute-start.22 = (bf16[1,4,96,768]{3,2,1,0:T(8,128)(2,1)}, bf16[1,4,96,768]{3,2,1,0:T(8,128)(2,1)}, u32[]{:S(2)}, u32[]{:S(2)}) collective-permute-start(bf16[1,4,96,768]{3,2,1,0:T(8,128)(2,1)} %get-tuple-element.200), channel_id=1, source_target_pairs={{0,4},{1,5},{2,6},{3,7},{4,0},{5,1},{6,2},{7,3},{8,12},{9,13},{10,... | collective-permute-start | bytes 1769480 | tf_op jit(solution)/shard_map/ppermute | solution.py:689
  158.6 45.4 %collective-permute-start.18 = (bf16[1,8,112,768]{3,2,1,0:T(8,128)(2,1)}, bf16[1,8,112,768]{3,2,1,0:T(8,128)(2,1)}, u32[]{:S(2)}, u32[]{:S(2)}) collective-permute-start(bf16[1,8,112,768]{3,2,1,0:T(8,128)(2,1)} %bitcast.101), channel_id=1, source_target_pairs={{0,1},{1,0},{2,3},{3,2},{4,5},{5,4},{6,7},{7,6},{8,9},{9,8},{10,11... | collective-permute-start | bytes 4128776 | tf_op jit(solution)/shard_map/ppermute | solution.py:689
  170.7 36.9 %collective-permute-start.19 = (bf16[1,4,96,768]{3,2,1,0:T(8,128)(2,1)}, bf16[1,4,96,768]{3,2,1,0:T(8,128)(2,1)}, u32[]{:S(2)}, u32[]{:S(2)}) collective-permute-start(bf16[1,4,96,768]{3,2,1,0:T(8,128)(2,1)} %get-tuple-element.191), channel_id=1, source_target_pairs={{0,4},{1,5},{2,6},{3,7},{4,0},{5,1},{6,2},{7,3},{8,12},{9,13},{10,... | collective-permute-start | bytes 1769480 | tf_op jit(solution)/shard_map/ppermute | solution.py:689
  203.6 17.5 %collective-permute-start.16 = (bf16[2576,768]{1,0:T(8,128)(2,1)}, bf16[2576,768]{1,0:T(8,128)(2,1)}, u32[]{:S(2)}, u32[]{:S(2)}) collective-permute-start(bf16[2576,768]{1,0:T(8,128)(2,1)} %get-tuple-element.196.own_ref), channel_id=1, source_target_pairs={{0,16},{16,0},{1,17},{17,1},{2,18},{18,2},{3,19},{19,3},{4,20},{20... | collective-permute-start | bytes 11870216 | tf_op jit(solution)/shard_map/ppermute | solution.py:895
  204.1 26.5 %collective-permute-start.21 = (bf16[1,8,96,768]{3,2,1,0:T(8,128)(2,1)}, bf16[1,8,96,768]{3,2,1,0:T(8,128)(2,1)}, u32[]{:S(2)}, u32[]{:S(2)}) collective-permute-start(bf16[1,8,96,768]{3,2,1,0:T(8,128)(2,1)} %bitcast.117), channel_id=1, source_target_pairs={{0,1},{1,0},{2,3},{3,2},{4,5},{5,4},{6,7},{7,6},{8,9},{9,8},{10,11... | collective-permute-start | bytes 3538952 | tf_op jit(solution)/shard_map/ppermute | solution.py:689
  209.8 26.9 %collective-permute-start.23 = (bf16[1,2,96,768]{3,2,1,0:T(8,128)(2,1)}, bf16[1,2,96,768]{3,2,1,0:T(8,128)(2,1)}, u32[]{:S(2)}, u32[]{:S(2)}) collective-permute-start(bf16[1,2,96,768]{3,2,1,0:T(8,128)(2,1)} %get-tuple-element.204), channel_id=1, source_target_pairs={{0,2},{1,3},{2,0},{3,1},{4,6},{5,7},{6,4},{7,5},{8,10},{9,11},{10,... | collective-permute-start | bytes 884744 | tf_op jit(solution)/shard_map/ppermute | solution.py:689
  211.7 29.5 %collective-permute-start.24 = (bf16[1,4,112,768]{3,2,1,0:T(8,128)(2,1)}, bf16[1,4,112,768]{3,2,1,0:T(8,128)(2,1)}, u32[]{:S(2)}, u32[]{:S(2)}) collective-permute-start(bf16[1,4,112,768]{3,2,1,0:T(8,128)(2,1)} %get-tuple-element.202), channel_id=1, source_target_pairs={{0,4},{1,5},{2,6},{3,7},{4,0},{5,1},{6,2},{7,3},{8,12},{9,13},{10,... | collective-permute-start | bytes 2064392 | tf_op jit(solution)/shard_map/ppermute | solution.py:689
  221.1 26.4 %collective-permute-start.26 = (bf16[1,8,96,768]{3,2,1,0:T(8,128)(2,1)}, bf16[1,8,96,768]{3,2,1,0:T(8,128)(2,1)}, u32[]{:S(2)}, u32[]{:S(2)}) collective-permute-start(bf16[1,8,96,768]{3,2,1,0:T(8,128)(2,1)} %bitcast.119), channel_id=1, source_target_pairs={{0,1},{1,0},{2,3},{3,2},{4,5},{5,4},{6,7},{7,6},{8,9},{9,8},{10,11... | collective-permute-start | bytes 3538952 | tf_op jit(solution)/shard_map/ppermute | solution.py:689
  233.5 18.8 %collective-permute-start.27 = (bf16[1,4,96,768]{3,2,1,0:T(8,128)(2,1)}, bf16[1,4,96,768]{3,2,1,0:T(8,128)(2,1)}, u32[]{:S(2)}, u32[]{:S(2)}) collective-permute-start(bf16[1,4,96,768]{3,2,1,0:T(8,128)(2,1)} %get-tuple-element.219), channel_id=1, source_target_pairs={{0,4},{1,5},{2,6},{3,7},{4,0},{5,1},{6,2},{7,3},{8,12},{9,13},{10,... | collective-permute-start | bytes 1769480 | tf_op jit(solution)/shard_map/ppermute | solution.py:689
  238.6 16.4 %collective-permute-start.28 = (bf16[1,1,96,768]{3,2,1,0:T(8,128)(2,1)}, bf16[1,1,96,768]{3,2,1,0:T(8,128)(2,1)}, u32[]{:S(2)}, u32[]{:S(2)}) collective-permute-start(bf16[1,1,96,768]{3,2,1,0:T(8,128)(2,1)} %get-tuple-element.226), channel_id=1, source_target_pairs={{0,8},{1,9},{2,10},{3,11},{4,12},{5,13},{6,14},{7,15},{8,0},{9,1},... | collective-permute-start | bytes 442376 | tf_op jit(solution)/shard_map/ppermute | solution.py:689
  243.5 14.2 %collective-permute-start.29 = (bf16[1,2,112,768]{3,2,1,0:T(8,128)(2,1)}, bf16[1,2,112,768]{3,2,1,0:T(8,128)(2,1)}, u32[]{:S(2)}, u32[]{:S(2)}) collective-permute-start(bf16[1,2,112,768]{3,2,1,0:T(8,128)(2,1)} %get-tuple-element.228), channel_id=1, source_target_pairs={{0,2},{1,3},{2,0},{3,1},{4,6},{5,7},{6,4},{7,5},{8,10},{9,11},{10,... | collective-permute-start | bytes 1032200 | tf_op jit(solution)/shard_map/ppermute | solution.py:689
  245.0 34.1 %collective-permute-start.35 = (bf16[1,8,112,768]{3,2,1,0:T(8,128)(2,1)}, bf16[1,8,112,768]{3,2,1,0:T(8,128)(2,1)}, u32[]{:S(2)}, u32[]{:S(2)}) collective-permute-start(bf16[1,8,112,768]{3,2,1,0:T(8,128)(2,1)} %bitcast.100), channel_id=1, source_target_pairs={{0,1},{1,0},{2,3},{3,2},{4,5},{5,4},{6,7},{7,6},{8,9},{9,8},{10,11... | collective-permute-start | bytes 4128776 | tf_op jit(solution)/shard_map/ppermute | solution.py:689
  247.5 14.2 %collective-permute-start.30 = (bf16[1,1,96,768]{3,2,1,0:T(8,128)(2,1)}, bf16[1,1,96,768]{3,2,1,0:T(8,128)(2,1)}, u32[]{:S(2)}, u32[]{:S(2)}) collective-permute-start(bf16[1,1,96,768]{3,2,1,0:T(8,128)(2,1)} %get-tuple-element.230), channel_id=1, source_target_pairs={{0,8},{1,9},{2,10},{3,11},{4,12},{5,13},{6,14},{7,15},{8,0},{9,1},... | collective-permute-start | bytes 442376 | tf_op jit(solution)/shard_map/ppermute | solution.py:689
  252.3 19.1 %collective-permute-start.33 = (bf16[1,4,96,768]{3,2,1,0:T(8,128)(2,1)}, bf16[1,4,96,768]{3,2,1,0:T(8,128)(2,1)}, u32[]{:S(2)}, u32[]{:S(2)}) collective-permute-start(bf16[1,4,96,768]{3,2,1,0:T(8,128)(2,1)} %get-tuple-element.232), channel_id=1, source_target_pairs={{0,4},{1,5},{2,6},{3,7},{4,0},{5,1},{6,2},{7,3},{8,12},{9,13},{10,... | collective-permute-start | bytes 1769480 | tf_op jit(solution)/shard_map/ppermute | solution.py:689
  255.0 10.3 %collective-permute-start.31 = (bf16[1,2,96,768]{3,2,1,0:T(8,128)(2,1)}, bf16[1,2,96,768]{3,2,1,0:T(8,128)(2,1)}, u32[]{:S(2)}, u32[]{:S(2)}) collective-permute-start(bf16[1,2,96,768]{3,2,1,0:T(8,128)(2,1)} %get-tuple-element.238), channel_id=1, source_target_pairs={{0,2},{1,3},{2,0},{3,1},{4,6},{5,7},{6,4},{7,5},{8,10},{9,11},{10,... | collective-permute-start | bytes 884744 | tf_op jit(solution)/shard_map/ppermute | solution.py:689
  259.8 9.5 %collective-permute-start.32 = (bf16[1,1,112,768]{3,2,1,0:T(8,128)(2,1)}, bf16[1,1,112,768]{3,2,1,0:T(8,128)(2,1)}, u32[]{:S(2)}, u32[]{:S(2)}) collective-permute-start(bf16[1,1,112,768]{3,2,1,0:T(8,128)(2,1)} %get-tuple-element.241), channel_id=1, source_target_pairs={{0,8},{1,9},{2,10},{3,11},{4,12},{5,13},{6,14},{7,15},{8,0},{9,1},... | collective-permute-start | bytes 516104 | tf_op jit(solution)/shard_map/ppermute | solution.py:689
  267.2 9.4 %collective-permute-start.34 = (bf16[1,1,96,768]{3,2,1,0:T(8,128)(2,1)}, bf16[1,1,96,768]{3,2,1,0:T(8,128)(2,1)}, u32[]{:S(2)}, u32[]{:S(2)}) collective-permute-start(bf16[1,1,96,768]{3,2,1,0:T(8,128)(2,1)} %get-tuple-element.247), channel_id=1, source_target_pairs={{0,8},{1,9},{2,10},{3,11},{4,12},{5,13},{6,14},{7,15},{8,0},{9,1},... | collective-permute-start | bytes 442376 | tf_op jit(solution)/shard_map/ppermute | solution.py:689
  273.6 11.5 %collective-permute-start.36 = (bf16[1,2,96,768]{3,2,1,0:T(8,128)(2,1)}, bf16[1,2,96,768]{3,2,1,0:T(8,128)(2,1)}, u32[]{:S(2)}, u32[]{:S(2)}) collective-permute-start(bf16[1,2,96,768]{3,2,1,0:T(8,128)(2,1)} %get-tuple-element.250), channel_id=1, source_target_pairs={{0,2},{1,3},{2,0},{3,1},{4,6},{5,7},{6,4},{7,5},{8,10},{9,11},{10,... | collective-permute-start | bytes 884744 | tf_op jit(solution)/shard_map/ppermute | solution.py:689
  282.2 28.3 %collective-permute-start.38 = (bf16[1,4,112,768]{3,2,1,0:T(8,128)(2,1)}, bf16[1,4,112,768]{3,2,1,0:T(8,128)(2,1)}, u32[]{:S(2)}, u32[]{:S(2)}) collective-permute-start(bf16[1,4,112,768]{3,2,1,0:T(8,128)(2,1)} %get-tuple-element.255), channel_id=1, source_target_pairs={{0,4},{1,5},{2,6},{3,7},{4,0},{5,1},{6,2},{7,3},{8,12},{9,13},{10,... | collective-permute-start | bytes 2064392 | tf_op jit(solution)/shard_map/ppermute | solution.py:689
  287.0 26.6 %collective-permute-start.39 = (bf16[1,1,96,768]{3,2,1,0:T(8,128)(2,1)}, bf16[1,1,96,768]{3,2,1,0:T(8,128)(2,1)}, u32[]{:S(2)}, u32[]{:S(2)}) collective-permute-start(bf16[1,1,96,768]{3,2,1,0:T(8,128)(2,1)} %get-tuple-element.257), channel_id=1, source_target_pairs={{0,8},{1,9},{2,10},{3,11},{4,12},{5,13},{6,14},{7,15},{8,0},{9,1},... | collective-permute-start | bytes 442376 | tf_op jit(solution)/shard_map/ppermute | solution.py:689
  288.7 26.7 %collective-permute-start.40 = (bf16[2,1,96,768]{3,2,1,0:T(8,128)(2,1)}, bf16[2,1,96,768]{3,2,1,0:T(8,128)(2,1)}, u32[]{:S(2)}, u32[]{:S(2)}) collective-permute-start(bf16[2,1,96,768]{3,2,1,0:T(8,128)(2,1)} %bitcast.130), channel_id=1, source_target_pairs={{0,8},{1,9},{2,10},{3,11},{4,12},{5,13},{6,14},{7,15},{8,0},{9,1},... | collective-permute-start | bytes 884744 | tf_op jit(solution)/shard_map/ppermute | solution.py:689
  318.2 10.2 %collective-permute-start.43 = (bf16[2,2,96,768]{3,2,1,0:T(8,128)(2,1)}, bf16[2,2,96,768]{3,2,1,0:T(8,128)(2,1)}, u32[]{:S(2)}, u32[]{:S(2)}) collective-permute-start(bf16[2,2,96,768]{3,2,1,0:T(8,128)(2,1)} %merge.10.a_ref), channel_id=1, source_target_pairs={{0,2},{1,3},{2,0},{3,1},{4,6},{5,7},{6,4},{7,5},{8,10},{9,11},{10,... | collective-permute-start | bytes 1769480 | tf_op jit(solution)/shard_map/ppermute | solution.py:689
  323.1 17.1 %collective-permute-start.44 = (bf16[1,1,112,768]{3,2,1,0:T(8,128)(2,1)}, bf16[1,1,112,768]{3,2,1,0:T(8,128)(2,1)}, u32[]{:S(2)}, u32[]{:S(2)}) collective-permute-start(bf16[1,1,112,768]{3,2,1,0:T(8,128)(2,1)} %get-tuple-element.267), channel_id=1, source_target_pairs={{0,8},{1,9},{2,10},{3,11},{4,12},{5,13},{6,14},{7,15},{8,0},{9,1},... | collective-permute-start | bytes 516104 | tf_op jit(solution)/shard_map/ppermute | solution.py:689
  324.8 21.7 %collective-permute-start.45 = (bf16[2,1,96,768]{3,2,1,0:T(8,128)(2,1)}, bf16[2,1,96,768]{3,2,1,0:T(8,128)(2,1)}, u32[]{:S(2)}, u32[]{:S(2)}) collective-permute-start(bf16[2,1,96,768]{3,2,1,0:T(8,128)(2,1)} %bitcast.128), channel_id=1, source_target_pairs={{0,8},{1,9},{2,10},{3,11},{4,12},{5,13},{6,14},{7,15},{8,0},{9,1},... | collective-permute-start | bytes 884744 | tf_op jit(solution)/shard_map/ppermute | solution.py:689
  331.6 50.9 %collective-permute-start.49 = (bf16[2,4,96,768]{3,2,1,0:T(8,128)(2,1)}, bf16[2,4,96,768]{3,2,1,0:T(8,128)(2,1)}, u32[]{:S(2)}, u32[]{:S(2)}) collective-permute-start(bf16[2,4,96,768]{3,2,1,0:T(8,128)(2,1)} %merge.12.refs_0_), channel_id=1, source_target_pairs={{0,4},{1,5},{2,6},{3,7},{4,0},{5,1},{6,2},{7,3},{8,12},{9,13},{10,... | collective-permute-start | bytes 3538952 | tf_op jit(solution)/shard_map/ppermute | solution.py:689
  349.3 10.2 %collective-permute-start.47 = (bf16[2,2,96,768]{3,2,1,0:T(8,128)(2,1)}, bf16[2,2,96,768]{3,2,1,0:T(8,128)(2,1)}, u32[]{:S(2)}, u32[]{:S(2)}) collective-permute-start(bf16[2,2,96,768]{3,2,1,0:T(8,128)(2,1)} %merge.13.a_ref), channel_id=1, source_target_pairs={{0,2},{1,3},{2,0},{3,1},{4,6},{5,7},{6,4},{7,5},{8,10},{9,11},{10,... | collective-permute-start | bytes 1769480 | tf_op jit(solution)/shard_map/ppermute | solution.py:689
  352.4 19.1 %collective-permute-start.48 = (bf16[2,1,112,768]{3,2,1,0:T(8,128)(2,1)}, bf16[2,1,112,768]{3,2,1,0:T(8,128)(2,1)}, u32[]{:S(2)}, u32[]{:S(2)}) collective-permute-start(bf16[2,1,112,768]{3,2,1,0:T(8,128)(2,1)} %bitcast.126), channel_id=1, source_target_pairs={{0,8},{1,9},{2,10},{3,11},{4,12},{5,13},{6,14},{7,15},{8,0},{9,1},... | collective-permute-start | bytes 1032200 | tf_op jit(solution)/shard_map/ppermute | solution.py:689
  374.4 14.9 %collective-permute-start.50 = (bf16[2,2,112,768]{3,2,1,0:T(8,128)(2,1)}, bf16[2,2,112,768]{3,2,1,0:T(8,128)(2,1)}, u32[]{:S(2)}, u32[]{:S(2)}) collective-permute-start(bf16[2,2,112,768]{3,2,1,0:T(8,128)(2,1)} %merge.16.a_ref), channel_id=1, source_target_pairs={{0,2},{1,3},{2,0},{3,1},{4,6},{5,7},{6,4},{7,5},{8,10},{9,11},{10,... | collective-permute-start | bytes 2064392 | tf_op jit(solution)/shard_map/ppermute | solution.py:689
  380.5 31.3 %collective-permute-start.52 = (bf16[2,4,96,768]{3,2,1,0:T(8,128)(2,1)}, bf16[2,4,96,768]{3,2,1,0:T(8,128)(2,1)}, u32[]{:S(2)}, u32[]{:S(2)}) collective-permute-start(bf16[2,4,96,768]{3,2,1,0:T(8,128)(2,1)} %merge.12.refs_0_), channel_id=1, source_target_pairs={{0,1},{1,0},{2,3},{3,2},{4,5},{5,4},{6,7},{7,6},{8,9},{9,8},{10,11... | collective-permute-start | bytes 3538952 | tf_op jit(solution)/shard_map/ppermute | solution.py:689
  380.9 29.2 %collective-permute-start.51 = (bf16[2,4,96,768]{3,2,1,0:T(8,128)(2,1)}, bf16[2,4,96,768]{3,2,1,0:T(8,128)(2,1)}, u32[]{:S(2)}, u32[]{:S(2)}) collective-permute-start(bf16[2,4,96,768]{3,2,1,0:T(8,128)(2,1)} %merge.15.refs_0_), channel_id=1, source_target_pairs={{0,4},{1,5},{2,6},{3,7},{4,0},{5,1},{6,2},{7,3},{8,12},{9,13},{10,... | collective-permute-start | bytes 3538952 | tf_op jit(solution)/shard_map/ppermute | solution.py:689
  380.9 58.5 %collective-permute-start.55 = (bf16[2,4,96,768]{3,2,1,0:T(8,128)(2,1)}, bf16[2,4,96,768]{3,2,1,0:T(8,128)(2,1)}, u32[]{:S(2)}, u32[]{:S(2)}) collective-permute-start(bf16[2,4,96,768]{3,2,1,0:T(8,128)(2,1)} %merge.15.refs_0_), channel_id=1, source_target_pairs={{0,1},{1,0},{2,3},{3,2},{4,5},{5,4},{6,7},{7,6},{8,9},{9,8},{10,11... | collective-permute-start | bytes 3538952 | tf_op jit(solution)/shard_map/ppermute | solution.py:689
  382.5 39.8 %collective-permute-start.53 = (bf16[2,4,96,768]{3,2,1,0:T(8,128)(2,1)}, bf16[2,4,96,768]{3,2,1,0:T(8,128)(2,1)}, u32[]{:S(2)}, u32[]{:S(2)}) collective-permute-start(bf16[2,4,96,768]{3,2,1,0:T(8,128)(2,1)} %collective-permute-done.49.refs_1_), channel_id=1, source_target_pairs={{0,1},{1,0},{2,3},{3,2},{4,5},{5,4},{6,7},{7,6},{8,9},{9,8},{10,11... | collective-permute-start | bytes 3538952 | tf_op jit(solution)/shard_map/ppermute | solution.py:689
  392.6 45.1 %collective-permute-start.54 = (bf16[2,4,112,768]{3,2,1,0:T(8,128)(2,1)}, bf16[2,4,112,768]{3,2,1,0:T(8,128)(2,1)}, u32[]{:S(2)}, u32[]{:S(2)}) collective-permute-start(bf16[2,4,112,768]{3,2,1,0:T(8,128)(2,1)} %merge.17.refs_0_), channel_id=1, source_target_pairs={{0,4},{1,5},{2,6},{3,7},{4,0},{5,1},{6,2},{7,3},{8,12},{9,13},{10,... | collective-permute-start | bytes 4128776 | tf_op jit(solution)/shard_map/ppermute | solution.py:689
  410.1 52.2 %collective-permute-start.57 = (bf16[2,4,112,768]{3,2,1,0:T(8,128)(2,1)}, bf16[2,4,112,768]{3,2,1,0:T(8,128)(2,1)}, u32[]{:S(2)}, u32[]{:S(2)}) collective-permute-start(bf16[2,4,112,768]{3,2,1,0:T(8,128)(2,1)} %merge.17.refs_0_), channel_id=1, source_target_pairs={{0,1},{1,0},{2,3},{3,2},{4,5},{5,4},{6,7},{7,6},{8,9},{9,8},{10,11... | collective-permute-start | bytes 4128776 | tf_op jit(solution)/shard_map/ppermute | solution.py:689
  411.7 37.9 %collective-permute-start.56 = (bf16[2,4,96,768]{3,2,1,0:T(8,128)(2,1)}, bf16[2,4,96,768]{3,2,1,0:T(8,128)(2,1)}, u32[]{:S(2)}, u32[]{:S(2)}) collective-permute-start(bf16[2,4,96,768]{3,2,1,0:T(8,128)(2,1)} %collective-permute-done.51.refs_1_), channel_id=1, source_target_pairs={{0,1},{1,0},{2,3},{3,2},{4,5},{5,4},{6,7},{7,6},{8,9},{9,8},{10,11... | collective-permute-start | bytes 3538952 | tf_op jit(solution)/shard_map/ppermute | solution.py:689
  437.7 26.7 %collective-permute-start.58 = (bf16[2,4,112,768]{3,2,1,0:T(8,128)(2,1)}, bf16[2,4,112,768]{3,2,1,0:T(8,128)(2,1)}, u32[]{:S(2)}, u32[]{:S(2)}) collective-permute-start(bf16[2,4,112,768]{3,2,1,0:T(8,128)(2,1)} %collective-permute-done.54.refs_1_), channel_id=1, source_target_pairs={{0,1},{1,0},{2,3},{3,2},{4,5},{5,4},{6,7},{7,6},{8,9},{9,8},{10,11... | collective-permute-start | bytes 4128776 | tf_op jit(solution)/shard_map/ppermute | solution.py:689
  (27 other events, 134.7 us)

commit v3 on v2

--- a/solution.py
+++ b/solution.py
@@ -29,7 +29,7 @@
 GAIN1, BIAS1, QBIAS, VBIAS, OBIAS, GAIN2, BIAS2, DBIAS, UBIAS = range(9)
 VEC_ROWS = 16
 
-TIME_SCALE = 0.5
+SMALL_STEP = 8
 
 
 def mm(left, right, dims=NN):
@@ -45,7 +45,7 @@
 
 
 def cost(micros):
-    return pl.CostEstimate(flops=int(1e11), bytes_accessed=1, transcendentals=0)
+    return pl.CostEstimate(flops=int(micros * 1.15e9), bytes_accessed=1, transcendentals=0)
 
 
 def start_fetch(mine, own, recv, dst, sem):
@@ -209,7 +209,7 @@
         out_specs=[ANY] * 9,
         scratch_shapes=scratch,
         compiler_params=params(),
-        cost_estimate=cost(15),
+        cost_estimate=cost(80),
         name="attn_forward",
     )(sec, x, r, start, vec, w["qo"], w["qr"], w["ko"], w["kr"], w["vo"], w["vr"], w["f"], w["oo"], w["or"])
 
@@ -296,7 +296,7 @@
                         pltpu.VMEM((2, rows, blk), f32), pltpu.VMEM((rows, d), bf16), pltpu.VMEM((rows, d), f32),
                         pltpu.SemaphoreType.DMA((3, n)), pltpu.SemaphoreType.DMA((4 * n + 1 + n,))] + scratch,
         compiler_params=params(),
-        cost_estimate=cost(15),
+        cost_estimate=cost(80),
         name="middle",
     )(sec, e, m, r, start, vec[0], vec[1], w["uo"], w["ur"], w["do"], w["dr"],
       w["qo"], w["qr"], w["ko"], w["kr"], w["vo"], w["vr"], w["f"], w["oo"], w["or"])
@@ -350,7 +350,7 @@
         out_specs=pl.BlockSpec((rows, d), lambda j: (0, 0)),
         scratch_shapes=[pltpu.VMEM((n, blk, d), bf16), pltpu.VMEM((rows, d), f32), pltpu.SemaphoreType.DMA((n,))],
         compiler_params=params(),
-        cost_estimate=cost(8),
+        cost_estimate=cost(80),
         name="feed_down",
     )(sec, a, m, vec, w["do"], w["dr"])
 
@@ -538,7 +538,7 @@
                         pltpu.VMEM(bundle, bf16), act, pltpu.VMEM((VEC_ROWS, rows), f32), pltpu.VMEM((rows, rows), f32),
                         dma((3, n)), dma((5,)), dma((5,)), dma((n + n // 2 + 2,))],
         compiler_params=params(),
-        cost_estimate=cost(30),
+        cost_estimate=cost(80),
         name="layer_backward",
     )(sec, dz, t["m"], t["lse"], start_row, vec, dr2, t["u"], t["x"], t["q"], t["k"], t["v"], t["o"],
       w["uo"], w["ur"], w["do"], w["dr"],
@@ -565,7 +565,7 @@
                        pl.BlockSpec((per,) + shape[1:], lambda g, s: (jnp.maximum(g - 2, 0), 0, 0))]),
         out_shape=[sds(shape, bf16)] * 2,
         compiler_params=params(),
-        cost_estimate=cost(8),
+        cost_estimate=cost(80),
         name=name,
     )(scalars, *operands)
 
@@ -666,7 +666,7 @@
             scratch_shapes=[pltpu.VMEM((VEC_ROWS, d), f32)]),
         out_shape=[sds(shape, bf16)] * 2,
         compiler_params=params(),
-        cost_estimate=cost(9),
+        cost_estimate=cost(80),
         name="attn_gradient",
     )(scalars, o, h, sent_got, bundle, bundle_got, small, bundle_got)
 
@@ -677,9 +677,7 @@
 
 def bit_orders(dp):
     bits = list(range(dp.bit_length() - 1))
-    if len(bits) < 3:
-        return bits, bits[::-1]
-    return [0, 2, 1] + bits[3:], [1, 2, 0] + bits[3:]
+    return bits, [1, 0] + bits[2:]
 
 
 def exchange(array, dp, step):
@@ -745,7 +743,7 @@
             out_specs=[pl.BlockSpec((1, cb, r, w), send_at), pl.BlockSpec((1, cb, r, w), keep_at)]),
         out_shape=[sds((n, h, r, w), bf16)] * 2,
         compiler_params=params(),
-        cost_estimate=cost(1.5 + 3.5 * n * c / 8),
+        cost_estimate=cost(SMALL_STEP),
         name="add_split",
     )(bit, *flat)
 
@@ -779,65 +777,59 @@
             out_specs=pl.BlockSpec((1, cb, r, w), lambda i, g, j, s: (i, g * nb + j, 0, 0))),
         out_shape=sds((n, 2 * c, r, w), bf16),
         compiler_params=params(),
-        cost_estimate=cost(1.5 + 2 * n * c / 8),
+        cost_estimate=cost(SMALL_STEP),
         name="merge",
     )(bit, cur, arrived)
 
 
-def assemble(scalars, sources, chunk_rows, outs, place, name, extra=0):
+def assemble(scalars, sources, chunk_rows, out_shapes, targets, name, finish=None, extra_specs=()):
     _, c, r, w = sources[0].shape
     cb = c // 2
     block = cb * chunk_rows
 
-    def position(g, s):
-        part, t = g // 8, g % 8
-        own = part == s[0]
-        top, mid, low = t // 4, (t // 2) % 2, t % 2
-        return jnp.where(own, top, low), mid, jnp.where(own, low, top)
-
-    def chosen(g, s):
-        top, mid, _ = position(g, s)
-        return 2 * jnp.where(top == s[1], 0, 1) + jnp.where(mid == s[2], 0, 1)
-
     def kernel(s_ref, *refs):
-        g = pl.program_id(0)
-        which = chosen(g, s_ref)
-        out_refs = refs[4:]
-        for i in range(4):
-            @pl.when(which == i)
-            def _():
-                held = refs[i][0].astype(f32)
-                value = held[:, :chunk_rows].reshape(block, w)
-                if len(outs) == 1:
-                    out_refs[0][...] = value
-                else:
-                    for t in range(len(outs)):
-                        @pl.when((g % 8) // 2 == t)
-                        def _():
-                            out_refs[t][...] = value
-                if extra:
-                    out_refs[len(outs)][0] = held[:, chunk_rows, :]
-
-    def source(i):
-        def index(g, s):
-            return (jnp.where(chosen(g, s) == i, g // 8, 0), jnp.where(chosen(g, s) == i, position(g, s)[2], 0), 0, 0)
-        return pl.BlockSpec((1, cb, r, w), index)
-
-    def out_at(t):
-        return pl.BlockSpec((block, w), lambda g, s: place(g // 8, g % 8, t))
-
-    out_specs = [out_at(t) for t in range(len(outs))]
-    out_shape = [sds(o, f32) for o in outs]
-    if extra:
-        out_specs.append(pl.BlockSpec((1, cb, w), lambda g, s: (g, 0, 0)))
-        out_shape.append(sds((16, cb, w), f32))
+        ins, outs = refs[:4], refs[4:4 + len(out_shapes)]
+        held, wide, in_sem, out_sem = refs[4 + len(out_shapes):]
+        loads = [pltpu.make_async_copy(ins[i], held.at[i], in_sem.at[i]) for i in range(4)]
+        for load in loads:
+            load.start()
+        for load in loads:
+            load.wait()
+
+        def chunks(part, t):
+            own = s_ref[0] == part
+            top, mid, low = t // 4, (t // 2) % 2, t % 2
+            first = jnp.where(own, top, mid)
+            second = jnp.where(own, mid, top)
+            which = 2 * jnp.where(first == s_ref[1], 0, 1) + jnp.where(low == s_ref[2], 0, 1)
+            return held.at[which, part, pl.ds(second * cb, cb)]
+
+        copies = []
+        for part in range(2):
+            for t in range(8):
+                at = part * 8 + t
+                rows = chunks(part, t)
+                for i in range(cb):
+                    wide[at, i * chunk_rows:(i + 1) * chunk_rows, :] = rows[i, :chunk_rows, :].astype(f32)
+                for source, target in targets(outs, part, t):
+                    copy = pltpu.make_async_copy(wide.at[at, :, source], target, out_sem.at[len(copies)])
+                    copy.start()
+                    copies.append(copy)
+        if finish is not None:
+            finish(s_ref, chunks, wide, outs)
+        for copy in copies:
+            copy.wait()
+
+    out_specs = [ANY] * (len(out_shapes) - len(extra_specs)) + list(extra_specs)
     return pl.pallas_call(
         kernel,
-        grid_spec=pltpu.PrefetchScalarGridSpec(
-            num_scalar_prefetch=1, grid=(16,), in_specs=[source(i) for i in range(4)], out_specs=out_specs),
-        out_shape=out_shape,
+        out_shape=[sds(o, f32) for o in out_shapes],
+        in_specs=[SMEM] + [ANY] * 4,
+        out_specs=out_specs,
+        scratch_shapes=[pltpu.VMEM((4, 2, c, r, w), bf16), pltpu.VMEM((16, block, w), f32),
+                        pltpu.SemaphoreType.DMA((4,)), pltpu.SemaphoreType.DMA((20,))],
         compiler_params=params(),
-        cost_estimate=cost(12),
+        cost_estimate=cost(16),
         name=name,
     )(scalars, *sources)
 
@@ -930,7 +922,7 @@
     levels = len(first_bits)
     bit = [((spot >> jnp.where(on_first, first_bits[s], second_bits[s])) & 1).astype(jnp.int32) for s in range(levels)]
     bits = [jnp.reshape(b, (1,)) for b in bit]
-    scalars = jnp.stack([sec[0], bit[0], bit[1]])
+    scalars = jnp.stack([sec[0], bit[0], bit[2]])
     order = Order()
 
     h, q, k, v, o, m, e, lse, sent = attn_forward(0, sec, x0, x0, start_col, vec[0], w)
@@ -940,8 +932,7 @@
     kept[0].update(u=u0, a=a0, a_got=(a_got, 0))
     kept.append(dict(x=x1, h=h, q=q, k=k, v=v, o=o, m=m, e=e, lse=lse, u=u1, a=a1, sent_got=swap(sent), a_got=(a_got, 1)))
     order.mark(x1)
-    y = feed_down(1, sec, a1, order.tie(m), vec[1], w)
-    order.mark(y, a_got, kept[0]["sent_got"], kept[1]["sent_got"])
+    order.mark(x1)
 
     def cut(level, parts):
         (first_keep, first_got), *rest = parts
@@ -954,12 +945,6 @@
             part = cut(s, [part])
         return part
 
-    def add_last(part):
-        keep, got = part
-        total = (order.tie(keep).astype(f32) + got.astype(f32)).astype(bf16)
-        order.mark(total)
-        return total
-
     def grow(level, cur, got):
         cur = merge(bits[level], order.tie(cur), got)
         order.mark(cur)
@@ -977,7 +962,7 @@
     def back_step(layer, dz, dz_at, dr2):
         du, sent, bundle, dr2, small = layer_backward(
             layer, sec, dz, dz_at, dict(kept[layer], u=order.tie(kept[layer]["u"])), start_row, vec[layer], dr2, w)
-        order.mark(dr2)
+        order.mark(bundle)
         return bundle, swap(bundle), dr2, small, du, swap(sent)
 
     def up_step(layer, back):
@@ -991,9 +976,14 @@
 
     to_second = lambda t: lax.ppermute(t, "section", [(0, 1)])
 
+    def summed(part, i):
+        keep, got = part
+        return (keep[i:i + 1].astype(f32) + got[i:i + 1].astype(f32)).astype(bf16)
+
     def hand_over(second, first):
+        own = order.tie(jnp.where(on_first, first, second))
         sent = jnp.where(on_first, second, first)
-        own = jnp.where(on_first, first, second)
+        order.mark(sent)
         return own, swap(sent)
 
     def both_parts(pair):
@@ -1005,9 +995,8 @@
             cur = grow(s, cur, exchange(cur, dp, s))
         return cur, exchange(cur, dp, 3)
 
-    y_moved = to_second(y)
     back1 = back_step(1, dz1, 0, jnp.zeros((rows, half), f32))
-    order.also(y_moved)
+    order.also(kept[0]["sent_got"], kept[1]["sent_got"])
     down1 = down_step(1, dz1, dz1_got, 0)
     up1 = up_step(1, back1)
     square1 = attn_grad_step(1, back1)
@@ -1017,39 +1006,24 @@
     dx0, dx_moved = (t[4 * rows:5 * rows] for t in back0[:2])
     up1 = cut(1, [up1])
     square1 = cut(1, [square1])
-    down1 = cut(2, [down1])
+    down0 = cut(1, [down0])
     up0 = up_step(0, back0)
+    feed = cut(2, [down1, up1, down0])
     square0 = attn_grad_step(0, back0)
-    down0 = cut(1, [down0])
-    up1 = cut(2, [up1])
-    down1 = deep(cut(3, [down1]))
     square1 = cut(2, [square1])
-    up1 = deep(cut(3, [up1]))
     up0 = cut(1, [up0])
-    down0 = cut(2, [down0])
-    down1 = add_last(down1)
+    feed = deep(cut(3, [feed]))
     square1 = deep(cut(3, [square1]))
-    up1 = add_last(up1)
-    down0 = deep(cut(3, [down0]))
-    square1 = add_last(square1)
     up0 = cut(2, [up0])
-    down0 = add_last(down0)
-    pair_d = hand_over(down1, down0)
     square0 = cut(1, [square0])
     up0 = deep(cut(3, [up0]))
+    square0 = cut(2, [square0])
+    pair_d = hand_over(summed(feed, 0), summed(feed, 2))
+    order.also(square1[1])
+    square0 = deep(cut(3, [square0]))
     cur_d, got_d = both_parts(pair_d)
-    square0 = cut(2, [square0])
-    up0 = add_last(up0)
-    pair_u = hand_over(up1, up0)
-    cur_d = grow(3, cur_d, got_d)
-    got_d = exchange(cur_d, dp, 2)
-    square0 = deep(cut(3, [square0]))
-    cur_u, got_u = both_parts(pair_u)
-    cur_d = grow(2, cur_d, got_d)
-    far_d = exchange(cur_d, dp, 1)
-    side_d = exchange(cur_d, dp, 0)
-    square0 = add_last(square0)
-    b, e = square1, square0
+    pair_u = hand_over(summed(feed, 1), summed(up0, 0))
+    b, e = summed(square1, 0), summed(square0, 0)
 
     chunk = sum(bit[s] << (levels - 1 - s) for s in range(levels))
     at_row = lax.broadcasted_iota(jnp.int32, e.shape, 2)
@@ -1060,57 +1034,94 @@
     b = jnp.where(matrix_rows | (vector_row & on_first), e, b)
     pair_a = hand_over(b, e)
 
+    cur_d = grow(3, cur_d, got_d)
+    got_d = exchange(cur_d, dp, 1)
+    cur_u, got_u = both_parts(pair_u)
+    cur_d = grow(1, cur_d, got_d)
+    far_d = exchange(cur_d, dp, 2)
+    side_d = exchange(cur_d, dp, 0)
+    cur_a, got_a = both_parts(pair_a)
     cur_u = grow(3, cur_u, got_u)
-    got_u = exchange(cur_u, dp, 2)
-    cur_a, got_a = both_parts(pair_a)
-    cur_u = grow(2, cur_u, got_u)
-    far_u = exchange(cur_u, dp, 1)
+    got_u = exchange(cur_u, dp, 1)
+    y = feed_down(1, sec, a1, order.tie(m), vec[1], w)
+    order.mark(y)
+    y_moved = to_second(y)
+    cur_a = grow(3, cur_a, got_a)
+    got_a = exchange(cur_a, dp, 1)
+    order.also(far_d, side_d)
+    last_d = exchange(order.tie(far_d), dp, 0)
+    cur_u = grow(1, cur_u, got_u)
+    far_u = exchange(cur_u, dp, 2)
     side_u = exchange(cur_u, dp, 0)
-    cur_a = grow(3, cur_a, got_a)
-    got_a = exchange(cur_a, dp, 2)
-    order.also(far_d)
-    last_d = exchange(order.tie(far_d), dp, 0)
-    cur_a = grow(2, cur_a, got_a)
-    far_a = exchange(cur_a, dp, 1)
+    order.also(y_moved)
+    cur_a = grow(1, cur_a, got_a)
+    far_a = exchange(cur_a, dp, 2)
     side_a = exchange(cur_a, dp, 0)
-    order.also(far_u)
+
+    all_columns = slice(None)
+    block = ff // 16
+    order.also(far_u, side_u)
     last_u = exchange(order.tie(far_u), dp, 0)
-    down_grad, = assemble(scalars, (order.tie(cur_d), far_d, side_d, last_d), chunk_rows, [(ff, d)],
-                          lambda part, block, t: (part * 8 + block, 0), "assemble_down")
-    order.mark(down_grad, far_a)
-    last_a = exchange(far_a, dp, 0)
-    up_grad, = assemble(scalars, (order.tie(cur_u), far_u, side_u, last_u), chunk_rows, [(d, ff)],
-                        lambda part, block, t: (block % 4, part * 2 + block // 4), "assemble_up")
+    down_grad, = assemble(
+        scalars, (order.tie(cur_d), far_d, side_d, last_d), chunk_rows, [(ff, d)],
+        lambda outs, part, t: [(all_columns, outs[0].at[pl.ds((8 * part + t) * block, block), :])], "assemble_down")
+    order.mark(down_grad, far_a, side_a)
+    last_a = exchange(order.tie(far_a), dp, 0)
+    up_grad, = assemble(
+        scalars, (order.tie(cur_u), far_u, side_u, last_u), chunk_rows, [(d, ff)],
+        lambda outs, part, t: [(all_columns, outs[0].at[pl.ds(t % 4 * block, block), pl.ds((2 * part + t // 4) * d, d)])],
+        "assemble_up")
     order.mark(up_grad)
-    out_grad, query_grad, key_grad, mixed_grad, vectors = assemble(
-        scalars, (order.tie(cur_a), far_a, side_a, last_a), chunk_rows, [(d, d)] * 4,
-        lambda part, block, t: (jnp.where(block // 2 == t, part * 2 + block % 2,
-                                          jnp.where(block // 2 < t, jnp.maximum(part * 2 - 1, 0), part * 2 + 1)), 0),
-        "assemble_attn", extra)
-    total = vectors[:, :, :share].reshape(-1)[:VEC_ROWS * d].reshape(VEC_ROWS, d)
+
+    def square_targets(outs, part, t):
+        at = pl.ds((2 * part + t % 2) * block, block)
+        if t // 2 < 3:
+            return [(all_columns, outs[t // 2].at[at, :])]
+        return [(pl.ds(half, half), outs[3].at[at, :]), (pl.ds(0, half), outs[4].at[at, :])]
+
+    def vectors(s_ref, chunks, wide, outs):
+        lines = outs[5]
+        for part in range(2):
+            for t in range(8):
+                rows_of = chunks(part, t)
+                for i in range(dp // 8):
+                    at = ((part * 8 + t) * (dp // 8) + i) * share
+                    if at < VEC_ROWS * d:
+                        lines[at // d:at // d + 1, at % d:at % d + share] = rows_of[i, chunk_rows:chunk_rows + 1, :share].astype(f32)
+        for i, row in enumerate((GAIN1, BIAS1, QBIAS, OBIAS, GAIN2, BIAS2, DBIAS)):
+            outs[6 + i][...] = lines[row:row + 1, :]
+        outs[13][...] = lines[VBIAS:VBIAS + 1, half:]
+        for i in range(ff // d):
+            outs[14][:, i * d:(i + 1) * d] = lines[UBIAS + i:UBIAS + i + 1, :]
+
+    (out_grad, query_grad, key_grad, value_grad, first_full, lines, gain1_grad, bias1_grad, qbias_grad, obias_grad,
+     gain2_grad, bias2_grad, dbias_grad, vbias_grad, ubias_grad) = assemble(
+        scalars, (order.tie(cur_a), far_a, side_a, last_a), chunk_rows,
+        [(d, d)] * 3 + [(d, half)] * 2 + [(VEC_ROWS, d)] + [(1, d)] * 7 + [(1, half), (1, ff)],
+        square_targets, "assemble_attn", vectors, [VMEM] * 10)
 
     spot_half = lambda t: jnp.where(on_first, t[:t.shape[0] // 2], t[t.shape[0] // 2:])
     block_ends = jnp.where(on_first, jnp.concatenate([dx0, dx_moved], axis=0),
                            jnp.concatenate([y_moved, y], axis=0))[None]
     return (
         block_ends,
-        total[GAIN1][None],
-        total[BIAS1][None],
+        gain1_grad,
+        bias1_grad,
         query_grad[None],
-        total[QBIAS][None],
+        qbias_grad,
         key_grad[None],
-        mixed_grad[None, :, half:],
-        total[VBIAS, half:][None],
-        spot_half(mixed_grad[:, :half]),
-        spot_half(total[VBIAS, :half]),
+        value_grad[None],
+        vbias_grad,
+        spot_half(first_full),
+        spot_half(lines[VBIAS, :half]),
         out_grad[None],
-        total[OBIAS][None],
-        total[GAIN2][None],
-        total[BIAS2][None],
+        obias_grad,
+        gain2_grad,
+        bias2_grad,
         up_grad[None],
-        total[UBIAS:UBIAS + ff // d].reshape(1, ff),
+        ubias_grad,
         down_grad[None],
-        total[DBIAS][None],
+        dbias_grad,
     )
 
 

time: 495 us -> 449 us (0.907)
  Pallas kernels: 278 us -> 258 us
  waiting for transfers between devices: 112 us -> 100 us
  other arithmetic: 27.4 us -> 18.9 us
  local copies, waits for them, and re-layouts: 12.7 us -> 5.8 us
    pallas_call x3, Pallas kernels: 39.3 us -> 21.4 us  [assemble(): pl.pallas_call(kernel, out_shape=[sds(o, f32) for o in out_shapes], in_sp...]
    ppermute x39 -> x35, waiting for transfers between devices: 112 us -> 100 us  [exchange(): return lax.ppermute(array, AXES, pairs)]
    convert_element_type x3 -> x0, other arithmetic: 5.06 us -> none  [add_last(): total = (order.tie(keep).astype(f32) + got.astype(f32)).astype(bf16)]
    pallas_call x18 -> x14, Pallas kernels: 43.6 us -> 40.9 us  [add_split(): pl.pallas_call(kernel, grid_spec=pltpu.PrefetchScalarGridSpec(num_scalar_...]
    ppermute x39 -> x35, starting transfers between devices: 46.1 us -> 48.7 us  [exchange(): return lax.ppermute(array, AXES, pairs)]
  transfers between devices with their start and end apart: 59 -> 55, of which waited for: 18 -> 17; matrix products, arithmetic and copies ran while one was open for 6% -> 4% of each run, Pallas kernels for 53% -> 56%
where the time goes in v3:
time: 449 us; the launch traced here: 443 us
  Pallas kernels  258 us (57%)
  waiting for transfers between devices  100 us (22%)
  starting transfers between devices  58.9 us (13%)
  other arithmetic  18.9 us (4%)
  local copies, waits for them, and re-layouts  5.8 us (1%)
    ppermute x35, waiting for transfers between devices, exchange(): return lax.ppermute(array, AXES, pairs)  100 us
    pallas_call x2, Pallas kernels, layer_backward(): pl.pallas_call(functools.partial(layer_backward_kernel, layer, blk), grid...  66 us
    ppermute x35, starting transfers between devices, exchange(): return lax.ppermute(array, AXES, pairs)  48.7 us
    pallas_call x14, Pallas kernels, add_split(): pl.pallas_call(kernel, grid_spec=pltpu.PrefetchScalarGridSpec(num_scalar_...  40.9 us
    pallas_call x1, Pallas kernels, middle(): pl.pallas_call(functools.partial(middle_kernel, blk), out_shape=[wide, wi...  35.5 us
    pallas_call x4, Pallas kernels, quarters(): pl.pallas_call(kernel, grid_spec=pltpu.PrefetchScalarGridSpec(num_scalar_...  30.8 us
    pallas_call x9, Pallas kernels, merge(): pl.pallas_call(kernel, grid_spec=pltpu.PrefetchScalarGridSpec(num_scalar_...  23.5 us
    pallas_call x3, Pallas kernels, assemble(): pl.pallas_call(kernel, out_shape=[sds(o, f32) for o in out_shapes], in_sp...  21.4 us
  transfers between devices with their start and end apart: 55, of which 17 were waited for; matrix products, arithmetic and copies ran while one was open for 4% of the time, Pallas kernels for 56%

profile of v3, /device:TPU:0, one launch (start us, length us, event | category | flops | bytes accessed | tf_op | source)
XLA Modules:
  0.0 442.8 jit_solution(13494717706592267447)
XLA Ops:
  12.0 3.0 broadcast_select_fusion
  15.5 15.5 %attn_forward.1 = (bf16[512,768]{1,0:T(8,128)(2,1)}, bf16[512,768]{1,0:T(8,128)(2,1)}, bf16[512,768]{1,0:T(8,128)(2,1)}, bf16[512,768]{1,0:T(8,128)(2,1)}, bf16[...) custom-call(s32[1]{0:T(128)} %bitcast.sec_ref.s_ref, ...), custom_call_target="tpu_custom_call" | custom-call | flops 92000002048 | bytes 1 | tf_op jit(solution)/shard_map/attn_forward/pallas_call | solution.py:205
  31.4 35.5 %middle.1 = (bf16[512,3072]{1,0:T(8,128)(2,1)}, bf16[512,3072]{1,0:T(8,128)(2,1)}, bf16[512,768]{1,0:T(8,128)(2,1)}, bf16[512,3072]{1,0:T(8,128)(2,1)}, bf16[512...) custom-call(s32[1]{0:T(128)} %bitcast.sec_ref.s_ref, ...), custom_call_target="tpu_custom_call" | custom-call | flops 92000002048 | bytes 1 | tf_op jit(solution)/shard_map/middle/pallas_call | solution.py:289
  68.5 33.7 %layer_backward.2 = (bf16[512,3072]{1,0:T(8,128)(2,1)}, bf16[2,512,768]{2,1,0:T(8,128)(2,1)}, bf16[2576,768]{1,0:T(8,128)(2,1)}, f32[512,384]{1,0:T(8,128)}, f32[16,768]{1,0:T(8,128)}) custom-call(s32[1]{0:T(128)} %bitcast.sec_ref.s_ref, bf16[512,768]{1,0:T(8,128)(2,1)} %get-tuple-element.281.dz_ref.x_ref, f32[512,768]{1,0:T(8,128)} %get-tuple-element.255.m_ref, ...), custom_call_target="tpu_custom_call" | custom-call | flops 92000002048 | bytes 1 | tf_op jit(solution)/shard_map/layer_backward/pallas_call | solution.py:529
  102.7 7.3 %down_gradient.2 = (bf16[8,96,768]{2,1,0:T(8,128)(2,1)}, bf16[8,96,768]{2,1,0:T(8,128)(2,1)}) custom-call(s32[3]{0:T(128)} %pad_add_fusion.s_ref, bf16[512,3072]{1,0:T(8,128)(2,1)} %get-tuple-element.170.a_ref, bf16[2,512,1536]{2,1,0:T(8,128)(2,1)} %collective-permute-done.10.b_ref, bf16[512,768]{1,0:T(8,128)(2,1)} %get-tuple-element.281.dz_ref.x_ref, ...), custom_call_target="tpu_custom_call" | custom-call | flops 92000002048 | bytes 1 | tf_op jit(solution)/shard_map/down_gradient/pallas_call | solution.py:560
  110.1 8.3 %up_gradient.2 = (bf16[8,96,768]{2,1,0:T(8,128)(2,1)}, bf16[8,96,768]{2,1,0:T(8,128)(2,1)}) custom-call(s32[3]{0:T(128)} %pad_add_fusion.s_ref, bf16[512,768]{1,0:T(8,128)(2,1)} %get-tuple-element.176.e_ref, bf16[2,512,768]{2,1,0:T(8,128)(2,1)} %collective-permute-done.9.f_ref.l_ref, bf16[512,3072]{1,0:T(8,128)(2,1)} %get-tuple-element.177.du_ref, ...), custom_call_target="tpu_custom_call" | custom-call | flops 92000002048 | bytes 1 | tf_op jit(solution)/shard_map/up_gradient/pallas_call | solution.py:560
  118.4 2.9 collective-permute-start.14
  121.3 8.1 %attn_gradient.2 = (bf16[8,112,768]{2,1,0:T(8,128)(2,1)}, bf16[8,112,768]{2,1,0:T(8,128)(2,1)}) custom-call(s32[3]{0:T(128)} %pad_add_fusion.s_ref, bf16[512,768]{1,0:T(8,128)(2,1)} %get-tuple-element.180.o_in.o_ref, bf16[512,768]{1,0:T(8,128)(2,1)} %get-tuple-element.181.h_ref, bf16[2,512,768]{2,1,0:T(8,128)(2,1)} %collective-permute-done.9.f_ref.l_ref, ...), custom_call_target="tpu_custom_call" | custom-call | flops 92000002048 | bytes 1 | tf_op jit(solution)/shard_map/attn_gradient/pallas_call | solution.py:656
  129.5 7.4 %down_gradient.3 = (bf16[8,96,768]{2,1,0:T(8,128)(2,1)}, bf16[8,96,768]{2,1,0:T(8,128)(2,1)}) custom-call(s32[3]{0:T(128)} %pad_add_fusion.s_ref, bf16[512,3072]{1,0:T(8,128)(2,1)} %get-tuple-element.184.a_ref, bf16[2,512,1536]{2,1,0:T(8,128)(2,1)} %collective-permute-done.10.b_ref, bf16[2576,768]{1,0:T(8,128)(2,1)} %get-tuple-element.163.own_ref.x_ref.dz_ref, ...), custom_call_target="tpu_custom_call" | custom-call | flops 92000002048 | bytes 1 | tf_op jit(solution)/shard_map/down_gradient/pallas_call | solution.py:560
  138.9 2.9 add_split.14
  143.8 32.3 %layer_backward.3 = (bf16[512,3072]{1,0:T(8,128)(2,1)}, bf16[2,512,768]{2,1,0:T(8,128)(2,1)}, bf16[2576,768]{1,0:T(8,128)(2,1)}, f32[512,384]{1,0:T(8,128)}, f32[16,768]{1,0:T(8,128)}) custom-call(s32[1]{0:T(128)} %bitcast.sec_ref.s_ref, bf16[2576,768]{1,0:T(8,128)(2,1)} %get-tuple-element.163.own_ref.x_ref.dz_ref, f32[512,768]{1,0:T(8,128)} %get-tuple-element.150.m_ref, ...), custom_call_target="tpu_custom_call" | custom-call | flops 92000002048 | bytes 1 | tf_op jit(solution)/shard_map/layer_backward/pallas_call | solution.py:529
  176.2 3.0 add_split.15
  180.7 3.1 add_split.16
  183.8 2.9 add_split.17
  188.8 7.8 %up_gradient.3 = (bf16[8,96,768]{2,1,0:T(8,128)(2,1)}, bf16[8,96,768]{2,1,0:T(8,128)(2,1)}) custom-call(s32[3]{0:T(128)} %pad_add_fusion.s_ref, bf16[512,768]{1,0:T(8,128)(2,1)} %get-tuple-element.202.e_ref, bf16[2,512,768]{2,1,0:T(8,128)(2,1)} %collective-permute-done.8.f_ref.l_ref, bf16[512,3072]{1,0:T(8,128)(2,1)} %get-tuple-element.203.du_ref, ...), custom_call_target="tpu_custom_call" | custom-call | flops 92000002048 | bytes 1 | tf_op jit(solution)/shard_map/up_gradient/pallas_call | solution.py:560
  197.7 5.3 %add_split.18 = (bf16[3,2,96,768]{3,2,1,0:T(8,128)(2,1)}, bf16[3,2,96,768]{3,2,1,0:T(8,128)(2,1)}) custom-call(s32[1]{0:T(128)} %bitcast.15.s_ref, bf16[1,4,96,768]{3,2,1,0:T(8,128)(2,1)} %get-tuple-element.209.refs_0_, bf16[1,4,96,768]{3,2,1,0:T(8,128)(2,1)} %collective-permute-done.20.refs_1_, bf16[1,4,96,768]{3,2,1,0:T(8,128)(2,1)} %get-tuple-element.210.refs_2_, ...), custom_call_target="tpu_custom_call" | custom-call | flops 9200000000 | bytes 1 | tf_op jit(solution)/shard_map/add_split/pallas_call | solution.py:738
  205.2 8.1 %attn_gradient.3 = (bf16[8,112,768]{2,1,0:T(8,128)(2,1)}, bf16[8,112,768]{2,1,0:T(8,128)(2,1)}) custom-call(s32[3]{0:T(128)} %pad_add_fusion.s_ref, bf16[512,768]{1,0:T(8,128)(2,1)} %get-tuple-element.213.o_in.o_ref, bf16[512,768]{1,0:T(8,128)(2,1)} %get-tuple-element.214.h_ref, bf16[2,512,768]{2,1,0:T(8,128)(2,1)} %collective-permute-done.8.f_ref.l_ref, ...), custom_call_target="tpu_custom_call" | custom-call | flops 92000002048 | bytes 1 | tf_op jit(solution)/shard_map/attn_gradient/pallas_call | solution.py:656
  216.0 2.9 add_split.20
  220.6 5.5 %collective-permute-done.25.refs_1_ = bf16[3,2,96,768]{3,2,1,0:T(8,128)(2,1)} collective-permute-done((bf16[3,2,96,768]{3,2,1,0:T(8,128)(2,1)}, bf16[3,2,96,768]{3,2,1,0:T(8,128)(2,1)}, u32[]{:S(2)}, u32[]{:S(2)}) %collective-permute-start.25) | collective-permute-done | bytes 884768 | tf_op jit(solution)/shard_map/ppermute | solution.py:687
  226.1 4.6 %add_split.21 = (bf16[3,1,96,768]{3,2,1,0:T(8,128)(2,1)}, bf16[3,1,96,768]{3,2,1,0:T(8,128)(2,1)}) custom-call(s32[1]{0:T(128)} %bitcast.20.s_ref, bf16[3,2,96,768]{3,2,1,0:T(8,128)(2,1)} %get-tuple-element.224.refs_0_, bf16[3,2,96,768]{3,2,1,0:T(8,128)(2,1)} %collective-permute-done.25.refs_1_), custom_call_target="tpu_custom_call" | custom-call | flops 9200000000 | bytes 1 | tf_op jit(solution)/shard_map/add_split/pallas_call | solution.py:738
  230.7 2.6 collective-permute-start.31
  236.3 2.4 add_split.23
  240.7 11.2 %collective-permute-done.28.refs_1_ = bf16[1,8,112,768]{3,2,1,0:T(8,128)(2,1)} collective-permute-done((bf16[1,8,112,768]{3,2,1,0:T(8,128)(2,1)}, bf16[1,8,112,768]{3,2,1,0:T(8,128)(2,1)}, u32[]{:S(2)}, u32[]{:S(2)}) %collective-permute-start.28) | collective-permute-done | bytes 1376288 | tf_op jit(solution)/shard_map/ppermute | solution.py:687
  252.0 3.1 add_split.24
  259.3 7.1 %collective-permute-done.32.refs_1_ = bf16[1,4,112,768]{3,2,1,0:T(8,128)(2,1)} collective-permute-done((bf16[1,4,112,768]{3,2,1,0:T(8,128)(2,1)}, bf16[1,4,112,768]{3,2,1,0:T(8,128)(2,1)}, u32[]{:S(2)}, u32[]{:S(2)}) %collective-permute-start.32) | collective-permute-done | bytes 688160 | tf_op jit(solution)/shard_map/ppermute | solution.py:687
  268.7 2.4 collective-permute-start.34
  273.9 8.0 %collective-permute-done.33 = bf16[1,1,112,768]{3,2,1,0:T(8,128)(2,1)} collective-permute-done((bf16[1,1,112,768]{3,2,1,0:T(8,128)(2,1)}, bf16[1,1,112,768]{3,2,1,0:T(8,128)(2,1)}, u32[]{:S(2)}, u32[]{:S(2)}) %collective-permute-start.33) | collective-permute-done | bytes 172064 | tf_op jit(solution)/shard_map/ppermute | solution.py:687
  285.7 3.0 collective-permute-start.37
  290.7 5.3 %collective-permute-done.36 = bf16[1,1,112,768]{3,2,1,0:T(8,128)(2,1)} collective-permute-done((bf16[1,1,112,768]{3,2,1,0:T(8,128)(2,1)}, bf16[1,1,112,768]{3,2,1,0:T(8,128)(2,1)}, u32[]{:S(2)}, u32[]{:S(2)}) %collective-permute-start.36) | collective-permute-done | bytes 172064 | tf_op jit(solution)/shard_map/ppermute | solution.py:687
  298.0 2.4 collective-permute-done.37.b_ref
  300.4 2.8 merge.10.a_ref
  307.0 6.5 %collective-permute-done.39.b_ref = bf16[2,2,96,768]{3,2,1,0:T(8,128)(2,1)} collective-permute-done((bf16[2,2,96,768]{3,2,1,0:T(8,128)(2,1)}, bf16[2,2,96,768]{3,2,1,0:T(8,128)(2,1)}, u32[]{:S(2)}, u32[]{:S(2)}) %collective-permute-start.39) | collective-permute-done | bytes 589856 | tf_op jit(solution)/shard_map/ppermute | solution.py:687
  313.5 3.2 merge.12.refs_0_
  319.8 2.8 merge.14.a_ref
  326.0 7.9 %feed_down.1 = bf16[512,768]{1,0:T(8,128)(2,1)} custom-call(s32[1]{0:T(128)} %bitcast.sec_ref.s_ref, bf16[512,3072]{1,0:T(8,128)(2,1)} %get-tuple-element.170.a_ref, f32[512,768]{1,0:T(8,128)} %get-tuple-element.255.m_ref, f32[16,768]{1,0:T(8,128)} %get-tuple-element.289.vec1_ref.vec_ref, bf16[3072,768]{1,0:T(8,128)(2,1)} %bitcast.11.refs_2_.dn_o, ...), custom_call_target="tpu_custom_call" | custom-call | flops 92000002048 | bytes 1 | tf_op jit(solution)/shard_map/feed_down/pallas_call | solution.py:345
  336.1 11.3 %collective-permute-done.43.b_ref = bf16[2,1,112,768]{3,2,1,0:T(8,128)(2,1)} collective-permute-done((bf16[2,1,112,768]{3,2,1,0:T(8,128)(2,1)}, bf16[2,1,112,768]{3,2,1,0:T(8,128)(2,1)}, u32[]{:S(2)}, u32[]{:S(2)}) %collective-permute-start.43) | collective-permute-done | bytes 344096 | tf_op jit(solution)/shard_map/ppermute | solution.py:687
  347.3 2.9 merge.15.a_ref
  352.4 3.2 merge.16.refs_0_
  355.6 3.4 collective-permute-start.48
  362.3 2.7 maximum_select_fusion
  365.2 3.4 merge.17.refs_0_
  368.6 5.3 %collective-permute-start.51 = (bf16[2,4,112,768]{3,2,1,0:T(8,128)(2,1)}, bf16[2,4,112,768]{3,2,1,0:T(8,128)(2,1)}, u32[]{:S(2)}, u32[]{:S(2)}) collective-permute-start(bf16[2,4,112,768]{3,2,1,0:T(8,128)(2,1)} %merge.17.refs_0_), channel_id=1, source_target_pairs={{0,4},{1,5},{2,6},{3,7},{4,0},{5,1},{6,2},{7,3},{8,12},{9,13},{10,... | collective-permute-start | bytes 4128776 | tf_op jit(solution)/shard_map/ppermute | solution.py:687
  373.9 12.3 %collective-permute-done.48.refs_1_ = bf16[2,4,96,768]{3,2,1,0:T(8,128)(2,1)} collective-permute-done((bf16[2,4,96,768]{3,2,1,0:T(8,128)(2,1)}, bf16[2,4,96,768]{3,2,1,0:T(8,128)(2,1)}, u32[]{:S(2)}, u32[]{:S(2)}) %collective-permute-start.48) | collective-permute-done | bytes 1179680 | tf_op jit(solution)/shard_map/ppermute | solution.py:687
  388.2 6.9 %assemble_down.1 = f32[3072,768]{1,0:T(8,128)} custom-call(s32[3]{0:T(128)} %pad_add_fusion.s_ref, bf16[2,4,96,768]{3,2,1,0:T(8,128)(2,1)} %merge.12.refs_0_, bf16[2,4,96,768]{3,2,1,0:T(8,128)(2,1)} %collective-permute-done.44.refs_1_, bf16[2,4,96,768]{3,2,1,0:T(8,128)(2,1)} %collective-permute-done.45.refs_2_, ...), custom_call_target="tpu_custom_call" | custom-call | flops 18400000000 | bytes 1 | tf_op jit(solution)/shard_map/assemble_down/pallas_call | solution.py:824
  395.0 17.4 %collective-permute-done.51.refs_1_ = bf16[2,4,112,768]{3,2,1,0:T(8,128)(2,1)} collective-permute-done((bf16[2,4,112,768]{3,2,1,0:T(8,128)(2,1)}, bf16[2,4,112,768]{3,2,1,0:T(8,128)(2,1)}, u32[]{:S(2)}, u32[]{:S(2)}) %collective-permute-start.51) | collective-permute-done | bytes 1376288 | tf_op jit(solution)/shard_map/ppermute | solution.py:687
  415.6 6.9 %assemble_up.1 = f32[768,3072]{1,0:T(8,128)} custom-call(s32[3]{0:T(128)} %pad_add_fusion.s_ref, bf16[2,4,96,768]{3,2,1,0:T(8,128)(2,1)} %merge.16.refs_0_, bf16[2,4,96,768]{3,2,1,0:T(8,128)(2,1)} %collective-permute-done.48.refs_1_, bf16[2,4,96,768]{3,2,1,0:T(8,128)(2,1)} %collective-permute-done.49.refs_2_, ...), custom_call_target="tpu_custom_call" | custom-call | flops 18400000000 | bytes 1 | tf_op jit(solution)/shard_map/assemble_up/pallas_call | solution.py:824
  422.4 8.9 %collective-permute-done.54.refs_3_ = bf16[2,4,112,768]{3,2,1,0:T(8,128)(2,1)} collective-permute-done((bf16[2,4,112,768]{3,2,1,0:T(8,128)(2,1)}, bf16[2,4,112,768]{3,2,1,0:T(8,128)(2,1)}, u32[]{:S(2)}, u32[]{:S(2)}) %collective-permute-start.54) | collective-permute-done | bytes 1376288 | tf_op jit(solution)/shard_map/ppermute | solution.py:687
  431.3 7.7 %assemble_attn.1 = (f32[768,768]{1,0:T(8,128)}, f32[768,768]{1,0:T(8,128)}, f32[768,768]{1,0:T(8,128)}, f32[768,384]{1,0:T(8,128)}, f32[768,384]{1,0:T(8,128)}, ...) custom-call(s32[3]{0:T(128)} %pad_add_fusion.s_ref, ...), custom_call_target="tpu_custom_call" | custom-call | flops 18400000000 | bytes 1 | tf_op jit(solution)/shard_map/assemble_attn/pallas_call | solution.py:824
  (166 shorter events, 78.1 us)
Async XLA Ops:
  5.8 9.4 %collective-permute-start.2 = (bf16[768,768]{1,0:T(8,128)(2,1)}, bf16[768,768]{1,0:T(8,128)(2,1)}, u32[]{:S(2)}, u32[]{:S(2)}) collective-permute-start(bf16[768,768]{1,0:T(8,128)(2,1)} %bitcast.6.refs_0_.refs_4_.qw_o), channel_id=1, source_target_pairs={{0,16},{16,0},{1,17},{17,1},{2,18},{18,2},{3,19},{19,3},{4,20},{20... | collective-permute-start | bytes 3538952 | tf_op jit(solution)/shard_map/ppermute | solution.py:887
  15.0 16.4 %collective-permute-start.7 = (bf16[3072,768]{1,0:T(8,128)(2,1)}, bf16[3072,768]{1,0:T(8,128)(2,1)}, u32[]{:S(2)}, u32[]{:S(2)}) collective-permute-start(bf16[3072,768]{1,0:T(8,128)(2,1)} %bitcast.11.refs_2_.dn_o), channel_id=1, source_target_pairs={{0,16},{16,0},{1,17},{17,1},{2,18},{18,2},{3,19},{19,3},{4,20},{20... | collective-permute-start | bytes 14155784 | tf_op jit(solution)/shard_map/ppermute | solution.py:887
  15.3 16.1 %collective-permute-start.6 = (bf16[768,3072]{1,0:T(8,128)(2,1)}, bf16[768,3072]{1,0:T(8,128)(2,1)}, u32[]{:S(2)}, u32[]{:S(2)}) collective-permute-start(bf16[768,3072]{1,0:T(8,128)(2,1)} %bitcast.10.refs_0_.up_o), channel_id=1, source_target_pairs={{0,16},{16,0},{1,17},{17,1},{2,18},{18,2},{3,19},{19,3},{4,20},{20... | collective-permute-start | bytes 14155784 | tf_op jit(solution)/shard_map/ppermute | solution.py:887
  31.1 71.7 %collective-permute-start.8 = (bf16[2,512,768]{2,1,0:T(8,128)(2,1)}, bf16[2,512,768]{2,1,0:T(8,128)(2,1)}, u32[]{:S(2)}, u32[]{:S(2)}) collective-permute-start(bf16[2,512,768]{2,1,0:T(8,128)(2,1)} %get-tuple-element.168), channel_id=1, source_target_pairs={{0,16},{16,0},{1,17},{17,1},{2,18},{18,2},{3,19},{19,3},{4,20},{20... | collective-permute-start | bytes 4718600 | tf_op jit(solution)/shard_map/ppermute | solution.py:887
  66.9 35.8 %collective-permute-start.9 = (bf16[2,512,768]{2,1,0:T(8,128)(2,1)}, bf16[2,512,768]{2,1,0:T(8,128)(2,1)}, u32[]{:S(2)}, u32[]{:S(2)}) collective-permute-start(bf16[2,512,768]{2,1,0:T(8,128)(2,1)} %get-tuple-element.169), channel_id=1, source_target_pairs={{0,16},{16,0},{1,17},{17,1},{2,18},{18,2},{3,19},{19,3},{4,20},{20... | collective-permute-start | bytes 4718600 | tf_op jit(solution)/shard_map/ppermute | solution.py:887
  67.2 35.5 %collective-permute-start.10 = (bf16[2,512,1536]{2,1,0:T(8,128)(2,1)}, bf16[2,512,1536]{2,1,0:T(8,128)(2,1)}, u32[]{:S(2)}, u32[]{:S(2)}) collective-permute-start(bf16[2,512,1536]{2,1,0:T(8,128)(2,1)} %get-tuple-element.171), channel_id=1, source_target_pairs={{0,16},{16,0},{1,17},{17,1},{2,18},{18,2},{3,19},{19,3},{4,20},{20... | collective-permute-start | bytes 9437192 | tf_op jit(solution)/shard_map/ppermute | solution.py:887
  102.5 18.9 %collective-permute-start.13 = (bf16[2576,768]{1,0:T(8,128)(2,1)}, bf16[2576,768]{1,0:T(8,128)(2,1)}, u32[]{:S(2)}, u32[]{:S(2)}) collective-permute-start(bf16[2576,768]{1,0:T(8,128)(2,1)} %get-tuple-element.163.own_ref.x_ref.dz_ref), channel_id=1, source_target_pairs={{0,16},{16,0},{1,17},{17,1},{2,18},{18,2},{3,19},{19,3},{4,20},{20... | collective-permute-start | bytes 11870216 | tf_op jit(solution)/shard_map/ppermute | solution.py:887
  118.4 20.5 %collective-permute-start.14 = (bf16[1,8,96,768]{3,2,1,0:T(8,128)(2,1)}, bf16[1,8,96,768]{3,2,1,0:T(8,128)(2,1)}, u32[]{:S(2)}, u32[]{:S(2)}) collective-permute-start(bf16[1,8,96,768]{3,2,1,0:T(8,128)(2,1)} %bitcast.71), channel_id=1, source_target_pairs={{0,1},{1,0},{2,3},{3,2},{4,5},{5,4},{6,7},{7,6},{8,9},{9,8},{10,11... | collective-permute-start | bytes 3538952 | tf_op jit(solution)/shard_map/ppermute | solution.py:687
  121.3 54.9 %collective-permute-start.16 = (bf16[1,8,96,768]{3,2,1,0:T(8,128)(2,1)}, bf16[1,8,96,768]{3,2,1,0:T(8,128)(2,1)}, u32[]{:S(2)}, u32[]{:S(2)}) collective-permute-start(bf16[1,8,96,768]{3,2,1,0:T(8,128)(2,1)} %bitcast.69), channel_id=1, source_target_pairs={{0,1},{1,0},{2,3},{3,2},{4,5},{5,4},{6,7},{7,6},{8,9},{9,8},{10,11... | collective-permute-start | bytes 3538952 | tf_op jit(solution)/shard_map/ppermute | solution.py:687
  136.8 42.5 %collective-permute-start.17 = (bf16[1,8,112,768]{3,2,1,0:T(8,128)(2,1)}, bf16[1,8,112,768]{3,2,1,0:T(8,128)(2,1)}, u32[]{:S(2)}, u32[]{:S(2)}) collective-permute-start(bf16[1,8,112,768]{3,2,1,0:T(8,128)(2,1)} %bitcast.66), channel_id=1, source_target_pairs={{0,1},{1,0},{2,3},{3,2},{4,5},{5,4},{6,7},{7,6},{8,9},{9,8},{10,11... | collective-permute-start | bytes 4128776 | tf_op jit(solution)/shard_map/ppermute | solution.py:687
  138.7 45.2 %collective-permute-start.18 = (bf16[1,8,96,768]{3,2,1,0:T(8,128)(2,1)}, bf16[1,8,96,768]{3,2,1,0:T(8,128)(2,1)}, u32[]{:S(2)}, u32[]{:S(2)}) collective-permute-start(bf16[1,8,96,768]{3,2,1,0:T(8,128)(2,1)} %bitcast.68), channel_id=1, source_target_pairs={{0,1},{1,0},{2,3},{3,2},{4,5},{5,4},{6,7},{7,6},{8,9},{9,8},{10,11... | collective-permute-start | bytes 3538952 | tf_op jit(solution)/shard_map/ppermute | solution.py:687
  141.8 56.0 %collective-permute-start.20 = (bf16[1,4,96,768]{3,2,1,0:T(8,128)(2,1)}, bf16[1,4,96,768]{3,2,1,0:T(8,128)(2,1)}, u32[]{:S(2)}, u32[]{:S(2)}) collective-permute-start(bf16[1,4,96,768]{3,2,1,0:T(8,128)(2,1)} %get-tuple-element.187), channel_id=1, source_target_pairs={{0,2},{1,3},{2,0},{3,1},{4,6},{5,7},{6,4},{7,5},{8,10},{9,11},{10,... | collective-permute-start | bytes 1769480 | tf_op jit(solution)/shard_map/ppermute | solution.py:687
  176.1 29.1 %collective-permute-start.15 = (bf16[2576,768]{1,0:T(8,128)(2,1)}, bf16[2576,768]{1,0:T(8,128)(2,1)}, u32[]{:S(2)}, u32[]{:S(2)}) collective-permute-start(bf16[2576,768]{1,0:T(8,128)(2,1)} %get-tuple-element.192.own_ref), channel_id=1, source_target_pairs={{0,16},{16,0},{1,17},{17,1},{2,18},{18,2},{3,19},{19,3},{4,20},{20... | collective-permute-start | bytes 11870216 | tf_op jit(solution)/shard_map/ppermute | solution.py:887
  179.2 17.5 %collective-permute-start.21 = (bf16[1,4,96,768]{3,2,1,0:T(8,128)(2,1)}, bf16[1,4,96,768]{3,2,1,0:T(8,128)(2,1)}, u32[]{:S(2)}, u32[]{:S(2)}) collective-permute-start(bf16[1,4,96,768]{3,2,1,0:T(8,128)(2,1)} %get-tuple-element.197), channel_id=1, source_target_pairs={{0,2},{1,3},{2,0},{3,1},{4,6},{5,7},{6,4},{7,5},{8,10},{9,11},{10,... | collective-permute-start | bytes 1769480 | tf_op jit(solution)/shard_map/ppermute | solution.py:687
  179.3 9.3 %collective-permute-start.19 = (bf16[2,512,768]{2,1,0:T(8,128)(2,1)}, bf16[2,512,768]{2,1,0:T(8,128)(2,1)}, u32[]{:S(2)}, u32[]{:S(2)}) collective-permute-start(bf16[2,512,768]{2,1,0:T(8,128)(2,1)} %get-tuple-element.204), channel_id=1, source_target_pairs={{0,16},{16,0},{1,17},{17,1},{2,18},{18,2},{3,19},{19,3},{4,20},{20... | collective-permute-start | bytes 4718600 | tf_op jit(solution)/shard_map/ppermute | solution.py:887
  186.8 11.0 %collective-permute-start.22 = (bf16[1,4,96,768]{3,2,1,0:T(8,128)(2,1)}, bf16[1,4,96,768]{3,2,1,0:T(8,128)(2,1)}, u32[]{:S(2)}, u32[]{:S(2)}) collective-permute-start(bf16[1,4,96,768]{3,2,1,0:T(8,128)(2,1)} %get-tuple-element.201), channel_id=1, source_target_pairs={{0,2},{1,3},{2,0},{3,1},{4,6},{5,7},{6,4},{7,5},{8,10},{9,11},{10,... | collective-permute-start | bytes 1769480 | tf_op jit(solution)/shard_map/ppermute | solution.py:687
  188.6 24.7 %collective-permute-start.23 = (bf16[1,4,112,768]{3,2,1,0:T(8,128)(2,1)}, bf16[1,4,112,768]{3,2,1,0:T(8,128)(2,1)}, u32[]{:S(2)}, u32[]{:S(2)}) collective-permute-start(bf16[1,4,112,768]{3,2,1,0:T(8,128)(2,1)} %get-tuple-element.199), channel_id=1, source_target_pairs={{0,2},{1,3},{2,0},{3,1},{4,6},{5,7},{6,4},{7,5},{8,10},{9,11},{10,... | collective-permute-start | bytes 2064392 | tf_op jit(solution)/shard_map/ppermute | solution.py:687
  196.6 19.4 %collective-permute-start.24 = (bf16[1,8,96,768]{3,2,1,0:T(8,128)(2,1)}, bf16[1,8,96,768]{3,2,1,0:T(8,128)(2,1)}, u32[]{:S(2)}, u32[]{:S(2)}) collective-permute-start(bf16[1,8,96,768]{3,2,1,0:T(8,128)(2,1)} %bitcast.70), channel_id=1, source_target_pairs={{0,1},{1,0},{2,3},{3,2},{4,5},{5,4},{6,7},{7,6},{8,9},{9,8},{10,11... | collective-permute-start | bytes 3538952 | tf_op jit(solution)/shard_map/ppermute | solution.py:687
  203.0 23.1 %collective-permute-start.25 = (bf16[3,2,96,768]{3,2,1,0:T(8,128)(2,1)}, bf16[3,2,96,768]{3,2,1,0:T(8,128)(2,1)}, u32[]{:S(2)}, u32[]{:S(2)}) collective-permute-start(bf16[3,2,96,768]{3,2,1,0:T(8,128)(2,1)} %get-tuple-element.212), channel_id=1, source_target_pairs={{0,4},{1,5},{2,6},{3,7},{4,0},{5,1},{6,2},{7,3},{8,12},{9,13},{10,... | collective-permute-start | bytes 2654216 | tf_op jit(solution)/shard_map/ppermute | solution.py:687
  215.7 18.6 %collective-permute-start.26 = (bf16[1,2,112,768]{3,2,1,0:T(8,128)(2,1)}, bf16[1,2,112,768]{3,2,1,0:T(8,128)(2,1)}, u32[]{:S(2)}, u32[]{:S(2)}) collective-permute-start(bf16[1,2,112,768]{3,2,1,0:T(8,128)(2,1)} %get-tuple-element.218), channel_id=1, source_target_pairs={{0,4},{1,5},{2,6},{3,7},{4,0},{5,1},{6,2},{7,3},{8,12},{9,13},{10,... | collective-permute-start | bytes 1032200 | tf_op jit(solution)/shard_map/ppermute | solution.py:687
  218.9 17.3 %collective-permute-start.27 = (bf16[1,4,96,768]{3,2,1,0:T(8,128)(2,1)}, bf16[1,4,96,768]{3,2,1,0:T(8,128)(2,1)}, u32[]{:S(2)}, u32[]{:S(2)}) collective-permute-start(bf16[1,4,96,768]{3,2,1,0:T(8,128)(2,1)} %get-tuple-element.223), channel_id=1, source_target_pairs={{0,2},{1,3},{2,0},{3,1},{4,6},{5,7},{6,4},{7,5},{8,10},{9,11},{10,... | collective-permute-start | bytes 1769480 | tf_op jit(solution)/shard_map/ppermute | solution.py:687
  230.7 40.9 %collective-permute-start.31 = (bf16[3,1,96,768]{3,2,1,0:T(8,128)(2,1)}, bf16[3,1,96,768]{3,2,1,0:T(8,128)(2,1)}, u32[]{:S(2)}, u32[]{:S(2)}) collective-permute-start(bf16[3,1,96,768]{3,2,1,0:T(8,128)(2,1)} %get-tuple-element.225), channel_id=1, source_target_pairs={{0,8},{1,9},{2,10},{3,11},{4,12},{5,13},{6,14},{7,15},{8,0},{9,1},... | collective-permute-start | bytes 1327112 | tf_op jit(solution)/shard_map/ppermute | solution.py:687
  233.3 18.6 %collective-permute-start.28 = (bf16[1,8,112,768]{3,2,1,0:T(8,128)(2,1)}, bf16[1,8,112,768]{3,2,1,0:T(8,128)(2,1)}, u32[]{:S(2)}, u32[]{:S(2)}) collective-permute-start(bf16[1,8,112,768]{3,2,1,0:T(8,128)(2,1)} %bitcast.67), channel_id=1, source_target_pairs={{0,1},{1,0},{2,3},{3,2},{4,5},{5,4},{6,7},{7,6},{8,9},{9,8},{10,11... | collective-permute-start | bytes 4128776 | tf_op jit(solution)/shard_map/ppermute | solution.py:687
  238.7 18.4 %collective-permute-start.29 = (bf16[1,2,96,768]{3,2,1,0:T(8,128)(2,1)}, bf16[1,2,96,768]{3,2,1,0:T(8,128)(2,1)}, u32[]{:S(2)}, u32[]{:S(2)}) collective-permute-start(bf16[1,2,96,768]{3,2,1,0:T(8,128)(2,1)} %get-tuple-element.231), channel_id=1, source_target_pairs={{0,4},{1,5},{2,6},{3,7},{4,0},{5,1},{6,2},{7,3},{8,12},{9,13},{10,... | collective-permute-start | bytes 884744 | tf_op jit(solution)/shard_map/ppermute | solution.py:687
  255.1 11.3 %collective-permute-start.32 = (bf16[1,4,112,768]{3,2,1,0:T(8,128)(2,1)}, bf16[1,4,112,768]{3,2,1,0:T(8,128)(2,1)}, u32[]{:S(2)}, u32[]{:S(2)}) collective-permute-start(bf16[1,4,112,768]{3,2,1,0:T(8,128)(2,1)} %get-tuple-element.233), channel_id=1, source_target_pairs={{0,2},{1,3},{2,0},{3,1},{4,6},{5,7},{6,4},{7,5},{8,10},{9,11},{10,... | collective-permute-start | bytes 2064392 | tf_op jit(solution)/shard_map/ppermute | solution.py:687
  259.0 12.6 %collective-permute-start.30 = (bf16[1,1,96,768]{3,2,1,0:T(8,128)(2,1)}, bf16[1,1,96,768]{3,2,1,0:T(8,128)(2,1)}, u32[]{:S(2)}, u32[]{:S(2)}) collective-permute-start(bf16[1,1,96,768]{3,2,1,0:T(8,128)(2,1)} %get-tuple-element.236), channel_id=1, source_target_pairs={{0,8},{1,9},{2,10},{3,11},{4,12},{5,13},{6,14},{7,15},{8,0},{9,1},... | collective-permute-start | bytes 442376 | tf_op jit(solution)/shard_map/ppermute | solution.py:687
  268.7 13.3 %collective-permute-start.34 = (bf16[1,2,112,768]{3,2,1,0:T(8,128)(2,1)}, bf16[1,2,112,768]{3,2,1,0:T(8,128)(2,1)}, u32[]{:S(2)}, u32[]{:S(2)}) collective-permute-start(bf16[1,2,112,768]{3,2,1,0:T(8,128)(2,1)} %get-tuple-element.240), channel_id=1, source_target_pairs={{0,4},{1,5},{2,6},{3,7},{4,0},{5,1},{6,2},{7,3},{8,12},{9,13},{10,... | collective-permute-start | bytes 1032200 | tf_op jit(solution)/shard_map/ppermute | solution.py:687
  271.6 10.3 %collective-permute-start.33 = (bf16[1,1,112,768]{3,2,1,0:T(8,128)(2,1)}, bf16[1,1,112,768]{3,2,1,0:T(8,128)(2,1)}, u32[]{:S(2)}, u32[]{:S(2)}) collective-permute-start(bf16[1,1,112,768]{3,2,1,0:T(8,128)(2,1)} %get-tuple-element.227), channel_id=1, source_target_pairs={{0,8},{1,9},{2,10},{3,11},{4,12},{5,13},{6,14},{7,15},{8,0},{9,1},... | collective-permute-start | bytes 516104 | tf_op jit(solution)/shard_map/ppermute | solution.py:687
  273.9 10.0 %collective-permute-start.35 = (bf16[1,1,96,768]{3,2,1,0:T(8,128)(2,1)}, bf16[1,1,96,768]{3,2,1,0:T(8,128)(2,1)}, u32[]{:S(2)}, u32[]{:S(2)}) collective-permute-start(bf16[1,1,96,768]{3,2,1,0:T(8,128)(2,1)} %get-tuple-element.286), channel_id=1, source_target_pairs={{0,16},{16,0},{1,17},{17,1},{2,18},{18,2},{3,19},{19,3},{4,20},{20... | collective-permute-start | bytes 442376 | tf_op jit(solution)/shard_map/ppermute | solution.py:887
  283.9 12.1 %collective-permute-start.36 = (bf16[1,1,112,768]{3,2,1,0:T(8,128)(2,1)}, bf16[1,1,112,768]{3,2,1,0:T(8,128)(2,1)}, u32[]{:S(2)}, u32[]{:S(2)}) collective-permute-start(bf16[1,1,112,768]{3,2,1,0:T(8,128)(2,1)} %get-tuple-element.244), channel_id=1, source_target_pairs={{0,8},{1,9},{2,10},{3,11},{4,12},{5,13},{6,14},{7,15},{8,0},{9,1},... | collective-permute-start | bytes 516104 | tf_op jit(solution)/shard_map/ppermute | solution.py:687
  285.7 14.8 %collective-permute-start.37 = (bf16[2,1,96,768]{3,2,1,0:T(8,128)(2,1)}, bf16[2,1,96,768]{3,2,1,0:T(8,128)(2,1)}, u32[]{:S(2)}, u32[]{:S(2)}) collective-permute-start(bf16[2,1,96,768]{3,2,1,0:T(8,128)(2,1)} %bitcast.79), channel_id=1, source_target_pairs={{0,8},{1,9},{2,10},{3,11},{4,12},{5,13},{6,14},{7,15},{8,0},{9,1},... | collective-permute-start | bytes 884744 | tf_op jit(solution)/shard_map/ppermute | solution.py:687
  290.7 14.6 %collective-permute-start.38 = (bf16[1,1,96,768]{3,2,1,0:T(8,128)(2,1)}, bf16[1,1,96,768]{3,2,1,0:T(8,128)(2,1)}, u32[]{:S(2)}, u32[]{:S(2)}) collective-permute-start(bf16[1,1,96,768]{3,2,1,0:T(8,128)(2,1)} %get-tuple-element.283), channel_id=1, source_target_pairs={{0,16},{16,0},{1,17},{17,1},{2,18},{18,2},{3,19},{19,3},{4,20},{20... | collective-permute-start | bytes 442376 | tf_op jit(solution)/shard_map/ppermute | solution.py:887
  298.0 19.2 %collective-permute-start.40 = (bf16[1,1,112,768]{3,2,1,0:T(8,128)(2,1)}, bf16[1,1,112,768]{3,2,1,0:T(8,128)(2,1)}, u32[]{:S(2)}, u32[]{:S(2)}) collective-permute-start(bf16[1,1,112,768]{3,2,1,0:T(8,128)(2,1)} %get-tuple-element.288), channel_id=1, source_target_pairs={{0,16},{16,0},{1,17},{17,1},{2,18},{18,2},{3,19},{19,3},{4,20},{20... | collective-permute-start | bytes 516104 | tf_op jit(solution)/shard_map/ppermute | solution.py:887
  303.3 10.2 %collective-permute-start.39 = (bf16[2,2,96,768]{3,2,1,0:T(8,128)(2,1)}, bf16[2,2,96,768]{3,2,1,0:T(8,128)(2,1)}, u32[]{:S(2)}, u32[]{:S(2)}) collective-permute-start(bf16[2,2,96,768]{3,2,1,0:T(8,128)(2,1)} %merge.10.a_ref), channel_id=1, source_target_pairs={{0,2},{1,3},{2,0},{3,1},{4,6},{5,7},{6,4},{7,5},{8,10},{9,11},{10,... | collective-permute-start | bytes 1769480 | tf_op jit(solution)/shard_map/ppermute | solution.py:687
  307.0 12.8 %collective-permute-start.41 = (bf16[2,1,96,768]{3,2,1,0:T(8,128)(2,1)}, bf16[2,1,96,768]{3,2,1,0:T(8,128)(2,1)}, u32[]{:S(2)}, u32[]{:S(2)}) collective-permute-start(bf16[2,1,96,768]{3,2,1,0:T(8,128)(2,1)} %bitcast.81), channel_id=1, source_target_pairs={{0,8},{1,9},{2,10},{3,11},{4,12},{5,13},{6,14},{7,15},{8,0},{9,1},... | collective-permute-start | bytes 884744 | tf_op jit(solution)/shard_map/ppermute | solution.py:687
  316.7 35.7 %collective-permute-start.44 = (bf16[2,4,96,768]{3,2,1,0:T(8,128)(2,1)}, bf16[2,4,96,768]{3,2,1,0:T(8,128)(2,1)}, u32[]{:S(2)}, u32[]{:S(2)}) collective-permute-start(bf16[2,4,96,768]{3,2,1,0:T(8,128)(2,1)} %merge.12.refs_0_), channel_id=1, source_target_pairs={{0,4},{1,5},{2,6},{3,7},{4,0},{5,1},{6,2},{7,3},{8,12},{9,13},{10,... | collective-permute-start | bytes 3538952 | tf_op jit(solution)/shard_map/ppermute | solution.py:687
  316.7 35.7 %collective-permute-start.45 = (bf16[2,4,96,768]{3,2,1,0:T(8,128)(2,1)}, bf16[2,4,96,768]{3,2,1,0:T(8,128)(2,1)}, u32[]{:S(2)}, u32[]{:S(2)}) collective-permute-start(bf16[2,4,96,768]{3,2,1,0:T(8,128)(2,1)} %merge.12.refs_0_), channel_id=1, source_target_pairs={{0,1},{1,0},{2,3},{3,2},{4,5},{5,4},{6,7},{7,6},{8,9},{9,8},{10,11... | collective-permute-start | bytes 3538952 | tf_op jit(solution)/shard_map/ppermute | solution.py:687
  322.6 29.7 %collective-permute-start.46 = (bf16[2,2,96,768]{3,2,1,0:T(8,128)(2,1)}, bf16[2,2,96,768]{3,2,1,0:T(8,128)(2,1)}, u32[]{:S(2)}, u32[]{:S(2)}) collective-permute-start(bf16[2,2,96,768]{3,2,1,0:T(8,128)(2,1)} %merge.14.a_ref), channel_id=1, source_target_pairs={{0,2},{1,3},{2,0},{3,1},{4,6},{5,7},{6,4},{7,5},{8,10},{9,11},{10,... | collective-permute-start | bytes 1769480 | tf_op jit(solution)/shard_map/ppermute | solution.py:687
  324.4 22.9 %collective-permute-start.43 = (bf16[2,1,112,768]{3,2,1,0:T(8,128)(2,1)}, bf16[2,1,112,768]{3,2,1,0:T(8,128)(2,1)}, u32[]{:S(2)}, u32[]{:S(2)}) collective-permute-start(bf16[2,1,112,768]{3,2,1,0:T(8,128)(2,1)} %bitcast.77), channel_id=1, source_target_pairs={{0,8},{1,9},{2,10},{3,11},{4,12},{5,13},{6,14},{7,15},{8,0},{9,1},... | collective-permute-start | bytes 1032200 | tf_op jit(solution)/shard_map/ppermute | solution.py:687
  333.9 28.4 %collective-permute-start.42 = (bf16[512,768]{1,0:T(8,128)(2,1)}, bf16[512,768]{1,0:T(8,128)(2,1)}, u32[]{:S(2)}, u32[]{:S(2)}) collective-permute-start(bf16[512,768]{1,0:T(8,128)(2,1)} %feed_down.1), channel_id=1, source_target_pairs={{0,16},{1,17},{2,18},{3,19},{4,20},{5,21},{6,22},{7,23},{8,24},{9,... | collective-permute-start | bytes 2359304 | tf_op jit(solution)/shard_map/ppermute | solution.py:977
  350.3 15.0 %collective-permute-start.47 = (bf16[2,2,112,768]{3,2,1,0:T(8,128)(2,1)}, bf16[2,2,112,768]{3,2,1,0:T(8,128)(2,1)}, u32[]{:S(2)}, u32[]{:S(2)}) collective-permute-start(bf16[2,2,112,768]{3,2,1,0:T(8,128)(2,1)} %merge.15.a_ref), channel_id=1, source_target_pairs={{0,2},{1,3},{2,0},{3,1},{4,6},{5,7},{6,4},{7,5},{8,10},{9,11},{10,... | collective-permute-start | bytes 2064392 | tf_op jit(solution)/shard_map/ppermute | solution.py:687
  355.6 30.6 %collective-permute-start.48 = (bf16[2,4,96,768]{3,2,1,0:T(8,128)(2,1)}, bf16[2,4,96,768]{3,2,1,0:T(8,128)(2,1)}, u32[]{:S(2)}, u32[]{:S(2)}) collective-permute-start(bf16[2,4,96,768]{3,2,1,0:T(8,128)(2,1)} %merge.16.refs_0_), channel_id=1, source_target_pairs={{0,4},{1,5},{2,6},{3,7},{4,0},{5,1},{6,2},{7,3},{8,12},{9,13},{10,... | collective-permute-start | bytes 3538952 | tf_op jit(solution)/shard_map/ppermute | solution.py:687
  359.0 27.2 %collective-permute-start.49 = (bf16[2,4,96,768]{3,2,1,0:T(8,128)(2,1)}, bf16[2,4,96,768]{3,2,1,0:T(8,128)(2,1)}, u32[]{:S(2)}, u32[]{:S(2)}) collective-permute-start(bf16[2,4,96,768]{3,2,1,0:T(8,128)(2,1)} %merge.16.refs_0_), channel_id=1, source_target_pairs={{0,1},{1,0},{2,3},{3,2},{4,5},{5,4},{6,7},{7,6},{8,9},{9,8},{10,11... | collective-permute-start | bytes 3538952 | tf_op jit(solution)/shard_map/ppermute | solution.py:687
  359.3 28.9 %collective-permute-start.50 = (bf16[2,4,96,768]{3,2,1,0:T(8,128)(2,1)}, bf16[2,4,96,768]{3,2,1,0:T(8,128)(2,1)}, u32[]{:S(2)}, u32[]{:S(2)}) collective-permute-start(bf16[2,4,96,768]{3,2,1,0:T(8,128)(2,1)} %collective-permute-done.44.refs_1_), channel_id=1, source_target_pairs={{0,1},{1,0},{2,3},{3,2},{4,5},{5,4},{6,7},{7,6},{8,9},{9,8},{10,11... | collective-permute-start | bytes 3538952 | tf_op jit(solution)/shard_map/ppermute | solution.py:687
  368.6 43.9 %collective-permute-start.51 = (bf16[2,4,112,768]{3,2,1,0:T(8,128)(2,1)}, bf16[2,4,112,768]{3,2,1,0:T(8,128)(2,1)}, u32[]{:S(2)}, u32[]{:S(2)}) collective-permute-start(bf16[2,4,112,768]{3,2,1,0:T(8,128)(2,1)} %merge.17.refs_0_), channel_id=1, source_target_pairs={{0,4},{1,5},{2,6},{3,7},{4,0},{5,1},{6,2},{7,3},{8,12},{9,13},{10,... | collective-permute-start | bytes 4128776 | tf_op jit(solution)/shard_map/ppermute | solution.py:687
  373.9 38.6 %collective-permute-start.52 = (bf16[2,4,112,768]{3,2,1,0:T(8,128)(2,1)}, bf16[2,4,112,768]{3,2,1,0:T(8,128)(2,1)}, u32[]{:S(2)}, u32[]{:S(2)}) collective-permute-start(bf16[2,4,112,768]{3,2,1,0:T(8,128)(2,1)} %merge.17.refs_0_), channel_id=1, source_target_pairs={{0,1},{1,0},{2,3},{3,2},{4,5},{5,4},{6,7},{7,6},{8,9},{9,8},{10,11... | collective-permute-start | bytes 4128776 | tf_op jit(solution)/shard_map/ppermute | solution.py:687
  386.2 29.3 %collective-permute-start.53 = (bf16[2,4,96,768]{3,2,1,0:T(8,128)(2,1)}, bf16[2,4,96,768]{3,2,1,0:T(8,128)(2,1)}, u32[]{:S(2)}, u32[]{:S(2)}) collective-permute-start(bf16[2,4,96,768]{3,2,1,0:T(8,128)(2,1)} %collective-permute-done.48.refs_1_), channel_id=1, source_target_pairs={{0,1},{1,0},{2,3},{3,2},{4,5},{5,4},{6,7},{7,6},{8,9},{9,8},{10,11... | collective-permute-start | bytes 3538952 | tf_op jit(solution)/shard_map/ppermute | solution.py:687
  412.5 18.9 %collective-permute-start.54 = (bf16[2,4,112,768]{3,2,1,0:T(8,128)(2,1)}, bf16[2,4,112,768]{3,2,1,0:T(8,128)(2,1)}, u32[]{:S(2)}, u32[]{:S(2)}) collective-permute-start(bf16[2,4,112,768]{3,2,1,0:T(8,128)(2,1)} %collective-permute-done.51.refs_1_), channel_id=1, source_target_pairs={{0,1},{1,0},{2,3},{3,2},{4,5},{5,4},{6,7},{7,6},{8,9},{9,8},{10,11... | collective-permute-start | bytes 4128776 | tf_op jit(solution)/shard_map/ppermute | solution.py:687
  (27 other events, 163.1 us)

commit v4 on v3

--- a/solution.py
+++ b/solution.py
@@ -76,6 +76,16 @@
         - jnp.mean(grad_t, axis=-1, keepdims=True)
         - n * jnp.mean(grad_t * n, axis=-1, keepdims=True)
     )
+
+
+def first_keys(sec_ref, lengths_ref, shape, dim):
+    at = lax.broadcasted_iota(jnp.int32, shape, dim)
+    begin = jnp.zeros(shape, jnp.int32)
+    cut = 0
+    for i in range(lengths_ref.shape[1]):
+        cut = cut + lengths_ref[sec_ref[0], i]
+        begin = jnp.where(at >= cut, cut, begin)
+    return begin
 
 
 def row_sum(x):
@@ -146,7 +156,7 @@
         put(h_s.at[:, theirs], sent_out.at[0, :, half:])
         at_row = lax.broadcasted_iota(jnp.int32, (rows, rows), 0)
         at_col = lax.broadcasted_iota(jnp.int32, (rows, rows), 1)
-        bias_s[...] = jnp.where((at_col <= at_row) & (at_col >= start_ref[...]), 0.0, neg_fill)
+        bias_s[...] = jnp.where((at_col <= at_row) & (at_col >= first_keys(sec_ref, start_ref, (rows, 1), 0)), 0.0, neg_fill)
         wait_fetch(qw_o, wq, in_sem.at[0])
         q_s[...] = (mm(h_s[...], wq[...]) + vec_ref[QBIAS:QBIAS + 1, :]).astype(bf16)
         put(q_s, q_out)
@@ -178,14 +188,22 @@
     return fetch, run, copies
 
 
-def attn_forward_kernel(layer, sec_ref, x_ref, r_ref, start_ref, vec_ref, *refs):
+def attn_forward_kernel(layer, sec_ref, start_ref, vec_ref, own_ref, arrived_ref, *refs):
+    x_out, x_s, x_sem = refs[18], refs[33], refs[34]
+    rows = x_s.shape[0]
+    slot = pl.ds(pl.multiple_of(sec_ref[0] * rows, rows), rows)
+    start_fetch(sec_ref[0] == 0, own_ref.at[slot, :], arrived_ref.at[slot, :], x_s, x_sem.at[0])
     fetch, run, copies = attn_forward_steps(
-        layer, sec_ref, x_ref, r_ref, start_ref, vec_ref, (refs[:9], refs[18:22]), refs[9:18], refs[22:32],
-        refs[32], refs[33])
+        layer, sec_ref, x_s, None, start_ref, vec_ref, (refs[:9], refs[19:23]), refs[9:18], refs[23:33],
+        refs[35], refs[36])
     fetch()
+    wait_fetch(own_ref.at[slot, :], x_s, x_sem.at[0])
+    keep = pltpu.make_async_copy(x_s, x_out, x_sem.at[1])
+    keep.start()
     run()
     for copy in copies:
         copy.wait()
+    keep.wait()
 
 
 def attn_forward_shapes(rows, d):
@@ -200,18 +218,19 @@
     return outs, scratch
 
 
-def attn_forward(layer, sec, x, r, start, vec, w):
-    outs, scratch = attn_forward_shapes(*x.shape)
+def attn_forward(layer, sec, start, vec, own, arrived, w):
+    rows, d = own.shape[0] // 2, own.shape[1]
+    outs, scratch = attn_forward_shapes(rows, d)
     return pl.pallas_call(
         functools.partial(attn_forward_kernel, layer),
-        out_shape=outs,
-        in_specs=[SMEM, VMEM, VMEM, VMEM, VMEM] + [ANY] * 9,
-        out_specs=[ANY] * 9,
-        scratch_shapes=scratch,
+        out_shape=outs + [sds((rows, d), bf16)],
+        in_specs=[SMEM, SMEM, VMEM] + [ANY] * 11,
+        out_specs=[ANY] * 10,
+        scratch_shapes=scratch[:-2] + [pltpu.VMEM((rows, d), bf16), pltpu.SemaphoreType.DMA((2,))] + scratch[-2:],
         compiler_params=params(),
         cost_estimate=cost(80),
         name="attn_forward",
-    )(sec, x, r, start, vec, w["qo"], w["qr"], w["ko"], w["kr"], w["vo"], w["vr"], w["f"], w["oo"], w["or"])
+    )(sec, start, vec, own, arrived, w["qo"], w["qr"], w["ko"], w["kr"], w["vo"], w["vr"], w["f"], w["oo"], w["or"])
 
 
 def gelu(u):
@@ -289,7 +308,7 @@
     return pl.pallas_call(
         functools.partial(middle_kernel, blk),
         out_shape=[wide, wide, sds((rows, d), bf16), wide, wide, sds((2, rows, ff // 2), bf16)] + outs,
-        in_specs=[SMEM] + [VMEM] * 6 + [ANY] * 13,
+        in_specs=[SMEM] + [VMEM] * 3 + [SMEM] + [VMEM] * 2 + [ANY] * 13,
         out_specs=[ANY] * 15,
         scratch_shapes=[pltpu.VMEM((n, d, blk), bf16), pltpu.VMEM((n, blk, d), bf16), pltpu.VMEM((n, d, blk), bf16),
                         pltpu.VMEM((2, n, rows, blk), bf16), pltpu.VMEM((2, n, rows, blk), bf16),
@@ -350,7 +369,7 @@
         out_specs=pl.BlockSpec((rows, d), lambda j: (0, 0)),
         scratch_shapes=[pltpu.VMEM((n, blk, d), bf16), pltpu.VMEM((rows, d), f32), pltpu.SemaphoreType.DMA((n,))],
         compiler_params=params(),
-        cost_estimate=cost(80),
+        cost_estimate=cost(2),
         name="feed_down",
     )(sec, a, m, vec, w["do"], w["dr"])
 
@@ -427,7 +446,7 @@
     low_ref[...] = dm_s[...].astype(bf16)
     at_key = lax.broadcasted_iota(jnp.int32, (rows, rows), 0)
     at_query = lax.broadcasted_iota(jnp.int32, (rows, rows), 1)
-    bias_s[...] = jnp.where((at_key <= at_query) & (at_key >= start_ref[...]), 0.0, neg_fill)
+    bias_s[...] = jnp.where((at_key <= at_query) & (at_key >= first_keys(sec_ref, start_ref, (1, rows), 1)), 0.0, neg_fill)
     wait_fetch(ow_o, wo, sem.at[4])
     do = mm(low_ref[...], wo[...], NT).astype(bf16)
     do_s[...] = do
@@ -531,7 +550,7 @@
         grid=(1,),
         out_shape=[sds((rows, ff), bf16), sds((n // 2, rows, blk), bf16), sds(bundle, bf16), sds((rows, half), f32),
                    sds((VEC_ROWS, d), f32)],
-        in_specs=[SMEM, pl.BlockSpec((rows, d), lambda i: (dz_at, 0))] + [VMEM] * 5 + [ANY] * 19,
+        in_specs=[SMEM, pl.BlockSpec((rows, d), lambda i: (dz_at, 0)), VMEM, VMEM, SMEM, VMEM, VMEM] + [ANY] * 19,
         out_specs=[ANY] * 3 + [VMEM] * 2,
         scratch_shapes=[pltpu.VMEM((n, d, blk), bf16), pltpu.VMEM((n, blk, d), bf16), wbuf, wbuf, wbuf, wbuf,
                         blocks, act, act, act, act, act, blocks, pltpu.VMEM((2, rows, blk), f32), wide, wide,
@@ -816,7 +835,7 @@
                     copy.start()
                     copies.append(copy)
         if finish is not None:
-            finish(s_ref, chunks, wide, outs)
+            finish(s_ref, chunks, wide, outs, [out_sem.at[len(copies) + i] for i in range(2)])
         for copy in copies:
             copy.wait()
 
@@ -850,6 +869,31 @@
 
     def tie(self, array):
         return after(array, *self.last) if self.last else array
+
+
+def pack_kernel(gain1, bias1, qbias, first_bias, vbias, obias, gain2, bias2, dbias, ubias, out_ref):
+    d = out_ref.shape[1]
+    half = first_bias.shape[1]
+    out_ref[...] = jnp.zeros(out_ref.shape, f32)
+    for row, ref in ((GAIN1, gain1), (BIAS1, bias1), (QBIAS, qbias), (OBIAS, obias), (GAIN2, gain2), (BIAS2, bias2),
+                     (DBIAS, dbias)):
+        out_ref[row:row + 1, :] = ref[...]
+    out_ref[VBIAS:VBIAS + 1, :half] = first_bias[...]
+    out_ref[VBIAS:VBIAS + 1, half:] = vbias[...]
+    for i in range(ubias.shape[1] // d):
+        out_ref[UBIAS + i:UBIAS + i + 1, :] = ubias[:, i * d:(i + 1) * d]
+
+
+def pack_vectors(*vectors):
+    return pl.pallas_call(
+        pack_kernel,
+        out_shape=sds((VEC_ROWS, vectors[0].shape[1]), f32),
+        in_specs=[VMEM] * len(vectors),
+        out_specs=VMEM,
+        compiler_params=params(),
+        cost_estimate=cost(2),
+        name="pack_vectors",
+    )(*vectors)
 
 
 def local(
@@ -886,21 +930,10 @@
     def swap(array):
         return lax.ppermute(array, "section", SWAP)
 
-    def row(vector):
-        return jnp.reshape(vector, (-1, d))
-
-    vec_own = jnp.concatenate([
-        norm_one_gain, norm_one_bias, query_bias,
-        jnp.concatenate([first_value_bias[None], value_bias], axis=1),
-        out_bias, norm_two_gain, norm_two_bias, down_bias, row(up_bias)], axis=0)
-    vec_own = jnp.pad(vec_own, ((0, VEC_ROWS - vec_own.shape[0]), (0, 0)))
-    top, bottom = boundary[0, :rows], boundary[0, rows:]
-    arrived_rows = swap(jnp.where(on_first, bottom, top))
-    kept_rows = jnp.where(on_first, top, bottom)
-    x0 = jnp.where(on_first, kept_rows, arrived_rows)
-    dz1 = jnp.where(on_first, arrived_rows, kept_rows)
-    dz1_moved = lax.ppermute(bottom, "section", [(1, 0)])
-    dz1_got = jnp.where(on_first, dz1_moved, top)
+    vec_own = pack_vectors(norm_one_gain, norm_one_bias, query_bias, first_value_bias[None], value_bias, out_bias,
+                           norm_two_gain, norm_two_bias, down_bias, up_bias)
+    own_rows = boundary[0]
+    arrived_rows = swap(own_rows)
     vec_arrived = swap(vec_own)
     vec = (jnp.where(on_first, vec_own, vec_arrived), jnp.where(on_first, vec_arrived, vec_own))
     w = {"qo": query_weight[0], "ko": key_weight[0], "vo": value_weight[0], "oo": out_weight[0],
@@ -910,12 +943,6 @@
     w["ur"] = swap(after(w["uo"], w["qr"]))
     w["dr"] = swap(after(w["do"], w["kr"]))
 
-    own_lengths = jnp.where(on_first, lengths[0], lengths[1])
-    cuts = jnp.cumsum(own_lengths)
-    at = jnp.arange(rows, dtype=jnp.int32)
-    start = jnp.max(jnp.where(at[:, None] >= cuts[None, :], cuts[None, :], 0), axis=1).astype(jnp.int32)
-    start_col, start_row = start[:, None], start[None, :]
-
     chunk_rows = ff // (2 * dp)
     extra = 16
     first_bits, second_bits = bit_orders(dp)
@@ -925,13 +952,16 @@
     scalars = jnp.stack([sec[0], bit[0], bit[2]])
     order = Order()
 
-    h, q, k, v, o, m, e, lse, sent = attn_forward(0, sec, x0, x0, start_col, vec[0], w)
+    h, q, k, v, o, m, e, lse, sent, x0 = attn_forward(0, sec, lengths, vec[0], own_rows, arrived_rows, w)
     kept = [dict(x=x0, h=h, q=q, k=k, v=v, o=o, m=m, e=e, lse=lse, sent_got=swap(sent))]
-    u0, a0, x1, u1, a1, a_sent, h, q, k, v, o, m, e, lse, sent = middle(sec, e, m, v, start_col, vec, w)
+    u0, a0, x1, u1, a1, a_sent, h, q, k, v, o, m, e, lse, sent = middle(sec, e, m, v, lengths, vec, w)
     a_got = swap(a_sent)
     kept[0].update(u=u0, a=a0, a_got=(a_got, 0))
     kept.append(dict(x=x1, h=h, q=q, k=k, v=v, o=o, m=m, e=e, lse=lse, u=u1, a=a1, sent_got=swap(sent), a_got=(a_got, 1)))
     order.mark(x1)
+    own_late = order.tie(own_rows)
+    dz1 = jnp.where(on_first, arrived_rows[:rows], own_late[rows:])
+    dz1_got = jnp.where(on_first, arrived_rows[rows:], own_late[:rows])
     order.mark(x1)
 
     def cut(level, parts):
@@ -961,7 +991,7 @@
 
     def back_step(layer, dz, dz_at, dr2):
         du, sent, bundle, dr2, small = layer_backward(
-            layer, sec, dz, dz_at, dict(kept[layer], u=order.tie(kept[layer]["u"])), start_row, vec[layer], dr2, w)
+            layer, sec, dz, dz_at, dict(kept[layer], u=order.tie(kept[layer]["u"])), lengths, vec[layer], dr2, w)
         order.mark(bundle)
         return bundle, swap(bundle), dr2, small, du, swap(sent)
 
@@ -1077,9 +1107,18 @@
         at = pl.ds((2 * part + t % 2) * block, block)
         if t // 2 < 3:
             return [(all_columns, outs[t // 2].at[at, :])]
-        return [(pl.ds(half, half), outs[3].at[at, :]), (pl.ds(0, half), outs[4].at[at, :])]
-
-    def vectors(s_ref, chunks, wide, outs):
+        return [(pl.ds(half, half), outs[3].at[at, :])]
+
+    def vectors(s_ref, chunks, wide, outs, sems):
+        for part in range(2):
+            @pl.when(s_ref[0] == part)
+            def _():
+                moves = [pltpu.make_async_copy(wide.at[8 * part + 6 + i, :, pl.ds(0, half)],
+                                               outs[4].at[pl.ds(i * block, block), :], sems[i]) for i in range(2)]
+                for move in moves:
+                    move.start()
+                for move in moves:
+                    move.wait()
         lines = outs[5]
         for part in range(2):
             for t in range(8):
@@ -1097,7 +1136,7 @@
     (out_grad, query_grad, key_grad, value_grad, first_full, lines, gain1_grad, bias1_grad, qbias_grad, obias_grad,
      gain2_grad, bias2_grad, dbias_grad, vbias_grad, ubias_grad) = assemble(
         scalars, (order.tie(cur_a), far_a, side_a, last_a), chunk_rows,
-        [(d, d)] * 3 + [(d, half)] * 2 + [(VEC_ROWS, d)] + [(1, d)] * 7 + [(1, half), (1, ff)],
+        [(d, d)] * 3 + [(d, half), (d // 2, half)] + [(VEC_ROWS, d)] + [(1, d)] * 7 + [(1, half), (1, ff)],
         square_targets, "assemble_attn", vectors, [VMEM] * 10)
 
     spot_half = lambda t: jnp.where(on_first, t[:t.shape[0] // 2], t[t.shape[0] // 2:])
@@ -1112,7 +1151,7 @@
         key_grad[None],
         value_grad[None],
         vbias_grad,
-        spot_half(first_full),
+        first_full,
         spot_half(lines[VBIAS, :half]),
         out_grad[None],
         obias_grad,

time: 449 us -> 447 us (level)
  starting transfers between devices: 58.9 us -> 53.3 us
  waiting for transfers between devices: 100 us -> 105 us
  transfers between devices with their start and end apart: 55 -> 54, of which waited for: 17 -> 17; matrix products, arithmetic and copies ran while one was open for 4% -> 4% of each run, Pallas kernels for 56% -> 57%
where the time goes in v4:
time: 447 us; the launch traced here: 441 us
  Pallas kernels  261 us (58%)
  waiting for transfers between devices  105 us (23%)
  starting transfers between devices  53.3 us (12%)
  other arithmetic  15.1 us (3%)
  local copies, waits for them, and re-layouts  5.45 us (1%)
    ppermute x35, waiting for transfers between devices, exchange(): return lax.ppermute(array, AXES, pairs)  104 us
    pallas_call x2, Pallas kernels, layer_backward(): pl.pallas_call(functools.partial(layer_backward_kernel, layer, blk), grid...  65.9 us
    ppermute x35, starting transfers between devices, exchange(): return lax.ppermute(array, AXES, pairs)  45.7 us
    pallas_call x14, Pallas kernels, add_split(): pl.pallas_call(kernel, grid_spec=pltpu.PrefetchScalarGridSpec(num_scalar_...  41.3 us
    pallas_call x1, Pallas kernels, middle(): pl.pallas_call(functools.partial(middle_kernel, blk), out_shape=[wide, wi...  35.7 us
    pallas_call x4, Pallas kernels, quarters(): pl.pallas_call(kernel, grid_spec=pltpu.PrefetchScalarGridSpec(num_scalar_...  30.4 us
    pallas_call x9, Pallas kernels, merge(): pl.pallas_call(kernel, grid_spec=pltpu.PrefetchScalarGridSpec(num_scalar_...  23.5 us
    pallas_call x3, Pallas kernels, assemble(): pl.pallas_call(kernel, out_shape=[sds(o, f32) for o in out_shapes], in_sp...  21.4 us
  transfers between devices with their start and end apart: 54, of which 17 were waited for; matrix products, arithmetic and copies ran while one was open for 4% of the time, Pallas kernels for 57%

profile of v4, /device:TPU:0, one launch (start us, length us, event | category | flops | bytes accessed | tf_op | source)
XLA Modules:
  0.0 440.8 jit_solution(17874022944957328674)
XLA Ops:
  10.5 17.0 %attn_forward.1 = (bf16[512,768]{1,0:T(8,128)(2,1)}, bf16[512,768]{1,0:T(8,128)(2,1)}, bf16[512,768]{1,0:T(8,128)(2,1)}, bf16[512,768]{1,0:T(8,128)(2,1)}, bf16[...) custom-call(s32[1]{0:T(128)} %bitcast.sec_ref.s_ref, ...), custom_call_target="tpu_custom_call" | custom-call | flops 92000002048 | bytes 1 | tf_op jit(solution)/shard_map/attn_forward/pallas_call | solution.py:224
  28.0 35.7 %middle.1 = (bf16[512,3072]{1,0:T(8,128)(2,1)}, bf16[512,3072]{1,0:T(8,128)(2,1)}, bf16[512,768]{1,0:T(8,128)(2,1)}, bf16[512,3072]{1,0:T(8,128)(2,1)}, bf16[512...) custom-call(s32[1]{0:T(128)} %bitcast.sec_ref.s_ref, ...), custom_call_target="tpu_custom_call" | custom-call | flops 92000002048 | bytes 1 | tf_op jit(solution)/shard_map/middle/pallas_call | solution.py:308
  64.3 3.2 slice_select_fusion
  68.4 33.6 %layer_backward.2 = (bf16[512,3072]{1,0:T(8,128)(2,1)}, bf16[2,512,768]{2,1,0:T(8,128)(2,1)}, bf16[2576,768]{1,0:T(8,128)(2,1)}, f32[512,384]{1,0:T(8,128)}, f32[16,768]{1,0:T(8,128)}) custom-call(s32[1]{0:T(128)} %bitcast.sec_ref.s_ref, bf16[512,768]{1,0:T(8,128)(2,1)} %get-tuple-element.285.dz_ref.x_ref, f32[512,768]{1,0:T(8,128)} %get-tuple-element.259.m_ref, ...), custom_call_target="tpu_custom_call" | custom-call | flops 92000002048 | bytes 1 | tf_op jit(solution)/shard_map/layer_backward/pallas_call | solution.py:548
  102.6 7.3 %down_gradient.2 = (bf16[8,96,768]{2,1,0:T(8,128)(2,1)}, bf16[8,96,768]{2,1,0:T(8,128)(2,1)}) custom-call(s32[3]{0:T(128)} %pad_add_fusion.s_ref, bf16[512,3072]{1,0:T(8,128)(2,1)} %get-tuple-element.173.a_ref, bf16[2,512,1536]{2,1,0:T(8,128)(2,1)} %collective-permute-done.10.b_ref, bf16[512,768]{1,0:T(8,128)(2,1)} %get-tuple-element.285.dz_ref.x_ref, ...), custom_call_target="tpu_custom_call" | custom-call | flops 92000002048 | bytes 1 | tf_op jit(solution)/shard_map/down_gradient/pallas_call | solution.py:579
  110.0 7.9 %up_gradient.2 = (bf16[8,96,768]{2,1,0:T(8,128)(2,1)}, bf16[8,96,768]{2,1,0:T(8,128)(2,1)}) custom-call(s32[3]{0:T(128)} %pad_add_fusion.s_ref, bf16[512,768]{1,0:T(8,128)(2,1)} %get-tuple-element.179.e_ref, bf16[2,512,768]{2,1,0:T(8,128)(2,1)} %collective-permute-done.9.f_ref.l_ref, bf16[512,3072]{1,0:T(8,128)(2,1)} %get-tuple-element.180.du_ref, ...), custom_call_target="tpu_custom_call" | custom-call | flops 92000002048 | bytes 1 | tf_op jit(solution)/shard_map/up_gradient/pallas_call | solution.py:579
  117.8 2.6 collective-permute-start.13
  120.5 8.1 %attn_gradient.2 = (bf16[8,112,768]{2,1,0:T(8,128)(2,1)}, bf16[8,112,768]{2,1,0:T(8,128)(2,1)}) custom-call(s32[3]{0:T(128)} %pad_add_fusion.s_ref, bf16[512,768]{1,0:T(8,128)(2,1)} %get-tuple-element.183.o_in.o_ref, bf16[512,768]{1,0:T(8,128)(2,1)} %get-tuple-element.184.h_ref, bf16[2,512,768]{2,1,0:T(8,128)(2,1)} %collective-permute-done.9.f_ref.l_ref, ...), custom_call_target="tpu_custom_call" | custom-call | flops 92000002048 | bytes 1 | tf_op jit(solution)/shard_map/attn_gradient/pallas_call | solution.py:675
  128.7 7.3 %down_gradient.3 = (bf16[8,96,768]{2,1,0:T(8,128)(2,1)}, bf16[8,96,768]{2,1,0:T(8,128)(2,1)}) custom-call(s32[3]{0:T(128)} %pad_add_fusion.s_ref, bf16[512,3072]{1,0:T(8,128)(2,1)} %get-tuple-element.187.a_ref, bf16[2,512,1536]{2,1,0:T(8,128)(2,1)} %collective-permute-done.10.b_ref, bf16[2576,768]{1,0:T(8,128)(2,1)} %get-tuple-element.166.own_ref.x_ref.dz_ref, ...), custom_call_target="tpu_custom_call" | custom-call | flops 92000002048 | bytes 1 | tf_op jit(solution)/shard_map/down_gradient/pallas_call | solution.py:579
  138.0 3.3 add_split.14
  143.4 32.3 %layer_backward.3 = (bf16[512,3072]{1,0:T(8,128)(2,1)}, bf16[2,512,768]{2,1,0:T(8,128)(2,1)}, bf16[2576,768]{1,0:T(8,128)(2,1)}, f32[512,384]{1,0:T(8,128)}, f32[16,768]{1,0:T(8,128)}) custom-call(s32[1]{0:T(128)} %bitcast.sec_ref.s_ref, bf16[2576,768]{1,0:T(8,128)(2,1)} %get-tuple-element.166.own_ref.x_ref.dz_ref, f32[512,768]{1,0:T(8,128)} %get-tuple-element.152.m_ref, ...), custom_call_target="tpu_custom_call" | custom-call | flops 92000002048 | bytes 1 | tf_op jit(solution)/shard_map/layer_backward/pallas_call | solution.py:548
  175.8 2.9 add_split.15
  180.3 3.2 add_split.16
  183.5 2.9 add_split.17
  188.4 7.8 %up_gradient.3 = (bf16[8,96,768]{2,1,0:T(8,128)(2,1)}, bf16[8,96,768]{2,1,0:T(8,128)(2,1)}) custom-call(s32[3]{0:T(128)} %pad_add_fusion.s_ref, bf16[512,768]{1,0:T(8,128)(2,1)} %get-tuple-element.206.e_ref, bf16[2,512,768]{2,1,0:T(8,128)(2,1)} %collective-permute-done.8.f_ref.l_ref, bf16[512,3072]{1,0:T(8,128)(2,1)} %get-tuple-element.207.du_ref, ...), custom_call_target="tpu_custom_call" | custom-call | flops 92000002048 | bytes 1 | tf_op jit(solution)/shard_map/up_gradient/pallas_call | solution.py:579
  197.0 5.3 %add_split.18 = (bf16[3,2,96,768]{3,2,1,0:T(8,128)(2,1)}, bf16[3,2,96,768]{3,2,1,0:T(8,128)(2,1)}) custom-call(s32[1]{0:T(128)} %bitcast.10.s_ref, bf16[1,4,96,768]{3,2,1,0:T(8,128)(2,1)} %get-tuple-element.213.refs_0_, bf16[1,4,96,768]{3,2,1,0:T(8,128)(2,1)} %collective-permute-done.19.refs_1_, bf16[1,4,96,768]{3,2,1,0:T(8,128)(2,1)} %get-tuple-element.214.refs_2_, ...), custom_call_target="tpu_custom_call" | custom-call | flops 9200000000 | bytes 1 | tf_op jit(solution)/shard_map/add_split/pallas_call | solution.py:757
  204.5 8.1 %attn_gradient.3 = (bf16[8,112,768]{2,1,0:T(8,128)(2,1)}, bf16[8,112,768]{2,1,0:T(8,128)(2,1)}) custom-call(s32[3]{0:T(128)} %pad_add_fusion.s_ref, bf16[512,768]{1,0:T(8,128)(2,1)} %get-tuple-element.217.o_in.o_ref, bf16[512,768]{1,0:T(8,128)(2,1)} %get-tuple-element.218.h_ref, bf16[2,512,768]{2,1,0:T(8,128)(2,1)} %collective-permute-done.8.f_ref.l_ref, ...), custom_call_target="tpu_custom_call" | custom-call | flops 92000002048 | bytes 1 | tf_op jit(solution)/shard_map/attn_gradient/pallas_call | solution.py:675
  212.5 2.4 add_split.19
  215.7 2.9 add_split.20
  219.5 5.8 %collective-permute-done.24.refs_1_ = bf16[3,2,96,768]{3,2,1,0:T(8,128)(2,1)} collective-permute-done((bf16[3,2,96,768]{3,2,1,0:T(8,128)(2,1)}, bf16[3,2,96,768]{3,2,1,0:T(8,128)(2,1)}, u32[]{:S(2)}, u32[]{:S(2)}) %collective-permute-start.24) | collective-permute-done | bytes 884768 | tf_op jit(solution)/shard_map/ppermute | solution.py:706
  225.3 4.6 %add_split.21 = (bf16[3,1,96,768]{3,2,1,0:T(8,128)(2,1)}, bf16[3,1,96,768]{3,2,1,0:T(8,128)(2,1)}) custom-call(s32[1]{0:T(128)} %bitcast.15.s_ref, bf16[3,2,96,768]{3,2,1,0:T(8,128)(2,1)} %get-tuple-element.228.refs_0_, bf16[3,2,96,768]{3,2,1,0:T(8,128)(2,1)} %collective-permute-done.24.refs_1_), custom_call_target="tpu_custom_call" | custom-call | flops 9200000000 | bytes 1 | tf_op jit(solution)/shard_map/add_split/pallas_call | solution.py:757
  229.9 2.6 collective-permute-start.30
  235.9 2.4 add_split.23
  240.3 10.8 %collective-permute-done.27.refs_1_ = bf16[1,8,112,768]{3,2,1,0:T(8,128)(2,1)} collective-permute-done((bf16[1,8,112,768]{3,2,1,0:T(8,128)(2,1)}, bf16[1,8,112,768]{3,2,1,0:T(8,128)(2,1)}, u32[]{:S(2)}, u32[]{:S(2)}) %collective-permute-start.27) | collective-permute-done | bytes 1376288 | tf_op jit(solution)/shard_map/ppermute | solution.py:706
  251.2 3.1 add_split.24
  258.1 7.5 %collective-permute-done.31.refs_1_ = bf16[1,4,112,768]{3,2,1,0:T(8,128)(2,1)} collective-permute-done((bf16[1,4,112,768]{3,2,1,0:T(8,128)(2,1)}, bf16[1,4,112,768]{3,2,1,0:T(8,128)(2,1)}, u32[]{:S(2)}, u32[]{:S(2)}) %collective-permute-start.31) | collective-permute-done | bytes 688160 | tf_op jit(solution)/shard_map/ppermute | solution.py:706
  273.1 7.7 %collective-permute-done.32 = bf16[1,1,112,768]{3,2,1,0:T(8,128)(2,1)} collective-permute-done((bf16[1,1,112,768]{3,2,1,0:T(8,128)(2,1)}, bf16[1,1,112,768]{3,2,1,0:T(8,128)(2,1)}, u32[]{:S(2)}, u32[]{:S(2)}) %collective-permute-start.32) | collective-permute-done | bytes 172064 | tf_op jit(solution)/shard_map/ppermute | solution.py:706
  284.5 3.0 collective-permute-start.36
  289.5 5.3 %collective-permute-done.35 = bf16[1,1,112,768]{3,2,1,0:T(8,128)(2,1)} collective-permute-done((bf16[1,1,112,768]{3,2,1,0:T(8,128)(2,1)}, bf16[1,1,112,768]{3,2,1,0:T(8,128)(2,1)}, u32[]{:S(2)}, u32[]{:S(2)}) %collective-permute-start.35) | collective-permute-done | bytes 172064 | tf_op jit(solution)/shard_map/ppermute | solution.py:706
  296.8 2.4 collective-permute-done.36.b_ref
  299.2 2.8 merge.10.a_ref
  305.3 7.0 %collective-permute-done.38.b_ref = bf16[2,2,96,768]{3,2,1,0:T(8,128)(2,1)} collective-permute-done((bf16[2,2,96,768]{3,2,1,0:T(8,128)(2,1)}, bf16[2,2,96,768]{3,2,1,0:T(8,128)(2,1)}, u32[]{:S(2)}, u32[]{:S(2)}) %collective-permute-start.38) | collective-permute-done | bytes 589856 | tf_op jit(solution)/shard_map/ppermute | solution.py:706
  312.3 3.2 merge.12.refs_0_
  318.6 2.7 collective-permute-start.42
  321.3 2.8 merge.14.a_ref
  324.7 7.9 %feed_down.1 = bf16[512,768]{1,0:T(8,128)(2,1)} custom-call(s32[1]{0:T(128)} %bitcast.sec_ref.s_ref, bf16[512,3072]{1,0:T(8,128)(2,1)} %get-tuple-element.173.a_ref, f32[512,768]{1,0:T(8,128)} %get-tuple-element.259.m_ref, f32[16,768]{1,0:T(8,128)} %get-tuple-element.292.vec1_ref.vec_ref, bf16[3072,768]{1,0:T(8,128)(2,1)} %bitcast.44, ...), custom_call_target="tpu_custom_call" | custom-call | flops 2300000000 | bytes 1 | tf_op jit(solution)/shard_map/feed_down/pallas_call | solution.py:364
  334.8 11.4 %collective-permute-done.42.b_ref = bf16[2,1,112,768]{3,2,1,0:T(8,128)(2,1)} collective-permute-done((bf16[2,1,112,768]{3,2,1,0:T(8,128)(2,1)}, bf16[2,1,112,768]{3,2,1,0:T(8,128)(2,1)}, u32[]{:S(2)}, u32[]{:S(2)}) %collective-permute-start.42) | collective-permute-done | bytes 344096 | tf_op jit(solution)/shard_map/ppermute | solution.py:706
  346.2 2.9 merge.15.a_ref
  352.0 3.2 merge.16.refs_0_
  360.5 2.7 maximum_select_fusion
  363.3 3.4 merge.17.refs_0_
  366.6 4.6 %collective-permute-start.50 = (bf16[2,4,112,768]{3,2,1,0:T(8,128)(2,1)}, bf16[2,4,112,768]{3,2,1,0:T(8,128)(2,1)}, u32[]{:S(2)}, u32[]{:S(2)}) collective-permute-start(bf16[2,4,112,768]{3,2,1,0:T(8,128)(2,1)} %merge.17.refs_0_), channel_id=1, source_target_pairs={{0,4},{1,5},{2,6},{3,7},{4,0},{5,1},{6,2},{7,3},{8,12},{9,13},{10,... | collective-permute-start | bytes 4128776 | tf_op jit(solution)/shard_map/ppermute | solution.py:706
  373.1 11.3 %collective-permute-done.47.refs_1_ = bf16[2,4,96,768]{3,2,1,0:T(8,128)(2,1)} collective-permute-done((bf16[2,4,96,768]{3,2,1,0:T(8,128)(2,1)}, bf16[2,4,96,768]{3,2,1,0:T(8,128)(2,1)}, u32[]{:S(2)}, u32[]{:S(2)}) %collective-permute-start.47) | collective-permute-done | bytes 1179680 | tf_op jit(solution)/shard_map/ppermute | solution.py:706
  386.4 6.9 %assemble_down.1 = f32[3072,768]{1,0:T(8,128)} custom-call(s32[3]{0:T(128)} %pad_add_fusion.s_ref, bf16[2,4,96,768]{3,2,1,0:T(8,128)(2,1)} %merge.12.refs_0_, bf16[2,4,96,768]{3,2,1,0:T(8,128)(2,1)} %collective-permute-done.43.refs_1_, bf16[2,4,96,768]{3,2,1,0:T(8,128)(2,1)} %collective-permute-done.44.refs_2_, ...), custom_call_target="tpu_custom_call" | custom-call | flops 18400000000 | bytes 1 | tf_op jit(solution)/shard_map/assemble_down/pallas_call | solution.py:843
  393.3 19.6 %collective-permute-done.50.refs_1_ = bf16[2,4,112,768]{3,2,1,0:T(8,128)(2,1)} collective-permute-done((bf16[2,4,112,768]{3,2,1,0:T(8,128)(2,1)}, bf16[2,4,112,768]{3,2,1,0:T(8,128)(2,1)}, u32[]{:S(2)}, u32[]{:S(2)}) %collective-permute-start.50) | collective-permute-done | bytes 1376288 | tf_op jit(solution)/shard_map/ppermute | solution.py:706
  413.8 6.9 %assemble_up.1 = f32[768,3072]{1,0:T(8,128)} custom-call(s32[3]{0:T(128)} %pad_add_fusion.s_ref, bf16[2,4,96,768]{3,2,1,0:T(8,128)(2,1)} %merge.16.refs_0_, bf16[2,4,96,768]{3,2,1,0:T(8,128)(2,1)} %collective-permute-done.47.refs_1_, bf16[2,4,96,768]{3,2,1,0:T(8,128)(2,1)} %collective-permute-done.48.refs_2_, ...), custom_call_target="tpu_custom_call" | custom-call | flops 18400000000 | bytes 1 | tf_op jit(solution)/shard_map/assemble_up/pallas_call | solution.py:843
  420.7 10.8 %collective-permute-done.53.refs_3_ = bf16[2,4,112,768]{3,2,1,0:T(8,128)(2,1)} collective-permute-done((bf16[2,4,112,768]{3,2,1,0:T(8,128)(2,1)}, bf16[2,4,112,768]{3,2,1,0:T(8,128)(2,1)}, u32[]{:S(2)}, u32[]{:S(2)}) %collective-permute-start.53) | collective-permute-done | bytes 1376288 | tf_op jit(solution)/shard_map/ppermute | solution.py:706
  431.5 7.6 %assemble_attn.1 = (f32[768,768]{1,0:T(8,128)}, f32[768,768]{1,0:T(8,128)}, f32[768,768]{1,0:T(8,128)}, f32[768,384]{1,0:T(8,128)}, f32[384,384]{1,0:T(8,128)}, ...) custom-call(s32[3]{0:T(128)} %pad_add_fusion.s_ref, ...), custom_call_target="tpu_custom_call" | custom-call | flops 18400000000 | bytes 1 | tf_op jit(solution)/shard_map/assemble_attn/pallas_call | solution.py:843
  (126 shorter events, 72.9 us)
Async XLA Ops:
  0.7 9.9 %collective-permute-start = (bf16[1024,768]{1,0:T(8,128)(2,1)}, bf16[1024,768]{1,0:T(8,128)(2,1)}, u32[]{:S(2)}, u32[]{:S(2)}) collective-permute-start(bf16[1024,768]{1,0:T(8,128)(2,1)} %bitcast.46), channel_id=1, source_target_pairs={{0,16},{16,0},{1,17},{17,1},{2,18},{18,2},{3,19},{19,3},{4,20},{20... | collective-permute-start | bytes 4718600 | tf_op jit(solution)/shard_map/ppermute | solution.py:931
  1.7 8.8 %collective-permute-start.5 = (bf16[768,768]{1,0:T(8,128)(2,1)}, bf16[768,768]{1,0:T(8,128)(2,1)}, u32[]{:S(2)}, u32[]{:S(2)}) collective-permute-start(bf16[768,768]{1,0:T(8,128)(2,1)} %bitcast.66), channel_id=1, source_target_pairs={{0,16},{16,0},{1,17},{17,1},{2,18},{18,2},{3,19},{19,3},{4,20},{20... | collective-permute-start | bytes 3538952 | tf_op jit(solution)/shard_map/ppermute | solution.py:931
  9.8 18.3 %collective-permute-start.7 = (bf16[3072,768]{1,0:T(8,128)(2,1)}, bf16[3072,768]{1,0:T(8,128)(2,1)}, u32[]{:S(2)}, u32[]{:S(2)}) collective-permute-start(bf16[3072,768]{1,0:T(8,128)(2,1)} %bitcast.40), channel_id=1, source_target_pairs={{0,16},{16,0},{1,17},{17,1},{2,18},{18,2},{3,19},{19,3},{4,20},{20... | collective-permute-start | bytes 14155784 | tf_op jit(solution)/shard_map/ppermute | solution.py:931
  9.9 18.1 %collective-permute-start.6 = (bf16[768,3072]{1,0:T(8,128)(2,1)}, bf16[768,3072]{1,0:T(8,128)(2,1)}, u32[]{:S(2)}, u32[]{:S(2)}) collective-permute-start(bf16[768,3072]{1,0:T(8,128)(2,1)} %bitcast.50), channel_id=1, source_target_pairs={{0,16},{16,0},{1,17},{17,1},{2,18},{18,2},{3,19},{19,3},{4,20},{20... | collective-permute-start | bytes 14155784 | tf_op jit(solution)/shard_map/ppermute | solution.py:931
  27.6 75.0 %collective-permute-start.8 = (bf16[2,512,768]{2,1,0:T(8,128)(2,1)}, bf16[2,512,768]{2,1,0:T(8,128)(2,1)}, u32[]{:S(2)}, u32[]{:S(2)}) collective-permute-start(bf16[2,512,768]{2,1,0:T(8,128)(2,1)} %get-tuple-element.171), channel_id=1, source_target_pairs={{0,16},{16,0},{1,17},{17,1},{2,18},{18,2},{3,19},{19,3},{4,20},{20... | collective-permute-start | bytes 4718600 | tf_op jit(solution)/shard_map/ppermute | solution.py:931
  63.7 38.9 %collective-permute-start.9 = (bf16[2,512,768]{2,1,0:T(8,128)(2,1)}, bf16[2,512,768]{2,1,0:T(8,128)(2,1)}, u32[]{:S(2)}, u32[]{:S(2)}) collective-permute-start(bf16[2,512,768]{2,1,0:T(8,128)(2,1)} %get-tuple-element.172), channel_id=1, source_target_pairs={{0,16},{16,0},{1,17},{17,1},{2,18},{18,2},{3,19},{19,3},{4,20},{20... | collective-permute-start | bytes 4718600 | tf_op jit(solution)/shard_map/ppermute | solution.py:931
  63.9 38.7 %collective-permute-start.10 = (bf16[2,512,1536]{2,1,0:T(8,128)(2,1)}, bf16[2,512,1536]{2,1,0:T(8,128)(2,1)}, u32[]{:S(2)}, u32[]{:S(2)}) collective-permute-start(bf16[2,512,1536]{2,1,0:T(8,128)(2,1)} %get-tuple-element.174), channel_id=1, source_target_pairs={{0,16},{16,0},{1,17},{17,1},{2,18},{18,2},{3,19},{19,3},{4,20},{20... | collective-permute-start | bytes 9437192 | tf_op jit(solution)/shard_map/ppermute | solution.py:931
  102.2 18.3 %collective-permute-start.12 = (bf16[2576,768]{1,0:T(8,128)(2,1)}, bf16[2576,768]{1,0:T(8,128)(2,1)}, u32[]{:S(2)}, u32[]{:S(2)}) collective-permute-start(bf16[2576,768]{1,0:T(8,128)(2,1)} %get-tuple-element.166.own_ref.x_ref.dz_ref), channel_id=1, source_target_pairs={{0,16},{16,0},{1,17},{17,1},{2,18},{18,2},{3,19},{19,3},{4,20},{20... | collective-permute-start | bytes 11870216 | tf_op jit(solution)/shard_map/ppermute | solution.py:931
  117.8 20.2 %collective-permute-start.13 = (bf16[1,8,96,768]{3,2,1,0:T(8,128)(2,1)}, bf16[1,8,96,768]{3,2,1,0:T(8,128)(2,1)}, u32[]{:S(2)}, u32[]{:S(2)}) collective-permute-start(bf16[1,8,96,768]{3,2,1,0:T(8,128)(2,1)} %bitcast.74), channel_id=1, source_target_pairs={{0,1},{1,0},{2,3},{3,2},{4,5},{5,4},{6,7},{7,6},{8,9},{9,8},{10,11... | collective-permute-start | bytes 3538952 | tf_op jit(solution)/shard_map/ppermute | solution.py:706
  120.5 55.3 %collective-permute-start.15 = (bf16[1,8,96,768]{3,2,1,0:T(8,128)(2,1)}, bf16[1,8,96,768]{3,2,1,0:T(8,128)(2,1)}, u32[]{:S(2)}, u32[]{:S(2)}) collective-permute-start(bf16[1,8,96,768]{3,2,1,0:T(8,128)(2,1)} %bitcast.72), channel_id=1, source_target_pairs={{0,1},{1,0},{2,3},{3,2},{4,5},{5,4},{6,7},{7,6},{8,9},{9,8},{10,11... | collective-permute-start | bytes 3538952 | tf_op jit(solution)/shard_map/ppermute | solution.py:706
  136.0 43.0 %collective-permute-start.16 = (bf16[1,8,112,768]{3,2,1,0:T(8,128)(2,1)}, bf16[1,8,112,768]{3,2,1,0:T(8,128)(2,1)}, u32[]{:S(2)}, u32[]{:S(2)}) collective-permute-start(bf16[1,8,112,768]{3,2,1,0:T(8,128)(2,1)} %bitcast.54), channel_id=1, source_target_pairs={{0,1},{1,0},{2,3},{3,2},{4,5},{5,4},{6,7},{7,6},{8,9},{9,8},{10,11... | collective-permute-start | bytes 4128776 | tf_op jit(solution)/shard_map/ppermute | solution.py:706
  137.8 45.6 %collective-permute-start.17 = (bf16[1,8,96,768]{3,2,1,0:T(8,128)(2,1)}, bf16[1,8,96,768]{3,2,1,0:T(8,128)(2,1)}, u32[]{:S(2)}, u32[]{:S(2)}) collective-permute-start(bf16[1,8,96,768]{3,2,1,0:T(8,128)(2,1)} %bitcast.71), channel_id=1, source_target_pairs={{0,1},{1,0},{2,3},{3,2},{4,5},{5,4},{6,7},{7,6},{8,9},{9,8},{10,11... | collective-permute-start | bytes 3538952 | tf_op jit(solution)/shard_map/ppermute | solution.py:706
  141.3 55.6 %collective-permute-start.19 = (bf16[1,4,96,768]{3,2,1,0:T(8,128)(2,1)}, bf16[1,4,96,768]{3,2,1,0:T(8,128)(2,1)}, u32[]{:S(2)}, u32[]{:S(2)}) collective-permute-start(bf16[1,4,96,768]{3,2,1,0:T(8,128)(2,1)} %get-tuple-element.190), channel_id=1, source_target_pairs={{0,2},{1,3},{2,0},{3,1},{4,6},{5,7},{6,4},{7,5},{8,10},{9,11},{10,... | collective-permute-start | bytes 1769480 | tf_op jit(solution)/shard_map/ppermute | solution.py:706
  175.7 28.8 %collective-permute-start.14 = (bf16[2576,768]{1,0:T(8,128)(2,1)}, bf16[2576,768]{1,0:T(8,128)(2,1)}, u32[]{:S(2)}, u32[]{:S(2)}) collective-permute-start(bf16[2576,768]{1,0:T(8,128)(2,1)} %get-tuple-element.196.own_ref), channel_id=1, source_target_pairs={{0,16},{16,0},{1,17},{17,1},{2,18},{18,2},{3,19},{19,3},{4,20},{20... | collective-permute-start | bytes 11870216 | tf_op jit(solution)/shard_map/ppermute | solution.py:931
  178.7 17.5 %collective-permute-start.20 = (bf16[1,4,96,768]{3,2,1,0:T(8,128)(2,1)}, bf16[1,4,96,768]{3,2,1,0:T(8,128)(2,1)}, u32[]{:S(2)}, u32[]{:S(2)}) collective-permute-start(bf16[1,4,96,768]{3,2,1,0:T(8,128)(2,1)} %get-tuple-element.201), channel_id=1, source_target_pairs={{0,2},{1,3},{2,0},{3,1},{4,6},{5,7},{6,4},{7,5},{8,10},{9,11},{10,... | collective-permute-start | bytes 1769480 | tf_op jit(solution)/shard_map/ppermute | solution.py:706
  186.4 10.6 %collective-permute-start.21 = (bf16[1,4,96,768]{3,2,1,0:T(8,128)(2,1)}, bf16[1,4,96,768]{3,2,1,0:T(8,128)(2,1)}, u32[]{:S(2)}, u32[]{:S(2)}) collective-permute-start(bf16[1,4,96,768]{3,2,1,0:T(8,128)(2,1)} %get-tuple-element.205), channel_id=1, source_target_pairs={{0,2},{1,3},{2,0},{3,1},{4,6},{5,7},{6,4},{7,5},{8,10},{9,11},{10,... | collective-permute-start | bytes 1769480 | tf_op jit(solution)/shard_map/ppermute | solution.py:706
  187.3 25.2 %collective-permute-start.22 = (bf16[1,4,112,768]{3,2,1,0:T(8,128)(2,1)}, bf16[1,4,112,768]{3,2,1,0:T(8,128)(2,1)}, u32[]{:S(2)}, u32[]{:S(2)}) collective-permute-start(bf16[1,4,112,768]{3,2,1,0:T(8,128)(2,1)} %get-tuple-element.203), channel_id=1, source_target_pairs={{0,2},{1,3},{2,0},{3,1},{4,6},{5,7},{6,4},{7,5},{8,10},{9,11},{10,... | collective-permute-start | bytes 2064392 | tf_op jit(solution)/shard_map/ppermute | solution.py:706
  196.3 19.4 %collective-permute-start.23 = (bf16[1,8,96,768]{3,2,1,0:T(8,128)(2,1)}, bf16[1,8,96,768]{3,2,1,0:T(8,128)(2,1)}, u32[]{:S(2)}, u32[]{:S(2)}) collective-permute-start(bf16[1,8,96,768]{3,2,1,0:T(8,128)(2,1)} %bitcast.73), channel_id=1, source_target_pairs={{0,1},{1,0},{2,3},{3,2},{4,5},{5,4},{6,7},{7,6},{8,9},{9,8},{10,11... | collective-permute-start | bytes 3538952 | tf_op jit(solution)/shard_map/ppermute | solution.py:706
  202.3 23.0 %collective-permute-start.24 = (bf16[3,2,96,768]{3,2,1,0:T(8,128)(2,1)}, bf16[3,2,96,768]{3,2,1,0:T(8,128)(2,1)}, u32[]{:S(2)}, u32[]{:S(2)}) collective-permute-start(bf16[3,2,96,768]{3,2,1,0:T(8,128)(2,1)} %get-tuple-element.216), channel_id=1, source_target_pairs={{0,4},{1,5},{2,6},{3,7},{4,0},{5,1},{6,2},{7,3},{8,12},{9,13},{10,... | collective-permute-start | bytes 2654216 | tf_op jit(solution)/shard_map/ppermute | solution.py:706
  214.9 19.0 %collective-permute-start.25 = (bf16[1,2,112,768]{3,2,1,0:T(8,128)(2,1)}, bf16[1,2,112,768]{3,2,1,0:T(8,128)(2,1)}, u32[]{:S(2)}, u32[]{:S(2)}) collective-permute-start(bf16[1,2,112,768]{3,2,1,0:T(8,128)(2,1)} %get-tuple-element.222), channel_id=1, source_target_pairs={{0,4},{1,5},{2,6},{3,7},{4,0},{5,1},{6,2},{7,3},{8,12},{9,13},{10,... | collective-permute-start | bytes 1032200 | tf_op jit(solution)/shard_map/ppermute | solution.py:706
  218.6 17.3 %collective-permute-start.26 = (bf16[1,4,96,768]{3,2,1,0:T(8,128)(2,1)}, bf16[1,4,96,768]{3,2,1,0:T(8,128)(2,1)}, u32[]{:S(2)}, u32[]{:S(2)}) collective-permute-start(bf16[1,4,96,768]{3,2,1,0:T(8,128)(2,1)} %get-tuple-element.227), channel_id=1, source_target_pairs={{0,2},{1,3},{2,0},{3,1},{4,6},{5,7},{6,4},{7,5},{8,10},{9,11},{10,... | collective-permute-start | bytes 1769480 | tf_op jit(solution)/shard_map/ppermute | solution.py:706
  229.9 40.8 %collective-permute-start.30 = (bf16[3,1,96,768]{3,2,1,0:T(8,128)(2,1)}, bf16[3,1,96,768]{3,2,1,0:T(8,128)(2,1)}, u32[]{:S(2)}, u32[]{:S(2)}) collective-permute-start(bf16[3,1,96,768]{3,2,1,0:T(8,128)(2,1)} %get-tuple-element.229), channel_id=1, source_target_pairs={{0,8},{1,9},{2,10},{3,11},{4,12},{5,13},{6,14},{7,15},{8,0},{9,1},... | collective-permute-start | bytes 1327112 | tf_op jit(solution)/shard_map/ppermute | solution.py:706
  232.5 18.6 %collective-permute-start.27 = (bf16[1,8,112,768]{3,2,1,0:T(8,128)(2,1)}, bf16[1,8,112,768]{3,2,1,0:T(8,128)(2,1)}, u32[]{:S(2)}, u32[]{:S(2)}) collective-permute-start(bf16[1,8,112,768]{3,2,1,0:T(8,128)(2,1)} %bitcast.55), channel_id=1, source_target_pairs={{0,1},{1,0},{2,3},{3,2},{4,5},{5,4},{6,7},{7,6},{8,9},{9,8},{10,11... | collective-permute-start | bytes 4128776 | tf_op jit(solution)/shard_map/ppermute | solution.py:706
  238.3 17.6 %collective-permute-start.28 = (bf16[1,2,96,768]{3,2,1,0:T(8,128)(2,1)}, bf16[1,2,96,768]{3,2,1,0:T(8,128)(2,1)}, u32[]{:S(2)}, u32[]{:S(2)}) collective-permute-start(bf16[1,2,96,768]{3,2,1,0:T(8,128)(2,1)} %get-tuple-element.235), channel_id=1, source_target_pairs={{0,4},{1,5},{2,6},{3,7},{4,0},{5,1},{6,2},{7,3},{8,12},{9,13},{10,... | collective-permute-start | bytes 884744 | tf_op jit(solution)/shard_map/ppermute | solution.py:706
  254.3 11.3 %collective-permute-start.31 = (bf16[1,4,112,768]{3,2,1,0:T(8,128)(2,1)}, bf16[1,4,112,768]{3,2,1,0:T(8,128)(2,1)}, u32[]{:S(2)}, u32[]{:S(2)}) collective-permute-start(bf16[1,4,112,768]{3,2,1,0:T(8,128)(2,1)} %get-tuple-element.237), channel_id=1, source_target_pairs={{0,2},{1,3},{2,0},{3,1},{4,6},{5,7},{6,4},{7,5},{8,10},{9,11},{10,... | collective-permute-start | bytes 2064392 | tf_op jit(solution)/shard_map/ppermute | solution.py:706
  257.8 13.0 %collective-permute-start.29 = (bf16[1,1,96,768]{3,2,1,0:T(8,128)(2,1)}, bf16[1,1,96,768]{3,2,1,0:T(8,128)(2,1)}, u32[]{:S(2)}, u32[]{:S(2)}) collective-permute-start(bf16[1,1,96,768]{3,2,1,0:T(8,128)(2,1)} %get-tuple-element.240), channel_id=1, source_target_pairs={{0,8},{1,9},{2,10},{3,11},{4,12},{5,13},{6,14},{7,15},{8,0},{9,1},... | collective-permute-start | bytes 442376 | tf_op jit(solution)/shard_map/ppermute | solution.py:706
  267.9 12.9 %collective-permute-start.33 = (bf16[1,2,112,768]{3,2,1,0:T(8,128)(2,1)}, bf16[1,2,112,768]{3,2,1,0:T(8,128)(2,1)}, u32[]{:S(2)}, u32[]{:S(2)}) collective-permute-start(bf16[1,2,112,768]{3,2,1,0:T(8,128)(2,1)} %get-tuple-element.244), channel_id=1, source_target_pairs={{0,4},{1,5},{2,6},{3,7},{4,0},{5,1},{6,2},{7,3},{8,12},{9,13},{10,... | collective-permute-start | bytes 1032200 | tf_op jit(solution)/shard_map/ppermute | solution.py:706
  270.4 10.3 %collective-permute-start.32 = (bf16[1,1,112,768]{3,2,1,0:T(8,128)(2,1)}, bf16[1,1,112,768]{3,2,1,0:T(8,128)(2,1)}, u32[]{:S(2)}, u32[]{:S(2)}) collective-permute-start(bf16[1,1,112,768]{3,2,1,0:T(8,128)(2,1)} %get-tuple-element.231), channel_id=1, source_target_pairs={{0,8},{1,9},{2,10},{3,11},{4,12},{5,13},{6,14},{7,15},{8,0},{9,1},... | collective-permute-start | bytes 516104 | tf_op jit(solution)/shard_map/ppermute | solution.py:706
  273.0 9.7 %collective-permute-start.34 = (bf16[1,1,96,768]{3,2,1,0:T(8,128)(2,1)}, bf16[1,1,96,768]{3,2,1,0:T(8,128)(2,1)}, u32[]{:S(2)}, u32[]{:S(2)}) collective-permute-start(bf16[1,1,96,768]{3,2,1,0:T(8,128)(2,1)} %get-tuple-element.289), channel_id=1, source_target_pairs={{0,16},{16,0},{1,17},{17,1},{2,18},{18,2},{3,19},{19,3},{4,20},{20... | collective-permute-start | bytes 442376 | tf_op jit(solution)/shard_map/ppermute | solution.py:931
  282.7 12.1 %collective-permute-start.35 = (bf16[1,1,112,768]{3,2,1,0:T(8,128)(2,1)}, bf16[1,1,112,768]{3,2,1,0:T(8,128)(2,1)}, u32[]{:S(2)}, u32[]{:S(2)}) collective-permute-start(bf16[1,1,112,768]{3,2,1,0:T(8,128)(2,1)} %get-tuple-element.248), channel_id=1, source_target_pairs={{0,8},{1,9},{2,10},{3,11},{4,12},{5,13},{6,14},{7,15},{8,0},{9,1},... | collective-permute-start | bytes 516104 | tf_op jit(solution)/shard_map/ppermute | solution.py:706
  284.5 14.7 %collective-permute-start.36 = (bf16[2,1,96,768]{3,2,1,0:T(8,128)(2,1)}, bf16[2,1,96,768]{3,2,1,0:T(8,128)(2,1)}, u32[]{:S(2)}, u32[]{:S(2)}) collective-permute-start(bf16[2,1,96,768]{3,2,1,0:T(8,128)(2,1)} %bitcast.82), channel_id=1, source_target_pairs={{0,8},{1,9},{2,10},{3,11},{4,12},{5,13},{6,14},{7,15},{8,0},{9,1},... | collective-permute-start | bytes 884744 | tf_op jit(solution)/shard_map/ppermute | solution.py:706
  289.5 14.0 %collective-permute-start.37 = (bf16[1,1,96,768]{3,2,1,0:T(8,128)(2,1)}, bf16[1,1,96,768]{3,2,1,0:T(8,128)(2,1)}, u32[]{:S(2)}, u32[]{:S(2)}) collective-permute-start(bf16[1,1,96,768]{3,2,1,0:T(8,128)(2,1)} %get-tuple-element.286), channel_id=1, source_target_pairs={{0,16},{16,0},{1,17},{17,1},{2,18},{18,2},{3,19},{19,3},{4,20},{20... | collective-permute-start | bytes 442376 | tf_op jit(solution)/shard_map/ppermute | solution.py:931
  296.8 20.1 %collective-permute-start.39 = (bf16[1,1,112,768]{3,2,1,0:T(8,128)(2,1)}, bf16[1,1,112,768]{3,2,1,0:T(8,128)(2,1)}, u32[]{:S(2)}, u32[]{:S(2)}) collective-permute-start(bf16[1,1,112,768]{3,2,1,0:T(8,128)(2,1)} %get-tuple-element.291), channel_id=1, source_target_pairs={{0,16},{16,0},{1,17},{17,1},{2,18},{18,2},{3,19},{19,3},{4,20},{20... | collective-permute-start | bytes 516104 | tf_op jit(solution)/shard_map/ppermute | solution.py:931
  302.1 10.2 %collective-permute-start.38 = (bf16[2,2,96,768]{3,2,1,0:T(8,128)(2,1)}, bf16[2,2,96,768]{3,2,1,0:T(8,128)(2,1)}, u32[]{:S(2)}, u32[]{:S(2)}) collective-permute-start(bf16[2,2,96,768]{3,2,1,0:T(8,128)(2,1)} %merge.10.a_ref), channel_id=1, source_target_pairs={{0,2},{1,3},{2,0},{3,1},{4,6},{5,7},{6,4},{7,5},{8,10},{9,11},{10,... | collective-permute-start | bytes 1769480 | tf_op jit(solution)/shard_map/ppermute | solution.py:706
  305.3 16.0 %collective-permute-start.40 = (bf16[2,1,96,768]{3,2,1,0:T(8,128)(2,1)}, bf16[2,1,96,768]{3,2,1,0:T(8,128)(2,1)}, u32[]{:S(2)}, u32[]{:S(2)}) collective-permute-start(bf16[2,1,96,768]{3,2,1,0:T(8,128)(2,1)} %bitcast.84), channel_id=1, source_target_pairs={{0,8},{1,9},{2,10},{3,11},{4,12},{5,13},{6,14},{7,15},{8,0},{9,1},... | collective-permute-start | bytes 884744 | tf_op jit(solution)/shard_map/ppermute | solution.py:706
  315.5 36.5 %collective-permute-start.43 = (bf16[2,4,96,768]{3,2,1,0:T(8,128)(2,1)}, bf16[2,4,96,768]{3,2,1,0:T(8,128)(2,1)}, u32[]{:S(2)}, u32[]{:S(2)}) collective-permute-start(bf16[2,4,96,768]{3,2,1,0:T(8,128)(2,1)} %merge.12.refs_0_), channel_id=1, source_target_pairs={{0,4},{1,5},{2,6},{3,7},{4,0},{5,1},{6,2},{7,3},{8,12},{9,13},{10,... | collective-permute-start | bytes 3538952 | tf_op jit(solution)/shard_map/ppermute | solution.py:706
  315.5 36.5 %collective-permute-start.44 = (bf16[2,4,96,768]{3,2,1,0:T(8,128)(2,1)}, bf16[2,4,96,768]{3,2,1,0:T(8,128)(2,1)}, u32[]{:S(2)}, u32[]{:S(2)}) collective-permute-start(bf16[2,4,96,768]{3,2,1,0:T(8,128)(2,1)} %merge.12.refs_0_), channel_id=1, source_target_pairs={{0,1},{1,0},{2,3},{3,2},{4,5},{5,4},{6,7},{7,6},{8,9},{9,8},{10,11... | collective-permute-start | bytes 3538952 | tf_op jit(solution)/shard_map/ppermute | solution.py:706
  318.6 27.6 %collective-permute-start.42 = (bf16[2,1,112,768]{3,2,1,0:T(8,128)(2,1)}, bf16[2,1,112,768]{3,2,1,0:T(8,128)(2,1)}, u32[]{:S(2)}, u32[]{:S(2)}) collective-permute-start(bf16[2,1,112,768]{3,2,1,0:T(8,128)(2,1)} %bitcast.80), channel_id=1, source_target_pairs={{0,8},{1,9},{2,10},{3,11},{4,12},{5,13},{6,14},{7,15},{8,0},{9,1},... | collective-permute-start | bytes 1032200 | tf_op jit(solution)/shard_map/ppermute | solution.py:706
  324.1 27.8 %collective-permute-start.45 = (bf16[2,2,96,768]{3,2,1,0:T(8,128)(2,1)}, bf16[2,2,96,768]{3,2,1,0:T(8,128)(2,1)}, u32[]{:S(2)}, u32[]{:S(2)}) collective-permute-start(bf16[2,2,96,768]{3,2,1,0:T(8,128)(2,1)} %merge.14.a_ref), channel_id=1, source_target_pairs={{0,2},{1,3},{2,0},{3,1},{4,6},{5,7},{6,4},{7,5},{8,10},{9,11},{10,... | collective-permute-start | bytes 1769480 | tf_op jit(solution)/shard_map/ppermute | solution.py:706
  332.6 27.9 %collective-permute-start.41 = (bf16[512,768]{1,0:T(8,128)(2,1)}, bf16[512,768]{1,0:T(8,128)(2,1)}, u32[]{:S(2)}, u32[]{:S(2)}) collective-permute-start(bf16[512,768]{1,0:T(8,128)(2,1)} %feed_down.1), channel_id=1, source_target_pairs={{0,16},{1,17},{2,18},{3,19},{4,20},{5,21},{6,22},{7,23},{8,24},{9,... | collective-permute-start | bytes 2359304 | tf_op jit(solution)/shard_map/ppermute | solution.py:1007
  349.1 14.2 %collective-permute-start.46 = (bf16[2,2,112,768]{3,2,1,0:T(8,128)(2,1)}, bf16[2,2,112,768]{3,2,1,0:T(8,128)(2,1)}, u32[]{:S(2)}, u32[]{:S(2)}) collective-permute-start(bf16[2,2,112,768]{3,2,1,0:T(8,128)(2,1)} %merge.15.a_ref), channel_id=1, source_target_pairs={{0,2},{1,3},{2,0},{3,1},{4,6},{5,7},{6,4},{7,5},{8,10},{9,11},{10,... | collective-permute-start | bytes 2064392 | tf_op jit(solution)/shard_map/ppermute | solution.py:706
  355.2 29.2 %collective-permute-start.47 = (bf16[2,4,96,768]{3,2,1,0:T(8,128)(2,1)}, bf16[2,4,96,768]{3,2,1,0:T(8,128)(2,1)}, u32[]{:S(2)}, u32[]{:S(2)}) collective-permute-start(bf16[2,4,96,768]{3,2,1,0:T(8,128)(2,1)} %merge.16.refs_0_), channel_id=1, source_target_pairs={{0,4},{1,5},{2,6},{3,7},{4,0},{5,1},{6,2},{7,3},{8,12},{9,13},{10,... | collective-permute-start | bytes 3538952 | tf_op jit(solution)/shard_map/ppermute | solution.py:706
  357.3 27.1 %collective-permute-start.48 = (bf16[2,4,96,768]{3,2,1,0:T(8,128)(2,1)}, bf16[2,4,96,768]{3,2,1,0:T(8,128)(2,1)}, u32[]{:S(2)}, u32[]{:S(2)}) collective-permute-start(bf16[2,4,96,768]{3,2,1,0:T(8,128)(2,1)} %merge.16.refs_0_), channel_id=1, source_target_pairs={{0,1},{1,0},{2,3},{3,2},{4,5},{5,4},{6,7},{7,6},{8,9},{9,8},{10,11... | collective-permute-start | bytes 3538952 | tf_op jit(solution)/shard_map/ppermute | solution.py:706
  357.7 28.8 %collective-permute-start.49 = (bf16[2,4,96,768]{3,2,1,0:T(8,128)(2,1)}, bf16[2,4,96,768]{3,2,1,0:T(8,128)(2,1)}, u32[]{:S(2)}, u32[]{:S(2)}) collective-permute-start(bf16[2,4,96,768]{3,2,1,0:T(8,128)(2,1)} %collective-permute-done.43.refs_1_), channel_id=1, source_target_pairs={{0,1},{1,0},{2,3},{3,2},{4,5},{5,4},{6,7},{7,6},{8,9},{9,8},{10,11... | collective-permute-start | bytes 3538952 | tf_op jit(solution)/shard_map/ppermute | solution.py:706
  366.6 46.3 %collective-permute-start.50 = (bf16[2,4,112,768]{3,2,1,0:T(8,128)(2,1)}, bf16[2,4,112,768]{3,2,1,0:T(8,128)(2,1)}, u32[]{:S(2)}, u32[]{:S(2)}) collective-permute-start(bf16[2,4,112,768]{3,2,1,0:T(8,128)(2,1)} %merge.17.refs_0_), channel_id=1, source_target_pairs={{0,4},{1,5},{2,6},{3,7},{4,0},{5,1},{6,2},{7,3},{8,12},{9,13},{10,... | collective-permute-start | bytes 4128776 | tf_op jit(solution)/shard_map/ppermute | solution.py:706
  371.2 41.7 %collective-permute-start.51 = (bf16[2,4,112,768]{3,2,1,0:T(8,128)(2,1)}, bf16[2,4,112,768]{3,2,1,0:T(8,128)(2,1)}, u32[]{:S(2)}, u32[]{:S(2)}) collective-permute-start(bf16[2,4,112,768]{3,2,1,0:T(8,128)(2,1)} %merge.17.refs_0_), channel_id=1, source_target_pairs={{0,1},{1,0},{2,3},{3,2},{4,5},{5,4},{6,7},{7,6},{8,9},{9,8},{10,11... | collective-permute-start | bytes 4128776 | tf_op jit(solution)/shard_map/ppermute | solution.py:706
  384.4 29.4 %collective-permute-start.52 = (bf16[2,4,96,768]{3,2,1,0:T(8,128)(2,1)}, bf16[2,4,96,768]{3,2,1,0:T(8,128)(2,1)}, u32[]{:S(2)}, u32[]{:S(2)}) collective-permute-start(bf16[2,4,96,768]{3,2,1,0:T(8,128)(2,1)} %collective-permute-done.47.refs_1_), channel_id=1, source_target_pairs={{0,1},{1,0},{2,3},{3,2},{4,5},{5,4},{6,7},{7,6},{8,9},{9,8},{10,11... | collective-permute-start | bytes 3538952 | tf_op jit(solution)/shard_map/ppermute | solution.py:706
  412.9 18.6 %collective-permute-start.53 = (bf16[2,4,112,768]{3,2,1,0:T(8,128)(2,1)}, bf16[2,4,112,768]{3,2,1,0:T(8,128)(2,1)}, u32[]{:S(2)}, u32[]{:S(2)}) collective-permute-start(bf16[2,4,112,768]{3,2,1,0:T(8,128)(2,1)} %collective-permute-done.50.refs_1_), channel_id=1, source_target_pairs={{0,1},{1,0},{2,3},{3,2},{4,5},{5,4},{6,7},{7,6},{8,9},{9,8},{10,11... | collective-permute-start | bytes 4128776 | tf_op jit(solution)/shard_map/ppermute | solution.py:706
  (13 other events, 102.1 us)

commit v5 on v4

--- a/solution.py
+++ b/solution.py
@@ -1073,9 +1073,6 @@
     cur_a, got_a = both_parts(pair_a)
     cur_u = grow(3, cur_u, got_u)
     got_u = exchange(cur_u, dp, 1)
-    y = feed_down(1, sec, a1, order.tie(m), vec[1], w)
-    order.mark(y)
-    y_moved = to_second(y)
     cur_a = grow(3, cur_a, got_a)
     got_a = exchange(cur_a, dp, 1)
     order.also(far_d, side_d)
@@ -1083,7 +1080,6 @@
     cur_u = grow(1, cur_u, got_u)
     far_u = exchange(cur_u, dp, 2)
     side_u = exchange(cur_u, dp, 0)
-    order.also(y_moved)
     cur_a = grow(1, cur_a, got_a)
     far_a = exchange(cur_a, dp, 2)
     side_a = exchange(cur_a, dp, 0)
@@ -1092,6 +1088,9 @@
     block = ff // 16
     order.also(far_u, side_u)
     last_u = exchange(order.tie(far_u), dp, 0)
+    y = feed_down(1, sec, a1, order.tie(m), vec[1], w)
+    order.mark(y)
+    y_moved = to_second(y)
     down_grad, = assemble(
         scalars, (order.tie(cur_d), far_d, side_d, last_d), chunk_rows, [(ff, d)],
         lambda outs, part, t: [(all_columns, outs[0].at[pl.ds((8 * part + t) * block, block), :])], "assemble_down")
@@ -1101,7 +1100,7 @@
         scalars, (order.tie(cur_u), far_u, side_u, last_u), chunk_rows, [(d, ff)],
         lambda outs, part, t: [(all_columns, outs[0].at[pl.ds(t % 4 * block, block), pl.ds((2 * part + t // 4) * d, d)])],
         "assemble_up")
-    order.mark(up_grad)
+    order.mark(up_grad, y_moved)
 
     def square_targets(outs, part, t):
         at = pl.ds((2 * part + t % 2) * block, block)

time: 447 us -> 446 us (level)
  transfers between devices with their start and end apart: 54 -> 54, of which waited for: 17 -> 15; matrix products, arithmetic and copies ran while one was open for 4% -> 5% of each run, Pallas kernels for 57% -> 57%
where the time goes in v5:
time: 446 us; the launch traced here: 441 us
  Pallas kernels  261 us (59%)
  waiting for transfers between devices  104 us (23%)
  starting transfers between devices  53 us (12%)
  other arithmetic  15.5 us (3%)
  local copies, waits for them, and re-layouts  6.3 us (1%)
    ppermute x35, waiting for transfers between devices, exchange(): return lax.ppermute(array, AXES, pairs)  102 us
    pallas_call x2, Pallas kernels, layer_backward(): pl.pallas_call(functools.partial(layer_backward_kernel, layer, blk), grid...  65.9 us
    ppermute x35, starting transfers between devices, exchange(): return lax.ppermute(array, AXES, pairs)  45.5 us
    pallas_call x14, Pallas kernels, add_split(): pl.pallas_call(kernel, grid_spec=pltpu.PrefetchScalarGridSpec(num_scalar_...  41.3 us
    pallas_call x1, Pallas kernels, middle(): pl.pallas_call(functools.partial(middle_kernel, blk), out_shape=[wide, wi...  35.7 us
    pallas_call x4, Pallas kernels, quarters(): pl.pallas_call(kernel, grid_spec=pltpu.PrefetchScalarGridSpec(num_scalar_...  30.4 us
    pallas_call x9, Pallas kernels, merge(): pl.pallas_call(kernel, grid_spec=pltpu.PrefetchScalarGridSpec(num_scalar_...  23.5 us
    pallas_call x3, Pallas kernels, assemble(): pl.pallas_call(kernel, out_shape=[sds(o, f32) for o in out_shapes], in_sp...  21.4 us
  transfers between devices with their start and end apart: 54, of which 15 were waited for; matrix products, arithmetic and copies ran while one was open for 5% of the time, Pallas kernels for 57%

profile of v5, /device:TPU:0, one launch (start us, length us, event | category | flops | bytes accessed | tf_op | source)
XLA Modules:
  0.0 440.8 jit_solution(6343688608110975067)
XLA Ops:
  10.5 17.0 %attn_forward.1 = (bf16[512,768]{1,0:T(8,128)(2,1)}, bf16[512,768]{1,0:T(8,128)(2,1)}, bf16[512,768]{1,0:T(8,128)(2,1)}, bf16[512,768]{1,0:T(8,128)(2,1)}, bf16[...) custom-call(s32[1]{0:T(128)} %bitcast.sec_ref.s_ref, ...), custom_call_target="tpu_custom_call" | custom-call | flops 92000002048 | bytes 1 | tf_op jit(solution)/shard_map/attn_forward/pallas_call | solution.py:224
  28.0 35.7 %middle.1 = (bf16[512,3072]{1,0:T(8,128)(2,1)}, bf16[512,3072]{1,0:T(8,128)(2,1)}, bf16[512,768]{1,0:T(8,128)(2,1)}, bf16[512,3072]{1,0:T(8,128)(2,1)}, bf16[512...) custom-call(s32[1]{0:T(128)} %bitcast.sec_ref.s_ref, ...), custom_call_target="tpu_custom_call" | custom-call | flops 92000002048 | bytes 1 | tf_op jit(solution)/shard_map/middle/pallas_call | solution.py:308
  64.3 3.1 slice_select_fusion
  68.4 33.6 %layer_backward.2 = (bf16[512,3072]{1,0:T(8,128)(2,1)}, bf16[2,512,768]{2,1,0:T(8,128)(2,1)}, bf16[2576,768]{1,0:T(8,128)(2,1)}, f32[512,384]{1,0:T(8,128)}, f32[16,768]{1,0:T(8,128)}) custom-call(s32[1]{0:T(128)} %bitcast.sec_ref.s_ref, bf16[512,768]{1,0:T(8,128)(2,1)} %get-tuple-element.285.dz_ref.x_ref, f32[512,768]{1,0:T(8,128)} %get-tuple-element.262.m_ref, ...), custom_call_target="tpu_custom_call" | custom-call | flops 92000002048 | bytes 1 | tf_op jit(solution)/shard_map/layer_backward/pallas_call | solution.py:548
  102.6 7.3 %down_gradient.2 = (bf16[8,96,768]{2,1,0:T(8,128)(2,1)}, bf16[8,96,768]{2,1,0:T(8,128)(2,1)}) custom-call(s32[3]{0:T(128)} %pad_add_fusion.s_ref, bf16[512,3072]{1,0:T(8,128)(2,1)} %get-tuple-element.173.a_ref, bf16[2,512,1536]{2,1,0:T(8,128)(2,1)} %collective-permute-done.10.b_ref, bf16[512,768]{1,0:T(8,128)(2,1)} %get-tuple-element.285.dz_ref.x_ref, ...), custom_call_target="tpu_custom_call" | custom-call | flops 92000002048 | bytes 1 | tf_op jit(solution)/shard_map/down_gradient/pallas_call | solution.py:579
  109.9 7.9 %up_gradient.2 = (bf16[8,96,768]{2,1,0:T(8,128)(2,1)}, bf16[8,96,768]{2,1,0:T(8,128)(2,1)}) custom-call(s32[3]{0:T(128)} %pad_add_fusion.s_ref, bf16[512,768]{1,0:T(8,128)(2,1)} %get-tuple-element.179.e_ref, bf16[2,512,768]{2,1,0:T(8,128)(2,1)} %collective-permute-done.9.f_ref.l_ref, bf16[512,3072]{1,0:T(8,128)(2,1)} %get-tuple-element.180.du_ref, ...), custom_call_target="tpu_custom_call" | custom-call | flops 92000002048 | bytes 1 | tf_op jit(solution)/shard_map/up_gradient/pallas_call | solution.py:579
  117.8 2.6 collective-permute-start.13
  120.5 8.1 %attn_gradient.2 = (bf16[8,112,768]{2,1,0:T(8,128)(2,1)}, bf16[8,112,768]{2,1,0:T(8,128)(2,1)}) custom-call(s32[3]{0:T(128)} %pad_add_fusion.s_ref, bf16[512,768]{1,0:T(8,128)(2,1)} %get-tuple-element.183.o_in.o_ref, bf16[512,768]{1,0:T(8,128)(2,1)} %get-tuple-element.184.h_ref, bf16[2,512,768]{2,1,0:T(8,128)(2,1)} %collective-permute-done.9.f_ref.l_ref, ...), custom_call_target="tpu_custom_call" | custom-call | flops 92000002048 | bytes 1 | tf_op jit(solution)/shard_map/attn_gradient/pallas_call | solution.py:675
  128.6 7.4 %down_gradient.3 = (bf16[8,96,768]{2,1,0:T(8,128)(2,1)}, bf16[8,96,768]{2,1,0:T(8,128)(2,1)}) custom-call(s32[3]{0:T(128)} %pad_add_fusion.s_ref, bf16[512,3072]{1,0:T(8,128)(2,1)} %get-tuple-element.187.a_ref, bf16[2,512,1536]{2,1,0:T(8,128)(2,1)} %collective-permute-done.10.b_ref, bf16[2576,768]{1,0:T(8,128)(2,1)} %get-tuple-element.166.own_ref.x_ref.dz_ref, ...), custom_call_target="tpu_custom_call" | custom-call | flops 92000002048 | bytes 1 | tf_op jit(solution)/shard_map/down_gradient/pallas_call | solution.py:579
  138.0 3.3 add_split.14
  143.4 32.3 %layer_backward.3 = (bf16[512,3072]{1,0:T(8,128)(2,1)}, bf16[2,512,768]{2,1,0:T(8,128)(2,1)}, bf16[2576,768]{1,0:T(8,128)(2,1)}, f32[512,384]{1,0:T(8,128)}, f32[16,768]{1,0:T(8,128)}) custom-call(s32[1]{0:T(128)} %bitcast.sec_ref.s_ref, bf16[2576,768]{1,0:T(8,128)(2,1)} %get-tuple-element.166.own_ref.x_ref.dz_ref, f32[512,768]{1,0:T(8,128)} %get-tuple-element.152.m_ref, ...), custom_call_target="tpu_custom_call" | custom-call | flops 92000002048 | bytes 1 | tf_op jit(solution)/shard_map/layer_backward/pallas_call | solution.py:548
  175.8 2.9 add_split.15
  180.3 3.2 add_split.16
  183.5 2.9 add_split.17
  188.4 7.8 %up_gradient.3 = (bf16[8,96,768]{2,1,0:T(8,128)(2,1)}, bf16[8,96,768]{2,1,0:T(8,128)(2,1)}) custom-call(s32[3]{0:T(128)} %pad_add_fusion.s_ref, bf16[512,768]{1,0:T(8,128)(2,1)} %get-tuple-element.207.e_ref, bf16[2,512,768]{2,1,0:T(8,128)(2,1)} %collective-permute-done.8.f_ref.l_ref, bf16[512,3072]{1,0:T(8,128)(2,1)} %get-tuple-element.208.du_ref, ...), custom_call_target="tpu_custom_call" | custom-call | flops 92000002048 | bytes 1 | tf_op jit(solution)/shard_map/up_gradient/pallas_call | solution.py:579
  197.0 5.3 %add_split.18 = (bf16[3,2,96,768]{3,2,1,0:T(8,128)(2,1)}, bf16[3,2,96,768]{3,2,1,0:T(8,128)(2,1)}) custom-call(s32[1]{0:T(128)} %bitcast.10.s_ref, bf16[1,4,96,768]{3,2,1,0:T(8,128)(2,1)} %get-tuple-element.211.refs_0_, bf16[1,4,96,768]{3,2,1,0:T(8,128)(2,1)} %collective-permute-done.19.refs_1_, bf16[1,4,96,768]{3,2,1,0:T(8,128)(2,1)} %get-tuple-element.212.refs_2_, ...), custom_call_target="tpu_custom_call" | custom-call | flops 9200000000 | bytes 1 | tf_op jit(solution)/shard_map/add_split/pallas_call | solution.py:757
  204.5 8.1 %attn_gradient.3 = (bf16[8,112,768]{2,1,0:T(8,128)(2,1)}, bf16[8,112,768]{2,1,0:T(8,128)(2,1)}) custom-call(s32[3]{0:T(128)} %pad_add_fusion.s_ref, bf16[512,768]{1,0:T(8,128)(2,1)} %get-tuple-element.215.o_in.o_ref, bf16[512,768]{1,0:T(8,128)(2,1)} %get-tuple-element.216.h_ref, bf16[2,512,768]{2,1,0:T(8,128)(2,1)} %collective-permute-done.8.f_ref.l_ref, ...), custom_call_target="tpu_custom_call" | custom-call | flops 92000002048 | bytes 1 | tf_op jit(solution)/shard_map/attn_gradient/pallas_call | solution.py:675
  212.5 2.4 add_split.19
  215.7 2.9 add_split.20
  219.5 5.8 %collective-permute-done.24.refs_1_ = bf16[3,2,96,768]{3,2,1,0:T(8,128)(2,1)} collective-permute-done((bf16[3,2,96,768]{3,2,1,0:T(8,128)(2,1)}, bf16[3,2,96,768]{3,2,1,0:T(8,128)(2,1)}, u32[]{:S(2)}, u32[]{:S(2)}) %collective-permute-start.24) | collective-permute-done | bytes 884768 | tf_op jit(solution)/shard_map/ppermute | solution.py:706
  225.3 4.6 %add_split.21 = (bf16[3,1,96,768]{3,2,1,0:T(8,128)(2,1)}, bf16[3,1,96,768]{3,2,1,0:T(8,128)(2,1)}) custom-call(s32[1]{0:T(128)} %bitcast.15.s_ref, bf16[3,2,96,768]{3,2,1,0:T(8,128)(2,1)} %get-tuple-element.229.refs_0_, bf16[3,2,96,768]{3,2,1,0:T(8,128)(2,1)} %collective-permute-done.24.refs_1_), custom_call_target="tpu_custom_call" | custom-call | flops 9200000000 | bytes 1 | tf_op jit(solution)/shard_map/add_split/pallas_call | solution.py:757
  230.0 2.6 collective-permute-start.30
  235.9 2.4 add_split.23
  240.4 10.8 %collective-permute-done.27.refs_1_ = bf16[1,8,112,768]{3,2,1,0:T(8,128)(2,1)} collective-permute-done((bf16[1,8,112,768]{3,2,1,0:T(8,128)(2,1)}, bf16[1,8,112,768]{3,2,1,0:T(8,128)(2,1)}, u32[]{:S(2)}, u32[]{:S(2)}) %collective-permute-start.27) | collective-permute-done | bytes 1376288 | tf_op jit(solution)/shard_map/ppermute | solution.py:706
  251.2 3.1 add_split.24
  258.1 7.5 %collective-permute-done.29.refs_1_ = bf16[1,4,112,768]{3,2,1,0:T(8,128)(2,1)} collective-permute-done((bf16[1,4,112,768]{3,2,1,0:T(8,128)(2,1)}, bf16[1,4,112,768]{3,2,1,0:T(8,128)(2,1)}, u32[]{:S(2)}, u32[]{:S(2)}) %collective-permute-start.29) | collective-permute-done | bytes 688160 | tf_op jit(solution)/shard_map/ppermute | solution.py:706
  265.6 2.3 add_split.26
  270.8 2.3 broadcast_select_fusion
  273.1 5.8 %collective-permute-done.31 = bf16[1,1,112,768]{3,2,1,0:T(8,128)(2,1)} collective-permute-done((bf16[1,1,112,768]{3,2,1,0:T(8,128)(2,1)}, bf16[1,1,112,768]{3,2,1,0:T(8,128)(2,1)}, u32[]{:S(2)}, u32[]{:S(2)}) %collective-permute-start.31) | collective-permute-done | bytes 172064 | tf_op jit(solution)/shard_map/ppermute | solution.py:706
  285.6 9.2 %collective-permute-done.33 = bf16[1,1,112,768]{3,2,1,0:T(8,128)(2,1)} collective-permute-done((bf16[1,1,112,768]{3,2,1,0:T(8,128)(2,1)}, bf16[1,1,112,768]{3,2,1,0:T(8,128)(2,1)}, u32[]{:S(2)}, u32[]{:S(2)}) %collective-permute-start.33) | collective-permute-done | bytes 172064 | tf_op jit(solution)/shard_map/ppermute | solution.py:706
  299.2 2.8 merge.10.a_ref
  305.2 7.0 %collective-permute-done.38.b_ref = bf16[2,2,96,768]{3,2,1,0:T(8,128)(2,1)} collective-permute-done((bf16[2,2,96,768]{3,2,1,0:T(8,128)(2,1)}, bf16[2,2,96,768]{3,2,1,0:T(8,128)(2,1)}, u32[]{:S(2)}, u32[]{:S(2)}) %collective-permute-start.38) | collective-permute-done | bytes 589856 | tf_op jit(solution)/shard_map/ppermute | solution.py:706
  312.2 3.2 merge.12.refs_0_
  318.5 2.8 collective-permute-start.41
  321.3 2.8 merge.14.a_ref
  324.7 21.5 %collective-permute-done.41.b_ref = bf16[2,1,112,768]{3,2,1,0:T(8,128)(2,1)} collective-permute-done((bf16[2,1,112,768]{3,2,1,0:T(8,128)(2,1)}, bf16[2,1,112,768]{3,2,1,0:T(8,128)(2,1)}, u32[]{:S(2)}, u32[]{:S(2)}) %collective-permute-start.41) | collective-permute-done | bytes 344096 | tf_op jit(solution)/shard_map/ppermute | solution.py:706
  346.1 2.9 merge.15.a_ref
  352.0 3.2 merge.16.refs_0_
  363.4 3.4 merge.17.refs_0_
  366.8 4.4 %collective-permute-start.50 = (bf16[2,4,112,768]{3,2,1,0:T(8,128)(2,1)}, bf16[2,4,112,768]{3,2,1,0:T(8,128)(2,1)}, u32[]{:S(2)}, u32[]{:S(2)}) collective-permute-start(bf16[2,4,112,768]{3,2,1,0:T(8,128)(2,1)} %merge.17.refs_0_), channel_id=1, source_target_pairs={{0,4},{1,5},{2,6},{3,7},{4,0},{5,1},{6,2},{7,3},{8,12},{9,13},{10,... | collective-permute-start | bytes 4128776 | tf_op jit(solution)/shard_map/ppermute | solution.py:706
  373.2 11.3 %collective-permute-done.46.refs_1_ = bf16[2,4,96,768]{3,2,1,0:T(8,128)(2,1)} collective-permute-done((bf16[2,4,96,768]{3,2,1,0:T(8,128)(2,1)}, bf16[2,4,96,768]{3,2,1,0:T(8,128)(2,1)}, u32[]{:S(2)}, u32[]{:S(2)}) %collective-permute-start.46) | collective-permute-done | bytes 1179680 | tf_op jit(solution)/shard_map/ppermute | solution.py:706
  384.4 7.9 %feed_down.1 = bf16[512,768]{1,0:T(8,128)(2,1)} custom-call(s32[1]{0:T(128)} %bitcast.sec_ref.s_ref, bf16[512,3072]{1,0:T(8,128)(2,1)} %get-tuple-element.173.a_ref, f32[512,768]{1,0:T(8,128)} %get-tuple-element.262.m_ref, f32[16,768]{1,0:T(8,128)} %get-tuple-element.292.vec1_ref.vec_ref, bf16[3072,768]{1,0:T(8,128)(2,1)} %bitcast.44, ...), custom_call_target="tpu_custom_call" | custom-call | flops 2300000000 | bytes 1 | tf_op jit(solution)/shard_map/feed_down/pallas_call | solution.py:364
  395.1 6.9 %assemble_down.1 = f32[3072,768]{1,0:T(8,128)} custom-call(s32[3]{0:T(128)} %pad_add_fusion.s_ref, bf16[2,4,96,768]{3,2,1,0:T(8,128)(2,1)} %merge.12.refs_0_, bf16[2,4,96,768]{3,2,1,0:T(8,128)(2,1)} %collective-permute-done.42.refs_1_, bf16[2,4,96,768]{3,2,1,0:T(8,128)(2,1)} %collective-permute-done.43.refs_2_, ...), custom_call_target="tpu_custom_call" | custom-call | flops 18400000000 | bytes 1 | tf_op jit(solution)/shard_map/assemble_down/pallas_call | solution.py:843
  402.0 10.9 %collective-permute-done.50.refs_1_ = bf16[2,4,112,768]{3,2,1,0:T(8,128)(2,1)} collective-permute-done((bf16[2,4,112,768]{3,2,1,0:T(8,128)(2,1)}, bf16[2,4,112,768]{3,2,1,0:T(8,128)(2,1)}, u32[]{:S(2)}, u32[]{:S(2)}) %collective-permute-start.50) | collective-permute-done | bytes 1376288 | tf_op jit(solution)/shard_map/ppermute | solution.py:706
  413.5 3.3 maximum_select_fusion
  416.9 6.9 %assemble_up.1 = f32[768,3072]{1,0:T(8,128)} custom-call(s32[3]{0:T(128)} %pad_add_fusion.s_ref, bf16[2,4,96,768]{3,2,1,0:T(8,128)(2,1)} %merge.16.refs_0_, bf16[2,4,96,768]{3,2,1,0:T(8,128)(2,1)} %collective-permute-done.46.refs_1_, bf16[2,4,96,768]{3,2,1,0:T(8,128)(2,1)} %collective-permute-done.47.refs_2_, ...), custom_call_target="tpu_custom_call" | custom-call | flops 18400000000 | bytes 1 | tf_op jit(solution)/shard_map/assemble_up/pallas_call | solution.py:843
  423.7 7.8 %collective-permute-done.53.refs_3_ = bf16[2,4,112,768]{3,2,1,0:T(8,128)(2,1)} collective-permute-done((bf16[2,4,112,768]{3,2,1,0:T(8,128)(2,1)}, bf16[2,4,112,768]{3,2,1,0:T(8,128)(2,1)}, u32[]{:S(2)}, u32[]{:S(2)}) %collective-permute-start.53) | collective-permute-done | bytes 1376288 | tf_op jit(solution)/shard_map/ppermute | solution.py:706
  431.5 7.6 %assemble_attn.1 = (f32[768,768]{1,0:T(8,128)}, f32[768,768]{1,0:T(8,128)}, f32[768,768]{1,0:T(8,128)}, f32[768,384]{1,0:T(8,128)}, f32[384,384]{1,0:T(8,128)}, ...) custom-call(s32[3]{0:T(128)} %pad_add_fusion.s_ref, ...), custom_call_target="tpu_custom_call" | custom-call | flops 18400000000 | bytes 1 | tf_op jit(solution)/shard_map/assemble_attn/pallas_call | solution.py:843
  (112 shorter events, 72.7 us)
Async XLA Ops:
  0.7 9.9 %collective-permute-start = (bf16[1024,768]{1,0:T(8,128)(2,1)}, bf16[1024,768]{1,0:T(8,128)(2,1)}, u32[]{:S(2)}, u32[]{:S(2)}) collective-permute-start(bf16[1024,768]{1,0:T(8,128)(2,1)} %bitcast.46), channel_id=1, source_target_pairs={{0,16},{16,0},{1,17},{17,1},{2,18},{18,2},{3,19},{19,3},{4,20},{20... | collective-permute-start | bytes 4718600 | tf_op jit(solution)/shard_map/ppermute | solution.py:931
  1.7 8.8 %collective-permute-start.5 = (bf16[768,768]{1,0:T(8,128)(2,1)}, bf16[768,768]{1,0:T(8,128)(2,1)}, u32[]{:S(2)}, u32[]{:S(2)}) collective-permute-start(bf16[768,768]{1,0:T(8,128)(2,1)} %bitcast.66), channel_id=1, source_target_pairs={{0,16},{16,0},{1,17},{17,1},{2,18},{18,2},{3,19},{19,3},{4,20},{20... | collective-permute-start | bytes 3538952 | tf_op jit(solution)/shard_map/ppermute | solution.py:931
  9.3 18.7 %collective-permute-start.7 = (bf16[3072,768]{1,0:T(8,128)(2,1)}, bf16[3072,768]{1,0:T(8,128)(2,1)}, u32[]{:S(2)}, u32[]{:S(2)}) collective-permute-start(bf16[3072,768]{1,0:T(8,128)(2,1)} %bitcast.40), channel_id=1, source_target_pairs={{0,16},{16,0},{1,17},{17,1},{2,18},{18,2},{3,19},{19,3},{4,20},{20... | collective-permute-start | bytes 14155784 | tf_op jit(solution)/shard_map/ppermute | solution.py:931
  9.4 18.6 %collective-permute-start.6 = (bf16[768,3072]{1,0:T(8,128)(2,1)}, bf16[768,3072]{1,0:T(8,128)(2,1)}, u32[]{:S(2)}, u32[]{:S(2)}) collective-permute-start(bf16[768,3072]{1,0:T(8,128)(2,1)} %bitcast.50), channel_id=1, source_target_pairs={{0,16},{16,0},{1,17},{17,1},{2,18},{18,2},{3,19},{19,3},{4,20},{20... | collective-permute-start | bytes 14155784 | tf_op jit(solution)/shard_map/ppermute | solution.py:931
  27.6 75.0 %collective-permute-start.8 = (bf16[2,512,768]{2,1,0:T(8,128)(2,1)}, bf16[2,512,768]{2,1,0:T(8,128)(2,1)}, u32[]{:S(2)}, u32[]{:S(2)}) collective-permute-start(bf16[2,512,768]{2,1,0:T(8,128)(2,1)} %get-tuple-element.171), channel_id=1, source_target_pairs={{0,16},{16,0},{1,17},{17,1},{2,18},{18,2},{3,19},{19,3},{4,20},{20... | collective-permute-start | bytes 4718600 | tf_op jit(solution)/shard_map/ppermute | solution.py:931
  63.7 38.9 %collective-permute-start.9 = (bf16[2,512,768]{2,1,0:T(8,128)(2,1)}, bf16[2,512,768]{2,1,0:T(8,128)(2,1)}, u32[]{:S(2)}, u32[]{:S(2)}) collective-permute-start(bf16[2,512,768]{2,1,0:T(8,128)(2,1)} %get-tuple-element.172), channel_id=1, source_target_pairs={{0,16},{16,0},{1,17},{17,1},{2,18},{18,2},{3,19},{19,3},{4,20},{20... | collective-permute-start | bytes 4718600 | tf_op jit(solution)/shard_map/ppermute | solution.py:931
  63.9 38.7 %collective-permute-start.10 = (bf16[2,512,1536]{2,1,0:T(8,128)(2,1)}, bf16[2,512,1536]{2,1,0:T(8,128)(2,1)}, u32[]{:S(2)}, u32[]{:S(2)}) collective-permute-start(bf16[2,512,1536]{2,1,0:T(8,128)(2,1)} %get-tuple-element.174), channel_id=1, source_target_pairs={{0,16},{16,0},{1,17},{17,1},{2,18},{18,2},{3,19},{19,3},{4,20},{20... | collective-permute-start | bytes 9437192 | tf_op jit(solution)/shard_map/ppermute | solution.py:931
  102.2 18.3 %collective-permute-start.12 = (bf16[2576,768]{1,0:T(8,128)(2,1)}, bf16[2576,768]{1,0:T(8,128)(2,1)}, u32[]{:S(2)}, u32[]{:S(2)}) collective-permute-start(bf16[2576,768]{1,0:T(8,128)(2,1)} %get-tuple-element.166.own_ref.x_ref.dz_ref), channel_id=1, source_target_pairs={{0,16},{16,0},{1,17},{17,1},{2,18},{18,2},{3,19},{19,3},{4,20},{20... | collective-permute-start | bytes 11870216 | tf_op jit(solution)/shard_map/ppermute | solution.py:931
  117.8 20.2 %collective-permute-start.13 = (bf16[1,8,96,768]{3,2,1,0:T(8,128)(2,1)}, bf16[1,8,96,768]{3,2,1,0:T(8,128)(2,1)}, u32[]{:S(2)}, u32[]{:S(2)}) collective-permute-start(bf16[1,8,96,768]{3,2,1,0:T(8,128)(2,1)} %bitcast.74), channel_id=1, source_target_pairs={{0,1},{1,0},{2,3},{3,2},{4,5},{5,4},{6,7},{7,6},{8,9},{9,8},{10,11... | collective-permute-start | bytes 3538952 | tf_op jit(solution)/shard_map/ppermute | solution.py:706
  120.4 55.3 %collective-permute-start.15 = (bf16[1,8,96,768]{3,2,1,0:T(8,128)(2,1)}, bf16[1,8,96,768]{3,2,1,0:T(8,128)(2,1)}, u32[]{:S(2)}, u32[]{:S(2)}) collective-permute-start(bf16[1,8,96,768]{3,2,1,0:T(8,128)(2,1)} %bitcast.72), channel_id=1, source_target_pairs={{0,1},{1,0},{2,3},{3,2},{4,5},{5,4},{6,7},{7,6},{8,9},{9,8},{10,11... | collective-permute-start | bytes 3538952 | tf_op jit(solution)/shard_map/ppermute | solution.py:706
  136.0 43.1 %collective-permute-start.16 = (bf16[1,8,112,768]{3,2,1,0:T(8,128)(2,1)}, bf16[1,8,112,768]{3,2,1,0:T(8,128)(2,1)}, u32[]{:S(2)}, u32[]{:S(2)}) collective-permute-start(bf16[1,8,112,768]{3,2,1,0:T(8,128)(2,1)} %bitcast.54), channel_id=1, source_target_pairs={{0,1},{1,0},{2,3},{3,2},{4,5},{5,4},{6,7},{7,6},{8,9},{9,8},{10,11... | collective-permute-start | bytes 4128776 | tf_op jit(solution)/shard_map/ppermute | solution.py:706
  137.8 45.6 %collective-permute-start.17 = (bf16[1,8,96,768]{3,2,1,0:T(8,128)(2,1)}, bf16[1,8,96,768]{3,2,1,0:T(8,128)(2,1)}, u32[]{:S(2)}, u32[]{:S(2)}) collective-permute-start(bf16[1,8,96,768]{3,2,1,0:T(8,128)(2,1)} %bitcast.71), channel_id=1, source_target_pairs={{0,1},{1,0},{2,3},{3,2},{4,5},{5,4},{6,7},{7,6},{8,9},{9,8},{10,11... | collective-permute-start | bytes 3538952 | tf_op jit(solution)/shard_map/ppermute | solution.py:706
  141.4 55.6 %collective-permute-start.19 = (bf16[1,4,96,768]{3,2,1,0:T(8,128)(2,1)}, bf16[1,4,96,768]{3,2,1,0:T(8,128)(2,1)}, u32[]{:S(2)}, u32[]{:S(2)}) collective-permute-start(bf16[1,4,96,768]{3,2,1,0:T(8,128)(2,1)} %get-tuple-element.190), channel_id=1, source_target_pairs={{0,2},{1,3},{2,0},{3,1},{4,6},{5,7},{6,4},{7,5},{8,10},{9,11},{10,... | collective-permute-start | bytes 1769480 | tf_op jit(solution)/shard_map/ppermute | solution.py:706
  175.7 28.8 %collective-permute-start.14 = (bf16[2576,768]{1,0:T(8,128)(2,1)}, bf16[2576,768]{1,0:T(8,128)(2,1)}, u32[]{:S(2)}, u32[]{:S(2)}) collective-permute-start(bf16[2576,768]{1,0:T(8,128)(2,1)} %get-tuple-element.196.own_ref), channel_id=1, source_target_pairs={{0,16},{16,0},{1,17},{17,1},{2,18},{18,2},{3,19},{19,3},{4,20},{20... | collective-permute-start | bytes 11870216 | tf_op jit(solution)/shard_map/ppermute | solution.py:931
  178.7 17.5 %collective-permute-start.20 = (bf16[1,4,96,768]{3,2,1,0:T(8,128)(2,1)}, bf16[1,4,96,768]{3,2,1,0:T(8,128)(2,1)}, u32[]{:S(2)}, u32[]{:S(2)}) collective-permute-start(bf16[1,4,96,768]{3,2,1,0:T(8,128)(2,1)} %get-tuple-element.202), channel_id=1, source_target_pairs={{0,2},{1,3},{2,0},{3,1},{4,6},{5,7},{6,4},{7,5},{8,10},{9,11},{10,... | collective-permute-start | bytes 1769480 | tf_op jit(solution)/shard_map/ppermute | solution.py:706
  186.4 10.6 %collective-permute-start.21 = (bf16[1,4,96,768]{3,2,1,0:T(8,128)(2,1)}, bf16[1,4,96,768]{3,2,1,0:T(8,128)(2,1)}, u32[]{:S(2)}, u32[]{:S(2)}) collective-permute-start(bf16[1,4,96,768]{3,2,1,0:T(8,128)(2,1)} %get-tuple-element.206), channel_id=1, source_target_pairs={{0,2},{1,3},{2,0},{3,1},{4,6},{5,7},{6,4},{7,5},{8,10},{9,11},{10,... | collective-permute-start | bytes 1769480 | tf_op jit(solution)/shard_map/ppermute | solution.py:706
  187.3 25.2 %collective-permute-start.22 = (bf16[1,4,112,768]{3,2,1,0:T(8,128)(2,1)}, bf16[1,4,112,768]{3,2,1,0:T(8,128)(2,1)}, u32[]{:S(2)}, u32[]{:S(2)}) collective-permute-start(bf16[1,4,112,768]{3,2,1,0:T(8,128)(2,1)} %get-tuple-element.204), channel_id=1, source_target_pairs={{0,2},{1,3},{2,0},{3,1},{4,6},{5,7},{6,4},{7,5},{8,10},{9,11},{10,... | collective-permute-start | bytes 2064392 | tf_op jit(solution)/shard_map/ppermute | solution.py:706
  196.2 19.4 %collective-permute-start.23 = (bf16[1,8,96,768]{3,2,1,0:T(8,128)(2,1)}, bf16[1,8,96,768]{3,2,1,0:T(8,128)(2,1)}, u32[]{:S(2)}, u32[]{:S(2)}) collective-permute-start(bf16[1,8,96,768]{3,2,1,0:T(8,128)(2,1)} %bitcast.73), channel_id=1, source_target_pairs={{0,1},{1,0},{2,3},{3,2},{4,5},{5,4},{6,7},{7,6},{8,9},{9,8},{10,11... | collective-permute-start | bytes 3538952 | tf_op jit(solution)/shard_map/ppermute | solution.py:706
  202.3 23.0 %collective-permute-start.24 = (bf16[3,2,96,768]{3,2,1,0:T(8,128)(2,1)}, bf16[3,2,96,768]{3,2,1,0:T(8,128)(2,1)}, u32[]{:S(2)}, u32[]{:S(2)}) collective-permute-start(bf16[3,2,96,768]{3,2,1,0:T(8,128)(2,1)} %get-tuple-element.214), channel_id=1, source_target_pairs={{0,4},{1,5},{2,6},{3,7},{4,0},{5,1},{6,2},{7,3},{8,12},{9,13},{10,... | collective-permute-start | bytes 2654216 | tf_op jit(solution)/shard_map/ppermute | solution.py:706
  214.9 19.0 %collective-permute-start.25 = (bf16[1,2,112,768]{3,2,1,0:T(8,128)(2,1)}, bf16[1,2,112,768]{3,2,1,0:T(8,128)(2,1)}, u32[]{:S(2)}, u32[]{:S(2)}) collective-permute-start(bf16[1,2,112,768]{3,2,1,0:T(8,128)(2,1)} %get-tuple-element.223), channel_id=1, source_target_pairs={{0,4},{1,5},{2,6},{3,7},{4,0},{5,1},{6,2},{7,3},{8,12},{9,13},{10,... | collective-permute-start | bytes 1032200 | tf_op jit(solution)/shard_map/ppermute | solution.py:706
  218.6 17.3 %collective-permute-start.26 = (bf16[1,4,96,768]{3,2,1,0:T(8,128)(2,1)}, bf16[1,4,96,768]{3,2,1,0:T(8,128)(2,1)}, u32[]{:S(2)}, u32[]{:S(2)}) collective-permute-start(bf16[1,4,96,768]{3,2,1,0:T(8,128)(2,1)} %get-tuple-element.228), channel_id=1, source_target_pairs={{0,2},{1,3},{2,0},{3,1},{4,6},{5,7},{6,4},{7,5},{8,10},{9,11},{10,... | collective-permute-start | bytes 1769480 | tf_op jit(solution)/shard_map/ppermute | solution.py:706
  230.0 40.8 %collective-permute-start.30 = (bf16[3,1,96,768]{3,2,1,0:T(8,128)(2,1)}, bf16[3,1,96,768]{3,2,1,0:T(8,128)(2,1)}, u32[]{:S(2)}, u32[]{:S(2)}) collective-permute-start(bf16[3,1,96,768]{3,2,1,0:T(8,128)(2,1)} %get-tuple-element.230), channel_id=1, source_target_pairs={{0,8},{1,9},{2,10},{3,11},{4,12},{5,13},{6,14},{7,15},{8,0},{9,1},... | collective-permute-start | bytes 1327112 | tf_op jit(solution)/shard_map/ppermute | solution.py:706
  232.5 18.6 %collective-permute-start.27 = (bf16[1,8,112,768]{3,2,1,0:T(8,128)(2,1)}, bf16[1,8,112,768]{3,2,1,0:T(8,128)(2,1)}, u32[]{:S(2)}, u32[]{:S(2)}) collective-permute-start(bf16[1,8,112,768]{3,2,1,0:T(8,128)(2,1)} %bitcast.55), channel_id=1, source_target_pairs={{0,1},{1,0},{2,3},{3,2},{4,5},{5,4},{6,7},{7,6},{8,9},{9,8},{10,11... | collective-permute-start | bytes 4128776 | tf_op jit(solution)/shard_map/ppermute | solution.py:706
  238.3 17.5 %collective-permute-start.28 = (bf16[1,2,96,768]{3,2,1,0:T(8,128)(2,1)}, bf16[1,2,96,768]{3,2,1,0:T(8,128)(2,1)}, u32[]{:S(2)}, u32[]{:S(2)}) collective-permute-start(bf16[1,2,96,768]{3,2,1,0:T(8,128)(2,1)} %get-tuple-element.234), channel_id=1, source_target_pairs={{0,4},{1,5},{2,6},{3,7},{4,0},{5,1},{6,2},{7,3},{8,12},{9,13},{10,... | collective-permute-start | bytes 884744 | tf_op jit(solution)/shard_map/ppermute | solution.py:706
  254.3 11.3 %collective-permute-start.29 = (bf16[1,4,112,768]{3,2,1,0:T(8,128)(2,1)}, bf16[1,4,112,768]{3,2,1,0:T(8,128)(2,1)}, u32[]{:S(2)}, u32[]{:S(2)}) collective-permute-start(bf16[1,4,112,768]{3,2,1,0:T(8,128)(2,1)} %get-tuple-element.238), channel_id=1, source_target_pairs={{0,2},{1,3},{2,0},{3,1},{4,6},{5,7},{6,4},{7,5},{8,10},{9,11},{10,... | collective-permute-start | bytes 2064392 | tf_op jit(solution)/shard_map/ppermute | solution.py:706
  257.7 13.1 %collective-permute-start.34 = (bf16[1,1,96,768]{3,2,1,0:T(8,128)(2,1)}, bf16[1,1,96,768]{3,2,1,0:T(8,128)(2,1)}, u32[]{:S(2)}, u32[]{:S(2)}) collective-permute-start(bf16[1,1,96,768]{3,2,1,0:T(8,128)(2,1)} %get-tuple-element.240), channel_id=1, source_target_pairs={{0,8},{1,9},{2,10},{3,11},{4,12},{5,13},{6,14},{7,15},{8,0},{9,1},... | collective-permute-start | bytes 442376 | tf_op jit(solution)/shard_map/ppermute | solution.py:706
  267.9 11.1 %collective-permute-start.32 = (bf16[1,2,112,768]{3,2,1,0:T(8,128)(2,1)}, bf16[1,2,112,768]{3,2,1,0:T(8,128)(2,1)}, u32[]{:S(2)}, u32[]{:S(2)}) collective-permute-start(bf16[1,2,112,768]{3,2,1,0:T(8,128)(2,1)} %get-tuple-element.245), channel_id=1, source_target_pairs={{0,4},{1,5},{2,6},{3,7},{4,0},{5,1},{6,2},{7,3},{8,12},{9,13},{10,... | collective-permute-start | bytes 1032200 | tf_op jit(solution)/shard_map/ppermute | solution.py:706
  270.4 8.5 %collective-permute-start.31 = (bf16[1,1,112,768]{3,2,1,0:T(8,128)(2,1)}, bf16[1,1,112,768]{3,2,1,0:T(8,128)(2,1)}, u32[]{:S(2)}, u32[]{:S(2)}) collective-permute-start(bf16[1,1,112,768]{3,2,1,0:T(8,128)(2,1)} %get-tuple-element.232), channel_id=1, source_target_pairs={{0,8},{1,9},{2,10},{3,11},{4,12},{5,13},{6,14},{7,15},{8,0},{9,1},... | collective-permute-start | bytes 516104 | tf_op jit(solution)/shard_map/ppermute | solution.py:706
  273.1 9.2 %collective-permute-start.35 = (bf16[1,1,96,768]{3,2,1,0:T(8,128)(2,1)}, bf16[1,1,96,768]{3,2,1,0:T(8,128)(2,1)}, u32[]{:S(2)}, u32[]{:S(2)}) collective-permute-start(bf16[1,1,96,768]{3,2,1,0:T(8,128)(2,1)} %get-tuple-element.289), channel_id=1, source_target_pairs={{0,16},{16,0},{1,17},{17,1},{2,18},{18,2},{3,19},{19,3},{4,20},{20... | collective-permute-start | bytes 442376 | tf_op jit(solution)/shard_map/ppermute | solution.py:931
  280.9 13.9 %collective-permute-start.33 = (bf16[1,1,112,768]{3,2,1,0:T(8,128)(2,1)}, bf16[1,1,112,768]{3,2,1,0:T(8,128)(2,1)}, u32[]{:S(2)}, u32[]{:S(2)}) collective-permute-start(bf16[1,1,112,768]{3,2,1,0:T(8,128)(2,1)} %get-tuple-element.247), channel_id=1, source_target_pairs={{0,8},{1,9},{2,10},{3,11},{4,12},{5,13},{6,14},{7,15},{8,0},{9,1},... | collective-permute-start | bytes 516104 | tf_op jit(solution)/shard_map/ppermute | solution.py:706
  283.9 15.2 %collective-permute-start.36 = (bf16[2,1,96,768]{3,2,1,0:T(8,128)(2,1)}, bf16[2,1,96,768]{3,2,1,0:T(8,128)(2,1)}, u32[]{:S(2)}, u32[]{:S(2)}) collective-permute-start(bf16[2,1,96,768]{3,2,1,0:T(8,128)(2,1)} %bitcast.82), channel_id=1, source_target_pairs={{0,8},{1,9},{2,10},{3,11},{4,12},{5,13},{6,14},{7,15},{8,0},{9,1},... | collective-permute-start | bytes 884744 | tf_op jit(solution)/shard_map/ppermute | solution.py:706
  285.6 17.9 %collective-permute-start.37 = (bf16[1,1,96,768]{3,2,1,0:T(8,128)(2,1)}, bf16[1,1,96,768]{3,2,1,0:T(8,128)(2,1)}, u32[]{:S(2)}, u32[]{:S(2)}) collective-permute-start(bf16[1,1,96,768]{3,2,1,0:T(8,128)(2,1)} %get-tuple-element.287), channel_id=1, source_target_pairs={{0,16},{16,0},{1,17},{17,1},{2,18},{18,2},{3,19},{19,3},{4,20},{20... | collective-permute-start | bytes 442376 | tf_op jit(solution)/shard_map/ppermute | solution.py:931
  296.9 19.9 %collective-permute-start.39 = (bf16[1,1,112,768]{3,2,1,0:T(8,128)(2,1)}, bf16[1,1,112,768]{3,2,1,0:T(8,128)(2,1)}, u32[]{:S(2)}, u32[]{:S(2)}) collective-permute-start(bf16[1,1,112,768]{3,2,1,0:T(8,128)(2,1)} %get-tuple-element.290), channel_id=1, source_target_pairs={{0,16},{16,0},{1,17},{17,1},{2,18},{18,2},{3,19},{19,3},{4,20},{20... | collective-permute-start | bytes 516104 | tf_op jit(solution)/shard_map/ppermute | solution.py:931
  302.0 10.2 %collective-permute-start.38 = (bf16[2,2,96,768]{3,2,1,0:T(8,128)(2,1)}, bf16[2,2,96,768]{3,2,1,0:T(8,128)(2,1)}, u32[]{:S(2)}, u32[]{:S(2)}) collective-permute-start(bf16[2,2,96,768]{3,2,1,0:T(8,128)(2,1)} %merge.10.a_ref), channel_id=1, source_target_pairs={{0,2},{1,3},{2,0},{3,1},{4,6},{5,7},{6,4},{7,5},{8,10},{9,11},{10,... | collective-permute-start | bytes 1769480 | tf_op jit(solution)/shard_map/ppermute | solution.py:706
  305.2 16.1 %collective-permute-start.40 = (bf16[2,1,96,768]{3,2,1,0:T(8,128)(2,1)}, bf16[2,1,96,768]{3,2,1,0:T(8,128)(2,1)}, u32[]{:S(2)}, u32[]{:S(2)}) collective-permute-start(bf16[2,1,96,768]{3,2,1,0:T(8,128)(2,1)} %bitcast.84), channel_id=1, source_target_pairs={{0,8},{1,9},{2,10},{3,11},{4,12},{5,13},{6,14},{7,15},{8,0},{9,1},... | collective-permute-start | bytes 884744 | tf_op jit(solution)/shard_map/ppermute | solution.py:706
  315.4 36.6 %collective-permute-start.42 = (bf16[2,4,96,768]{3,2,1,0:T(8,128)(2,1)}, bf16[2,4,96,768]{3,2,1,0:T(8,128)(2,1)}, u32[]{:S(2)}, u32[]{:S(2)}) collective-permute-start(bf16[2,4,96,768]{3,2,1,0:T(8,128)(2,1)} %merge.12.refs_0_), channel_id=1, source_target_pairs={{0,4},{1,5},{2,6},{3,7},{4,0},{5,1},{6,2},{7,3},{8,12},{9,13},{10,... | collective-permute-start | bytes 3538952 | tf_op jit(solution)/shard_map/ppermute | solution.py:706
  315.4 36.6 %collective-permute-start.43 = (bf16[2,4,96,768]{3,2,1,0:T(8,128)(2,1)}, bf16[2,4,96,768]{3,2,1,0:T(8,128)(2,1)}, u32[]{:S(2)}, u32[]{:S(2)}) collective-permute-start(bf16[2,4,96,768]{3,2,1,0:T(8,128)(2,1)} %merge.12.refs_0_), channel_id=1, source_target_pairs={{0,1},{1,0},{2,3},{3,2},{4,5},{5,4},{6,7},{7,6},{8,9},{9,8},{10,11... | collective-permute-start | bytes 3538952 | tf_op jit(solution)/shard_map/ppermute | solution.py:706
  318.5 27.6 %collective-permute-start.41 = (bf16[2,1,112,768]{3,2,1,0:T(8,128)(2,1)}, bf16[2,1,112,768]{3,2,1,0:T(8,128)(2,1)}, u32[]{:S(2)}, u32[]{:S(2)}) collective-permute-start(bf16[2,1,112,768]{3,2,1,0:T(8,128)(2,1)} %bitcast.80), channel_id=1, source_target_pairs={{0,8},{1,9},{2,10},{3,11},{4,12},{5,13},{6,14},{7,15},{8,0},{9,1},... | collective-permute-start | bytes 1032200 | tf_op jit(solution)/shard_map/ppermute | solution.py:706
  324.2 27.8 %collective-permute-start.44 = (bf16[2,2,96,768]{3,2,1,0:T(8,128)(2,1)}, bf16[2,2,96,768]{3,2,1,0:T(8,128)(2,1)}, u32[]{:S(2)}, u32[]{:S(2)}) collective-permute-start(bf16[2,2,96,768]{3,2,1,0:T(8,128)(2,1)} %merge.14.a_ref), channel_id=1, source_target_pairs={{0,2},{1,3},{2,0},{3,1},{4,6},{5,7},{6,4},{7,5},{8,10},{9,11},{10,... | collective-permute-start | bytes 1769480 | tf_op jit(solution)/shard_map/ppermute | solution.py:706
  349.1 14.4 %collective-permute-start.45 = (bf16[2,2,112,768]{3,2,1,0:T(8,128)(2,1)}, bf16[2,2,112,768]{3,2,1,0:T(8,128)(2,1)}, u32[]{:S(2)}, u32[]{:S(2)}) collective-permute-start(bf16[2,2,112,768]{3,2,1,0:T(8,128)(2,1)} %merge.15.a_ref), channel_id=1, source_target_pairs={{0,2},{1,3},{2,0},{3,1},{4,6},{5,7},{6,4},{7,5},{8,10},{9,11},{10,... | collective-permute-start | bytes 2064392 | tf_op jit(solution)/shard_map/ppermute | solution.py:706
  355.2 29.2 %collective-permute-start.46 = (bf16[2,4,96,768]{3,2,1,0:T(8,128)(2,1)}, bf16[2,4,96,768]{3,2,1,0:T(8,128)(2,1)}, u32[]{:S(2)}, u32[]{:S(2)}) collective-permute-start(bf16[2,4,96,768]{3,2,1,0:T(8,128)(2,1)} %merge.16.refs_0_), channel_id=1, source_target_pairs={{0,4},{1,5},{2,6},{3,7},{4,0},{5,1},{6,2},{7,3},{8,12},{9,13},{10,... | collective-permute-start | bytes 3538952 | tf_op jit(solution)/shard_map/ppermute | solution.py:706
  357.3 27.1 %collective-permute-start.47 = (bf16[2,4,96,768]{3,2,1,0:T(8,128)(2,1)}, bf16[2,4,96,768]{3,2,1,0:T(8,128)(2,1)}, u32[]{:S(2)}, u32[]{:S(2)}) collective-permute-start(bf16[2,4,96,768]{3,2,1,0:T(8,128)(2,1)} %merge.16.refs_0_), channel_id=1, source_target_pairs={{0,1},{1,0},{2,3},{3,2},{4,5},{5,4},{6,7},{7,6},{8,9},{9,8},{10,11... | collective-permute-start | bytes 3538952 | tf_op jit(solution)/shard_map/ppermute | solution.py:706
  359.7 35.4 %collective-permute-start.49 = (bf16[2,4,96,768]{3,2,1,0:T(8,128)(2,1)}, bf16[2,4,96,768]{3,2,1,0:T(8,128)(2,1)}, u32[]{:S(2)}, u32[]{:S(2)}) collective-permute-start(bf16[2,4,96,768]{3,2,1,0:T(8,128)(2,1)} %collective-permute-done.42.refs_1_), channel_id=1, source_target_pairs={{0,1},{1,0},{2,3},{3,2},{4,5},{5,4},{6,7},{7,6},{8,9},{9,8},{10,11... | collective-permute-start | bytes 3538952 | tf_op jit(solution)/shard_map/ppermute | solution.py:706
  366.8 46.1 %collective-permute-start.50 = (bf16[2,4,112,768]{3,2,1,0:T(8,128)(2,1)}, bf16[2,4,112,768]{3,2,1,0:T(8,128)(2,1)}, u32[]{:S(2)}, u32[]{:S(2)}) collective-permute-start(bf16[2,4,112,768]{3,2,1,0:T(8,128)(2,1)} %merge.17.refs_0_), channel_id=1, source_target_pairs={{0,4},{1,5},{2,6},{3,7},{4,0},{5,1},{6,2},{7,3},{8,12},{9,13},{10,... | collective-permute-start | bytes 4128776 | tf_op jit(solution)/shard_map/ppermute | solution.py:706
  371.2 41.7 %collective-permute-start.51 = (bf16[2,4,112,768]{3,2,1,0:T(8,128)(2,1)}, bf16[2,4,112,768]{3,2,1,0:T(8,128)(2,1)}, u32[]{:S(2)}, u32[]{:S(2)}) collective-permute-start(bf16[2,4,112,768]{3,2,1,0:T(8,128)(2,1)} %merge.17.refs_0_), channel_id=1, source_target_pairs={{0,1},{1,0},{2,3},{3,2},{4,5},{5,4},{6,7},{7,6},{8,9},{9,8},{10,11... | collective-permute-start | bytes 4128776 | tf_op jit(solution)/shard_map/ppermute | solution.py:706
  392.3 21.2 %collective-permute-start.48 = (bf16[512,768]{1,0:T(8,128)(2,1)}, bf16[512,768]{1,0:T(8,128)(2,1)}, u32[]{:S(2)}, u32[]{:S(2)}) collective-permute-start(bf16[512,768]{1,0:T(8,128)(2,1)} %feed_down.1), channel_id=1, source_target_pairs={{0,16},{1,17},{2,18},{3,19},{4,20},{5,21},{6,22},{7,23},{8,24},{9,... | collective-permute-start | bytes 2359304 | tf_op jit(solution)/shard_map/ppermute | solution.py:1007
  394.5 22.4 %collective-permute-start.52 = (bf16[2,4,96,768]{3,2,1,0:T(8,128)(2,1)}, bf16[2,4,96,768]{3,2,1,0:T(8,128)(2,1)}, u32[]{:S(2)}, u32[]{:S(2)}) collective-permute-start(bf16[2,4,96,768]{3,2,1,0:T(8,128)(2,1)} %collective-permute-done.46.refs_1_), channel_id=1, source_target_pairs={{0,1},{1,0},{2,3},{3,2},{4,5},{5,4},{6,7},{7,6},{8,9},{9,8},{10,11... | collective-permute-start | bytes 3538952 | tf_op jit(solution)/shard_map/ppermute | solution.py:706
  412.9 18.6 %collective-permute-start.53 = (bf16[2,4,112,768]{3,2,1,0:T(8,128)(2,1)}, bf16[2,4,112,768]{3,2,1,0:T(8,128)(2,1)}, u32[]{:S(2)}, u32[]{:S(2)}) collective-permute-start(bf16[2,4,112,768]{3,2,1,0:T(8,128)(2,1)} %collective-permute-done.50.refs_1_), channel_id=1, source_target_pairs={{0,1},{1,0},{2,3},{3,2},{4,5},{5,4},{6,7},{7,6},{8,9},{9,8},{10,11... | collective-permute-start | bytes 4128776 | tf_op jit(solution)/shard_map/ppermute | solution.py:706
  (6 other events, 38.5 us)
